TPU v7x, 32 devices: a whole 2x2x4 slice. The times are simulated.
32 devices in a mesh: blk: 32 (over z, y, x, core).
Axes of the slice: x: 2, y: 2, z: 4, core: 2. Of those that a mesh axis runs over, the one named last changes fastest.
Arguments:
- images: bfloat16 [12800, 768], P('blk'), may hold values from -6 to 6
- captions: bfloat16 [20480, 768], P('blk'), may hold values from -6 to 6
- img_gain1: bfloat16 [768], replicated, may hold values from 0.5 to 1.5
- img_bias1: bfloat16 [768], replicated, may hold values from -3 to 3
- img_qkv: bfloat16 [1769472], P('blk'), may hold values from -0.21875 to 0.21875
- img_out: bfloat16 [589824], P('blk'), may hold values from -0.5 to 0.5
- img_gain2: bfloat16 [768], replicated, may hold values from 0.5 to 1.5
- img_bias2: bfloat16 [768], replicated, may hold values from -3 to 3
- img_up: bfloat16 [2359296], P('blk'), may hold values from -0.21875 to 0.21875
- img_down: bfloat16 [2359296], P('blk'), may hold values from -0.109375 to 0.109375
- txt_gain1: float32 [768], replicated, may hold values from 0.5 to 1.5
- txt_bias1: float32 [768], replicated, may hold values from -3 to 3
- txt_qkv: bfloat16 [768, 2304], replicated, may hold values from -0.21875 to 0.21875
- txt_out: bfloat16 [768, 768], replicated, may hold values from -0.4375 to 0.4375
- txt_gain2: float32 [768], replicated, may hold values from 0.5 to 1.5
- txt_bias2: float32 [768], replicated, may hold values from -3 to 3
- txt_up: bfloat16 [768, 3072], replicated, may hold values from -0.21875 to 0.21875
- txt_down: bfloat16 [3072, 768], replicated, may hold values from -0.109375 to 0.109375
- counts: int32 [256], P('blk'), may hold values from 1 to 5, as said below
- matches: int32 [1280, 256], P('blk'), may hold values 0 or 1
Outputs:
- loss: float32 [], replicated
- caption_grad: float32 [20480, 768], P('blk')
- grad_gain1: float32 [768], replicated
- grad_bias1: float32 [768], replicated
- grad_qkv: float32 [1769472], P('blk')
- grad_out: float32 [589824], P('blk')
- grad_gain2: float32 [768], replicated
- grad_bias2: float32 [768], replicated
- grad_up: float32 [2359296], P('blk')
- grad_down: float32 [2359296], P('blk')
Inputs may be any that keep to these rules, and one draw needn't show every extreme that they name: `counts`: each image has 1 to 5 captions; in every draw all 8 images of one block have 5, so that block's 40 caption slots are all live.
All inputs are finite; a program needn't handle non-finite values. No bound on the sum of `matches` on one device may be relied on, other than what follows from the above.
Results may differ from a plain program's by a relative error of at most 0.015.
Values may be sent and summed in bfloat16 or wider, within the bound.
No kernel may reach another device: no remote copies, remote signals or barrier semaphores. Data moves between devices by JAX's collectives and lax.ppermute only.
A program may use at most 192 MiB of HBM per device.

v0:
```python
import functools

import jax
import jax.numpy as jnp
from jax import lax
from jax.experimental import pallas as pl
from jax.experimental.pallas import tpu as pltpu
from jax.sharding import PartitionSpec as P

D = 768
FF = 3072
HEAD = 64
HEADS = D // HEAD
IMG_LEN = 50
TXT_LEN = 16
AXIS = "blk"

norm_eps = 1e-06
logit_scale = 50.0
f32 = jnp.float32
bf16 = jnp.bfloat16


def swapped(value, mask):
    peers = lax.axis_size(AXIS)
    return lax.ppermute(value, AXIS, [(i, i ^ mask) for i in range(peers)])


def bit_masks():
    peers = lax.axis_size(AXIS)
    return [1 << k for k in range(peers.bit_length() - 1)]


def joined(held, other, mask, outer=None):
    upper = (lax.axis_index(AXIS) & mask) > 0
    first = jnp.where(upper, other, held)
    second = jnp.where(upper, held, other)
    outer = held.shape[0] if outer is None else outer
    parts = [part.reshape((outer, -1) + held.shape[1:]) for part in (first, second)]
    return jnp.stack(parts, axis=1).reshape((-1,) + held.shape[1:])


def spread(block):
    peers = lax.axis_size(AXIS)
    copies = jnp.broadcast_to(block[None], (peers,) + block.shape)
    return lax.all_to_all(copies, AXIS, split_axis=0, concat_axis=0, tiled=True)


def stage_orders():
    masks = bit_masks()
    head, tail = masks[:-2], masks[-2:]
    order_a = list(head)
    order_b = list(head)
    for k in range(1, len(head) - 1, 2):
        order_b[k], order_b[k + 1] = order_b[k + 1], order_b[k]
    return order_a, order_b, tail


def row_order(bits):
    peers = lax.axis_size(AXIS)
    own = lax.axis_index(AXIS)
    per = D // peers
    places = lax.iota(jnp.int32, D)
    block = places // per
    target = jnp.zeros_like(block) + own
    for k, mask in enumerate(bits):
        target = target ^ (((block >> (len(bits) - 1 - k)) & 1) * mask)
    source = target * per + places % per
    return (source[:, None] == lax.iota(jnp.int32, D)[None, :]).astype(bf16)


def gathered_line(shard):
    return jnp.concatenate([shard] + [swapped(shard, mask) for mask in (8, 16, 24)], axis=0)


def diagonal(beside, above):
    half = beside.shape[0] // 2
    return swapped(beside[:half], 4), swapped(above[half:], 2)


def in_turn(first, then):
    return lax.optimization_barrier((first, then))


def placed(order, values):
    return mul_bt(order, values).astype(bf16)


def hand_on(parts, stage):
    order_a, order_b, _ = stage_orders()
    keep_a, send_a, keep_b, send_b = parts
    return keep_a, swapped(send_a, order_a[stage]), keep_b, swapped(send_b, order_b[stage])


def hand_on_last(blocks):
    low, high = stage_orders()[2]
    own, *others = blocks
    return own, [swapped(block, mask) for block, mask in zip(others, (low, high, low | high))]


def sum_last(own, others):
    total = own
    for other in others:
        total = total + other.astype(f32)
    return total


VMEM_BYTES = 56 << 20
TILE = 512


def norm_parts(values):
    average = jnp.mean(values, axis=-1, keepdims=True)
    centred = values - average
    variance = jnp.mean(centred * centred, axis=-1, keepdims=True)
    scale = lax.rsqrt(variance + norm_eps)
    return centred * scale, scale


def norm_back(unit, scale, gain, grad):
    inner = grad * gain
    shift = jnp.mean(inner, axis=-1, keepdims=True)
    along = jnp.mean(inner * unit, axis=-1, keepdims=True)
    return scale * (inner - shift - unit * along)


def mul(lhs, rhs):
    return jnp.dot(lhs, rhs, preferred_element_type=f32)


def mul_bt(lhs, rhs):
    return lax.dot_general(lhs, rhs, (((1,), (1,)), ((), ())), preferred_element_type=f32)


def mul_at(lhs, rhs):
    return lax.dot_general(lhs, rhs, (((0,), (0,)), ((), ())), preferred_element_type=f32)


def params(**more):
    return pltpu.CompilerParams(vmem_limit_bytes=VMEM_BYTES, **more)


def cost(flops, moved, transcendentals=0):
    return pl.CostEstimate(flops=flops, bytes_accessed=moved, transcendentals=transcendentals)


def lane_halves(dtype):
    lane = lax.broadcasted_iota(jnp.int32, (1, 2 * HEAD), 1)
    low = jnp.where(lane < HEAD, 1.0, 0.0)
    return low.astype(dtype), (1.0 - low).astype(dtype)


def two_heads(pair):
    low, high = lane_halves(bf16)
    return jnp.concatenate([pair * low, pair * high], axis=0)


def same_sequence(rows, row0, cols, col0, seq_len):
    row = (lax.broadcasted_iota(jnp.int32, (rows, cols), 0) + row0) // seq_len
    col = (lax.broadcasted_iota(jnp.int32, (rows, cols), 1) + col0) // seq_len
    return row == col


def softmax_down(scores, mask):
    keys = mask.shape[0]
    parts, sums = [], []
    for k in range(2):
        part = jnp.where(mask, scores[k * keys : (k + 1) * keys], -1e30)
        most = jnp.max(part, axis=0, keepdims=True)
        raised = jnp.exp(part - most)
        total = jnp.sum(raised, axis=0, keepdims=True)
        parts.append(raised * (1.0 / total))
        sums.append(most + jnp.log(total))
    return parts, sums


def fold_kernel(keep_a, got_a, keep_b, got_b, *refs):
    outs = refs[-4:]
    half = outs[0].shape[0]
    for k, (kept, got) in enumerate(((keep_a, got_a), (keep_b, got_b))):
        for j in range(2):
            at = slice(j * half, (j + 1) * half)
            outs[2 * k + j][...] = (kept[at, :].astype(f32) + got[at, :].astype(f32)).astype(bf16)


def fold(parts, after=()):
    rows, cols = parts[0].shape
    if rows % 32:
        whole = [
            (kept.astype(f32) + got.astype(f32)).astype(bf16)
            for kept, got in (parts[:2], parts[2:])
        ]
        return [part for one in whole for part in (one[: rows // 2], one[rows // 2 :])]
    tile = 512
    return pl.pallas_call(
        fold_kernel,
        grid=(cols // tile,),
        out_shape=[jax.ShapeDtypeStruct((rows // 2, cols), bf16)] * 4,
        in_specs=[pl.BlockSpec((rows, tile), lambda i: (0, i))] * 4 + anywhere(after),
        out_specs=[pl.BlockSpec((rows // 2, tile), lambda i: (0, i))] * 4,
        compiler_params=params(),
        cost_estimate=cost(2 * rows * cols, 12 * rows * cols),
        name="fold",
    )(*parts, *after)


def fold_last_kernel(keep_a, got_a, keep_b, got_b, *refs):
    own_ref, *outs = refs[-4:]
    rows = own_ref.shape[0]
    cols = keep_a.shape[1]
    for k, (kept, got) in enumerate(((keep_a, got_a), (keep_b, got_b))):
        total = kept[...].astype(f32) + got[...].astype(f32)
        at = slice(k * cols, (k + 1) * cols)
        own_ref[:, at] = total[:rows]
        for j, out in enumerate(outs):
            out[:, at] = total[(j + 1) * rows : (j + 2) * rows].astype(bf16)


def fold_last(parts, after=()):
    rows, cols = parts[0].shape
    shape = (rows // 4, 2 * cols)
    if rows % 32:
        pairs = (parts[:2], parts[2:])
        both = [kept.astype(f32) + got.astype(f32) for kept, got in pairs]
        own, *others = jnp.split(jnp.concatenate(both, axis=1), 4)
        return [own] + [other.astype(bf16) for other in others]
    return pl.pallas_call(
        fold_last_kernel,
        out_shape=[jax.ShapeDtypeStruct(shape, f32)] + [jax.ShapeDtypeStruct(shape, bf16)] * 3,
        in_specs=[pl.BlockSpec(memory_space=pltpu.VMEM)] * 4 + anywhere(after),
        compiler_params=params(),
        cost_estimate=cost(2 * rows * cols, 12 * rows * cols),
        name="fold_last",
    )(*parts, *after)


def anywhere(after):
    return [pl.BlockSpec(memory_space=pl.ANY)] * len(after)


def pair_cols(part, pair):
    start = part * D + pair * 2 * HEAD
    return slice(start, start + 2 * HEAD)


def norm_rows(src, dst, gain, bias, step_rows):
    @pl.loop(0, src.shape[0] // step_rows)
    def _(step):
        at = pl.ds(pl.multiple_of(step * step_rows, step_rows), step_rows)
        unit, _ = norm_parts(src[at, :].astype(f32))
        dst[at, :] = (unit * gain + bias).astype(bf16)


def attend_along(qkv_ref, att_ref, q_rows, k_rows, mask):
    low, high = lane_halves(f32)
    for pair in range(HEADS // 2):
        queries = two_heads(qkv_ref[q_rows, pair_cols(0, pair)] * bf16(HEAD ** (-0.5)))
        scores = mul_bt(queries, qkv_ref[k_rows, pair_cols(1, pair)])
        scores = jnp.where(mask, scores, -1e30)
        raised = jnp.exp(scores - jnp.max(scores, axis=-1, keepdims=True))
        probs = (raised * (1.0 / jnp.sum(raised, axis=-1, keepdims=True))).astype(bf16)
        half = probs.shape[0] // 2
        mixed = mul(probs, qkv_ref[k_rows, pair_cols(2, pair)])
        att_ref[q_rows, pair_cols(0, pair)] = (mixed[:half] * low + mixed[half:] * high).astype(bf16)


def attend(qkv_ref, att_ref, q_rows, k_rows, mask, keep_sums):
    for pair in range(HEADS // 2):
        queries = qkv_ref[q_rows, pair_cols(0, pair)] * bf16(HEAD ** (-0.5))
        scores = mul_bt(two_heads(qkv_ref[k_rows, pair_cols(1, pair)]), queries)
        probs, sums = softmax_down(scores, mask)
        vals = two_heads(qkv_ref[k_rows, pair_cols(2, pair)])
        mixed = mul_at(jnp.concatenate(probs, axis=0).astype(bf16), vals)
        att_ref[q_rows, pair_cols(0, pair)] = mixed.astype(bf16)
        for k in range(2):
            keep_sums(2 * pair + k, sums[k])


def text_front_kernel(
    x_ref, g1_ref, b1_ref, wqkv_ref, wo_ref, g2_ref, b2_ref, h1_ref, qkv_ref, att_ref, mid_ref,
    h2_ref, sum_ref, lse_ref
):
    rows, chunk = x_ref.shape[0], 128
    norm_rows(x_ref, h1_ref, g1_ref[...], b1_ref[...], chunk)

    @pl.loop(0, 3 * D // 256)
    def _(step):
        at = pl.ds(pl.multiple_of(step * 256, 256), 256)
        qkv_ref[:, at] = mul(h1_ref[...], wqkv_ref[:, at]).astype(bf16)

    mask = same_sequence(chunk, 0, chunk, 0, TXT_LEN)

    @pl.loop(0, rows // chunk)
    def _(step):
        at = pl.ds(pl.multiple_of(step * chunk, chunk), chunk)

        def keep_sums(head, value):
            lse_ref[pl.ds(step * 16 + head, 1), :] = value

        attend(qkv_ref, att_ref, at, at, mask, keep_sums)

    @pl.loop(0, D // 256)
    def _(step):
        at = pl.ds(pl.multiple_of(step * 256, 256), 256)
        mid_ref[:, at] = x_ref[:, at].astype(f32) + mul(att_ref[...], wo_ref[:, at])

    norm_rows(mid_ref, h2_ref, g2_ref[...], b2_ref[...], chunk)
    per = chunk // TXT_LEN

    @pl.loop(0, rows // chunk)
    def _(step):
        values = mid_ref[pl.ds(pl.multiple_of(step * chunk, chunk), chunk), :]
        sum_ref[pl.ds(pl.multiple_of(step * per, per), per), :] = jnp.sum(
            values.reshape(per, TXT_LEN, D), axis=1
        )


def text_front(rows_in, gain1, bias1, wqkv, wo, gain2, bias2):
    rows = rows_in.shape[0]
    shapes = [
        ((rows, D), bf16),
        ((rows, 3 * D), bf16),
        ((rows, D), bf16),
        ((rows, D), f32),
        ((rows, D), bf16),
        ((rows // TXT_LEN, D), f32),
        ((rows // 128 * 16, 128), f32),
    ]
    return pl.pallas_call(
        text_front_kernel,
        out_shape=[jax.ShapeDtypeStruct(*item) for item in shapes],
        compiler_params=params(),
        cost_estimate=cost(rows * D * D * 8, 14 * D * rows + 8 * D * D, rows * 128 * HEADS),
        name="text_front",
    )(rows_in, gain1[None], bias1[None], wqkv, wo, gain2[None], bias2[None])


def image_front_kernel(
    windows, x_ref, perm_ref, g1_ref, b1_ref, g2_ref, b2_ref, *refs
):
    h2_ref, sum_ref, w_ref, h1_ref, placed_ref, qkv_ref, att_ref, mid_ref, sems = refs[-9:]
    rows, chunk = x_ref.shape[0], 80
    copies, row = [], 0
    for k, piece in enumerate(refs[:-9]):
        place = w_ref.at[pl.ds(row, piece.shape[0]), :]
        copies.append(pltpu.make_async_copy(piece, place, sems.at[k]))
        row += piece.shape[0]
    for copy in copies:
        copy.start()

    def place_columns(src, dst):
        @pl.loop(0, D // 256)
        def _(step):
            at = pl.ds(pl.multiple_of(step * 256, 256), 256)
            dst[:, at] = mul_bt(src[...], perm_ref[at, :]).astype(bf16)

    norm_rows(x_ref, h1_ref, g1_ref[...].astype(f32), b1_ref[...].astype(f32), chunk)
    place_columns(h1_ref, placed_ref)
    for copy in copies:
        copy.wait()

    @pl.loop(0, 3 * D // 256)
    def _(step):
        at = pl.ds(pl.multiple_of(step * 256, 256), 256)
        qkv_ref[:, at] = mul(placed_ref[...], w_ref[:, at]).astype(bf16)

    for row0, count, key0, keys in windows:
        one = same_sequence(count, row0, keys, key0, IMG_LEN)
        mask = jnp.concatenate([one, one], axis=0)
        attend_along(qkv_ref, att_ref, pl.ds(row0, count), pl.ds(key0, keys), mask)
    place_columns(att_ref, placed_ref)

    @pl.loop(0, D // 256)
    def _(step):
        at = pl.ds(pl.multiple_of(step * 256, 256), 256)
        there = pl.ds(pl.multiple_of(step * 256 + 3 * D, 256), 256)
        mid_ref[:, at] = x_ref[:, at].astype(f32) + mul(placed_ref[...], w_ref[:, there])

    norm_rows(mid_ref, h2_ref, g2_ref[...].astype(f32), b2_ref[...].astype(f32), chunk)
    for k in range(rows // IMG_LEN):
        first, last = k * IMG_LEN, (k + 1) * IMG_LEN
        start, end = first // 8 * 8, -(-last // 8) * 8
        values = mid_ref[start:end, :]
        place = lax.broadcasted_iota(jnp.int32, values.shape, 0) + start
        inside = (place >= first) & (place < last)
        sum_ref[k : k + 1, :] = jnp.sum(jnp.where(inside, values, 0.0), axis=0, keepdims=True)


def image_front(rows_in, pieces, perm, gain1, bias1, gain2, bias2):
    rows = rows_in.shape[0]
    windows = ((0, 208, 0, 256), (208, 192, 192, 208))
    vmem = pl.BlockSpec(memory_space=pltpu.VMEM)
    return pl.pallas_call(
        functools.partial(image_front_kernel, windows),
        out_shape=[
            jax.ShapeDtypeStruct((rows, D), bf16),
            jax.ShapeDtypeStruct((rows // IMG_LEN, D), f32),
        ],
        in_specs=[vmem] * 6 + anywhere(pieces),
        out_specs=[vmem] * 2,
        scratch_shapes=[
            pltpu.VMEM((D, 4 * D), bf16),
            pltpu.VMEM((rows, D), bf16),
            pltpu.VMEM((rows, D), bf16),
            pltpu.VMEM((rows, 3 * D), bf16),
            pltpu.VMEM((rows, D), bf16),
            pltpu.VMEM((rows, D), f32),
            pltpu.SemaphoreType.DMA((len(pieces),)),
        ],
        compiler_params=params(),
        cost_estimate=cost(rows * D * D * 12, 8 * D * D, rows * 256 * HEADS),
        name="image_front",
    )(rows_in, perm, gain1[None], bias1[None], gain2[None], bias2[None], *pieces)


def gelu_parts(inner):
    half = 0.5 * (1.0 + lax.erf(inner * (0.5**0.5)))
    return inner * half, half


def pack_kernel(unit_ref, pos_ref, *refs):
    refs[-1][:, :D] = unit_ref[...].astype(bf16)
    refs[-1][:, D:] = pos_ref[...]


def packed(unit, positive, after):
    shape = (unit.shape[0], D + positive.shape[1])
    return pl.pallas_call(
        pack_kernel,
        out_shape=jax.ShapeDtypeStruct(shape, bf16),
        in_specs=[pl.BlockSpec(memory_space=pltpu.VMEM)] * 2 + anywhere(after),
        compiler_params=params(),
        cost_estimate=cost(shape[0] * shape[1], 4 * shape[0] * shape[1]),
        name="packed",
    )(unit, positive, *after)


def pool_matrix(count, rows, row0, seq_len):
    row = (lax.broadcasted_iota(jnp.int32, (count, rows), 1) + row0) // seq_len
    return jnp.where(row == lax.broadcasted_iota(jnp.int32, (count, rows), 0), 1.0, 0.0).astype(bf16)


def two_terms(mean):
    high = mean.astype(bf16)
    low = (mean - high.astype(f32)).astype(bf16)
    return jnp.concatenate([high, low], axis=0)


def unit_rows(pooled):
    inverse = lax.rsqrt(jnp.sum(pooled * pooled, axis=-1, keepdims=True) + norm_eps)
    return pooled * inverse, inverse


def text_up_kernel(h2_ref, wu_ref, wd_ref, sum_ref, *refs):
    slope_ref, hid_ref, unit_ref, inv_ref, acc = refs[-5:]
    step = pl.program_id(0)
    chunk = 128
    per = chunk // TXT_LEN
    pool = pool_matrix(per, chunk, 0, TXT_LEN)
    for k in range(h2_ref.shape[0] // chunk):
        inner = mul(h2_ref[k * chunk : (k + 1) * chunk, :], wu_ref[...])
        value, half = gelu_parts(inner)
        slope = half + inner * (jnp.exp(-0.5 * inner * inner) * 0.3989422804014327)
        slope_ref[k * chunk : (k + 1) * chunk, :] = slope.astype(bf16)
        hid_ref[k * per : (k + 1) * per, :] = mul(pool, value.astype(bf16))
    terms = mul(two_terms(hid_ref[...] * (1.0 / TXT_LEN)), wd_ref[...])
    count = hid_ref.shape[0]
    added = terms[:count] + terms[count:]

    @pl.when(step == 0)
    def _():
        acc[...] = sum_ref[...] * (1.0 / TXT_LEN) + added

    @pl.when(step > 0)
    def _():
        acc[...] += added

    @pl.when(step == pl.num_programs(0) - 1)
    def _():
        unit, inverse = unit_rows(acc[...])
        unit_ref[...] = unit
        inv_ref[...] = jnp.broadcast_to(inverse, inv_ref.shape)


def text_up(normed2, weight_up, weight_down, middle_sum, after=()):
    rows, count = normed2.shape[0], middle_sum.shape[0]
    fixed = lambda shape: pl.BlockSpec(shape, lambda i: (0, 0))
    return pl.pallas_call(
        text_up_kernel,
        grid=(FF // TILE,),
        out_shape=[
            jax.ShapeDtypeStruct((rows, FF), bf16),
            jax.ShapeDtypeStruct((count, FF), f32),
            jax.ShapeDtypeStruct((count, D), f32),
            jax.ShapeDtypeStruct((count, 128), f32),
        ],
        in_specs=[
            fixed((rows, D)),
            pl.BlockSpec((D, TILE), lambda i: (0, i)),
            pl.BlockSpec((TILE, D), lambda i: (i, 0)),
            fixed((count, D)),
        ]
        + anywhere(after),
        out_specs=[
            pl.BlockSpec((rows, TILE), lambda i: (0, i)),
            pl.BlockSpec((count, TILE), lambda i: (0, i)),
            fixed((count, D)),
            fixed((count, 128)),
        ],
        scratch_shapes=[pltpu.VMEM((count, D), f32)],
        compiler_params=params(),
        cost_estimate=cost(2 * rows * D * FF, 4 * D * FF + 2 * rows * FF, 20 * rows * FF),
        name="text_up",
    )(normed2, weight_up, weight_down, middle_sum, *after)


def image_up_kernel(fold, h2_ref, wu_ref, wd_ref, sum_ref, *refs):
    out_ref, acc = refs[-2:]
    step = pl.program_id(0)
    rows, count = h2_ref.shape[0], sum_ref.shape[0]
    chunk = 80
    summed = jnp.zeros((count, TILE), f32)
    for k in range(rows // chunk):
        inner = mul(h2_ref[k * chunk : (k + 1) * chunk, :], wu_ref[...])
        value, _ = gelu_parts(inner)
        pool = pool_matrix(count, chunk, k * chunk, IMG_LEN)
        summed = summed + mul(pool, value.astype(bf16))
    mean = two_terms(summed * (1.0 / IMG_LEN))
    place = lax.broadcasted_iota(jnp.int32, (TILE, TILE // fold), 0)
    picked = lax.broadcasted_iota(jnp.int32, (TILE, TILE // fold), 1) * fold
    terms = jnp.zeros((2 * count, D), f32)
    for k in range(fold):
        chosen = jnp.where(place == picked + k, 1.0, 0.0).astype(bf16)
        part = mul(mean, chosen).astype(bf16)
        terms = terms + mul(part, wd_ref[:, k * D : (k + 1) * D])
    added = terms[:count] + terms[count:]

    @pl.when(step == 0)
    def _():
        acc[...] = sum_ref[...] * (1.0 / IMG_LEN) + added

    @pl.when(step > 0)
    def _():
        acc[...] += added

    @pl.when(step == pl.num_programs(0) - 1)
    def _():
        out_ref[...] = unit_rows(acc[...])[0].astype(bf16)


def image_up(normed2, whole, up_col, down_col, middle_sum, after=()):
    rows, count = normed2.shape[0], middle_sum.shape[0]
    fold = FF // D
    fixed = lambda shape: pl.BlockSpec(shape, lambda i: (0, 0))
    return pl.pallas_call(
        functools.partial(image_up_kernel, fold),
        grid=(FF // TILE,),
        out_shape=jax.ShapeDtypeStruct((count, D), bf16),
        in_specs=[
            fixed((rows, D)),
            pl.BlockSpec((D, TILE), lambda i: (0, up_col // TILE + i)),
            pl.BlockSpec((TILE // fold, fold * D), lambda i: (i, down_col // (fold * D))),
            fixed((count, D)),
        ]
        + anywhere(after),
        out_specs=fixed((count, D)),
        scratch_shapes=[pltpu.VMEM((count, D), f32)],
        compiler_params=params(),
        cost_estimate=cost(2 * rows * D * FF, 4 * D * FF, 15 * rows * FF),
        name="image_up",
    )(normed2, whole, whole, middle_sum, *after)


def loss_parts(text_rows, pos, image_all):
    similar = mul_bt(text_rows, image_all) * logit_scale
    shifted = jnp.exp(similar - logit_scale)
    alive = jnp.max(pos, axis=1, keepdims=True)
    row_sum = jnp.sum(shifted, axis=1, keepdims=True)
    row_count = jnp.maximum(jnp.sum(pos, axis=1, keepdims=True), 1.0)
    return similar, shifted, alive, row_sum, row_count


def sums_over_captions(text_rows, pos, image_all):
    similar, shifted, alive, row_sum, row_count = loss_parts(text_rows, pos, image_all)
    pos_similar = pos * similar
    cap_term = alive * (
        logit_scale + jnp.log(row_sum) - jnp.sum(pos_similar, axis=1, keepdims=True) / row_count
    )
    return (
        jnp.sum(alive * shifted, axis=0, keepdims=True),
        jnp.sum(pos, axis=0, keepdims=True),
        jnp.sum(pos_similar, axis=0, keepdims=True),
        jnp.sum(cap_term, axis=0, keepdims=True),
        jnp.sum(alive, axis=0, keepdims=True),
    )


def loss_from(sums):
    col_sum, col_count, col_pos, cap_total, live_total = sums
    img_term = logit_scale + jnp.log(col_sum) - col_pos / col_count
    return 0.5 * cap_total / live_total + 0.5 * jnp.mean(img_term, axis=1, keepdims=True)


def grad_of_unit(text_rows, pos, image_all, col_sum, col_count, live_total):
    _, shifted, alive, row_sum, row_count = loss_parts(text_rows, pos, image_all)
    cap_share, img_share = 0.5 / live_total, 0.5 / image_all.shape[0]
    grad_sims = alive * shifted * (cap_share / row_sum + img_share / col_sum) - pos * (
        cap_share / row_count + img_share / col_count
    )
    return mul(grad_sims.astype(bf16), image_all) * logit_scale


def turned(grad, unit):
    return grad - unit * jnp.sum(grad * unit, axis=-1, keepdims=True)


def loss_kernel(
    pack_ref, image_ref, own_ref, unit_ref, inv_ref, loss_ref, row_ref, low_ref, col_sum_ref,
    col_count_ref, live_ref
):
    image_all = image_ref[...]
    chunk = 256
    total = None
    for k in range(pack_ref.shape[0] // chunk):
        at = slice(k * chunk, (k + 1) * chunk)
        part = sums_over_captions(pack_ref[at, :D], pack_ref[at, D:].astype(f32), image_all)
        total = part if total is None else [a + b for a, b in zip(total, part)]
    loss_ref[...] = jnp.broadcast_to(loss_from(total), loss_ref.shape)
    col_sum, col_count, _, _, live_total = total
    col_sum_ref[...] = col_sum
    col_count_ref[...] = col_count
    live_ref[...] = jnp.broadcast_to(live_total, live_ref.shape)
    grad = grad_of_unit(
        own_ref[:, :D], own_ref[:, D:].astype(f32), image_all, col_sum, col_count, live_total
    )
    row = inv_ref[:, :1] * turned(grad, unit_ref[...]) * (1.0 / TXT_LEN)
    row_ref[...] = row
    low_ref[...] = row.astype(bf16)


def loss_and_rows(pack, image_all, own_pack, unit, inverse):
    images, count = image_all.shape[0], own_pack.shape[0]
    shapes = [(1, 128), (count, D), (count, D), (1, images), (1, images), (1, 128)]
    kinds = [f32, f32, bf16, f32, f32, f32]
    return pl.pallas_call(
        loss_kernel,
        out_shape=[jax.ShapeDtypeStruct(*item) for item in zip(shapes, kinds)],
        compiler_params=params(),
        cost_estimate=cost(2 * pack.shape[0] * images * D, 2 * pack.size, pack.shape[0] * images),
        name="loss_and_rows",
    )(pack, image_all, own_pack, unit, inverse)


def down_kernel(pack_ref, image_ref, col_sum_ref, col_count_ref, live_ref, hid_ref, *refs):
    step, out_ref = pl.program_id(0), refs[-1]
    text_rows = pack_ref[:, :D]
    grad = grad_of_unit(
        text_rows, pack_ref[:, D:].astype(f32), image_ref[...], col_sum_ref[...],
        col_count_ref[...], live_ref[:, :1]
    )
    rows = (turned(grad, text_rows.astype(f32)) * (1.0 / TXT_LEN)).astype(bf16)
    part = mul_at(hid_ref[...], rows)

    @pl.when(step == 0)
    def _():
        out_ref[...] = part

    @pl.when(step > 0)
    def _():
        out_ref[...] += part


def grad_of_down(pack, image_all, col_sum, col_count, live_total, hidden_cols, after):
    images, chunk = image_all.shape[0], 256
    fixed = lambda shape: pl.BlockSpec(shape, lambda i: (0, 0))
    per = hidden_cols.shape[1]
    return pl.pallas_call(
        down_kernel,
        grid=(pack.shape[0] // chunk,),
        out_shape=jax.ShapeDtypeStruct((per, D), f32),
        in_specs=[
            pl.BlockSpec((chunk, pack.shape[1]), lambda i: (i, 0)),
            fixed((images, D)), fixed((1, images)), fixed((1, images)), fixed((1, 128)),
            pl.BlockSpec((chunk, per), lambda i: (i, 0)),
        ]
        + anywhere(after),
        out_specs=fixed((per, D)),
        compiler_params=params(),
        cost_estimate=cost(4 * pack.shape[0] * images * D, 2 * pack.size, pack.shape[0] * images),
        name="grad_of_down",
    )(pack, image_all, col_sum, col_count, live_total, hidden_cols, *after)


def mlp_back_kernel(
    low_ref, wd_ref, slope_ref, wu_ref, lhs_ref, mid_ref, gain_ref, row_ref, keep_a, send_a, keep_b,
    send_b, out_ref, gain_out, bias_out, acc
):
    step = pl.program_id(0)
    count, rows = low_ref.shape[0], slope_ref.shape[0]
    half = D // 2
    hidden = mul_bt(low_ref[...], wd_ref[...])
    wide = jnp.broadcast_to(hidden[:, None, :], (count, TXT_LEN, TILE)).reshape(rows, TILE)
    inner = (wide * slope_ref[...].astype(f32)).astype(bf16)
    weight = mul(lhs_ref[0], inner).astype(bf16)

    @pl.when(step < pl.num_programs(0) // 2)
    def _():
        keep_a[...] = weight[:half]
        send_a[...] = weight[half:]

    @pl.when(step >= pl.num_programs(0) // 2)
    def _():
        keep_b[...] = weight[:half]
        send_b[...] = weight[half:]

    added = mul_bt(inner, wu_ref[...])

    @pl.when(step == 0)
    def _():
        acc[...] = added

    @pl.when(step > 0)
    def _():
        acc[...] += added

    @pl.when(step == pl.num_programs(0) - 1)
    def _():
        chunk = 128
        per = chunk // TXT_LEN
        gain = gain_ref[...]
        gain_out[...] = jnp.zeros_like(gain_out)
        bias_out[...] = jnp.zeros_like(bias_out)

        @pl.loop(0, rows // chunk)
        def _(k):
            at = pl.ds(pl.multiple_of(k * chunk, chunk), chunk)
            unit, scale = norm_parts(mid_ref[at, :])
            grad = acc[at, :]
            gain_out[...] += jnp.sum(grad * unit, axis=0, keepdims=True)
            bias_out[...] += jnp.sum(grad, axis=0, keepdims=True)
            row = row_ref[pl.ds(pl.multiple_of(k * per, per), per), :]
            row = jnp.broadcast_to(row[:, None, :], (per, TXT_LEN, D)).reshape(chunk, D)
            out_ref[at, :] = row + norm_back(unit, scale, gain, grad)


def mlp_back(grad_row, grad_low, weight_down, slope, weight_up, lhs, middle, gain):
    rows, count = slope.shape[0], grad_row.shape[0]
    steps = FF // TILE
    fixed = lambda shape: pl.BlockSpec(shape, lambda i: (0, 0))
    first = pl.BlockSpec((D // 2, TILE), lambda i: (0, jnp.minimum(i, steps // 2 - 1)))
    second = pl.BlockSpec((D // 2, TILE), lambda i: (0, jnp.maximum(i - steps // 2, 0)))
    part = jax.ShapeDtypeStruct((D // 2, FF // 2), bf16)
    line = jax.ShapeDtypeStruct((1, D), f32)
    return pl.pallas_call(
        mlp_back_kernel,
        grid=(steps,),
        out_shape=[part] * 4 + [jax.ShapeDtypeStruct((rows, D), f32), line, line],
        in_specs=[
            fixed((count, D)),
            pl.BlockSpec((TILE, D), lambda i: (i, 0)),
            pl.BlockSpec((rows, TILE), lambda i: (0, i)),
            pl.BlockSpec((D, TILE), lambda i: (0, i)),
            pl.BlockSpec((1, D, rows), lambda i: (i // (steps // 2), 0, 0)),
            fixed((rows, D)),
            fixed((1, D)),
            fixed((count, D)),
        ],
        out_specs=[first, first, second, second, fixed((rows, D)), fixed((1, D)), fixed((1, D))],
        scratch_shapes=[pltpu.VMEM((rows, D), f32)],
        compiler_params=params(),
        cost_estimate=cost(4 * rows * D * FF, 4 * D * FF + 2 * rows * FF + 2 * D * FF, rows * FF),
        name="mlp_back",
    )(grad_low, weight_down, slope, weight_up, lhs, middle, gain[None], grad_row)


def attention_back_kernel(grad_ref, wo_ref, qkv_ref, lse_ref, *refs):
    low_ref, out_ref = refs[-2:]
    chunk = grad_ref.shape[0]
    mask = same_sequence(chunk, 0, chunk, 0, TXT_LEN)
    low = grad_ref[...].astype(bf16)
    low_ref[...] = low
    grad_att = mul_bt(low, wo_ref[...]).astype(bf16)
    for pair in range(HEADS // 2):
        queries = qkv_ref[:, pair_cols(0, pair)] * bf16(HEAD ** (-0.5))
        keys = two_heads(qkv_ref[:, pair_cols(1, pair)])
        vals = two_heads(qkv_ref[:, pair_cols(2, pair)])
        grads = grad_att[:, pair_cols(0, pair)]
        scores, grad_probs = mul_bt(keys, queries), mul_bt(vals, grads)
        probs, grad_scores = [], []
        for k in range(2):
            at = slice(k * chunk, (k + 1) * chunk)
            head = 2 * pair + k
            shifted = scores[at] - lse_ref[head : head + 1, :]
            prob = jnp.where(mask, jnp.exp(jnp.where(mask, shifted, 0.0)), 0.0)
            along = jnp.sum(grad_probs[at] * prob, axis=0, keepdims=True)
            grad_scores.append((prob * (grad_probs[at] - along)).astype(bf16))
            probs.append(prob.astype(bf16))
        grad_q = mul_at(jnp.concatenate(grad_scores, axis=0), keys) * HEAD ** (-0.5)
        grad_k = mul(jnp.concatenate(grad_scores, axis=1), two_heads(queries))
        grad_v = mul(jnp.concatenate(probs, axis=1), two_heads(grads))
        out_ref[:, pair_cols(0, pair)] = grad_q.astype(bf16)
        out_ref[:, pair_cols(1, pair)] = grad_k.astype(bf16)
        out_ref[:, pair_cols(2, pair)] = grad_v.astype(bf16)


def attention_back(grad_middle, weight_out, project, log_sums, first, count, after=()):
    chunk = 128
    rows = count * chunk
    return pl.pallas_call(
        attention_back_kernel,
        grid=(count,),
        out_shape=[
            jax.ShapeDtypeStruct((rows, D), bf16),
            jax.ShapeDtypeStruct((rows, 3 * D), bf16),
        ],
        in_specs=[
            pl.BlockSpec((chunk, D), lambda i: (i + first, 0)),
            pl.BlockSpec((D, D), lambda i: (0, 0)),
            pl.BlockSpec((chunk, 3 * D), lambda i: (i + first, 0)),
            pl.BlockSpec((16, chunk), lambda i: (i + first, 0)),
        ]
        + anywhere(after),
        out_specs=[
            pl.BlockSpec((chunk, D), lambda i: (i, 0)),
            pl.BlockSpec((chunk, 3 * D), lambda i: (i, 0)),
        ],
        compiler_params=params(),
        cost_estimate=cost(10 * rows * D * D, 16 * rows * D + 2 * D * D, rows * 128 * HEADS),
        name="attention_back",
    )(grad_middle, weight_out, project, log_sums, *after)


def mul_rows(lhs, parts):
    total, row = 0.0, 0
    for part in parts:
        total = total + mul(lhs[:, row : row + part.shape[0]], part[...])
        row += part.shape[0]
    return total


def weight_back_kernel(counts, lhs_ref, *refs):
    step, half = pl.program_id(0), D // 2
    keep, send = refs[-2:]
    row = 0
    for k, count in enumerate(counts):
        parts = refs[row : row + count]
        row += count

        @pl.when(step == k if len(counts) > 1 else step >= 0)
        def _(parts=parts):
            weight = mul_rows(lhs_ref[0], parts).astype(bf16)
            keep[...] = weight[:half]
            send[...] = weight[half:]


def weight_back(lhs, first, groups, blocks, after=()):
    rows = lhs.shape[2]
    steps = 2
    many = len(groups) > 1
    given = [part for group in groups for part in group]
    return pl.pallas_call(
        functools.partial(weight_back_kernel, [len(group) for group in groups]),
        grid=(steps,),
        out_shape=[jax.ShapeDtypeStruct((D // 2, steps * D), bf16)] * 2,
        in_specs=[pl.BlockSpec((1, D, rows), lambda i: (first + (i if many else 0), 0, 0))]
        + [
            pl.BlockSpec((part.shape[0], D), lambda i, col=col: (0, col + (0 if many else i)))
            for group, col in zip(groups, blocks)
            for part in group
        ]
        + anywhere(after),
        out_specs=[pl.BlockSpec((D // 2, D), lambda i: (0, i))] * 2,
        compiler_params=params(),
        cost_estimate=cost(4 * rows * D * D, 4 * rows * D + 7 * D * D),
        name="weight_back",
    )(lhs, *given, *after)


def input_back_kernel(count, *refs):
    projs = refs[:count]
    w_ref, x_ref, gain_ref, mid_ref = refs[count : count + 4]
    out_ref, gain_out, bias_out, acc = refs[-4:]
    step = pl.program_id(0)
    rows, chunk = x_ref.shape[0], 128
    row = 0
    for part in projs:
        at = slice(row, row + part.shape[0])
        row += part.shape[0]
        added = mul_bt(part[...], w_ref[...])

        @pl.when(step == 0)
        def _(at=at, added=added):
            acc[at, :] = added

        @pl.when(step > 0)
        def _(at=at, added=added):
            acc[at, :] += added

    @pl.when(step == pl.num_programs(0) - 1)
    def _():
        gain = gain_ref[...]
        gain_out[...] = jnp.zeros_like(gain_out)
        bias_out[...] = jnp.zeros_like(bias_out)

        @pl.loop(0, rows // chunk)
        def _(k):
            at = pl.ds(pl.multiple_of(k * chunk, chunk), chunk)
            unit, scale = norm_parts(x_ref[at, :].astype(f32))
            grad = acc[at, :]
            gain_out[...] += jnp.sum(grad * unit, axis=0, keepdims=True)
            bias_out[...] += jnp.sum(grad, axis=0, keepdims=True)
            out_ref[at, :] = mid_ref[at, :] + norm_back(unit, scale, gain, grad)


def input_back(grad_projs, weight, rows_in, gain, grad_middle, after=()):
    rows = rows_in.shape[0]
    fixed = lambda shape: pl.BlockSpec(shape, lambda i: (0, 0))
    line = jax.ShapeDtypeStruct((1, D), f32)
    return pl.pallas_call(
        functools.partial(input_back_kernel, len(grad_projs)),
        grid=(3,),
        out_shape=[jax.ShapeDtypeStruct((rows, D), f32), line, line],
        in_specs=[pl.BlockSpec((part.shape[0], D), lambda i: (0, i)) for part in grad_projs]
        + [
            pl.BlockSpec((D, D), lambda i: (0, i)),
            fixed((rows, D)), fixed((1, D)), fixed((rows, D)),
        ]
        + anywhere(after),
        out_specs=[fixed((rows, D)), fixed((1, D)), fixed((1, D))],
        scratch_shapes=[pltpu.VMEM((rows, D), f32)],
        compiler_params=params(),
        cost_estimate=cost(6 * rows * D * D, 14 * rows * D + 6 * D * D),
        name="input_back",
    )(*grad_projs, weight, rows_in, gain[None], grad_middle, *after)


def local(
    images,
    captions,
    img_gain1,
    img_bias1,
    img_qkv,
    img_out,
    img_gain2,
    img_bias2,
    img_up,
    img_down,
    txt_gain1,
    txt_bias1,
    txt_qkv,
    txt_out,
    txt_gain2,
    txt_bias2,
    txt_up,
    txt_down,
    counts,
    matches,
):
    peers = lax.axis_size(AXIS)
    own = lax.axis_index(AXIS)
    per = D // peers
    img_local = counts.shape[0]
    cap_local = matches.shape[0]
    total_images = matches.shape[1]

    whole = lax.all_gather(
        jnp.concatenate([img_up.reshape(per, FF), img_down.reshape(per, FF)], axis=1),
        AXIS,
        axis=0,
        tiled=True,
    )
    small = peers == 32
    shard = jnp.concatenate([img_qkv.reshape(per, 3 * D), img_out.reshape(per, D)], axis=1)
    if small:
        line, perm = gathered_line(shard), row_order((1, 4, 2, 16, 8))
    else:
        line, perm = lax.all_gather(shard, AXIS, axis=0, tiled=True), jnp.eye(D, dtype=bf16)

    normed1, project, attended, middle, normed2, middle_sum, log_sums = text_front(
        captions, txt_gain1, txt_bias1, txt_qkv, txt_out, txt_gain2, txt_bias2
    )
    middle_sum, line = in_turn(middle_sum, line)
    beside, above = (swapped(line, 2), swapped(line, 4)) if small else (line, line)
    slope, hidden_sum, text_unit, inverse = text_up(
        normed2, txt_up, txt_down, middle_sum, (line,)
    )
    text_unit, (beside, above) = in_turn(text_unit, (beside, above))

    ends_at = jnp.cumsum(counts)
    slot_ids = lax.iota(jnp.int32, cap_local)
    owner = jnp.sum((ends_at[None, :] <= slot_ids[:, None]).astype(jnp.int32), axis=1)
    owner = owner + own * img_local
    live = slot_ids < ends_at[-1]
    columns = lax.iota(jnp.int32, total_images)
    positive = ((matches > 0) | (owner[:, None] == columns[None, :])) & live[:, None]

    own_pack = packed(text_unit, positive.astype(bf16), ())
    pieces = [line]
    if small:
        held = own_pack[None]
        first, second = diagonal(beside, above)
        others = [swapped(held, mask) for mask in (8, 16, 24)]
        others, first, second = lax.optimization_barrier((others, first, second))
        held = joined(joined(held, others[0], 8), joined(others[1], others[2], 8), 16, 1)
        text_beside, text_above = swapped(held, 2), swapped(held, 4)
        pieces = [line, beside, above, first, second]
        pieces = pieces + [swapped(piece, 1) for piece in pieces]

    normed_img, middle_img = image_front(
        images, pieces, perm, img_gain1, img_bias1, img_gain2, img_bias2
    )
    if small:
        scaled_sum = (hidden_sum * inverse[:, :1]).astype(bf16)
        normed_img, scaled_sum, text_beside, text_above = lax.optimization_barrier(
            (normed_img, scaled_sum, text_beside, text_above)
        )
        hidden_cols = lax.all_to_all(scaled_sum, AXIS, split_axis=1, concat_axis=0, tiled=True)
        across = jnp.concatenate(diagonal(text_beside, text_above), axis=0)
        held = joined(joined(held, text_beside, 2), joined(text_above, across, 2), 4, 4)

    order_a, order_b, tail = stage_orders()
    matrix_a, matrix_b = row_order(order_a + tail[::-1]), row_order(order_b + tail[::-1])
    lhs_up = jnp.stack([placed(matrix_a, normed2), placed(matrix_b, normed2)])
    lhs_rest = jnp.stack(
        [placed(matrix_a, normed1), placed(matrix_b, normed1), placed(matrix_b, attended)]
    )
    if small:
        whole, lhs_up, lhs_rest, held = lax.optimization_barrier((whole, lhs_up, lhs_rest, held))
        other = swapped(held, 1)
    image_low = image_up(normed_img, whole, 0, FF, middle_img)
    if small:
        image_low, hidden_cols = in_turn(image_low, hidden_cols)
        text_pack = joined(held, other, 1).reshape(-1, D + total_images)
    image_all = spread(image_low).reshape(total_images, D)

    if small:
        loss_value, grad_row, row_low, col_sum, col_count, live_total = loss_and_rows(
            text_pack, image_all, own_pack, text_unit, inverse
        )
        loss_value = loss_value[0, 0]
    else:
        text_low, pos = own_pack[:, :D], own_pack[:, D:].astype(f32)
        sums = lax.psum(sums_over_captions(text_low, pos, image_all), AXIS)
        loss_value = loss_from(sums)[0, 0]
        grad = grad_of_unit(text_low, pos, image_all, sums[0], sums[1], sums[4])
        grad_row = inverse[:, :1] * turned(grad, text_unit) * (1.0 / TXT_LEN)
        row_low = grad_row.astype(bf16)

    *up, grad_middle, gain_two, bias_two = mlp_back(
        grad_row, row_low, txt_down, slope, txt_up, lhs_up, middle, txt_gain2
    )
    stages = len(order_a)
    low_one, proj_one = attention_back(grad_middle, txt_out, project, log_sums, 0, 2)
    for stage in range(stages - 2):
        up = fold(hand_on(up, stage), (proj_one,))
    low_two, proj_two = attention_back(grad_middle, txt_out, project, log_sums, 2, 3, up)
    up = fold(hand_on(up, stages - 2), (proj_two,))
    projs, lows = (proj_one, proj_two), (low_one, low_two)
    rest_a = weight_back(lhs_rest, 0, [projs], [0], up)
    up = hand_on_last(fold_last(hand_on(up, stages - 1), rest_a[1:]))
    rest_b = weight_back(lhs_rest, 1, [projs, lows], [2, 0], up[:1])
    rest = [*rest_a, *rest_b]
    for stage in range(stages - 2):
        rest = fold(hand_on(rest, stage))
    caption_grad, gain_one, bias_one = input_back(
        projs, txt_qkv, captions, txt_gain1, grad_middle, rest[:1]
    )
    caption_grad, up = in_turn(caption_grad, up)
    rest = fold(hand_on(rest, stages - 2), (caption_grad,))
    norms = jnp.concatenate([gain_one, bias_one, gain_two, bias_two], axis=0)
    norms, rest = in_turn(norms, rest)
    norms = jnp.sum(spread(norms[None]), axis=0).reshape(4, D)
    rest = fold_last(hand_on(rest, stages - 1))
    if small:
        grad_down = grad_of_down(
            text_pack, image_all, col_sum, col_count, live_total, hidden_cols, (rest[0], norms)
        )
    else:
        grad_down = lax.psum_scatter(
            mul_at(hidden_sum.astype(bf16), row_low), AXIS, scatter_dimension=0, tiled=True
        )
    grad_down, rest = in_turn(grad_down, hand_on_last(rest))
    up_share = sum_last(*up)
    rest_share = sum_last(*rest)
    return (
        loss_value,
        caption_grad,
        norms[0],
        norms[1],
        rest_share[:, : 3 * D].reshape(-1),
        rest_share[:, 3 * D :].reshape(-1),
        norms[2],
        norms[3],
        up_share.reshape(-1),
        grad_down.reshape(-1),
    )


def solution(mesh):
    split, flat, whole = P("blk", None), P("blk"), P()
    image_block = (whole, whole, flat, flat, whole, whole, flat, flat)
    return jax.shard_map(
        local,
        mesh=mesh,
        in_specs=(split, split) + image_block + (whole,) * 8 + (flat, split),
        out_specs=(whole, split, whole, whole, flat, flat, whole, whole, flat, flat),
        check_vma=False,
    )
```

profile of v0, /device:TPU:0, one launch (start us, length us, event | category | flops | bytes accessed | tf_op | source)
XLA Modules:
  0.0 317.3 jit_solution(8915133174130123624)
XLA Ops:
  22.8 18.0 %text_front.1 = (bf16[640,768]{1,0:T(8,128)(2,1)}, bf16[640,2304]{1,0:T(8,128)(2,1)}, bf16[640,768]{1,0:T(8,128)(2,1)}, f32[640,768]{1,0:T(8,128)}, bf16[640,768...) custom-call(bf16[640,768]{1,0:T(8,128)(2,1)} %refs_3_.1, f32[1,768]{1,0:T(1,128)} %broadcast_in_dim.22.g1_ref.refs_4_, ...), custom_call_target="tpu_custom_call" | custom-call | flops 3019898880 | bytes 11599872 | tf_op jit(solution)/shard_map/text_front/pallas_call | solution.py:329
  57.4 13.8 %text_up.1 = (bf16[640,3072]{1,0:T(8,128)(2,1)}, f32[40,3072]{1,0:T(8,128)}, f32[40,768]{1,0:T(8,128)}, f32[40,128]{1,0:T(8,128)}) custom-call(bf16[640,768]{1,0:T(8,128)(2,1)} %get-tuple-element.106.h2_ref, bf16[768,3072]{1,0:T(8,128)(2,1)} %wu_ref.3, bf16[3072,768]{1,0:T(8,128)(2,1)} %wd_ref.3, f32[40,768]{1,0:T(8,128)} %get-tuple-element.111.sum_ref, ...), custom_call_target="tpu_custom_call" | custom-call | flops 3019898880 | bytes 13369344 | tf_op jit(solution)/shard_map/text_up/pallas_call | solution.py:488
  81.2 5.8 %collective-permute-done.5 = bf16[1,40,1024]{2,1,0:T(8,128)(2,1)S(1)} collective-permute-done((bf16[1,40,1024]{2,1,0:T(8,128)(2,1)}, bf16[1,40,1024]{2,1,0:T(8,128)(2,1)S(1)}, u32[]{:S(2)}, u32[]{:S(2)}) %collective-permute-start.5) | collective-permute-done | bytes 81952 | tf_op jit(solution)/shard_map/ppermute | solution.py:26
  100.1 14.0 %image_front.1 = (bf16[400,768]{1,0:T(8,128)(2,1)}, f32[8,768]{1,0:T(8,128)}) custom-call(bf16[400,768]{1,0:T(8,128)(2,1)} %x_ref.3, bf16[768,768]{1,0:T(8,128)(2,1)} %fusion.perm_ref, bf16[1,768]{1,0:T(2,128)(2,1)} %broadcast_in_dim.26.g1_ref, bf16[1,768]{1,0:T(2,128)(2,1)} %broadcast_in_dim.27.b1_ref, bf16[1,768]{1,0:T(2,128)(2,1)} %broadcast_in_dim.28.g2_ref, ...), custom_call_target="tpu_custom_call" | custom-call | flops 2831155200 | bytes 4718592 | tf_op jit(solution)/shard_map/image_front/pallas_call | solution.py:393
  114.7 5.8 %collective-permute-done.17 = bf16[2,40,1024]{2,1,0:T(8,128)(2,1)S(1)} collective-permute-done((bf16[2,40,1024]{2,1,0:T(8,128)(2,1)S(1)}, bf16[2,40,1024]{2,1,0:T(8,128)(2,1)S(1)}, u32[]{:S(2)}, u32[]{:S(2)}) %collective-permute-start.17) | collective-permute-done | bytes 163872 | tf_op jit(solution)/shard_map/ppermute | solution.py:26
  122.5 5.4 %all-to-all-start = ((bf16[40,32,96]{2,0,1:T(8,128)(2,1)}), bf16[40,32,96]{2,0,1:T(8,128)(2,1)S(1)}, u32[]{:S(2)}, u32[]{:S(2)}) async-start(bf16[40,32,96]{2,0,1:T(8,128)(2,1)} %copy.73), calls=%async_computation | async-start | bytes 655360 | tf_op jit(solution)/shard_map/all_to_all | solution.py:1017
  127.8 14.1 %image_up.1 = bf16[8,768]{1,0:T(8,128)(2,1)} custom-call(bf16[400,768]{1,0:T(8,128)(2,1)} %get-tuple-element.127.h2_ref, bf16[768,6144]{1,0:T(8,128)(2,1)} %all-gather.2.cloned.1.call-done.wu_ref.wd_ref, bf16[768,6144]{1,0:T(8,128)(2,1)} %all-gather.2.cloned.1.call-done.wu_ref.wd_ref, f32[8,768]{1,0:T(8,128)} %get-tuple-element.129.sum_ref), custom_call_target="tpu_custom_call" | custom-call | flops 1887436800 | bytes 9437184 | tf_op jit(solution)/shard_map/image_up/pallas_call | solution.py:555
  143.4 5.8 %all-to-all-start.1 = ((bf16[32,8,768]{2,1,0:T(8,128)(2,1)}), bf16[32,8,768]{2,1,0:T(8,128)(2,1)S(1)}, u32[]{:S(2)}, u32[]{:S(2)}) async-start(bf16[32,8,768]{2,1,0:T(8,128)(2,1)} %broadcast_in_dim.60), calls=%async_computation.1 | async-start | bytes 786432 | tf_op jit(solution)/shard_map/all_to_all | solution.py:46
  151.2 11.3 %all-to-all-done.1 = bf16[32,8,768]{2,1,0:T(8,128)(2,1)S(1)} async-done(((bf16[32,8,768]{2,1,0:T(8,128)(2,1)}), bf16[32,8,768]{2,1,0:T(8,128)(2,1)S(1)}, u32[]{:S(2)}, u32[]{:S(2)}) %all-to-all-start.1) | async-done | bytes 393248 | tf_op jit(solution)/shard_map/all_to_all | solution.py:46
  163.2 4.0 %loss_and_rows.1 = (f32[1,128]{1,0:T(1,128)}, f32[40,768]{1,0:T(8,128)}, bf16[40,768]{1,0:T(8,128)(2,1)}, f32[1,256]{1,0:T(1,128)}, f32[1,256]{1,0:T(1,128)}, /*index=5*/f32[1,128]{1,0:T(1,128)}) custom-call(bf16[1280,1024]{1,0:T(8,128)(2,1)} %bitcast.90, bf16[256,768]{1,0:T(8,128)(2,1)} %bitcast.94, bf16[40,1024]{1,0:T(8,128)(2,1)} %packed.1.own_ref, ...), custom_call_target="tpu_custom_call" | custom-call | flops 503316480 | bytes 2621440 | tf_op jit(solution)/shard_map/loss_and_rows/pallas_call | solution.py:645
  167.3 21.4 %mlp_back.1 = (bf16[384,1536]{1,0:T(8,128)(2,1)}, bf16[384,1536]{1,0:T(8,128)(2,1)}, bf16[384,1536]{1,0:T(8,128)(2,1)}, bf16[384,1536]{1,0:T(8,128)(2,1)}, f32[6...) custom-call(bf16[40,768]{1,0:T(8,128)(2,1)} %get-tuple-element.133.low_ref, bf16[3072,768]{1,0:T(8,128)(2,1)} %wd_ref.3, ...), custom_call_target="tpu_custom_call" | custom-call | flops 6039797760 | bytes 18087936 | tf_op jit(solution)/shard_map/mlp_back/pallas_call | solution.py:754
  189.3 7.2 %attention_back.2 = (bf16[256,768]{1,0:T(8,128)(2,1)}, bf16[256,2304]{1,0:T(8,128)(2,1)}) custom-call(f32[640,768]{1,0:T(8,128)} %get-tuple-element.138.grad_ref.refs_5_, bf16[768,768]{1,0:T(8,128)(2,1)} %wo_ref.5, bf16[640,2304]{1,0:T(8,128)(2,1)} %get-tuple-element.139.qkv_ref, f32[80,128]{1,0:T(8,128)} %get-tuple-element.140.lse_ref), custom_call_target="tpu_custom_call" | custom-call | flops 1509949440 | bytes 4325376 | tf_op jit(solution)/shard_map/attention_back/pallas_call | solution.py:809
  197.9 4.6 %fold.4 = (bf16[192,1536]{1,0:T(8,128)(2,1)}, bf16[192,1536]{1,0:T(8,128)(2,1)}, bf16[192,1536]{1,0:T(8,128)(2,1)}, bf16[192,1536]{1,0:T(8,128)(2,1)}) custom-call(bf16[384,1536]{1,0:T(8,128)(2,1)} %get-tuple-element.142.keep_a, bf16[384,1536]{1,0:T(8,128)(2,1)} %copy-done.6, bf16[384,1536]{1,0:T(8,128)(2,1)} %get-tuple-element.144.keep_b, ...), custom_call_target="tpu_custom_call" | custom-call | flops 1179648 | bytes 7077888 | tf_op jit(solution)/shard_map/fold/pallas_call | solution.py:195
  204.5 9.5 %attention_back.3 = (bf16[384,768]{1,0:T(8,128)(2,1)}, bf16[384,2304]{1,0:T(8,128)(2,1)}) custom-call(f32[640,768]{1,0:T(8,128)} %get-tuple-element.138.grad_ref.refs_5_, bf16[768,768]{1,0:T(8,128)(2,1)} %wo_ref.5, bf16[640,2304]{1,0:T(8,128)(2,1)} %get-tuple-element.139.qkv_ref, f32[80,128]{1,0:T(8,128)} %get-tuple-element.140.lse_ref, ...), custom_call_target="tpu_custom_call" | custom-call | flops 2264924160 | bytes 5898240 | tf_op jit(solution)/shard_map/attention_back/pallas_call | solution.py:809
  214.0 4.0 %collective-permute-done.22.got_a = bf16[192,1536]{1,0:T(8,128)(2,1)S(1)} collective-permute-done((bf16[192,1536]{1,0:T(8,128)(2,1)}, bf16[192,1536]{1,0:T(8,128)(2,1)S(1)}, u32[]{:S(2)}, u32[]{:S(2)}) %collective-permute-start.22) | collective-permute-done | bytes 589856 | tf_op jit(solution)/shard_map/ppermute | solution.py:26
  219.5 3.5 %fold.5 = (bf16[96,1536]{1,0:T(8,128)(2,1)}, bf16[96,1536]{1,0:T(8,128)(2,1)}, bf16[96,1536]{1,0:T(8,128)(2,1)}, bf16[96,1536]{1,0:T(8,128)(2,1)}) custom-call(bf16[192,1536]{1,0:T(8,128)(2,1)} %get-tuple-element.146.refs_0_.keep_a, bf16[192,1536]{1,0:T(8,128)(2,1)} %copy-done.13, bf16[192,1536]{1,0:T(8,128)(2,1)} %get-tuple-element.148.refs_2_.keep_b, ...), custom_call_target="tpu_custom_call" | custom-call | flops 589824 | bytes 3538944 | tf_op jit(solution)/shard_map/fold/pallas_call | solution.py:195
  225.1 4.8 %weight_back.2 = (bf16[384,1536]{1,0:T(8,128)(2,1)}, bf16[384,1536]{1,0:T(8,128)(2,1)}) custom-call(bf16[3,768,640]{2,1,0:T(8,128)(2,1)} %pad_maximum_fusion.lhs_ref, bf16[256,2304]{1,0:T(8,128)(2,1)} %get-tuple-element.141.refs_0_, bf16[384,2304]{1,0:T(8,128)(2,1)} %get-tuple-element.150.refs_0_.refs_1_, ...), custom_call_target="tpu_custom_call" | custom-call | flops 1509949440 | bytes 6094848 | tf_op jit(solution)/shard_map/weight_back/pallas_call | solution.py:861
  235.0 5.0 %weight_back.3 = (bf16[384,1536]{1,0:T(8,128)(2,1)}, bf16[384,1536]{1,0:T(8,128)(2,1)}) custom-call(bf16[3,768,640]{2,1,0:T(8,128)(2,1)} %pad_maximum_fusion.lhs_ref, bf16[256,2304]{1,0:T(8,128)(2,1)} %get-tuple-element.141.refs_0_, bf16[384,2304]{1,0:T(8,128)(2,1)} %get-tuple-element.150.refs_0_.refs_1_, bf16[256,768]{1,0:T(8,128)(2,1)} %get-tuple-element.158.refs_2_, ...), custom_call_target="tpu_custom_call" | custom-call | flops 1509949440 | bytes 6094848 | tf_op jit(solution)/shard_map/weight_back/pallas_call | solution.py:861
  244.1 4.6 %fold.6 = (bf16[192,1536]{1,0:T(8,128)(2,1)}, bf16[192,1536]{1,0:T(8,128)(2,1)}, bf16[192,1536]{1,0:T(8,128)(2,1)}, bf16[192,1536]{1,0:T(8,128)(2,1)}) custom-call(bf16[384,1536]{1,0:T(8,128)(2,1)} %get-tuple-element.156.keep_a, bf16[384,1536]{1,0:T(8,128)(2,1)} %copy-done.5, bf16[384,1536]{1,0:T(8,128)(2,1)} %get-tuple-element.161.keep_b, ...), custom_call_target="tpu_custom_call" | custom-call | flops 1179648 | bytes 7077888 | tf_op jit(solution)/shard_map/fold/pallas_call | solution.py:195
  254.9 10.4 %input_back.1 = (f32[640,768]{1,0:T(8,128)}, f32[1,768]{1,0:T(1,128)}, f32[1,768]{1,0:T(1,128)}) custom-call(bf16[256,2304]{1,0:T(8,128)(2,1)} %get-tuple-element.141.refs_0_, bf16[384,2304]{1,0:T(8,128)(2,1)} %get-tuple-element.150.refs_0_.refs_1_, bf16[768,2304]{1,0:T(8,128)(2,1)} %refs_2_.1, bf16[640,768]{1,0:T(8,128)(2,1)} %refs_3_.1, ...), custom_call_target="tpu_custom_call" | custom-call | flops 2264924160 | bytes 10420224 | tf_op jit(solution)/shard_map/input_back/pallas_call | solution.py:919
  267.1 3.5 %fold.7 = (bf16[96,1536]{1,0:T(8,128)(2,1)}, bf16[96,1536]{1,0:T(8,128)(2,1)}, bf16[96,1536]{1,0:T(8,128)(2,1)}, bf16[96,1536]{1,0:T(8,128)(2,1)}) custom-call(bf16[192,1536]{1,0:T(8,128)(2,1)} %get-tuple-element.163.refs_6_.keep_a, bf16[192,1536]{1,0:T(8,128)(2,1)} %copy-done.11, bf16[192,1536]{1,0:T(8,128)(2,1)} %get-tuple-element.174.keep_b, ...), custom_call_target="tpu_custom_call" | custom-call | flops 589824 | bytes 3538944 | tf_op jit(solution)/shard_map/fold/pallas_call | solution.py:195
  271.4 3.5 %all-to-all-start.2 = ((f32[32,1,4,768]{3,2,1,0:T(4,128)}), f32[32,1,4,768]{3,2,1,0:T(4,128)S(1)}, u32[]{:S(2)}, u32[]{:S(2)}) async-start(f32[32,1,4,768]{3,2,1,0:T(4,128)} %broadcast_in_dim.61), calls=%async_computation.2 | async-start | bytes 786432 | tf_op jit(solution)/shard_map/all_to_all | solution.py:46
  278.3 10.1 %collective-permute-done.33.got_a = bf16[96,1536]{1,0:T(8,128)(2,1)S(1)} collective-permute-done((bf16[96,1536]{1,0:T(8,128)(2,1)}, bf16[96,1536]{1,0:T(8,128)(2,1)S(1)}, u32[]{:S(2)}, u32[]{:S(2)}) %collective-permute-start.33) | collective-permute-done | bytes 294944 | tf_op jit(solution)/shard_map/ppermute | solution.py:26
  297.9 7.9 %grad_of_down.1 = f32[96,768]{1,0:T(8,128)} custom-call(bf16[1280,1024]{1,0:T(8,128)(2,1)} %bitcast.91, bf16[256,768]{1,0:T(8,128)(2,1)} %bitcast.95, f32[1,256]{1,0:T(1,128)} %get-tuple-element.181.col_sum_ref, f32[1,256]{1,0:T(1,128)} %get-tuple-element.182.col_count_ref, f32[1,128]{1,0:T(1,128)} %get-tuple-element.183.live_ref, ...), custom_call_target="tpu_custom_call" | custom-call | flops 1006632960 | bytes 2621440 | tf_op jit(solution)/shard_map/grad_of_down/pallas_call | solution.py:677
  (241 shorter events, 104.4 us)
Async XLA Ops:
  7.2 114.0 %all-gather.2.cloned.1.call-start = ((), (), s32[]{:S(2)}) async-start(), calls=%async_computation.3 | async-start | bytes 9732096 | tf_op jit(solution)/shard_map/all_gather | solution.py:966
  11.9 35.7 %collective-permute-start = (bf16[24,3072]{1,0:T(8,128)(2,1)S(1)}, bf16[24,3072]{1,0:T(8,128)(2,1)S(1)}, u32[]{:S(2)}, u32[]{:S(2)}) collective-permute-start(bf16[24,3072]{1,0:T(8,128)(2,1)S(1)} %constant_dynamic-update-slice_fusion), channel_id=1, source_target_pairs={{0,8},{1,9},{2,10},{3,11},{4,12},{5,13},{6,14},{7,15},{8,0},{9,1},... | collective-permute-start | bytes 442376 | tf_op jit(solution)/shard_map/ppermute | solution.py:26
  15.0 32.7 %collective-permute-start.1 = (bf16[24,3072]{1,0:T(8,128)(2,1)S(1)}, bf16[24,3072]{1,0:T(8,128)(2,1)S(1)}, u32[]{:S(2)}, u32[]{:S(2)}) collective-permute-start(bf16[24,3072]{1,0:T(8,128)(2,1)S(1)} %constant_dynamic-update-slice_fusion), channel_id=1, source_target_pairs={{0,16},{1,17},{2,18},{3,19},{4,20},{5,21},{6,22},{7,23},{8,24},{9,... | collective-permute-start | bytes 442376 | tf_op jit(solution)/shard_map/ppermute | solution.py:26
  17.6 30.1 %collective-permute-start.2 = (bf16[24,3072]{1,0:T(8,128)(2,1)S(1)}, bf16[24,3072]{1,0:T(8,128)(2,1)S(1)}, u32[]{:S(2)}, u32[]{:S(2)}) collective-permute-start(bf16[24,3072]{1,0:T(8,128)(2,1)S(1)} %constant_dynamic-update-slice_fusion), channel_id=1, source_target_pairs={{0,24},{1,25},{2,26},{3,27},{4,28},{5,29},{6,30},{7,31},{8,16},{9,... | collective-permute-start | bytes 442376 | tf_op jit(solution)/shard_map/ppermute | solution.py:26
  47.8 23.4 %collective-permute-start.3 = (bf16[96,3072]{1,0:T(8,128)(2,1)S(1)}, bf16[96,3072]{1,0:T(8,128)(2,1)S(1)}, u32[]{:S(2)}, u32[]{:S(2)}) collective-permute-start(bf16[96,3072]{1,0:T(8,128)(2,1)S(1)} %pad_maximum_fusion.6.refs_0_), channel_id=1, source_target_pairs={{0,2},{1,3},{2,0},{3,1},{4,6},{5,7},{6,4},{7,5},{8,10},{9,11},{10,... | collective-permute-start | bytes 1769480 | tf_op jit(solution)/shard_map/ppermute | solution.py:26
  49.6 21.6 %collective-permute-start.4 = (bf16[96,3072]{1,0:T(8,128)(2,1)S(1)}, bf16[96,3072]{1,0:T(8,128)(2,1)}, u32[]{:S(2)}, u32[]{:S(2)}) collective-permute-start(bf16[96,3072]{1,0:T(8,128)(2,1)S(1)} %pad_maximum_fusion.6.refs_0_), channel_id=1, source_target_pairs={{0,4},{1,5},{2,6},{3,7},{4,0},{5,1},{6,2},{7,3},{8,12},{9,13},{10,... | collective-permute-start | bytes 1769480 | tf_op jit(solution)/shard_map/ppermute | solution.py:26
  71.2 20.6 %collective-permute-start.8 = (bf16[48,3072]{1,0:T(8,128)(2,1)S(1)}, bf16[48,3072]{1,0:T(8,128)(2,1)S(1)}, u32[]{:S(2)}, u32[]{:S(2)}) collective-permute-start(bf16[48,3072]{1,0:T(8,128)(2,1)S(1)} %slice.45), channel_id=1, source_target_pairs={{0,4},{1,5},{2,6},{3,7},{4,0},{5,1},{6,2},{7,3},{8,12},{9,13},{10,... | collective-permute-start | bytes 884744 | tf_op jit(solution)/shard_map/ppermute | solution.py:26
  72.8 19.1 %collective-permute-start.9 = (bf16[48,3072]{1,0:T(8,128)(2,1)S(1)}, bf16[48,3072]{1,0:T(8,128)(2,1)S(1)}, u32[]{:S(2)}, u32[]{:S(2)}) collective-permute-start(bf16[48,3072]{1,0:T(8,128)(2,1)S(1)} %slice.46), channel_id=1, source_target_pairs={{0,2},{1,3},{2,0},{3,1},{4,6},{5,7},{6,4},{7,5},{8,10},{9,11},{10,... | collective-permute-start | bytes 884744 | tf_op jit(solution)/shard_map/ppermute | solution.py:26
  93.0 21.1 %collective-permute-start.15 = (bf16[4,40,1024]{2,1,0:T(8,128)(2,1)S(1)}, bf16[4,40,1024]{2,1,0:T(8,128)(2,1)S(1)}, u32[]{:S(2)}, u32[]{:S(2)}) collective-permute-start(bf16[4,40,1024]{2,1,0:T(8,128)(2,1)S(1)} %bitcast.97), channel_id=1, source_target_pairs={{0,2},{1,3},{2,0},{3,1},{4,6},{5,7},{6,4},{7,5},{8,10},{9,11},{10,... | collective-permute-start | bytes 983048 | tf_op jit(solution)/shard_map/ppermute | solution.py:26
  95.4 18.7 %collective-permute-start.16 = (bf16[4,40,1024]{2,1,0:T(8,128)(2,1)S(1)}, bf16[4,40,1024]{2,1,0:T(8,128)(2,1)S(1)}, u32[]{:S(2)}, u32[]{:S(2)}) collective-permute-start(bf16[4,40,1024]{2,1,0:T(8,128)(2,1)S(1)} %bitcast.98), channel_id=1, source_target_pairs={{0,4},{1,5},{2,6},{3,7},{4,0},{5,1},{6,2},{7,3},{8,12},{9,13},{10,... | collective-permute-start | bytes 983048 | tf_op jit(solution)/shard_map/ppermute | solution.py:26
  121.2 28.0 %collective-permute-start.19 = (bf16[16,40,1024]{2,1,0:T(8,128)(2,1)S(1)}, bf16[16,40,1024]{2,1,0:T(8,128)(2,1)S(1)}, u32[]{:S(2)}, u32[]{:S(2)}) collective-permute-start(bf16[16,40,1024]{2,1,0:T(8,128)(2,1)S(1)} %bitcast.92), channel_id=1, source_target_pairs={{0,1},{1,0},{2,3},{3,2},{4,5},{5,4},{6,7},{7,6},{8,9},{9,8},{10,11... | collective-permute-start | bytes 3932168 | tf_op jit(solution)/shard_map/ppermute | solution.py:26
  122.5 19.4 %all-to-all-start = ((bf16[40,32,96]{2,0,1:T(8,128)(2,1)}), bf16[40,32,96]{2,0,1:T(8,128)(2,1)S(1)}, u32[]{:S(2)}, u32[]{:S(2)}) async-start(bf16[40,32,96]{2,0,1:T(8,128)(2,1)} %copy.73), calls=%async_computation | async-start | bytes 655360 | tf_op jit(solution)/shard_map/all_to_all | solution.py:1017
  143.4 19.0 %all-to-all-start.1 = ((bf16[32,8,768]{2,1,0:T(8,128)(2,1)}), bf16[32,8,768]{2,1,0:T(8,128)(2,1)S(1)}, u32[]{:S(2)}, u32[]{:S(2)}) async-start(bf16[32,8,768]{2,1,0:T(8,128)(2,1)} %broadcast_in_dim.60), calls=%async_computation.1 | async-start | bytes 786432 | tf_op jit(solution)/shard_map/all_to_all | solution.py:46
  202.5 15.5 %collective-permute-start.22 = (bf16[192,1536]{1,0:T(8,128)(2,1)}, bf16[192,1536]{1,0:T(8,128)(2,1)S(1)}, u32[]{:S(2)}, u32[]{:S(2)}) collective-permute-start(bf16[192,1536]{1,0:T(8,128)(2,1)} %get-tuple-element.147.refs_1_), channel_id=1, source_target_pairs={{0,2},{1,3},{2,0},{3,1},{4,6},{5,7},{6,4},{7,5},{8,10},{9,11},{10,... | collective-permute-start | bytes 1769480 | tf_op jit(solution)/shard_map/ppermute | solution.py:26
  203.0 15.6 %collective-permute-start.23 = (bf16[192,1536]{1,0:T(8,128)(2,1)}, bf16[192,1536]{1,0:T(8,128)(2,1)S(1)}, u32[]{:S(2)}, u32[]{:S(2)}) collective-permute-start(bf16[192,1536]{1,0:T(8,128)(2,1)} %get-tuple-element.149.refs_3_), channel_id=1, source_target_pairs={{0,4},{1,5},{2,6},{3,7},{4,0},{5,1},{6,2},{7,3},{8,12},{9,13},{10,... | collective-permute-start | bytes 1769480 | tf_op jit(solution)/shard_map/ppermute | solution.py:26
  248.7 17.4 %collective-permute-start.31 = (bf16[192,1536]{1,0:T(8,128)(2,1)}, bf16[192,1536]{1,0:T(8,128)(2,1)S(1)}, u32[]{:S(2)}, u32[]{:S(2)}) collective-permute-start(bf16[192,1536]{1,0:T(8,128)(2,1)} %get-tuple-element.173), channel_id=1, source_target_pairs={{0,2},{1,3},{2,0},{3,1},{4,6},{5,7},{6,4},{7,5},{8,10},{9,11},{10,... | collective-permute-start | bytes 1769480 | tf_op jit(solution)/shard_map/ppermute | solution.py:26
  249.5 16.6 %collective-permute-start.32 = (bf16[192,1536]{1,0:T(8,128)(2,1)}, bf16[192,1536]{1,0:T(8,128)(2,1)S(1)}, u32[]{:S(2)}, u32[]{:S(2)}) collective-permute-start(bf16[192,1536]{1,0:T(8,128)(2,1)} %get-tuple-element.175), channel_id=1, source_target_pairs={{0,4},{1,5},{2,6},{3,7},{4,0},{5,1},{6,2},{7,3},{8,12},{9,13},{10,... | collective-permute-start | bytes 1769480 | tf_op jit(solution)/shard_map/ppermute | solution.py:26
  250.5 14.8 %collective-permute-start.28 = (bf16[24,3072]{1,0:T(8,128)(2,1)S(1)}, bf16[24,3072]{1,0:T(8,128)(2,1)S(1)}, u32[]{:S(2)}, u32[]{:S(2)}) collective-permute-start(bf16[24,3072]{1,0:T(8,128)(2,1)S(1)} %copy-done.43), channel_id=1, source_target_pairs={{0,8},{1,9},{2,10},{3,11},{4,12},{5,13},{6,14},{7,15},{8,0},{9,1},... | collective-permute-start | bytes 442376 | tf_op jit(solution)/shard_map/ppermute | solution.py:26
  251.5 13.9 %collective-permute-start.29 = (bf16[24,3072]{1,0:T(8,128)(2,1)S(1)}, bf16[24,3072]{1,0:T(8,128)(2,1)S(1)}, u32[]{:S(2)}, u32[]{:S(2)}) collective-permute-start(bf16[24,3072]{1,0:T(8,128)(2,1)S(1)} %copy-done.42), channel_id=1, source_target_pairs={{0,16},{1,17},{2,18},{3,19},{4,20},{5,21},{6,22},{7,23},{8,24},{9,... | collective-permute-start | bytes 442376 | tf_op jit(solution)/shard_map/ppermute | solution.py:26
  252.2 13.2 %collective-permute-start.30 = (bf16[24,3072]{1,0:T(8,128)(2,1)S(1)}, bf16[24,3072]{1,0:T(8,128)(2,1)S(1)}, u32[]{:S(2)}, u32[]{:S(2)}) collective-permute-start(bf16[24,3072]{1,0:T(8,128)(2,1)S(1)} %copy-done.41), channel_id=1, source_target_pairs={{0,24},{1,25},{2,26},{3,27},{4,28},{5,29},{6,30},{7,31},{8,16},{9,... | collective-permute-start | bytes 442376 | tf_op jit(solution)/shard_map/ppermute | solution.py:26
  271.4 25.8 %all-to-all-start.2 = ((f32[32,1,4,768]{3,2,1,0:T(4,128)}), f32[32,1,4,768]{3,2,1,0:T(4,128)S(1)}, u32[]{:S(2)}, u32[]{:S(2)}) async-start(f32[32,1,4,768]{3,2,1,0:T(4,128)} %broadcast_in_dim.61), calls=%async_computation.2 | async-start | bytes 786432 | tf_op jit(solution)/shard_map/all_to_all | solution.py:46
  275.0 13.4 %collective-permute-start.33 = (bf16[96,1536]{1,0:T(8,128)(2,1)}, bf16[96,1536]{1,0:T(8,128)(2,1)S(1)}, u32[]{:S(2)}, u32[]{:S(2)}) collective-permute-start(bf16[96,1536]{1,0:T(8,128)(2,1)} %get-tuple-element.186), channel_id=1, source_target_pairs={{0,4},{1,5},{2,6},{3,7},{4,0},{5,1},{6,2},{7,3},{8,12},{9,13},{10,... | collective-permute-start | bytes 884744 | tf_op jit(solution)/shard_map/ppermute | solution.py:26
  292.0 13.8 %collective-permute-start.35 = (bf16[24,3072]{1,0:T(8,128)(2,1)}, bf16[24,3072]{1,0:T(8,128)(2,1)S(1)}, u32[]{:S(2)}, u32[]{:S(2)}) collective-permute-start(bf16[24,3072]{1,0:T(8,128)(2,1)} %get-tuple-element.190), channel_id=1, source_target_pairs={{0,8},{1,9},{2,10},{3,11},{4,12},{5,13},{6,14},{7,15},{8,0},{9,1},... | collective-permute-start | bytes 442376 | tf_op jit(solution)/shard_map/ppermute | solution.py:26
  293.6 14.1 %collective-permute-start.36 = (bf16[24,3072]{1,0:T(8,128)(2,1)}, bf16[24,3072]{1,0:T(8,128)(2,1)S(1)}, u32[]{:S(2)}, u32[]{:S(2)}) collective-permute-start(bf16[24,3072]{1,0:T(8,128)(2,1)} %get-tuple-element.191), channel_id=1, source_target_pairs={{0,16},{1,17},{2,18},{3,19},{4,20},{5,21},{6,22},{7,23},{8,24},{9,... | collective-permute-start | bytes 442376 | tf_op jit(solution)/shard_map/ppermute | solution.py:26
  (65 other events, 424.1 us)
Sparse Core Ops, SparseCore 0:
  11.0 97.0 all-gather.1
where the time goes:
time: 319 us; the launch traced here: 317 us
  Pallas kernels  152 us (48%)
  starting transfers between devices  52.8 us (17%)
  waiting for transfers between devices  51.3 us (16%)
  local copies, waits for them, and re-layouts  25.5 us (8%)
  between operations  14.8 us (5%)
  other arithmetic  12.2 us (4%)
  matrix products  8.46 us (3%)
    ppermute x38, waiting for transfers between devices, swapped(): return lax.ppermute(value, AXIS, [(i, i ^ mask) for i in range(peers)])  40 us
    ppermute x38, starting transfers between devices, swapped(): return lax.ppermute(value, AXIS, [(i, i ^ mask) for i in range(peers)])  38 us
    pallas_call x1, Pallas kernels, mlp_back(): pl.pallas_call(mlp_back_kernel, grid=(steps,), out_shape=[part] * 4 + [ja...  21.4 us
    pallas_call x1, Pallas kernels, text_front(): pl.pallas_call(text_front_kernel, out_shape=[jax.ShapeDtypeStruct(*item)...  18 us
    pallas_call x2, Pallas kernels, attention_back(): pl.pallas_call(attention_back_kernel, grid=(count,), out_shape=[jax.Shape...  16.8 us
    pallas_call x4, Pallas kernels, fold(): pl.pallas_call(fold_kernel, grid=(cols // tile,), out_shape=[jax.ShapeDty...  16.1 us
    pallas_call x1, Pallas kernels, image_up(): pl.pallas_call(functools.partial(image_up_kernel, fold), grid=(FF // TILE...  14.1 us
    pallas_call x1, Pallas kernels, image_front(): pl.pallas_call(functools.partial(image_front_kernel, windows), out_shape=...  14 us
  transfers between devices with their start and end apart: 42, of which 16 were waited for; matrix products, arithmetic and copies ran while one was open for 10% of the time, Pallas kernels for 35%

commit v1 on v0

--- a/solution.py
+++ b/solution.py
@@ -569,6 +569,48 @@
         cost_estimate=cost(2 * rows * D * FF, 4 * D * FF, 15 * rows * FF),
         name="image_up",
     )(normed2, whole, whole, middle_sum, *after)
+
+
+def left_kernel(order_ref, h2_ref, h1_ref, att_ref, up_ref, rest_ref):
+    step = pl.program_id(0)
+
+    @pl.when(step < 2)
+    def _():
+        up_ref[0] = placed(order_ref[0], h2_ref[...])
+
+    @pl.when((step == 2) | (step == 3))
+    def _():
+        rest_ref[0] = placed(order_ref[0], h1_ref[...])
+
+    @pl.when(step == 4)
+    def _():
+        rest_ref[0] = placed(order_ref[0], att_ref[...])
+
+
+def left_factors(orders, normed2, normed1, attended):
+    rows = normed1.shape[0]
+    fixed = pl.BlockSpec((rows, D), lambda i: (0, 0))
+    return pl.pallas_call(
+        left_kernel,
+        grid=(5,),
+        out_shape=[
+            jax.ShapeDtypeStruct((2, D, rows), bf16),
+            jax.ShapeDtypeStruct((3, D, rows), bf16),
+        ],
+        in_specs=[
+            pl.BlockSpec((1, D, D), lambda i: (jnp.minimum(i % 2 + i // 4, 1), 0, 0)),
+            fixed,
+            fixed,
+            fixed,
+        ],
+        out_specs=[
+            pl.BlockSpec((1, D, rows), lambda i: (jnp.minimum(i, 1), 0, 0)),
+            pl.BlockSpec((1, D, rows), lambda i: (jnp.maximum(i - 2, 0), 0, 0)),
+        ],
+        compiler_params=params(),
+        cost_estimate=cost(10 * rows * D * D, 16 * rows * D + 10 * D * D),
+        name="left_factors",
+    )(orders, normed2, normed1, attended)
 
 
 def loss_parts(text_rows, pos, image_all):
@@ -1000,7 +1042,11 @@
         held = own_pack[None]
         first, second = diagonal(beside, above)
         others = [swapped(held, mask) for mask in (8, 16, 24)]
-        others, first, second = lax.optimization_barrier((others, first, second))
+        scaled_sum = (hidden_sum * inverse[:, :1]).astype(bf16)
+        hidden_cols = lax.all_to_all(scaled_sum, AXIS, split_axis=1, concat_axis=0, tiled=True)
+        others, first, second, hidden_cols = lax.optimization_barrier(
+            (others, first, second, hidden_cols)
+        )
         held = joined(joined(held, others[0], 8), joined(others[1], others[2], 8), 16, 1)
         text_beside, text_above = swapped(held, 2), swapped(held, 4)
         pieces = [line, beside, above, first, second]
@@ -1010,28 +1056,24 @@
         images, pieces, perm, img_gain1, img_bias1, img_gain2, img_bias2
     )
     if small:
-        scaled_sum = (hidden_sum * inverse[:, :1]).astype(bf16)
-        normed_img, scaled_sum, text_beside, text_above = lax.optimization_barrier(
-            (normed_img, scaled_sum, text_beside, text_above)
+        normed_img, text_beside, text_above = lax.optimization_barrier(
+            (normed_img, text_beside, text_above)
         )
-        hidden_cols = lax.all_to_all(scaled_sum, AXIS, split_axis=1, concat_axis=0, tiled=True)
         across = jnp.concatenate(diagonal(text_beside, text_above), axis=0)
         held = joined(joined(held, text_beside, 2), joined(text_above, across, 2), 4, 4)
 
     order_a, order_b, tail = stage_orders()
-    matrix_a, matrix_b = row_order(order_a + tail[::-1]), row_order(order_b + tail[::-1])
-    lhs_up = jnp.stack([placed(matrix_a, normed2), placed(matrix_b, normed2)])
-    lhs_rest = jnp.stack(
-        [placed(matrix_a, normed1), placed(matrix_b, normed1), placed(matrix_b, attended)]
-    )
+    orders = jnp.stack([row_order(order_a + tail[::-1]), row_order(order_b + tail[::-1])])
     if small:
-        whole, lhs_up, lhs_rest, held = lax.optimization_barrier((whole, lhs_up, lhs_rest, held))
+        whole, held, orders = lax.optimization_barrier((whole, held, orders))
         other = swapped(held, 1)
     image_low = image_up(normed_img, whole, 0, FF, middle_img)
     if small:
-        image_low, hidden_cols = in_turn(image_low, hidden_cols)
         text_pack = joined(held, other, 1).reshape(-1, D + total_images)
+    image_low, normed2 = in_turn(image_low, normed2)
     image_all = spread(image_low).reshape(total_images, D)
+    lhs_up, lhs_rest = left_factors(orders, normed2, normed1, attended)
+    image_all, lhs_up = in_turn(image_all, lhs_up)
 
     if small:
         loss_value, grad_row, row_low, col_sum, col_count, live_total = loss_and_rows(
@@ -1050,10 +1092,10 @@
         grad_row, row_low, txt_down, slope, txt_up, lhs_up, middle, txt_gain2
     )
     stages = len(order_a)
-    low_one, proj_one = attention_back(grad_middle, txt_out, project, log_sums, 0, 2)
+    low_one, proj_one = attention_back(grad_middle, txt_out, project, log_sums, 0, 1)
     for stage in range(stages - 2):
         up = fold(hand_on(up, stage), (proj_one,))
-    low_two, proj_two = attention_back(grad_middle, txt_out, project, log_sums, 2, 3, up)
+    low_two, proj_two = attention_back(grad_middle, txt_out, project, log_sums, 1, 4, up)
     up = fold(hand_on(up, stages - 2), (proj_two,))
     projs, lows = (proj_one, proj_two), (low_one, low_two)
     rest_a = weight_back(lhs_rest, 0, [projs], [0], up)
@@ -1069,7 +1111,7 @@
     rest = fold(hand_on(rest, stages - 2), (caption_grad,))
     norms = jnp.concatenate([gain_one, bias_one, gain_two, bias_two], axis=0)
     norms, rest = in_turn(norms, rest)
-    norms = jnp.sum(spread(norms[None]), axis=0).reshape(4, D)
+    norms = jnp.sum(spread(norms[None].astype(bf16)).astype(f32), axis=0).reshape(4, D)
     rest = fold_last(hand_on(rest, stages - 1))
     if small:
         grad_down = grad_of_down(

time: 319 us -> 305 us (0.956)
  waiting for transfers between devices: 51.3 us -> 33.1 us
  Pallas kernels: 152 us -> 162 us
  matrix products: 8.46 us -> 0 us
  starting transfers between devices: 52.8 us -> 58.7 us
    ppermute x38, waiting for transfers between devices: 40 us -> 29.9 us  [swapped(): return lax.ppermute(value, AXIS, [(i, i ^ mask) for i in range(peers)])]
    pallas_call x0 -> x1, Pallas kernels: none -> 9.76 us  [left_factors(): pl.pallas_call(left_kernel, grid=(5,), out_shape=[jax.ShapeDtypeStruct((2...]
    dot_general x5 -> x0, matrix products: 8.46 us -> none  [mul_bt(): lax.dot_general(lhs, rhs, (((1,), (1,)), ((), ())), preferred_element_typ...]
    all_to_all x2, waiting for transfers between devices: 11.3 us -> 3.19 us  [spread(): return lax.all_to_all(copies, AXIS, split_axis=0, concat_axis=0, tiled=True)]
    all_to_all x2, starting transfers between devices: 9.38 us -> 13.8 us  [spread(): return lax.all_to_all(copies, AXIS, split_axis=0, concat_axis=0, tiled=True)]
    unnamed x97 -> x79, local copies, waits for them, and re-layouts: 8.99 us -> 7.52 us
  transfers between devices with their start and end apart: 42 -> 42, of which waited for: 16 -> 13; matrix products, arithmetic and copies ran while one was open for 10% -> 7% of each run, Pallas kernels for 35% -> 40%
where the time goes in v1:
time: 305 us; the launch traced here: 304 us
  Pallas kernels  162 us (53%)
  starting transfers between devices  58.7 us (19%)
  waiting for transfers between devices  33.1 us (11%)
  local copies, waits for them, and re-layouts  23 us (8%)
  between operations  14.7 us (5%)
  other arithmetic  12.4 us (4%)
    ppermute x38, starting transfers between devices, swapped(): return lax.ppermute(value, AXIS, [(i, i ^ mask) for i in range(peers)])  40.5 us
    ppermute x38, waiting for transfers between devices, swapped(): return lax.ppermute(value, AXIS, [(i, i ^ mask) for i in range(peers)])  29.9 us
    pallas_call x1, Pallas kernels, mlp_back(): pl.pallas_call(mlp_back_kernel, grid=(steps,), out_shape=[part] * 4 + [ja...  21.4 us
    pallas_call x1, Pallas kernels, text_front(): pl.pallas_call(text_front_kernel, out_shape=[jax.ShapeDtypeStruct(*item)...  18 us
    pallas_call x2, Pallas kernels, attention_back(): pl.pallas_call(attention_back_kernel, grid=(count,), out_shape=[jax.Shape...  16.6 us
    pallas_call x4, Pallas kernels, fold(): pl.pallas_call(fold_kernel, grid=(cols // tile,), out_shape=[jax.ShapeDty...  16.1 us
    pallas_call x1, Pallas kernels, image_up(): pl.pallas_call(functools.partial(image_up_kernel, fold), grid=(FF // TILE...  14.1 us
    pallas_call x1, Pallas kernels, image_front(): pl.pallas_call(functools.partial(image_front_kernel, windows), out_shape=...  13.8 us
  transfers between devices with their start and end apart: 42, of which 13 were waited for; matrix products, arithmetic and copies ran while one was open for 7% of the time, Pallas kernels for 40%

profile of v1, /device:TPU:0, one launch (start us, length us, event | category | flops | bytes accessed | tf_op | source)
XLA Modules:
  0.0 304.3 jit_solution(7547016463913343792)
XLA Ops:
  10.3 3.1 %collective-permute-start = (bf16[24,3072]{1,0:T(8,128)(2,1)S(1)}, bf16[24,3072]{1,0:T(8,128)(2,1)S(1)}, u32[]{:S(2)}, u32[]{:S(2)}) collective-permute-start(bf16[24,3072]{1,0:T(8,128)(2,1)S(1)} %constant_dynamic-update-slice_fusion), channel_id=1, source_target_pairs={{0,8},{1,9},{2,10},{3,11},{4,12},{5,13},{6,14},{7,15},{8,0},{9,1},... | collective-permute-start | bytes 442376 | tf_op jit(solution)/shard_map/ppermute | solution.py:26
  18.6 18.0 %text_front.1 = (bf16[640,768]{1,0:T(8,128)(2,1)}, bf16[640,2304]{1,0:T(8,128)(2,1)}, bf16[640,768]{1,0:T(8,128)(2,1)}, f32[640,768]{1,0:T(8,128)}, bf16[640,768...) custom-call(bf16[640,768]{1,0:T(8,128)(2,1)} %refs_3_.1, f32[1,768]{1,0:T(1,128)} %broadcast_in_dim.26.g1_ref.refs_4_, ...), custom_call_target="tpu_custom_call" | custom-call | flops 3019898880 | bytes 11599872 | tf_op jit(solution)/shard_map/text_front/pallas_call | solution.py:329
  42.1 13.7 %text_up.1 = (bf16[640,3072]{1,0:T(8,128)(2,1)}, f32[40,3072]{1,0:T(8,128)}, f32[40,768]{1,0:T(8,128)}, f32[40,128]{1,0:T(8,128)}) custom-call(bf16[640,768]{1,0:T(8,128)(2,1)} %get-tuple-element.133.h2_ref, bf16[768,3072]{1,0:T(8,128)(2,1)} %wu_ref.3, bf16[3072,768]{1,0:T(8,128)(2,1)} %wd_ref.3, f32[40,768]{1,0:T(8,128)} %get-tuple-element.112.sum_ref, ...), custom_call_target="tpu_custom_call" | custom-call | flops 3019898880 | bytes 13369344 | tf_op jit(solution)/shard_map/text_up/pallas_call | solution.py:488
  58.9 4.4 %all-to-all-start = ((bf16[40,32,96]{2,0,1:T(8,128)(2,1)}), bf16[40,32,96]{2,0,1:T(8,128)(2,1)S(1)}, u32[]{:S(2)}, u32[]{:S(2)}) async-start(bf16[40,32,96]{2,0,1:T(8,128)(2,1)} %copy.75), calls=%async_computation | async-start | bytes 655360 | tf_op jit(solution)/shard_map/all_to_all | solution.py:1046
  76.3 8.0 %collective-permute-done.6 = bf16[1,40,1024]{2,1,0:T(8,128)(2,1)S(1)} collective-permute-done((bf16[1,40,1024]{2,1,0:T(8,128)(2,1)}, bf16[1,40,1024]{2,1,0:T(8,128)(2,1)S(1)}, u32[]{:S(2)}, u32[]{:S(2)}) %collective-permute-start.6) | collective-permute-done | bytes 81952 | tf_op jit(solution)/shard_map/ppermute | solution.py:26
  92.5 13.8 %image_front.1 = (bf16[400,768]{1,0:T(8,128)(2,1)}, f32[8,768]{1,0:T(8,128)}) custom-call(bf16[400,768]{1,0:T(8,128)(2,1)} %x_ref.3, bf16[768,768]{1,0:T(8,128)(2,1)} %fusion.perm_ref, bf16[1,768]{1,0:T(2,128)(2,1)} %broadcast_in_dim.22.g1_ref, bf16[1,768]{1,0:T(2,128)(2,1)} %broadcast_in_dim.23.b1_ref, bf16[1,768]{1,0:T(2,128)(2,1)} %broadcast_in_dim.24.g2_ref, ...), custom_call_target="tpu_custom_call" | custom-call | flops 2831155200 | bytes 4718592 | tf_op jit(solution)/shard_map/image_front/pallas_call | solution.py:393
  108.9 3.2 %collective-permute-done.17 = bf16[2,40,1024]{2,1,0:T(8,128)(2,1)S(1)} collective-permute-done((bf16[2,40,1024]{2,1,0:T(8,128)(2,1)S(1)}, bf16[2,40,1024]{2,1,0:T(8,128)(2,1)S(1)}, u32[]{:S(2)}, u32[]{:S(2)}) %collective-permute-start.17) | collective-permute-done | bytes 163872 | tf_op jit(solution)/shard_map/ppermute | solution.py:26
  113.3 14.1 %image_up.1 = bf16[8,768]{1,0:T(8,128)(2,1)} custom-call(bf16[400,768]{1,0:T(8,128)(2,1)} %get-tuple-element.128.h2_ref, bf16[768,6144]{1,0:T(8,128)(2,1)} %all-gather.2.cloned.1.call-done.wu_ref.wd_ref, bf16[768,6144]{1,0:T(8,128)(2,1)} %all-gather.2.cloned.1.call-done.wu_ref.wd_ref, f32[8,768]{1,0:T(8,128)} %get-tuple-element.130.sum_ref), custom_call_target="tpu_custom_call" | custom-call | flops 1887436800 | bytes 9437184 | tf_op jit(solution)/shard_map/image_up/pallas_call | solution.py:555
  128.8 10.7 %all-to-all-start.1 = ((bf16[32,8,768]{2,1,0:T(8,128)(2,1)}), bf16[32,8,768]{2,1,0:T(8,128)(2,1)S(1)}, u32[]{:S(2)}, u32[]{:S(2)}) async-start(bf16[32,8,768]{2,1,0:T(8,128)(2,1)} %broadcast_in_dim.62), calls=%async_computation.1 | async-start | bytes 786432 | tf_op jit(solution)/shard_map/all_to_all | solution.py:46
  139.6 9.8 %left_factors.1 = (bf16[2,768,640]{2,1,0:T(8,128)(2,1)}, bf16[3,768,640]{2,1,0:T(8,128)(2,1)}) custom-call(bf16[2,768,768]{2,1,0:T(8,128)(2,1)} %add_convert_fusion.order_ref, bf16[640,768]{1,0:T(8,128)(2,1)} %get-tuple-element.133.h2_ref, bf16[640,768]{1,0:T(8,128)(2,1)} %get-tuple-element.134.h1_ref, bf16[640,768]{1,0:T(8,128)(2,1)} %get-tuple-element.135.att_ref), custom_call_target="tpu_custom_call" | custom-call | flops 3774873600 | bytes 13762560 | tf_op jit(solution)/shard_map/left_factors/pallas_call | solution.py:593
  149.3 3.2 %all-to-all-done.1 = bf16[32,8,768]{2,1,0:T(8,128)(2,1)S(1)} async-done(((bf16[32,8,768]{2,1,0:T(8,128)(2,1)}), bf16[32,8,768]{2,1,0:T(8,128)(2,1)S(1)}, u32[]{:S(2)}, u32[]{:S(2)}) %all-to-all-start.1) | async-done | bytes 393248 | tf_op jit(solution)/shard_map/all_to_all | solution.py:46
  155.0 4.0 %loss_and_rows.1 = (f32[1,128]{1,0:T(1,128)}, f32[40,768]{1,0:T(8,128)}, bf16[40,768]{1,0:T(8,128)(2,1)}, f32[1,256]{1,0:T(1,128)}, f32[1,256]{1,0:T(1,128)}, /*index=5*/f32[1,128]{1,0:T(1,128)}) custom-call(bf16[1280,1024]{1,0:T(8,128)(2,1)} %bitcast.75, bf16[256,768]{1,0:T(8,128)(2,1)} %bitcast.79, bf16[40,1024]{1,0:T(8,128)(2,1)} %packed.1.own_ref, ...), custom_call_target="tpu_custom_call" | custom-call | flops 503316480 | bytes 2621440 | tf_op jit(solution)/shard_map/loss_and_rows/pallas_call | solution.py:687
  159.1 21.4 %mlp_back.1 = (bf16[384,1536]{1,0:T(8,128)(2,1)}, bf16[384,1536]{1,0:T(8,128)(2,1)}, bf16[384,1536]{1,0:T(8,128)(2,1)}, bf16[384,1536]{1,0:T(8,128)(2,1)}, f32[6...) custom-call(bf16[40,768]{1,0:T(8,128)(2,1)} %get-tuple-element.139.low_ref, bf16[3072,768]{1,0:T(8,128)(2,1)} %wd_ref.3, ...), custom_call_target="tpu_custom_call" | custom-call | flops 6039797760 | bytes 18087936 | tf_op jit(solution)/shard_map/mlp_back/pallas_call | solution.py:796
  181.1 4.6 %attention_back.2 = (bf16[128,768]{1,0:T(8,128)(2,1)}, bf16[128,2304]{1,0:T(8,128)(2,1)}) custom-call(f32[640,768]{1,0:T(8,128)} %get-tuple-element.144.grad_ref.refs_5_, bf16[768,768]{1,0:T(8,128)(2,1)} %wo_ref.5, bf16[640,2304]{1,0:T(8,128)(2,1)} %get-tuple-element.145.qkv_ref, f32[80,128]{1,0:T(8,128)} %get-tuple-element.146.lse_ref), custom_call_target="tpu_custom_call" | custom-call | flops 754974720 | bytes 2752512 | tf_op jit(solution)/shard_map/attention_back/pallas_call | solution.py:851
  187.1 4.5 %fold.4 = (bf16[192,1536]{1,0:T(8,128)(2,1)}, bf16[192,1536]{1,0:T(8,128)(2,1)}, bf16[192,1536]{1,0:T(8,128)(2,1)}, bf16[192,1536]{1,0:T(8,128)(2,1)}) custom-call(bf16[384,1536]{1,0:T(8,128)(2,1)} %get-tuple-element.148.keep_a, bf16[384,1536]{1,0:T(8,128)(2,1)} %copy-done.6, bf16[384,1536]{1,0:T(8,128)(2,1)} %get-tuple-element.150.keep_b, ...), custom_call_target="tpu_custom_call" | custom-call | flops 1179648 | bytes 7077888 | tf_op jit(solution)/shard_map/fold/pallas_call | solution.py:195
  193.6 11.9 %attention_back.3 = (bf16[512,768]{1,0:T(8,128)(2,1)}, bf16[512,2304]{1,0:T(8,128)(2,1)}) custom-call(f32[640,768]{1,0:T(8,128)} %get-tuple-element.144.grad_ref.refs_5_, bf16[768,768]{1,0:T(8,128)(2,1)} %wo_ref.5, bf16[640,2304]{1,0:T(8,128)(2,1)} %get-tuple-element.145.qkv_ref, f32[80,128]{1,0:T(8,128)} %get-tuple-element.146.lse_ref, ...), custom_call_target="tpu_custom_call" | custom-call | flops 3019898880 | bytes 7471104 | tf_op jit(solution)/shard_map/attention_back/pallas_call | solution.py:851
  208.6 3.5 %fold.5 = (bf16[96,1536]{1,0:T(8,128)(2,1)}, bf16[96,1536]{1,0:T(8,128)(2,1)}, bf16[96,1536]{1,0:T(8,128)(2,1)}, bf16[96,1536]{1,0:T(8,128)(2,1)}) custom-call(bf16[192,1536]{1,0:T(8,128)(2,1)} %get-tuple-element.152.refs_0_.keep_a, bf16[192,1536]{1,0:T(8,128)(2,1)} %copy-done.9, bf16[192,1536]{1,0:T(8,128)(2,1)} %get-tuple-element.154.refs_2_.keep_b, ...), custom_call_target="tpu_custom_call" | custom-call | flops 589824 | bytes 3538944 | tf_op jit(solution)/shard_map/fold/pallas_call | solution.py:195
  214.2 4.8 %weight_back.2 = (bf16[384,1536]{1,0:T(8,128)(2,1)}, bf16[384,1536]{1,0:T(8,128)(2,1)}) custom-call(bf16[3,768,640]{2,1,0:T(8,128)(2,1)} %get-tuple-element.157.lhs_ref, bf16[128,2304]{1,0:T(8,128)(2,1)} %get-tuple-element.147.refs_0_, bf16[512,2304]{1,0:T(8,128)(2,1)} %get-tuple-element.156.refs_0_.refs_1_, ...), custom_call_target="tpu_custom_call" | custom-call | flops 1509949440 | bytes 6094848 | tf_op jit(solution)/shard_map/weight_back/pallas_call | solution.py:903
  224.2 5.4 %weight_back.3 = (bf16[384,1536]{1,0:T(8,128)(2,1)}, bf16[384,1536]{1,0:T(8,128)(2,1)}) custom-call(bf16[3,768,640]{2,1,0:T(8,128)(2,1)} %get-tuple-element.157.lhs_ref, bf16[128,2304]{1,0:T(8,128)(2,1)} %get-tuple-element.147.refs_0_, bf16[512,2304]{1,0:T(8,128)(2,1)} %get-tuple-element.156.refs_0_.refs_1_, bf16[128,768]{1,0:T(8,128)(2,1)} %get-tuple-element.164.refs_2_, ...), custom_call_target="tpu_custom_call" | custom-call | flops 1509949440 | bytes 6094848 | tf_op jit(solution)/shard_map/weight_back/pallas_call | solution.py:903
  233.6 4.6 %fold.6 = (bf16[192,1536]{1,0:T(8,128)(2,1)}, bf16[192,1536]{1,0:T(8,128)(2,1)}, bf16[192,1536]{1,0:T(8,128)(2,1)}, bf16[192,1536]{1,0:T(8,128)(2,1)}) custom-call(bf16[384,1536]{1,0:T(8,128)(2,1)} %get-tuple-element.162.keep_a, bf16[384,1536]{1,0:T(8,128)(2,1)} %copy-done.5, bf16[384,1536]{1,0:T(8,128)(2,1)} %get-tuple-element.167.keep_b, ...), custom_call_target="tpu_custom_call" | custom-call | flops 1179648 | bytes 7077888 | tf_op jit(solution)/shard_map/fold/pallas_call | solution.py:195
  244.4 10.9 %input_back.1 = (f32[640,768]{1,0:T(8,128)}, f32[1,768]{1,0:T(1,128)}, f32[1,768]{1,0:T(1,128)}) custom-call(bf16[128,2304]{1,0:T(8,128)(2,1)} %get-tuple-element.147.refs_0_, bf16[512,2304]{1,0:T(8,128)(2,1)} %get-tuple-element.156.refs_0_.refs_1_, bf16[768,2304]{1,0:T(8,128)(2,1)} %refs_2_.1, bf16[640,768]{1,0:T(8,128)(2,1)} %refs_3_.1, ...), custom_call_target="tpu_custom_call" | custom-call | flops 2264924160 | bytes 10420224 | tf_op jit(solution)/shard_map/input_back/pallas_call | solution.py:961
  257.2 3.5 %fold.7 = (bf16[96,1536]{1,0:T(8,128)(2,1)}, bf16[96,1536]{1,0:T(8,128)(2,1)}, bf16[96,1536]{1,0:T(8,128)(2,1)}, bf16[96,1536]{1,0:T(8,128)(2,1)}) custom-call(bf16[192,1536]{1,0:T(8,128)(2,1)} %get-tuple-element.169.refs_6_.keep_a, bf16[192,1536]{1,0:T(8,128)(2,1)} %copy-done.13, bf16[192,1536]{1,0:T(8,128)(2,1)} %get-tuple-element.180.keep_b, ...), custom_call_target="tpu_custom_call" | custom-call | flops 589824 | bytes 3538944 | tf_op jit(solution)/shard_map/fold/pallas_call | solution.py:195
  268.5 7.3 %collective-permute-done.33.got_a = bf16[96,1536]{1,0:T(8,128)(2,1)S(1)} collective-permute-done((bf16[96,1536]{1,0:T(8,128)(2,1)}, bf16[96,1536]{1,0:T(8,128)(2,1)S(1)}, u32[]{:S(2)}, u32[]{:S(2)}) %collective-permute-start.33) | collective-permute-done | bytes 294944 | tf_op jit(solution)/shard_map/ppermute | solution.py:26
  284.5 7.9 %grad_of_down.1 = f32[96,768]{1,0:T(8,128)} custom-call(bf16[1280,1024]{1,0:T(8,128)(2,1)} %bitcast.76, bf16[256,768]{1,0:T(8,128)(2,1)} %bitcast.80, f32[1,256]{1,0:T(1,128)} %get-tuple-element.187.col_sum_ref, f32[1,256]{1,0:T(1,128)} %get-tuple-element.188.col_count_ref, f32[1,128]{1,0:T(1,128)} %get-tuple-element.189.live_ref, ...), custom_call_target="tpu_custom_call" | custom-call | flops 1006632960 | bytes 2621440 | tf_op jit(solution)/shard_map/grad_of_down/pallas_call | solution.py:719
  (219 shorter events, 93.3 us)
Async XLA Ops:
  7.2 105.9 %all-gather.2.cloned.1.call-start = ((), (), s32[]{:S(2)}) async-start(), calls=%async_computation.3 | async-start | bytes 9732096 | tf_op jit(solution)/shard_map/all_gather | solution.py:1008
  10.3 28.3 %collective-permute-start = (bf16[24,3072]{1,0:T(8,128)(2,1)S(1)}, bf16[24,3072]{1,0:T(8,128)(2,1)S(1)}, u32[]{:S(2)}, u32[]{:S(2)}) collective-permute-start(bf16[24,3072]{1,0:T(8,128)(2,1)S(1)} %constant_dynamic-update-slice_fusion), channel_id=1, source_target_pairs={{0,8},{1,9},{2,10},{3,11},{4,12},{5,13},{6,14},{7,15},{8,0},{9,1},... | collective-permute-start | bytes 442376 | tf_op jit(solution)/shard_map/ppermute | solution.py:26
  13.4 25.3 %collective-permute-start.1 = (bf16[24,3072]{1,0:T(8,128)(2,1)S(1)}, bf16[24,3072]{1,0:T(8,128)(2,1)S(1)}, u32[]{:S(2)}, u32[]{:S(2)}) collective-permute-start(bf16[24,3072]{1,0:T(8,128)(2,1)S(1)} %constant_dynamic-update-slice_fusion), channel_id=1, source_target_pairs={{0,16},{1,17},{2,18},{3,19},{4,20},{5,21},{6,22},{7,23},{8,24},{9,... | collective-permute-start | bytes 442376 | tf_op jit(solution)/shard_map/ppermute | solution.py:26
  16.0 22.7 %collective-permute-start.2 = (bf16[24,3072]{1,0:T(8,128)(2,1)S(1)}, bf16[24,3072]{1,0:T(8,128)(2,1)S(1)}, u32[]{:S(2)}, u32[]{:S(2)}) collective-permute-start(bf16[24,3072]{1,0:T(8,128)(2,1)S(1)} %constant_dynamic-update-slice_fusion), channel_id=1, source_target_pairs={{0,24},{1,25},{2,26},{3,27},{4,28},{5,29},{6,30},{7,31},{8,16},{9,... | collective-permute-start | bytes 442376 | tf_op jit(solution)/shard_map/ppermute | solution.py:26
  38.8 24.5 %collective-permute-start.3 = (bf16[96,3072]{1,0:T(8,128)(2,1)S(1)}, bf16[96,3072]{1,0:T(8,128)(2,1)S(1)}, u32[]{:S(2)}, u32[]{:S(2)}) collective-permute-start(bf16[96,3072]{1,0:T(8,128)(2,1)S(1)} %pad_maximum_fusion.4.refs_0_), channel_id=1, source_target_pairs={{0,2},{1,3},{2,0},{3,1},{4,6},{5,7},{6,4},{7,5},{8,10},{9,11},{10,... | collective-permute-start | bytes 1769480 | tf_op jit(solution)/shard_map/ppermute | solution.py:26
  40.5 22.8 %collective-permute-start.4 = (bf16[96,3072]{1,0:T(8,128)(2,1)S(1)}, bf16[96,3072]{1,0:T(8,128)(2,1)}, u32[]{:S(2)}, u32[]{:S(2)}) collective-permute-start(bf16[96,3072]{1,0:T(8,128)(2,1)S(1)} %pad_maximum_fusion.4.refs_0_), channel_id=1, source_target_pairs={{0,4},{1,5},{2,6},{3,7},{4,0},{5,1},{6,2},{7,3},{8,12},{9,13},{10,... | collective-permute-start | bytes 1769480 | tf_op jit(solution)/shard_map/ppermute | solution.py:26
  58.9 25.9 %all-to-all-start = ((bf16[40,32,96]{2,0,1:T(8,128)(2,1)}), bf16[40,32,96]{2,0,1:T(8,128)(2,1)S(1)}, u32[]{:S(2)}, u32[]{:S(2)}) async-start(bf16[40,32,96]{2,0,1:T(8,128)(2,1)} %copy.75), calls=%async_computation | async-start | bytes 655360 | tf_op jit(solution)/shard_map/all_to_all | solution.py:1046
  63.3 21.5 %collective-permute-start.8 = (bf16[48,3072]{1,0:T(8,128)(2,1)S(1)}, bf16[48,3072]{1,0:T(8,128)(2,1)}, u32[]{:S(2)}, u32[]{:S(2)}) collective-permute-start(bf16[48,3072]{1,0:T(8,128)(2,1)S(1)} %slice.45), channel_id=1, source_target_pairs={{0,4},{1,5},{2,6},{3,7},{4,0},{5,1},{6,2},{7,3},{8,12},{9,13},{10,... | collective-permute-start | bytes 884744 | tf_op jit(solution)/shard_map/ppermute | solution.py:26
  66.0 18.8 %collective-permute-start.9 = (bf16[48,3072]{1,0:T(8,128)(2,1)S(1)}, bf16[48,3072]{1,0:T(8,128)(2,1)}, u32[]{:S(2)}, u32[]{:S(2)}) collective-permute-start(bf16[48,3072]{1,0:T(8,128)(2,1)S(1)} %slice.46), channel_id=1, source_target_pairs={{0,2},{1,3},{2,0},{3,1},{4,6},{5,7},{6,4},{7,5},{8,10},{9,11},{10,... | collective-permute-start | bytes 884744 | tf_op jit(solution)/shard_map/ppermute | solution.py:26
  71.2 13.0 %collective-permute-start.6 = (bf16[1,40,1024]{2,1,0:T(8,128)(2,1)}, bf16[1,40,1024]{2,1,0:T(8,128)(2,1)S(1)}, u32[]{:S(2)}, u32[]{:S(2)}) collective-permute-start(bf16[1,40,1024]{2,1,0:T(8,128)(2,1)} %bitcast.85), channel_id=1, source_target_pairs={{0,16},{1,17},{2,18},{3,19},{4,20},{5,21},{6,22},{7,23},{8,24},{9,... | collective-permute-start | bytes 245768 | tf_op jit(solution)/shard_map/ppermute | solution.py:26
  86.5 19.9 %collective-permute-start.15 = (bf16[4,40,1024]{2,1,0:T(8,128)(2,1)S(1)}, bf16[4,40,1024]{2,1,0:T(8,128)(2,1)S(1)}, u32[]{:S(2)}, u32[]{:S(2)}) collective-permute-start(bf16[4,40,1024]{2,1,0:T(8,128)(2,1)S(1)} %bitcast.82), channel_id=1, source_target_pairs={{0,2},{1,3},{2,0},{3,1},{4,6},{5,7},{6,4},{7,5},{8,10},{9,11},{10,... | collective-permute-start | bytes 983048 | tf_op jit(solution)/shard_map/ppermute | solution.py:26
  86.8 19.5 %collective-permute-start.16 = (bf16[4,40,1024]{2,1,0:T(8,128)(2,1)S(1)}, bf16[4,40,1024]{2,1,0:T(8,128)(2,1)S(1)}, u32[]{:S(2)}, u32[]{:S(2)}) collective-permute-start(bf16[4,40,1024]{2,1,0:T(8,128)(2,1)S(1)} %bitcast.83), channel_id=1, source_target_pairs={{0,4},{1,5},{2,6},{3,7},{4,0},{5,1},{6,2},{7,3},{8,12},{9,13},{10,... | collective-permute-start | bytes 983048 | tf_op jit(solution)/shard_map/ppermute | solution.py:26
  113.2 39.3 %collective-permute-start.19 = (bf16[16,40,1024]{2,1,0:T(8,128)(2,1)S(1)}, bf16[16,40,1024]{2,1,0:T(8,128)(2,1)S(1)}, u32[]{:S(2)}, u32[]{:S(2)}) collective-permute-start(bf16[16,40,1024]{2,1,0:T(8,128)(2,1)S(1)} %bitcast.77), channel_id=1, source_target_pairs={{0,1},{1,0},{2,3},{3,2},{4,5},{5,4},{6,7},{7,6},{8,9},{9,8},{10,11... | collective-permute-start | bytes 3932168 | tf_op jit(solution)/shard_map/ppermute | solution.py:26
  128.8 23.7 %all-to-all-start.1 = ((bf16[32,8,768]{2,1,0:T(8,128)(2,1)}), bf16[32,8,768]{2,1,0:T(8,128)(2,1)S(1)}, u32[]{:S(2)}, u32[]{:S(2)}) async-start(bf16[32,8,768]{2,1,0:T(8,128)(2,1)} %broadcast_in_dim.62), calls=%async_computation.1 | async-start | bytes 786432 | tf_op jit(solution)/shard_map/all_to_all | solution.py:46
  191.6 15.5 %collective-permute-start.22 = (bf16[192,1536]{1,0:T(8,128)(2,1)}, bf16[192,1536]{1,0:T(8,128)(2,1)S(1)}, u32[]{:S(2)}, u32[]{:S(2)}) collective-permute-start(bf16[192,1536]{1,0:T(8,128)(2,1)} %get-tuple-element.153.refs_1_), channel_id=1, source_target_pairs={{0,2},{1,3},{2,0},{3,1},{4,6},{5,7},{6,4},{7,5},{8,10},{9,11},{10,... | collective-permute-start | bytes 1769480 | tf_op jit(solution)/shard_map/ppermute | solution.py:26
  192.2 15.6 %collective-permute-start.23 = (bf16[192,1536]{1,0:T(8,128)(2,1)}, bf16[192,1536]{1,0:T(8,128)(2,1)S(1)}, u32[]{:S(2)}, u32[]{:S(2)}) collective-permute-start(bf16[192,1536]{1,0:T(8,128)(2,1)} %get-tuple-element.155.refs_3_), channel_id=1, source_target_pairs={{0,4},{1,5},{2,6},{3,7},{4,0},{5,1},{6,2},{7,3},{8,12},{9,13},{10,... | collective-permute-start | bytes 1769480 | tf_op jit(solution)/shard_map/ppermute | solution.py:26
  238.2 17.9 %collective-permute-start.31 = (bf16[192,1536]{1,0:T(8,128)(2,1)}, bf16[192,1536]{1,0:T(8,128)(2,1)S(1)}, u32[]{:S(2)}, u32[]{:S(2)}) collective-permute-start(bf16[192,1536]{1,0:T(8,128)(2,1)} %get-tuple-element.179), channel_id=1, source_target_pairs={{0,2},{1,3},{2,0},{3,1},{4,6},{5,7},{6,4},{7,5},{8,10},{9,11},{10,... | collective-permute-start | bytes 1769480 | tf_op jit(solution)/shard_map/ppermute | solution.py:26
  239.0 17.2 %collective-permute-start.32 = (bf16[192,1536]{1,0:T(8,128)(2,1)}, bf16[192,1536]{1,0:T(8,128)(2,1)S(1)}, u32[]{:S(2)}, u32[]{:S(2)}) collective-permute-start(bf16[192,1536]{1,0:T(8,128)(2,1)} %get-tuple-element.181), channel_id=1, source_target_pairs={{0,4},{1,5},{2,6},{3,7},{4,0},{5,1},{6,2},{7,3},{8,12},{9,13},{10,... | collective-permute-start | bytes 1769480 | tf_op jit(solution)/shard_map/ppermute | solution.py:26
  240.0 15.3 %collective-permute-start.28 = (bf16[24,3072]{1,0:T(8,128)(2,1)S(1)}, bf16[24,3072]{1,0:T(8,128)(2,1)S(1)}, u32[]{:S(2)}, u32[]{:S(2)}) collective-permute-start(bf16[24,3072]{1,0:T(8,128)(2,1)S(1)} %copy-done.36), channel_id=1, source_target_pairs={{0,8},{1,9},{2,10},{3,11},{4,12},{5,13},{6,14},{7,15},{8,0},{9,1},... | collective-permute-start | bytes 442376 | tf_op jit(solution)/shard_map/ppermute | solution.py:26
  241.0 14.4 %collective-permute-start.29 = (bf16[24,3072]{1,0:T(8,128)(2,1)S(1)}, bf16[24,3072]{1,0:T(8,128)(2,1)S(1)}, u32[]{:S(2)}, u32[]{:S(2)}) collective-permute-start(bf16[24,3072]{1,0:T(8,128)(2,1)S(1)} %copy-done.35), channel_id=1, source_target_pairs={{0,16},{1,17},{2,18},{3,19},{4,20},{5,21},{6,22},{7,23},{8,24},{9,... | collective-permute-start | bytes 442376 | tf_op jit(solution)/shard_map/ppermute | solution.py:26
  241.7 13.7 %collective-permute-start.30 = (bf16[24,3072]{1,0:T(8,128)(2,1)S(1)}, bf16[24,3072]{1,0:T(8,128)(2,1)S(1)}, u32[]{:S(2)}, u32[]{:S(2)}) collective-permute-start(bf16[24,3072]{1,0:T(8,128)(2,1)S(1)} %copy-done.34), channel_id=1, source_target_pairs={{0,24},{1,25},{2,26},{3,27},{4,28},{5,29},{6,30},{7,31},{8,16},{9,... | collective-permute-start | bytes 442376 | tf_op jit(solution)/shard_map/ppermute | solution.py:26
  261.4 22.4 %all-to-all-start.2 = ((bf16[32,1,4,768]{3,2,1,0:T(4,128)(2,1)}), bf16[32,1,4,768]{3,2,1,0:T(4,128)(2,1)S(1)}, u32[]{:S(2)}, u32[]{:S(2)}) async-start(bf16[32,1,4,768]{3,2,1,0:T(4,128)(2,1)} %broadcast_in_dim.63), calls=%async_computation.2 | async-start | bytes 393216 | tf_op jit(solution)/shard_map/all_to_all | solution.py:46
  279.4 13.6 %collective-permute-start.35 = (bf16[24,3072]{1,0:T(8,128)(2,1)}, bf16[24,3072]{1,0:T(8,128)(2,1)S(1)}, u32[]{:S(2)}, u32[]{:S(2)}) collective-permute-start(bf16[24,3072]{1,0:T(8,128)(2,1)} %get-tuple-element.196), channel_id=1, source_target_pairs={{0,8},{1,9},{2,10},{3,11},{4,12},{5,13},{6,14},{7,15},{8,0},{9,1},... | collective-permute-start | bytes 442376 | tf_op jit(solution)/shard_map/ppermute | solution.py:26
  281.1 14.2 %collective-permute-start.36 = (bf16[24,3072]{1,0:T(8,128)(2,1)}, bf16[24,3072]{1,0:T(8,128)(2,1)S(1)}, u32[]{:S(2)}, u32[]{:S(2)}) collective-permute-start(bf16[24,3072]{1,0:T(8,128)(2,1)} %get-tuple-element.197), channel_id=1, source_target_pairs={{0,16},{1,17},{2,18},{3,19},{4,20},{5,21},{6,22},{7,23},{8,24},{9,... | collective-permute-start | bytes 442376 | tf_op jit(solution)/shard_map/ppermute | solution.py:26
  (56 other events, 347.9 us)
Sparse Core Ops, SparseCore 0:
  11.6 98.0 all-gather.1

commit v2 on v1

--- a/solution.py
+++ b/solution.py
@@ -105,7 +105,7 @@
     return total
 
 
-VMEM_BYTES = 56 << 20
+VMEM_BYTES = 40 << 20
 TILE = 512
 
 
@@ -136,8 +136,16 @@
     return lax.dot_general(lhs, rhs, (((0,), (0,)), ((), ())), preferred_element_type=f32)
 
 
-def params(**more):
-    return pltpu.CompilerParams(vmem_limit_bytes=VMEM_BYTES, **more)
+def params(limit=VMEM_BYTES):
+    return pltpu.CompilerParams(vmem_limit_bytes=limit)
+
+
+def in_vmem(count):
+    return [pl.BlockSpec(memory_space=pltpu.VMEM)] * count
+
+
+def stays(shape, dtype):
+    return pltpu.VMEM(shape, dtype)
 
 
 def cost(flops, moved, transcendentals=0):
@@ -176,11 +184,16 @@
 
 def fold_kernel(keep_a, got_a, keep_b, got_b, *refs):
     outs = refs[-4:]
-    half = outs[0].shape[0]
-    for k, (kept, got) in enumerate(((keep_a, got_a), (keep_b, got_b))):
-        for j in range(2):
-            at = slice(j * half, (j + 1) * half)
-            outs[2 * k + j][...] = (kept[at, :].astype(f32) + got[at, :].astype(f32)).astype(bf16)
+    half, tile = outs[0].shape[0], 256
+
+    @pl.loop(0, keep_a.shape[1] // tile)
+    def _(step):
+        cols = pl.ds(pl.multiple_of(step * tile, tile), tile)
+        for k, (kept, got) in enumerate(((keep_a, got_a), (keep_b, got_b))):
+            for j in range(2):
+                at = slice(j * half, (j + 1) * half)
+                total = kept[at, cols].astype(f32) + got[at, cols].astype(f32)
+                outs[2 * k + j][:, cols] = total.astype(bf16)
 
 
 def fold(parts, after=()):
@@ -191,14 +204,12 @@
             for kept, got in (parts[:2], parts[2:])
         ]
         return [part for one in whole for part in (one[: rows // 2], one[rows // 2 :])]
-    tile = 512
     return pl.pallas_call(
         fold_kernel,
-        grid=(cols // tile,),
-        out_shape=[jax.ShapeDtypeStruct((rows // 2, cols), bf16)] * 4,
-        in_specs=[pl.BlockSpec((rows, tile), lambda i: (0, i))] * 4 + anywhere(after),
-        out_specs=[pl.BlockSpec((rows // 2, tile), lambda i: (0, i))] * 4,
-        compiler_params=params(),
+        out_shape=[stays((rows // 2, cols), bf16)] * 4,
+        in_specs=in_vmem(4) + anywhere(after),
+        out_specs=in_vmem(4),
+        compiler_params=params(8 << 20),
         cost_estimate=cost(2 * rows * cols, 12 * rows * cols),
         name="fold",
     )(*parts, *after)
@@ -226,9 +237,10 @@
         return [own] + [other.astype(bf16) for other in others]
     return pl.pallas_call(
         fold_last_kernel,
-        out_shape=[jax.ShapeDtypeStruct(shape, f32)] + [jax.ShapeDtypeStruct(shape, bf16)] * 3,
-        in_specs=[pl.BlockSpec(memory_space=pltpu.VMEM)] * 4 + anywhere(after),
-        compiler_params=params(),
+        out_shape=[stays(shape, f32)] + [stays(shape, bf16)] * 3,
+        in_specs=in_vmem(4) + anywhere(after),
+        out_specs=in_vmem(4),
+        compiler_params=params(8 << 20),
         cost_estimate=cost(2 * rows * cols, 12 * rows * cols),
         name="fold_last",
     )(*parts, *after)
@@ -735,184 +747,144 @@
 
 def mlp_back_kernel(
     low_ref, wd_ref, slope_ref, wu_ref, lhs_ref, mid_ref, gain_ref, row_ref, keep_a, send_a, keep_b,
-    send_b, out_ref, gain_out, bias_out, acc
+    send_b, out_ref, gain_out, bias_out
 ):
-    step = pl.program_id(0)
     count, rows = low_ref.shape[0], slope_ref.shape[0]
-    half = D // 2
-    hidden = mul_bt(low_ref[...], wd_ref[...])
-    wide = jnp.broadcast_to(hidden[:, None, :], (count, TXT_LEN, TILE)).reshape(rows, TILE)
-    inner = (wide * slope_ref[...].astype(f32)).astype(bf16)
-    weight = mul(lhs_ref[0], inner).astype(bf16)
-
-    @pl.when(step < pl.num_programs(0) // 2)
-    def _():
-        keep_a[...] = weight[:half]
-        send_a[...] = weight[half:]
-
-    @pl.when(step >= pl.num_programs(0) // 2)
-    def _():
-        keep_b[...] = weight[:half]
-        send_b[...] = weight[half:]
-
-    added = mul_bt(inner, wu_ref[...])
-
-    @pl.when(step == 0)
-    def _():
-        acc[...] = added
-
-    @pl.when(step > 0)
-    def _():
-        acc[...] += added
-
-    @pl.when(step == pl.num_programs(0) - 1)
-    def _():
-        chunk = 128
-        per = chunk // TXT_LEN
-        gain = gain_ref[...]
-        gain_out[...] = jnp.zeros_like(gain_out)
-        bias_out[...] = jnp.zeros_like(bias_out)
-
-        @pl.loop(0, rows // chunk)
-        def _(k):
-            at = pl.ds(pl.multiple_of(k * chunk, chunk), chunk)
-            unit, scale = norm_parts(mid_ref[at, :])
-            grad = acc[at, :]
-            gain_out[...] += jnp.sum(grad * unit, axis=0, keepdims=True)
-            bias_out[...] += jnp.sum(grad, axis=0, keepdims=True)
-            row = row_ref[pl.ds(pl.multiple_of(k * per, per), per), :]
-            row = jnp.broadcast_to(row[:, None, :], (per, TXT_LEN, D)).reshape(chunk, D)
-            out_ref[at, :] = row + norm_back(unit, scale, gain, grad)
+    half, steps = D // 2, FF // 2 // TILE
+    for k, (keep, send) in enumerate(((keep_a, send_a), (keep_b, send_b))):
+
+        @pl.loop(0, steps)
+        def _(step, k=k, keep=keep, send=send):
+            at = pl.ds(pl.multiple_of(k * (FF // 2) + step * TILE, TILE), TILE)
+            there = pl.ds(pl.multiple_of(step * TILE, TILE), TILE)
+            hidden = mul_bt(low_ref[...], wd_ref[at, :])
+            wide = jnp.broadcast_to(hidden[:, None, :], (count, TXT_LEN, TILE))
+            inner = (wide.reshape(rows, TILE) * slope_ref[:, at].astype(f32)).astype(bf16)
+            weight = mul(lhs_ref[k], inner).astype(bf16)
+            keep[:, there] = weight[:half]
+            send[:, there] = weight[half:]
+            added = mul_bt(inner, wu_ref[:, at])
+            if k == 0:
+
+                @pl.when(step == 0)
+                def _():
+                    out_ref[...] = added
+
+                @pl.when(step > 0)
+                def _():
+                    out_ref[...] += added
+            else:
+                out_ref[...] += added
+
+    chunk = 128
+    per = chunk // TXT_LEN
+    gain = gain_ref[...]
+    gain_out[...] = jnp.zeros_like(gain_out)
+    bias_out[...] = jnp.zeros_like(bias_out)
+
+    @pl.loop(0, rows // chunk)
+    def _(k):
+        at = pl.ds(pl.multiple_of(k * chunk, chunk), chunk)
+        unit, scale = norm_parts(mid_ref[at, :])
+        grad = out_ref[at, :]
+        gain_out[...] += jnp.sum(grad * unit, axis=0, keepdims=True)
+        bias_out[...] += jnp.sum(grad, axis=0, keepdims=True)
+        row = row_ref[pl.ds(pl.multiple_of(k * per, per), per), :]
+        row = jnp.broadcast_to(row[:, None, :], (per, TXT_LEN, D)).reshape(chunk, D)
+        out_ref[at, :] = row + norm_back(unit, scale, gain, grad)
 
 
 def mlp_back(grad_row, grad_low, weight_down, slope, weight_up, lhs, middle, gain):
-    rows, count = slope.shape[0], grad_row.shape[0]
-    steps = FF // TILE
-    fixed = lambda shape: pl.BlockSpec(shape, lambda i: (0, 0))
-    first = pl.BlockSpec((D // 2, TILE), lambda i: (0, jnp.minimum(i, steps // 2 - 1)))
-    second = pl.BlockSpec((D // 2, TILE), lambda i: (0, jnp.maximum(i - steps // 2, 0)))
-    part = jax.ShapeDtypeStruct((D // 2, FF // 2), bf16)
+    rows = slope.shape[0]
     line = jax.ShapeDtypeStruct((1, D), f32)
     return pl.pallas_call(
         mlp_back_kernel,
-        grid=(steps,),
-        out_shape=[part] * 4 + [jax.ShapeDtypeStruct((rows, D), f32), line, line],
-        in_specs=[
-            fixed((count, D)),
-            pl.BlockSpec((TILE, D), lambda i: (i, 0)),
-            pl.BlockSpec((rows, TILE), lambda i: (0, i)),
-            pl.BlockSpec((D, TILE), lambda i: (0, i)),
-            pl.BlockSpec((1, D, rows), lambda i: (i // (steps // 2), 0, 0)),
-            fixed((rows, D)),
-            fixed((1, D)),
-            fixed((count, D)),
-        ],
-        out_specs=[first, first, second, second, fixed((rows, D)), fixed((1, D)), fixed((1, D))],
-        scratch_shapes=[pltpu.VMEM((rows, D), f32)],
-        compiler_params=params(),
+        out_shape=[stays((D // 2, FF // 2), bf16)] * 4 + [stays((rows, D), f32), line, line],
+        in_specs=in_vmem(8),
+        out_specs=in_vmem(7),
+        compiler_params=params(16 << 20),
         cost_estimate=cost(4 * rows * D * FF, 4 * D * FF + 2 * rows * FF + 2 * D * FF, rows * FF),
         name="mlp_back",
     )(grad_low, weight_down, slope, weight_up, lhs, middle, gain[None], grad_row)
 
 
-def attention_back_kernel(grad_ref, wo_ref, qkv_ref, lse_ref, *refs):
+def attention_back_kernel(first, grad_ref, wo_ref, qkv_ref, lse_ref, *refs):
     low_ref, out_ref = refs[-2:]
-    chunk = grad_ref.shape[0]
+    chunk = 128
     mask = same_sequence(chunk, 0, chunk, 0, TXT_LEN)
-    low = grad_ref[...].astype(bf16)
-    low_ref[...] = low
-    grad_att = mul_bt(low, wo_ref[...]).astype(bf16)
-    for pair in range(HEADS // 2):
-        queries = qkv_ref[:, pair_cols(0, pair)] * bf16(HEAD ** (-0.5))
-        keys = two_heads(qkv_ref[:, pair_cols(1, pair)])
-        vals = two_heads(qkv_ref[:, pair_cols(2, pair)])
-        grads = grad_att[:, pair_cols(0, pair)]
-        scores, grad_probs = mul_bt(keys, queries), mul_bt(vals, grads)
-        probs, grad_scores = [], []
-        for k in range(2):
-            at = slice(k * chunk, (k + 1) * chunk)
-            head = 2 * pair + k
-            shifted = scores[at] - lse_ref[head : head + 1, :]
-            prob = jnp.where(mask, jnp.exp(jnp.where(mask, shifted, 0.0)), 0.0)
-            along = jnp.sum(grad_probs[at] * prob, axis=0, keepdims=True)
-            grad_scores.append((prob * (grad_probs[at] - along)).astype(bf16))
-            probs.append(prob.astype(bf16))
-        grad_q = mul_at(jnp.concatenate(grad_scores, axis=0), keys) * HEAD ** (-0.5)
-        grad_k = mul(jnp.concatenate(grad_scores, axis=1), two_heads(queries))
-        grad_v = mul(jnp.concatenate(probs, axis=1), two_heads(grads))
-        out_ref[:, pair_cols(0, pair)] = grad_q.astype(bf16)
-        out_ref[:, pair_cols(1, pair)] = grad_k.astype(bf16)
-        out_ref[:, pair_cols(2, pair)] = grad_v.astype(bf16)
+
+    @pl.loop(0, low_ref.shape[0] // chunk)
+    def _(step):
+        here = pl.ds(pl.multiple_of((first + step) * chunk, chunk), chunk)
+        there = pl.ds(pl.multiple_of(step * chunk, chunk), chunk)
+        sums = lse_ref[pl.ds(pl.multiple_of((first + step) * 16, 16), 16), :]
+        low = grad_ref[here, :].astype(bf16)
+        low_ref[there, :] = low
+        grad_att = mul_bt(low, wo_ref[...]).astype(bf16)
+        for pair in range(HEADS // 2):
+            queries = qkv_ref[here, pair_cols(0, pair)] * bf16(HEAD ** (-0.5))
+            keys = two_heads(qkv_ref[here, pair_cols(1, pair)])
+            vals = two_heads(qkv_ref[here, pair_cols(2, pair)])
+            grads = grad_att[:, pair_cols(0, pair)]
+            scores, grad_probs = mul_bt(keys, queries), mul_bt(vals, grads)
+            probs, grad_scores = [], []
+            for k in range(2):
+                at = slice(k * chunk, (k + 1) * chunk)
+                head = 2 * pair + k
+                shifted = scores[at] - sums[head : head + 1, :]
+                prob = jnp.where(mask, jnp.exp(jnp.where(mask, shifted, 0.0)), 0.0)
+                along = jnp.sum(grad_probs[at] * prob, axis=0, keepdims=True)
+                grad_scores.append((prob * (grad_probs[at] - along)).astype(bf16))
+                probs.append(prob.astype(bf16))
+            grad_q = mul_at(jnp.concatenate(grad_scores, axis=0), keys) * HEAD ** (-0.5)
+            grad_k = mul(jnp.concatenate(grad_scores, axis=1), two_heads(queries))
+            grad_v = mul(jnp.concatenate(probs, axis=1), two_heads(grads))
+            out_ref[there, pair_cols(0, pair)] = grad_q.astype(bf16)
+            out_ref[there, pair_cols(1, pair)] = grad_k.astype(bf16)
+            out_ref[there, pair_cols(2, pair)] = grad_v.astype(bf16)
 
 
 def attention_back(grad_middle, weight_out, project, log_sums, first, count, after=()):
-    chunk = 128
-    rows = count * chunk
-    return pl.pallas_call(
-        attention_back_kernel,
-        grid=(count,),
-        out_shape=[
-            jax.ShapeDtypeStruct((rows, D), bf16),
-            jax.ShapeDtypeStruct((rows, 3 * D), bf16),
-        ],
-        in_specs=[
-            pl.BlockSpec((chunk, D), lambda i: (i + first, 0)),
-            pl.BlockSpec((D, D), lambda i: (0, 0)),
-            pl.BlockSpec((chunk, 3 * D), lambda i: (i + first, 0)),
-            pl.BlockSpec((16, chunk), lambda i: (i + first, 0)),
-        ]
-        + anywhere(after),
-        out_specs=[
-            pl.BlockSpec((chunk, D), lambda i: (i, 0)),
-            pl.BlockSpec((chunk, 3 * D), lambda i: (i, 0)),
-        ],
-        compiler_params=params(),
+    rows = count * 128
+    return pl.pallas_call(
+        functools.partial(attention_back_kernel, first),
+        out_shape=[stays((rows, D), bf16), stays((rows, 3 * D), bf16)],
+        in_specs=in_vmem(4) + anywhere(after),
+        out_specs=in_vmem(2),
+        compiler_params=params(16 << 20),
         cost_estimate=cost(10 * rows * D * D, 16 * rows * D + 2 * D * D, rows * 128 * HEADS),
         name="attention_back",
     )(grad_middle, weight_out, project, log_sums, *after)
 
 
-def mul_rows(lhs, parts):
+def mul_rows(lhs, parts, cols):
     total, row = 0.0, 0
     for part in parts:
-        total = total + mul(lhs[:, row : row + part.shape[0]], part[...])
+        total = total + mul(lhs[:, row : row + part.shape[0]], part[:, cols])
         row += part.shape[0]
     return total
 
 
-def weight_back_kernel(counts, lhs_ref, *refs):
-    step, half = pl.program_id(0), D // 2
+def weight_back_kernel(factors, groups, lhs_ref, *refs):
     keep, send = refs[-2:]
-    row = 0
-    for k, count in enumerate(counts):
-        parts = refs[row : row + count]
-        row += count
-
-        @pl.when(step == k if len(counts) > 1 else step >= 0)
-        def _(parts=parts):
-            weight = mul_rows(lhs_ref[0], parts).astype(bf16)
-            keep[...] = weight[:half]
-            send[...] = weight[half:]
-
-
-def weight_back(lhs, first, groups, blocks, after=()):
+    half = D // 2
+    for k, (factor, group, col) in enumerate(factors):
+        parts = refs[sum(groups[:group]) : sum(groups[: group + 1])]
+        weight = mul_rows(lhs_ref.at[factor], parts, slice(col * D, (col + 1) * D)).astype(bf16)
+        at = slice(k * D, (k + 1) * D)
+        keep[:, at] = weight[:half]
+        send[:, at] = weight[half:]
+
+
+def weight_back(lhs, groups, factors, after=()):
     rows = lhs.shape[2]
-    steps = 2
-    many = len(groups) > 1
     given = [part for group in groups for part in group]
     return pl.pallas_call(
-        functools.partial(weight_back_kernel, [len(group) for group in groups]),
-        grid=(steps,),
-        out_shape=[jax.ShapeDtypeStruct((D // 2, steps * D), bf16)] * 2,
-        in_specs=[pl.BlockSpec((1, D, rows), lambda i: (first + (i if many else 0), 0, 0))]
-        + [
-            pl.BlockSpec((part.shape[0], D), lambda i, col=col: (0, col + (0 if many else i)))
-            for group, col in zip(groups, blocks)
-            for part in group
-        ]
-        + anywhere(after),
-        out_specs=[pl.BlockSpec((D // 2, D), lambda i: (0, i))] * 2,
-        compiler_params=params(),
+        functools.partial(weight_back_kernel, factors, [len(group) for group in groups]),
+        out_shape=[stays((D // 2, len(factors) * D), bf16)] * 2,
+        in_specs=in_vmem(1 + len(given)) + anywhere(after),
+        out_specs=in_vmem(2),
+        compiler_params=params(16 << 20),
         cost_estimate=cost(4 * rows * D * D, 4 * rows * D + 7 * D * D),
         name="weight_back",
     )(lhs, *given, *after)
@@ -921,56 +893,41 @@
 def input_back_kernel(count, *refs):
     projs = refs[:count]
     w_ref, x_ref, gain_ref, mid_ref = refs[count : count + 4]
-    out_ref, gain_out, bias_out, acc = refs[-4:]
-    step = pl.program_id(0)
+    out_ref, gain_out, bias_out = refs[-3:]
     rows, chunk = x_ref.shape[0], 128
-    row = 0
-    for part in projs:
-        at = slice(row, row + part.shape[0])
-        row += part.shape[0]
-        added = mul_bt(part[...], w_ref[...])
-
-        @pl.when(step == 0)
-        def _(at=at, added=added):
-            acc[at, :] = added
-
-        @pl.when(step > 0)
-        def _(at=at, added=added):
-            acc[at, :] += added
-
-    @pl.when(step == pl.num_programs(0) - 1)
-    def _():
-        gain = gain_ref[...]
-        gain_out[...] = jnp.zeros_like(gain_out)
-        bias_out[...] = jnp.zeros_like(bias_out)
-
-        @pl.loop(0, rows // chunk)
-        def _(k):
-            at = pl.ds(pl.multiple_of(k * chunk, chunk), chunk)
-            unit, scale = norm_parts(x_ref[at, :].astype(f32))
-            grad = acc[at, :]
-            gain_out[...] += jnp.sum(grad * unit, axis=0, keepdims=True)
-            bias_out[...] += jnp.sum(grad, axis=0, keepdims=True)
-            out_ref[at, :] = mid_ref[at, :] + norm_back(unit, scale, gain, grad)
+
+    @pl.loop(0, D // 256)
+    def _(step):
+        at = pl.ds(pl.multiple_of(step * 256, 256), 256)
+        row = 0
+        for part in projs:
+            there = slice(row, row + part.shape[0])
+            out_ref[there, at] = mul_bt(part[...], w_ref[at, :])
+            row += part.shape[0]
+
+    gain = gain_ref[...]
+    gain_out[...] = jnp.zeros_like(gain_out)
+    bias_out[...] = jnp.zeros_like(bias_out)
+
+    @pl.loop(0, rows // chunk)
+    def _(k):
+        at = pl.ds(pl.multiple_of(k * chunk, chunk), chunk)
+        unit, scale = norm_parts(x_ref[at, :].astype(f32))
+        grad = out_ref[at, :]
+        gain_out[...] += jnp.sum(grad * unit, axis=0, keepdims=True)
+        bias_out[...] += jnp.sum(grad, axis=0, keepdims=True)
+        out_ref[at, :] = mid_ref[at, :] + norm_back(unit, scale, gain, grad)
 
 
 def input_back(grad_projs, weight, rows_in, gain, grad_middle, after=()):
     rows = rows_in.shape[0]
-    fixed = lambda shape: pl.BlockSpec(shape, lambda i: (0, 0))
     line = jax.ShapeDtypeStruct((1, D), f32)
     return pl.pallas_call(
         functools.partial(input_back_kernel, len(grad_projs)),
-        grid=(3,),
         out_shape=[jax.ShapeDtypeStruct((rows, D), f32), line, line],
-        in_specs=[pl.BlockSpec((part.shape[0], D), lambda i: (0, i)) for part in grad_projs]
-        + [
-            pl.BlockSpec((D, D), lambda i: (0, i)),
-            fixed((rows, D)), fixed((1, D)), fixed((rows, D)),
-        ]
-        + anywhere(after),
-        out_specs=[fixed((rows, D)), fixed((1, D)), fixed((1, D))],
-        scratch_shapes=[pltpu.VMEM((rows, D), f32)],
-        compiler_params=params(),
+        in_specs=in_vmem(len(grad_projs) + 4) + anywhere(after),
+        out_specs=in_vmem(3),
+        compiler_params=params(16 << 20),
         cost_estimate=cost(6 * rows * D * D, 14 * rows * D + 6 * D * D),
         name="input_back",
     )(*grad_projs, weight, rows_in, gain[None], grad_middle, *after)
@@ -1098,9 +1055,9 @@
     low_two, proj_two = attention_back(grad_middle, txt_out, project, log_sums, 1, 4, up)
     up = fold(hand_on(up, stages - 2), (proj_two,))
     projs, lows = (proj_one, proj_two), (low_one, low_two)
-    rest_a = weight_back(lhs_rest, 0, [projs], [0], up)
+    rest_a = weight_back(lhs_rest, [projs], [(0, 0, 0), (0, 0, 1)], up)
     up = hand_on_last(fold_last(hand_on(up, stages - 1), rest_a[1:]))
-    rest_b = weight_back(lhs_rest, 1, [projs, lows], [2, 0], up[:1])
+    rest_b = weight_back(lhs_rest, [projs, lows], [(1, 0, 2), (2, 1, 0)], up[:1])
     rest = [*rest_a, *rest_b]
     for stage in range(stages - 2):
         rest = fold(hand_on(rest, stage))

time: 305 us -> 289 us (0.948)
  Pallas kernels: 162 us -> 99.6 us
  local copies, waits for them, and re-layouts: 23 us -> 54 us
  waiting for transfers between devices: 33.1 us -> 43.9 us
  other arithmetic: 12.4 us -> 15.9 us
    pallas_call x12, Pallas kernels: 79.5 us -> 36.9 us  [the longest x1 12.2 us: mlp_back(): pl.pallas_call(mlp_back_kernel, out_shape=[stays((D // 2, FF // 2), bf16)...]
    unnamed x79 -> x155, local copies, waits for them, and re-layouts: 7.52 us -> 41.4 us
    ppermute x38, waiting for transfers between devices: 29.9 us -> 43.1 us  [swapped(): return lax.ppermute(value, AXIS, [(i, i ^ mask) for i in range(peers)])]
    pallas_call x1, Pallas kernels: 18 us -> 12.2 us  [text_front(): pl.pallas_call(text_front_kernel, out_shape=[jax.ShapeDtypeStruct(*item)...]
    pallas_call x1, Pallas kernels: 9.76 us -> 5.67 us  [left_factors(): pl.pallas_call(left_kernel, grid=(5,), out_shape=[jax.ShapeDtypeStruct((2...]
  transfers between devices with their start and end apart: 42 -> 42, of which waited for: 13 -> 15; matrix products, arithmetic and copies ran while one was open for 7% -> 7% of each run, Pallas kernels for 40% -> 29%
where the time goes in v2:
time: 289 us; the launch traced here: 287 us
  Pallas kernels  99.6 us (34%)
  starting transfers between devices  58.9 us (20%)
  local copies, waits for them, and re-layouts  54 us (19%)
  waiting for transfers between devices  43.9 us (15%)
  other arithmetic  15.9 us (6%)
  between operations  15.1 us (5%)
    ppermute x38, waiting for transfers between devices, swapped(): return lax.ppermute(value, AXIS, [(i, i ^ mask) for i in range(peers)])  43.1 us
    unnamed x155, local copies, waits for them, and re-layouts  41.4 us
    ppermute x38, starting transfers between devices, swapped(): return lax.ppermute(value, AXIS, [(i, i ^ mask) for i in range(peers)])  40.9 us
    all_to_all x2, starting transfers between devices, spread(): return lax.all_to_all(copies, AXIS, split_axis=0, concat_axis=0, tiled=True)  13.6 us
    pallas_call x1, Pallas kernels, text_up(): pl.pallas_call(text_up_kernel, grid=(FF // TILE,), out_shape=[jax.ShapeDt...  12.6 us
    pallas_call x1, Pallas kernels, image_up(): pl.pallas_call(functools.partial(image_up_kernel, fold), grid=(FF // TILE...  12.5 us
    pallas_call x1, Pallas kernels, mlp_back(): pl.pallas_call(mlp_back_kernel, out_shape=[stays((D // 2, FF // 2), bf16)...  12.2 us
    pallas_call x1, Pallas kernels, text_front(): pl.pallas_call(text_front_kernel, out_shape=[jax.ShapeDtypeStruct(*item)...  12.2 us
  transfers between devices with their start and end apart: 42, of which 15 were waited for; matrix products, arithmetic and copies ran while one was open for 7% of the time, Pallas kernels for 29%

profile of v2, /device:TPU:0, one launch (start us, length us, event | category | flops | bytes accessed | tf_op | source)
XLA Modules:
  0.0 287.4 jit_solution(11181692045680810886)
XLA Ops:
  10.3 3.1 %collective-permute-start = (bf16[24,3072]{1,0:T(8,128)(2,1)S(1)}, bf16[24,3072]{1,0:T(8,128)(2,1)S(1)}, u32[]{:S(2)}, u32[]{:S(2)}) collective-permute-start(bf16[24,3072]{1,0:T(8,128)(2,1)S(1)} %constant_dynamic-update-slice_fusion), channel_id=1, source_target_pairs={{0,8},{1,9},{2,10},{3,11},{4,12},{5,13},{6,14},{7,15},{8,0},{9,1},... | collective-permute-start | bytes 442376 | tf_op jit(solution)/shard_map/ppermute | solution.py:26
  13.4 2.6 collective-permute-start.1
  20.9 12.2 %text_front.1 = (bf16[640,768]{1,0:T(8,128)(2,1)S(1)}, bf16[640,2304]{1,0:T(8,128)(2,1)S(1)}, bf16[640,768]{1,0:T(8,128)(2,1)S(1)}, f32[640,768]{1,0:T(8,128)S(1...) custom-call(bf16[640,768]{1,0:T(8,128)(2,1)S(1)} %copy-done.15, ...), custom_call_target="tpu_custom_call" | custom-call | flops 3019898880 | bytes 11599872 | tf_op jit(solution)/shard_map/text_front/pallas_call | solution.py:341
  43.2 2.3 copy-done.36
  45.5 12.6 %text_up.1 = (bf16[640,3072]{1,0:T(8,128)(2,1)S(1)}, f32[40,3072]{1,0:T(8,128)S(1)}, f32[40,768]{1,0:T(8,128)S(1)}, f32[40,128]{1,0:T(8,128)S(1)}) custom-call(bf16[640,768]{1,0:T(8,128)(2,1)S(1)} %get-tuple-element.133.h2_ref, bf16[768,3072]{1,0:T(8,128)(2,1)S(1)} %copy-done.36, bf16[3072,768]{1,0:T(8,128)(2,1)} %wd_ref.3, ...), custom_call_target="tpu_custom_call" | custom-call | flops 3019898880 | bytes 13369344 | tf_op jit(solution)/shard_map/text_up/pallas_call | solution.py:500
  61.5 4.3 %all-to-all-start = ((bf16[40,32,96]{2,0,1:T(8,128)(2,1)}), bf16[40,32,96]{2,0,1:T(8,128)(2,1)S(1)}, u32[]{:S(2)}, u32[]{:S(2)}) async-start(bf16[40,32,96]{2,0,1:T(8,128)(2,1)} %copy.75), calls=%async_computation | async-start | bytes 655360 | tf_op jit(solution)/shard_map/all_to_all | solution.py:1003
  71.7 2.5 collective-permute-start.6
  76.4 12.5 %collective-permute-done.6 = bf16[1,40,1024]{2,1,0:T(8,128)(2,1)S(1)} collective-permute-done((bf16[1,40,1024]{2,1,0:T(8,128)(2,1)S(1)}, bf16[1,40,1024]{2,1,0:T(8,128)(2,1)S(1)}, u32[]{:S(2)}, u32[]{:S(2)}) %collective-permute-start.6) | collective-permute-done | bytes 81952 | tf_op jit(solution)/shard_map/ppermute | solution.py:26
  102.2 11.8 %image_front.1 = (bf16[400,768]{1,0:T(8,128)(2,1)S(1)}, f32[8,768]{1,0:T(8,128)S(1)}) custom-call(bf16[400,768]{1,0:T(8,128)(2,1)S(1)} %copy-done.38, bf16[768,768]{1,0:T(8,128)(2,1)S(1)} %copy-done.12, bf16[1,768]{1,0:T(2,128)(2,1)S(1)} %broadcast_in_dim.22.g1_ref, bf16[1,768]{1,0:T(2,128)(2,1)S(1)} %broadcast_in_dim.23.b1_ref, ...), custom_call_target="tpu_custom_call" | custom-call | flops 2831155200 | bytes 4718592 | tf_op jit(solution)/shard_map/image_front/pallas_call | solution.py:405
  118.4 2.4 collective-permute-done.17
  124.7 3.7 %copy-done.35 = bf16[768,6144]{1,0:T(8,128)(2,1)S(1)} copy-done((bf16[768,6144]{1,0:T(8,128)(2,1)S(1)}, bf16[768,6144]{1,0:T(8,128)(2,1)}, u32[]{:S(2)}) %copy-start.35) | copy-done | bytes 9437208
  129.5 12.5 %image_up.1 = bf16[8,768]{1,0:T(8,128)(2,1)S(1)} custom-call(bf16[400,768]{1,0:T(8,128)(2,1)S(1)} %copy-done.50, bf16[768,6144]{1,0:T(8,128)(2,1)S(1)} %copy-done.35, bf16[768,6144]{1,0:T(8,128)(2,1)S(1)} %copy-done.35, f32[8,768]{1,0:T(8,128)S(1)} %get-tuple-element.130.sum_ref), custom_call_target="tpu_custom_call" | custom-call | flops 1887436800 | bytes 9437184 | tf_op jit(solution)/shard_map/image_up/pallas_call | solution.py:567
  142.8 8.4 %all-to-all-start.1 = ((bf16[32,8,768]{2,1,0:T(8,128)(2,1)}), bf16[32,8,768]{2,1,0:T(8,128)(2,1)S(1)}, u32[]{:S(2)}, u32[]{:S(2)}) async-start(bf16[32,8,768]{2,1,0:T(8,128)(2,1)} %broadcast_in_dim.62), calls=%async_computation.1 | async-start | bytes 786432 | tf_op jit(solution)/shard_map/all_to_all | solution.py:46
  154.9 5.7 %left_factors.1 = (bf16[2,768,640]{2,1,0:T(8,128)(2,1)S(1)}, bf16[3,768,640]{2,1,0:T(8,128)(2,1)S(1)}) custom-call(bf16[2,768,768]{2,1,0:T(8,128)(2,1)S(1)} %add_convert_fusion.order_ref, bf16[640,768]{1,0:T(8,128)(2,1)S(1)} %copy-done.56, bf16[640,768]{1,0:T(8,128)(2,1)S(1)} %copy-done.52, bf16[640,768]{1,0:T(8,128)(2,1)S(1)} %copy-done.54), custom_call_target="tpu_custom_call" | custom-call | flops 3774873600 | bytes 13762560 | tf_op jit(solution)/shard_map/left_factors/pallas_call | solution.py:605
  172.2 12.2 %mlp_back.1 = (bf16[384,1536]{1,0:T(8,128)(2,1)S(1)}, bf16[384,1536]{1,0:T(8,128)(2,1)S(1)}, bf16[384,1536]{1,0:T(8,128)(2,1)S(1)}, bf16[384,1536]{1,0:T(8,128)(...) custom-call(bf16[40,768]{1,0:T(8,128)(2,1)S(1)} %get-tuple-element.139.low_ref, ...), custom_call_target="tpu_custom_call" | custom-call | flops 6039797760 | bytes 18087936 | tf_op jit(solution)/shard_map/mlp_back/pallas_call | solution.py:800
  191.9 9.2 %attention_back.3 = (bf16[512,768]{1,0:T(8,128)(2,1)S(1)}, bf16[512,2304]{1,0:T(8,128)(2,1)S(1)}) custom-call(f32[640,768]{1,0:T(8,128)S(1)} %get-tuple-element.144.grad_ref.refs_5_, bf16[768,768]{1,0:T(8,128)(2,1)S(1)} %copy-done.14, bf16[640,2304]{1,0:T(8,128)(2,1)S(1)} %copy-done.5, f32[80,128]{1,0:T(8,128)S(1)} %copy-done.28, ...), custom_call_target="tpu_custom_call" | custom-call | flops 3019898880 | bytes 7471104 | tf_op jit(solution)/shard_map/attention_back/pallas_call | solution.py:849
  201.0 3.9 %collective-permute-done.22.got_a = bf16[192,1536]{1,0:T(8,128)(2,1)S(1)} collective-permute-done((bf16[192,1536]{1,0:T(8,128)(2,1)S(1)}, bf16[192,1536]{1,0:T(8,128)(2,1)S(1)}, u32[]{:S(2)}, u32[]{:S(2)}) %collective-permute-start.22) | collective-permute-done | bytes 589856 | tf_op jit(solution)/shard_map/ppermute | solution.py:26
  210.4 3.7 %collective-permute-done.25.got_a = bf16[96,1536]{1,0:T(8,128)(2,1)S(1)} collective-permute-done((bf16[96,1536]{1,0:T(8,128)(2,1)S(1)}, bf16[96,1536]{1,0:T(8,128)(2,1)S(1)}, u32[]{:S(2)}, u32[]{:S(2)}) %collective-permute-start.25) | collective-permute-done | bytes 294944 | tf_op jit(solution)/shard_map/ppermute | solution.py:26
  217.5 2.8 collective-permute-done.27.got_b
  227.1 6.4 %input_back.1 = (f32[640,768]{1,0:T(8,128)}, f32[1,768]{1,0:T(1,128)S(1)}, f32[1,768]{1,0:T(1,128)S(1)}) custom-call(bf16[128,2304]{1,0:T(8,128)(2,1)S(1)} %get-tuple-element.147.refs_0_, bf16[512,2304]{1,0:T(8,128)(2,1)S(1)} %get-tuple-element.156.refs_0_.refs_1_, bf16[768,2304]{1,0:T(8,128)(2,1)S(1)} %copy-done.3, bf16[640,768]{1,0:T(8,128)(2,1)S(1)} %copy-done.16, ...), custom_call_target="tpu_custom_call" | custom-call | flops 2264924160 | bytes 10420224 | tf_op jit(solution)/shard_map/input_back/pallas_call | solution.py:925
  233.5 4.1 %collective-permute-done.29 = bf16[24,3072]{1,0:T(8,128)(2,1)S(1)} collective-permute-done((bf16[24,3072]{1,0:T(8,128)(2,1)S(1)}, bf16[24,3072]{1,0:T(8,128)(2,1)S(1)}, u32[]{:S(2)}, u32[]{:S(2)}) %collective-permute-start.29) | collective-permute-done | bytes 147488 | tf_op jit(solution)/shard_map/ppermute | solution.py:26
  243.1 5.2 %all-to-all-start.2 = ((bf16[32,1,4,768]{3,2,1,0:T(4,128)(2,1)}), bf16[32,1,4,768]{3,2,1,0:T(4,128)(2,1)}, u32[]{:S(2)}, u32[]{:S(2)}) async-start(bf16[32,1,4,768]{3,2,1,0:T(4,128)(2,1)} %broadcast_in_dim.63), calls=%async_computation.2 | async-start | bytes 393216 | tf_op jit(solution)/shard_map/all_to_all | solution.py:46
  253.6 6.1 %collective-permute-done.33.got_a = bf16[96,1536]{1,0:T(8,128)(2,1)S(1)} collective-permute-done((bf16[96,1536]{1,0:T(8,128)(2,1)}, bf16[96,1536]{1,0:T(8,128)(2,1)S(1)}, u32[]{:S(2)}, u32[]{:S(2)}) %collective-permute-start.33) | collective-permute-done | bytes 294944 | tf_op jit(solution)/shard_map/ppermute | solution.py:26
  268.2 5.9 %grad_of_down.1 = f32[96,768]{1,0:T(8,128)S(1)} custom-call(bf16[1280,1024]{1,0:T(8,128)(2,1)S(1)} %bitcast.76, bf16[256,768]{1,0:T(8,128)(2,1)S(1)} %bitcast.78, f32[1,256]{1,0:T(1,128)S(1)} %copy-done.30, f32[1,256]{1,0:T(1,128)S(1)} %copy-done.32, f32[1,128]{1,0:T(1,128)S(1)} %copy-done.34, bf16[1280,96]{1,0:T(8,128)(2,1)S(1)} %bitcast.79, ...), custom_call_target="tpu_custom_call" | custom-call | flops 1006632960 | bytes 2621440 | tf_op jit(solution)/shard_map/grad_of_down/pallas_call | solution.py:731
  (296 shorter events, 116.3 us)
Async XLA Ops:
  7.2 117.5 %all-gather.2.cloned.1.call-start = ((), (), s32[]{:S(2)}) async-start(), calls=%async_computation.3 | async-start | bytes 9732096 | tf_op jit(solution)/shard_map/all_gather | solution.py:965
  10.3 29.5 %collective-permute-start = (bf16[24,3072]{1,0:T(8,128)(2,1)S(1)}, bf16[24,3072]{1,0:T(8,128)(2,1)S(1)}, u32[]{:S(2)}, u32[]{:S(2)}) collective-permute-start(bf16[24,3072]{1,0:T(8,128)(2,1)S(1)} %constant_dynamic-update-slice_fusion), channel_id=1, source_target_pairs={{0,8},{1,9},{2,10},{3,11},{4,12},{5,13},{6,14},{7,15},{8,0},{9,1},... | collective-permute-start | bytes 442376 | tf_op jit(solution)/shard_map/ppermute | solution.py:26
  13.4 26.4 %collective-permute-start.1 = (bf16[24,3072]{1,0:T(8,128)(2,1)S(1)}, bf16[24,3072]{1,0:T(8,128)(2,1)S(1)}, u32[]{:S(2)}, u32[]{:S(2)}) collective-permute-start(bf16[24,3072]{1,0:T(8,128)(2,1)S(1)} %constant_dynamic-update-slice_fusion), channel_id=1, source_target_pairs={{0,16},{1,17},{2,18},{3,19},{4,20},{5,21},{6,22},{7,23},{8,24},{9,... | collective-permute-start | bytes 442376 | tf_op jit(solution)/shard_map/ppermute | solution.py:26
  16.0 23.8 %collective-permute-start.2 = (bf16[24,3072]{1,0:T(8,128)(2,1)S(1)}, bf16[24,3072]{1,0:T(8,128)(2,1)S(1)}, u32[]{:S(2)}, u32[]{:S(2)}) collective-permute-start(bf16[24,3072]{1,0:T(8,128)(2,1)S(1)} %constant_dynamic-update-slice_fusion), channel_id=1, source_target_pairs={{0,24},{1,25},{2,26},{3,27},{4,28},{5,29},{6,30},{7,31},{8,16},{9,... | collective-permute-start | bytes 442376 | tf_op jit(solution)/shard_map/ppermute | solution.py:26
  39.9 26.0 %collective-permute-start.3 = (bf16[96,3072]{1,0:T(8,128)(2,1)S(1)}, bf16[96,3072]{1,0:T(8,128)(2,1)S(1)}, u32[]{:S(2)}, u32[]{:S(2)}) collective-permute-start(bf16[96,3072]{1,0:T(8,128)(2,1)S(1)} %pad_maximum_fusion.4.refs_0_), channel_id=1, source_target_pairs={{0,2},{1,3},{2,0},{3,1},{4,6},{5,7},{6,4},{7,5},{8,10},{9,11},{10,... | collective-permute-start | bytes 1769480 | tf_op jit(solution)/shard_map/ppermute | solution.py:26
  41.7 24.2 %collective-permute-start.4 = (bf16[96,3072]{1,0:T(8,128)(2,1)S(1)}, bf16[96,3072]{1,0:T(8,128)(2,1)}, u32[]{:S(2)}, u32[]{:S(2)}) collective-permute-start(bf16[96,3072]{1,0:T(8,128)(2,1)S(1)} %pad_maximum_fusion.4.refs_0_), channel_id=1, source_target_pairs={{0,4},{1,5},{2,6},{3,7},{4,0},{5,1},{6,2},{7,3},{8,12},{9,13},{10,... | collective-permute-start | bytes 1769480 | tf_op jit(solution)/shard_map/ppermute | solution.py:26
  61.5 27.9 %all-to-all-start = ((bf16[40,32,96]{2,0,1:T(8,128)(2,1)}), bf16[40,32,96]{2,0,1:T(8,128)(2,1)S(1)}, u32[]{:S(2)}, u32[]{:S(2)}) async-start(bf16[40,32,96]{2,0,1:T(8,128)(2,1)} %copy.75), calls=%async_computation | async-start | bytes 655360 | tf_op jit(solution)/shard_map/all_to_all | solution.py:1003
  65.9 23.5 %collective-permute-start.8 = (bf16[48,3072]{1,0:T(8,128)(2,1)S(1)}, bf16[48,3072]{1,0:T(8,128)(2,1)}, u32[]{:S(2)}, u32[]{:S(2)}) collective-permute-start(bf16[48,3072]{1,0:T(8,128)(2,1)S(1)} %slice.45), channel_id=1, source_target_pairs={{0,4},{1,5},{2,6},{3,7},{4,0},{5,1},{6,2},{7,3},{8,12},{9,13},{10,... | collective-permute-start | bytes 884744 | tf_op jit(solution)/shard_map/ppermute | solution.py:26
  68.6 20.8 %collective-permute-start.9 = (bf16[48,3072]{1,0:T(8,128)(2,1)S(1)}, bf16[48,3072]{1,0:T(8,128)(2,1)}, u32[]{:S(2)}, u32[]{:S(2)}) collective-permute-start(bf16[48,3072]{1,0:T(8,128)(2,1)S(1)} %slice.46), channel_id=1, source_target_pairs={{0,2},{1,3},{2,0},{3,1},{4,6},{5,7},{6,4},{7,5},{8,10},{9,11},{10,... | collective-permute-start | bytes 884744 | tf_op jit(solution)/shard_map/ppermute | solution.py:26
  71.7 17.2 %collective-permute-start.6 = (bf16[1,40,1024]{2,1,0:T(8,128)(2,1)S(1)}, bf16[1,40,1024]{2,1,0:T(8,128)(2,1)S(1)}, u32[]{:S(2)}, u32[]{:S(2)}) collective-permute-start(bf16[1,40,1024]{2,1,0:T(8,128)(2,1)S(1)} %bitcast.81), channel_id=1, source_target_pairs={{0,16},{1,17},{2,18},{3,19},{4,20},{5,21},{6,22},{7,23},{8,24},{9,... | collective-permute-start | bytes 245768 | tf_op jit(solution)/shard_map/ppermute | solution.py:26
  74.2 14.7 %collective-permute-start.7 = (bf16[1,40,1024]{2,1,0:T(8,128)(2,1)S(1)}, bf16[1,40,1024]{2,1,0:T(8,128)(2,1)S(1)}, u32[]{:S(2)}, u32[]{:S(2)}) collective-permute-start(bf16[1,40,1024]{2,1,0:T(8,128)(2,1)S(1)} %bitcast.82), channel_id=1, source_target_pairs={{0,24},{1,25},{2,26},{3,27},{4,28},{5,29},{6,30},{7,31},{8,16},{9,... | collective-permute-start | bytes 245768 | tf_op jit(solution)/shard_map/ppermute | solution.py:26
  76.4 14.5 %collective-permute-start.10 = (bf16[96,3072]{1,0:T(8,128)(2,1)S(1)}, bf16[96,3072]{1,0:T(8,128)(2,1)S(1)}, u32[]{:S(2)}, u32[]{:S(2)}) collective-permute-start(bf16[96,3072]{1,0:T(8,128)(2,1)S(1)} %pad_maximum_fusion.4.refs_0_), channel_id=1, source_target_pairs={{0,1},{1,0},{2,3},{3,2},{4,5},{5,4},{6,7},{7,6},{8,9},{9,8},{10,11... | collective-permute-start | bytes 1769480 | tf_op jit(solution)/shard_map/ppermute | solution.py:26
  91.7 22.3 %collective-permute-start.15 = (bf16[4,40,1024]{2,1,0:T(8,128)(2,1)}, bf16[4,40,1024]{2,1,0:T(8,128)(2,1)}, u32[]{:S(2)}, u32[]{:S(2)}) collective-permute-start(bf16[4,40,1024]{2,1,0:T(8,128)(2,1)} %bitcast.16), channel_id=1, source_target_pairs={{0,2},{1,3},{2,0},{3,1},{4,6},{5,7},{6,4},{7,5},{8,10},{9,11},{10,... | collective-permute-start | bytes 983048 | tf_op jit(solution)/shard_map/ppermute | solution.py:26
  93.2 20.9 %collective-permute-start.16 = (bf16[4,40,1024]{2,1,0:T(8,128)(2,1)}, bf16[4,40,1024]{2,1,0:T(8,128)(2,1)}, u32[]{:S(2)}, u32[]{:S(2)}) collective-permute-start(bf16[4,40,1024]{2,1,0:T(8,128)(2,1)} %bitcast.16), channel_id=1, source_target_pairs={{0,4},{1,5},{2,6},{3,7},{4,0},{5,1},{6,2},{7,3},{8,12},{9,13},{10,... | collective-permute-start | bytes 983048 | tf_op jit(solution)/shard_map/ppermute | solution.py:26
  124.7 39.5 %collective-permute-start.19 = (bf16[16,40,1024]{2,1,0:T(8,128)(2,1)}, bf16[16,40,1024]{2,1,0:T(8,128)(2,1)}, u32[]{:S(2)}, u32[]{:S(2)}) collective-permute-start(bf16[16,40,1024]{2,1,0:T(8,128)(2,1)} %bitcast.86), channel_id=1, source_target_pairs={{0,1},{1,0},{2,3},{3,2},{4,5},{5,4},{6,7},{7,6},{8,9},{9,8},{10,11... | collective-permute-start | bytes 3932168 | tf_op jit(solution)/shard_map/ppermute | solution.py:26
  142.8 21.4 %all-to-all-start.1 = ((bf16[32,8,768]{2,1,0:T(8,128)(2,1)}), bf16[32,8,768]{2,1,0:T(8,128)(2,1)S(1)}, u32[]{:S(2)}, u32[]{:S(2)}) async-start(bf16[32,8,768]{2,1,0:T(8,128)(2,1)} %broadcast_in_dim.62), calls=%async_computation.1 | async-start | bytes 786432 | tf_op jit(solution)/shard_map/all_to_all | solution.py:46
  189.5 15.4 %collective-permute-start.22 = (bf16[192,1536]{1,0:T(8,128)(2,1)S(1)}, bf16[192,1536]{1,0:T(8,128)(2,1)S(1)}, u32[]{:S(2)}, u32[]{:S(2)}) collective-permute-start(bf16[192,1536]{1,0:T(8,128)(2,1)S(1)} %get-tuple-element.153.refs_1_), channel_id=1, source_target_pairs={{0,2},{1,3},{2,0},{3,1},{4,6},{5,7},{6,4},{7,5},{8,10},{9,11},{10,... | collective-permute-start | bytes 1769480 | tf_op jit(solution)/shard_map/ppermute | solution.py:26
  190.4 15.1 %collective-permute-start.23 = (bf16[192,1536]{1,0:T(8,128)(2,1)S(1)}, bf16[192,1536]{1,0:T(8,128)(2,1)S(1)}, u32[]{:S(2)}, u32[]{:S(2)}) collective-permute-start(bf16[192,1536]{1,0:T(8,128)(2,1)S(1)} %get-tuple-element.155.refs_3_), channel_id=1, source_target_pairs={{0,4},{1,5},{2,6},{3,7},{4,0},{5,1},{6,2},{7,3},{8,12},{9,13},{10,... | collective-permute-start | bytes 1769480 | tf_op jit(solution)/shard_map/ppermute | solution.py:26
  220.9 16.7 %collective-permute-start.31 = (bf16[192,1536]{1,0:T(8,128)(2,1)S(1)}, bf16[192,1536]{1,0:T(8,128)(2,1)S(1)}, u32[]{:S(2)}, u32[]{:S(2)}) collective-permute-start(bf16[192,1536]{1,0:T(8,128)(2,1)S(1)} %get-tuple-element.179), channel_id=1, source_target_pairs={{0,2},{1,3},{2,0},{3,1},{4,6},{5,7},{6,4},{7,5},{8,10},{9,11},{10,... | collective-permute-start | bytes 1769480 | tf_op jit(solution)/shard_map/ppermute | solution.py:26
  221.6 15.9 %collective-permute-start.32 = (bf16[192,1536]{1,0:T(8,128)(2,1)S(1)}, bf16[192,1536]{1,0:T(8,128)(2,1)S(1)}, u32[]{:S(2)}, u32[]{:S(2)}) collective-permute-start(bf16[192,1536]{1,0:T(8,128)(2,1)S(1)} %get-tuple-element.181), channel_id=1, source_target_pairs={{0,4},{1,5},{2,6},{3,7},{4,0},{5,1},{6,2},{7,3},{8,12},{9,13},{10,... | collective-permute-start | bytes 1769480 | tf_op jit(solution)/shard_map/ppermute | solution.py:26
  223.7 13.8 %collective-permute-start.29 = (bf16[24,3072]{1,0:T(8,128)(2,1)S(1)}, bf16[24,3072]{1,0:T(8,128)(2,1)S(1)}, u32[]{:S(2)}, u32[]{:S(2)}) collective-permute-start(bf16[24,3072]{1,0:T(8,128)(2,1)S(1)} %get-tuple-element.172), channel_id=1, source_target_pairs={{0,16},{1,17},{2,18},{3,19},{4,20},{5,21},{6,22},{7,23},{8,24},{9,... | collective-permute-start | bytes 442376 | tf_op jit(solution)/shard_map/ppermute | solution.py:26
  243.1 23.1 %all-to-all-start.2 = ((bf16[32,1,4,768]{3,2,1,0:T(4,128)(2,1)}), bf16[32,1,4,768]{3,2,1,0:T(4,128)(2,1)}, u32[]{:S(2)}, u32[]{:S(2)}) async-start(bf16[32,1,4,768]{3,2,1,0:T(4,128)(2,1)} %broadcast_in_dim.63), calls=%async_computation.2 | async-start | bytes 393216 | tf_op jit(solution)/shard_map/all_to_all | solution.py:46
  261.8 13.6 %collective-permute-start.35 = (bf16[24,3072]{1,0:T(8,128)(2,1)}, bf16[24,3072]{1,0:T(8,128)(2,1)}, u32[]{:S(2)}, u32[]{:S(2)}) collective-permute-start(bf16[24,3072]{1,0:T(8,128)(2,1)} %get-tuple-element.196), channel_id=1, source_target_pairs={{0,8},{1,9},{2,10},{3,11},{4,12},{5,13},{6,14},{7,15},{8,0},{9,1},... | collective-permute-start | bytes 442376 | tf_op jit(solution)/shard_map/ppermute | solution.py:26
  263.2 14.0 %collective-permute-start.36 = (bf16[24,3072]{1,0:T(8,128)(2,1)}, bf16[24,3072]{1,0:T(8,128)(2,1)}, u32[]{:S(2)}, u32[]{:S(2)}) collective-permute-start(bf16[24,3072]{1,0:T(8,128)(2,1)} %get-tuple-element.197), channel_id=1, source_target_pairs={{0,16},{1,17},{2,18},{3,19},{4,20},{5,21},{6,22},{7,23},{8,24},{9,... | collective-permute-start | bytes 442376 | tf_op jit(solution)/shard_map/ppermute | solution.py:26
  (94 other events, 560.4 us)
Sparse Core Ops, SparseCore 0:
  11.6 99.5 all-gather.1

commit v3 on v2

--- a/solution.py
+++ b/solution.py
@@ -105,7 +105,7 @@
     return total
 
 
-VMEM_BYTES = 40 << 20
+VMEM_BYTES = 56 << 20
 TILE = 512
 
 
@@ -466,7 +466,7 @@
 def text_up_kernel(h2_ref, wu_ref, wd_ref, sum_ref, *refs):
     slope_ref, hid_ref, unit_ref, inv_ref, acc = refs[-5:]
     step = pl.program_id(0)
-    chunk = 128
+    chunk = 320
     per = chunk // TXT_LEN
     pool = pool_matrix(per, chunk, 0, TXT_LEN)
     for k in range(h2_ref.shape[0] // chunk):
@@ -527,24 +527,25 @@
 
 
 def image_up_kernel(fold, h2_ref, wu_ref, wd_ref, sum_ref, *refs):
-    out_ref, acc = refs[-2:]
+    out_ref, acc, chosen_ref = refs[-3:]
     step = pl.program_id(0)
     rows, count = h2_ref.shape[0], sum_ref.shape[0]
-    chunk = 80
-    summed = jnp.zeros((count, TILE), f32)
-    for k in range(rows // chunk):
-        inner = mul(h2_ref[k * chunk : (k + 1) * chunk, :], wu_ref[...])
-        value, _ = gelu_parts(inner)
-        pool = pool_matrix(count, chunk, k * chunk, IMG_LEN)
-        summed = summed + mul(pool, value.astype(bf16))
+    part = TILE // fold
+
+    @pl.when(step == 0)
+    def _():
+        place = lax.broadcasted_iota(jnp.int32, (TILE, TILE), 0)
+        col = lax.broadcasted_iota(jnp.int32, (TILE, TILE), 1)
+        source = (col % part) * fold + col // part
+        chosen_ref[...] = jnp.where(place == source, 1.0, 0.0).astype(bf16)
+
+    inner = mul(h2_ref[...], wu_ref[...])
+    value, _ = gelu_parts(inner)
+    summed = mul(pool_matrix(count, rows, 0, IMG_LEN), value.astype(bf16))
     mean = two_terms(summed * (1.0 / IMG_LEN))
-    place = lax.broadcasted_iota(jnp.int32, (TILE, TILE // fold), 0)
-    picked = lax.broadcasted_iota(jnp.int32, (TILE, TILE // fold), 1) * fold
-    terms = jnp.zeros((2 * count, D), f32)
-    for k in range(fold):
-        chosen = jnp.where(place == picked + k, 1.0, 0.0).astype(bf16)
-        part = mul(mean, chosen).astype(bf16)
-        terms = terms + mul(part, wd_ref[:, k * D : (k + 1) * D])
+    moved = mul(mean, chosen_ref[...]).astype(bf16)
+    weight = jnp.concatenate([wd_ref[:, k * D : (k + 1) * D] for k in range(fold)], axis=0)
+    terms = mul(moved, weight)
     added = terms[:count] + terms[count:]
 
     @pl.when(step == 0)
@@ -576,7 +577,7 @@
         ]
         + anywhere(after),
         out_specs=fixed((count, D)),
-        scratch_shapes=[pltpu.VMEM((count, D), f32)],
+        scratch_shapes=[pltpu.VMEM((count, D), f32), pltpu.VMEM((TILE, TILE), bf16)],
         compiler_params=params(),
         cost_estimate=cost(2 * rows * D * FF, 4 * D * FF, 15 * rows * FF),
         name="image_up",
@@ -619,7 +620,7 @@
             pl.BlockSpec((1, D, rows), lambda i: (jnp.minimum(i, 1), 0, 0)),
             pl.BlockSpec((1, D, rows), lambda i: (jnp.maximum(i - 2, 0), 0, 0)),
         ],
-        compiler_params=params(),
+        compiler_params=params(24 << 20),
         cost_estimate=cost(10 * rows * D * D, 16 * rows * D + 10 * D * D),
         name="left_factors",
     )(orders, normed2, normed1, attended)
@@ -699,7 +700,9 @@
     return pl.pallas_call(
         loss_kernel,
         out_shape=[jax.ShapeDtypeStruct(*item) for item in zip(shapes, kinds)],
-        compiler_params=params(),
+        in_specs=in_vmem(5),
+        out_specs=in_vmem(len(shapes)),
+        compiler_params=params(16 << 20),
         cost_estimate=cost(2 * pack.shape[0] * images * D, 2 * pack.size, pack.shape[0] * images),
         name="loss_and_rows",
     )(pack, image_all, own_pack, unit, inverse)
@@ -739,7 +742,7 @@
         ]
         + anywhere(after),
         out_specs=fixed((per, D)),
-        compiler_params=params(),
+        compiler_params=params(16 << 20),
         cost_estimate=cost(4 * pack.shape[0] * images * D, 2 * pack.size, pack.shape[0] * images),
         name="grad_of_down",
     )(pack, image_all, col_sum, col_count, live_total, hidden_cols, *after)
@@ -866,14 +869,14 @@
 
 
 def weight_back_kernel(factors, groups, lhs_ref, *refs):
-    keep, send = refs[-2:]
+    keep_a, send_a, keep_b, send_b = refs[-4:]
     half = D // 2
     for k, (factor, group, col) in enumerate(factors):
         parts = refs[sum(groups[:group]) : sum(groups[: group + 1])]
         weight = mul_rows(lhs_ref.at[factor], parts, slice(col * D, (col + 1) * D)).astype(bf16)
-        at = slice(k * D, (k + 1) * D)
-        keep[:, at] = weight[:half]
-        send[:, at] = weight[half:]
+        at = slice(k % 2 * D, (k % 2 + 1) * D)
+        (keep_b if k > 1 else keep_a)[:, at] = weight[:half]
+        (send_b if k > 1 else send_a)[:, at] = weight[half:]
 
 
 def weight_back(lhs, groups, factors, after=()):
@@ -881,11 +884,11 @@
     given = [part for group in groups for part in group]
     return pl.pallas_call(
         functools.partial(weight_back_kernel, factors, [len(group) for group in groups]),
-        out_shape=[stays((D // 2, len(factors) * D), bf16)] * 2,
+        out_shape=[stays((D // 2, 2 * D), bf16)] * 4,
         in_specs=in_vmem(1 + len(given)) + anywhere(after),
-        out_specs=in_vmem(2),
+        out_specs=in_vmem(4),
         compiler_params=params(16 << 20),
-        cost_estimate=cost(4 * rows * D * D, 4 * rows * D + 7 * D * D),
+        cost_estimate=cost(8 * rows * D * D, 8 * rows * D + 14 * D * D),
         name="weight_back",
     )(lhs, *given, *after)
 
@@ -1055,30 +1058,30 @@
     low_two, proj_two = attention_back(grad_middle, txt_out, project, log_sums, 1, 4, up)
     up = fold(hand_on(up, stages - 2), (proj_two,))
     projs, lows = (proj_one, proj_two), (low_one, low_two)
-    rest_a = weight_back(lhs_rest, [projs], [(0, 0, 0), (0, 0, 1)], up)
-    up = hand_on_last(fold_last(hand_on(up, stages - 1), rest_a[1:]))
-    rest_b = weight_back(lhs_rest, [projs, lows], [(1, 0, 2), (2, 1, 0)], up[:1])
-    rest = [*rest_a, *rest_b]
-    for stage in range(stages - 2):
-        rest = fold(hand_on(rest, stage))
+    rest = weight_back(lhs_rest, [projs, lows], [(0, 0, 0), (0, 0, 1), (1, 0, 2), (2, 1, 0)], up)
+    up = hand_on(up, stages - 1)
     caption_grad, gain_one, bias_one = input_back(
         projs, txt_qkv, captions, txt_gain1, grad_middle, rest[:1]
     )
     caption_grad, up = in_turn(caption_grad, up)
-    rest = fold(hand_on(rest, stages - 2), (caption_grad,))
+    up = fold_last(up)
+    for stage in range(stages - 2):
+        rest = fold(hand_on(rest, stage), up[:1])
+    up = hand_on_last(up)
     norms = jnp.concatenate([gain_one, bias_one, gain_two, bias_two], axis=0)
-    norms, rest = in_turn(norms, rest)
     norms = jnp.sum(spread(norms[None].astype(bf16)).astype(f32), axis=0).reshape(4, D)
-    rest = fold_last(hand_on(rest, stages - 1))
+    rest = hand_on(rest, stages - 2)
     if small:
         grad_down = grad_of_down(
-            text_pack, image_all, col_sum, col_count, live_total, hidden_cols, (rest[0], norms)
+            text_pack, image_all, col_sum, col_count, live_total, hidden_cols, (caption_grad,)
         )
     else:
         grad_down = lax.psum_scatter(
             mul_at(hidden_sum.astype(bf16), row_low), AXIS, scatter_dimension=0, tiled=True
         )
-    grad_down, rest = in_turn(grad_down, hand_on_last(rest))
+    grad_down, rest, norms, up = lax.optimization_barrier((grad_down, rest, norms, up))
+    rest = fold(rest)
+    rest = hand_on_last(fold_last(hand_on(rest, stages - 1)))
     up_share = sum_last(*up)
     rest_share = sum_last(*rest)
     return (

time: 289 us -> 277 us (0.958)
  local copies, waits for them, and re-layouts: 54 us -> 37.7 us
  Pallas kernels: 99.6 us -> 107 us
  waiting for transfers between devices: 43.9 us -> 37.5 us
  starting transfers between devices: 58.9 us -> 63.9 us
    unnamed x155 -> x105, local copies, waits for them, and re-layouts: 41.4 us -> 20 us
    ppermute x38, waiting for transfers between devices: 43.1 us -> 36.9 us  [swapped(): return lax.ppermute(value, AXIS, [(i, i ^ mask) for i in range(peers)])]
    pallas_call x1, Pallas kernels: 12.2 us -> 18 us  [text_front(): pl.pallas_call(text_front_kernel, out_shape=[jax.ShapeDtypeStruct(*item)...]
    pallas_call x1, Pallas kernels: 12.5 us -> 9.34 us  [image_up(): pl.pallas_call(functools.partial(image_up_kernel, fold), grid=(FF // TILE...]
    all_to_all x2, starting transfers between devices: 13.6 us -> 16.7 us  [spread(): return lax.all_to_all(copies, AXIS, split_axis=0, concat_axis=0, tiled=True)]
  transfers between devices with their start and end apart: 42 -> 42, of which waited for: 15 -> 14; matrix products, arithmetic and copies ran while one was open for 7% -> 10% of each run, Pallas kernels for 29% -> 31%
where the time goes in v3:
time: 277 us; the launch traced here: 276 us
  Pallas kernels  107 us (39%)
  starting transfers between devices  63.9 us (23%)
  local copies, waits for them, and re-layouts  37.7 us (14%)
  waiting for transfers between devices  37.5 us (14%)
  other arithmetic  15.4 us (6%)
  between operations  14.8 us (5%)
    ppermute x38, starting transfers between devices, swapped(): return lax.ppermute(value, AXIS, [(i, i ^ mask) for i in range(peers)])  42.8 us
    ppermute x38, waiting for transfers between devices, swapped(): return lax.ppermute(value, AXIS, [(i, i ^ mask) for i in range(peers)])  36.9 us
    unnamed x105, local copies, waits for them, and re-layouts  20 us
    pallas_call x1, Pallas kernels, text_front(): pl.pallas_call(text_front_kernel, out_shape=[jax.ShapeDtypeStruct(*item)...  18 us
    all_to_all x2, starting transfers between devices, spread(): return lax.all_to_all(copies, AXIS, split_axis=0, concat_axis=0, tiled=True)  16.7 us
    pallas_call x1, Pallas kernels, image_front(): pl.pallas_call(functools.partial(image_front_kernel, windows), out_shape=...  13.8 us
    pallas_call x1, Pallas kernels, mlp_back(): pl.pallas_call(mlp_back_kernel, out_shape=[stays((D // 2, FF // 2), bf16)...  12.2 us
    pallas_call x1, Pallas kernels, text_up(): pl.pallas_call(text_up_kernel, grid=(FF // TILE,), out_shape=[jax.ShapeDt...  12 us
  transfers between devices with their start and end apart: 42, of which 14 were waited for; matrix products, arithmetic and copies ran while one was open for 10% of the time, Pallas kernels for 31%

profile of v3, /device:TPU:0, one launch (start us, length us, event | category | flops | bytes accessed | tf_op | source)
XLA Modules:
  0.0 275.9 jit_solution(4646559611225032064)
XLA Ops:
  10.3 3.1 %collective-permute-start = (bf16[24,3072]{1,0:T(8,128)(2,1)S(1)}, bf16[24,3072]{1,0:T(8,128)(2,1)S(1)}, u32[]{:S(2)}, u32[]{:S(2)}) collective-permute-start(bf16[24,3072]{1,0:T(8,128)(2,1)S(1)} %constant_dynamic-update-slice_fusion), channel_id=1, source_target_pairs={{0,8},{1,9},{2,10},{3,11},{4,12},{5,13},{6,14},{7,15},{8,0},{9,1},... | collective-permute-start | bytes 442376 | tf_op jit(solution)/shard_map/ppermute | solution.py:26
  13.4 2.6 collective-permute-start.1
  18.6 18.0 %text_front.1 = (bf16[640,768]{1,0:T(8,128)(2,1)}, bf16[640,2304]{1,0:T(8,128)(2,1)}, bf16[640,768]{1,0:T(8,128)(2,1)}, f32[640,768]{1,0:T(8,128)}, bf16[640,768...) custom-call(bf16[640,768]{1,0:T(8,128)(2,1)} %refs_3_.1, f32[1,768]{1,0:T(1,128)} %broadcast_in_dim.26.g1_ref.refs_4_, ...), custom_call_target="tpu_custom_call" | custom-call | flops 3019898880 | bytes 11599872 | tf_op jit(solution)/shard_map/text_front/pallas_call | solution.py:341
  43.1 12.0 %text_up.1 = (bf16[640,3072]{1,0:T(8,128)(2,1)}, f32[40,3072]{1,0:T(8,128)}, f32[40,768]{1,0:T(8,128)}, f32[40,128]{1,0:T(8,128)}) custom-call(bf16[640,768]{1,0:T(8,128)(2,1)} %get-tuple-element.133.h2_ref, bf16[768,3072]{1,0:T(8,128)(2,1)} %wu_ref.3, bf16[3072,768]{1,0:T(8,128)(2,1)} %wd_ref.3, f32[40,768]{1,0:T(8,128)} %get-tuple-element.112.sum_ref, ...), custom_call_target="tpu_custom_call" | custom-call | flops 3019898880 | bytes 13369344 | tf_op jit(solution)/shard_map/text_up/pallas_call | solution.py:500
  58.3 4.3 %all-to-all-start = ((bf16[40,32,96]{2,0,1:T(8,128)(2,1)}), bf16[40,32,96]{2,0,1:T(8,128)(2,1)S(1)}, u32[]{:S(2)}, u32[]{:S(2)}) async-start(bf16[40,32,96]{2,0,1:T(8,128)(2,1)} %copy.75), calls=%async_computation | async-start | bytes 655360 | tf_op jit(solution)/shard_map/all_to_all | solution.py:1006
  70.6 2.7 collective-permute-start.6
  74.9 7.3 %collective-permute-done.6 = bf16[1,40,1024]{2,1,0:T(8,128)(2,1)S(1)} collective-permute-done((bf16[1,40,1024]{2,1,0:T(8,128)(2,1)}, bf16[1,40,1024]{2,1,0:T(8,128)(2,1)S(1)}, u32[]{:S(2)}, u32[]{:S(2)}) %collective-permute-start.6) | collective-permute-done | bytes 81952 | tf_op jit(solution)/shard_map/ppermute | solution.py:26
  91.7 13.8 %image_front.1 = (bf16[400,768]{1,0:T(8,128)(2,1)}, f32[8,768]{1,0:T(8,128)}) custom-call(bf16[400,768]{1,0:T(8,128)(2,1)} %x_ref.3, bf16[768,768]{1,0:T(8,128)(2,1)} %fusion.perm_ref, bf16[1,768]{1,0:T(2,128)(2,1)} %broadcast_in_dim.22.g1_ref, bf16[1,768]{1,0:T(2,128)(2,1)} %broadcast_in_dim.23.b1_ref, bf16[1,768]{1,0:T(2,128)(2,1)} %broadcast_in_dim.24.g2_ref, ...), custom_call_target="tpu_custom_call" | custom-call | flops 2831155200 | bytes 4718592 | tf_op jit(solution)/shard_map/image_front/pallas_call | solution.py:405
  108.9 3.5 %collective-permute-done.17 = bf16[2,40,1024]{2,1,0:T(8,128)(2,1)S(1)} collective-permute-done((bf16[2,40,1024]{2,1,0:T(8,128)(2,1)S(1)}, bf16[2,40,1024]{2,1,0:T(8,128)(2,1)S(1)}, u32[]{:S(2)}, u32[]{:S(2)}) %collective-permute-start.17) | collective-permute-done | bytes 163872 | tf_op jit(solution)/shard_map/ppermute | solution.py:26
  114.3 9.3 %image_up.1 = bf16[8,768]{1,0:T(8,128)(2,1)} custom-call(bf16[400,768]{1,0:T(8,128)(2,1)} %get-tuple-element.128.h2_ref, bf16[768,6144]{1,0:T(8,128)(2,1)} %all-gather.2.cloned.1.call-done.wu_ref.wd_ref, bf16[768,6144]{1,0:T(8,128)(2,1)} %all-gather.2.cloned.1.call-done.wu_ref.wd_ref, f32[8,768]{1,0:T(8,128)} %get-tuple-element.130.sum_ref), custom_call_target="tpu_custom_call" | custom-call | flops 1887436800 | bytes 9437184 | tf_op jit(solution)/shard_map/image_up/pallas_call | solution.py:568
  125.2 11.5 %all-to-all-start.1 = ((bf16[32,8,768]{2,1,0:T(8,128)(2,1)}), bf16[32,8,768]{2,1,0:T(8,128)(2,1)S(1)}, u32[]{:S(2)}, u32[]{:S(2)}) async-start(bf16[32,8,768]{2,1,0:T(8,128)(2,1)} %broadcast_in_dim.62), calls=%async_computation.1 | async-start | bytes 786432 | tf_op jit(solution)/shard_map/all_to_all | solution.py:46
  140.3 5.7 %left_factors.1 = (bf16[2,768,640]{2,1,0:T(8,128)(2,1)S(1)}, bf16[3,768,640]{2,1,0:T(8,128)(2,1)S(1)}) custom-call(bf16[2,768,768]{2,1,0:T(8,128)(2,1)S(1)} %add_convert_fusion.order_ref, bf16[640,768]{1,0:T(8,128)(2,1)S(1)} %copy-done.30, bf16[640,768]{1,0:T(8,128)(2,1)S(1)} %copy-done.28, bf16[640,768]{1,0:T(8,128)(2,1)S(1)} %copy-done.29), custom_call_target="tpu_custom_call" | custom-call | flops 3774873600 | bytes 13762560 | tf_op jit(solution)/shard_map/left_factors/pallas_call | solution.py:606
  157.8 12.2 %mlp_back.1 = (bf16[384,1536]{1,0:T(8,128)(2,1)S(1)}, bf16[384,1536]{1,0:T(8,128)(2,1)S(1)}, bf16[384,1536]{1,0:T(8,128)(2,1)S(1)}, bf16[384,1536]{1,0:T(8,128)(...) custom-call(bf16[40,768]{1,0:T(8,128)(2,1)S(1)} %get-tuple-element.139.low_ref, ...), custom_call_target="tpu_custom_call" | custom-call | flops 6039797760 | bytes 18087936 | tf_op jit(solution)/shard_map/mlp_back/pallas_call | solution.py:803
  177.6 9.2 %attention_back.3 = (bf16[512,768]{1,0:T(8,128)(2,1)S(1)}, bf16[512,2304]{1,0:T(8,128)(2,1)S(1)}) custom-call(f32[640,768]{1,0:T(8,128)S(1)} %get-tuple-element.144.grad_ref.refs_5_, bf16[768,768]{1,0:T(8,128)(2,1)S(1)} %copy-done.5, bf16[640,2304]{1,0:T(8,128)(2,1)S(1)} %copy-done.1, f32[80,128]{1,0:T(8,128)S(1)} %copy-done.16, ...), custom_call_target="tpu_custom_call" | custom-call | flops 3019898880 | bytes 7471104 | tf_op jit(solution)/shard_map/attention_back/pallas_call | solution.py:852
  186.8 3.7 %collective-permute-done.22.got_a = bf16[192,1536]{1,0:T(8,128)(2,1)S(1)} collective-permute-done((bf16[192,1536]{1,0:T(8,128)(2,1)S(1)}, bf16[192,1536]{1,0:T(8,128)(2,1)S(1)}, u32[]{:S(2)}, u32[]{:S(2)}) %collective-permute-start.22) | collective-permute-done | bytes 589856 | tf_op jit(solution)/shard_map/ppermute | solution.py:26
  193.1 3.9 %weight_back.1 = (bf16[384,1536]{1,0:T(8,128)(2,1)S(1)}, bf16[384,1536]{1,0:T(8,128)(2,1)S(1)}, bf16[384,1536]{1,0:T(8,128)(2,1)S(1)}, bf16[384,1536]{1,0:T(8,128)(2,1)S(1)}) custom-call(bf16[3,768,640]{2,1,0:T(8,128)(2,1)S(1)} %copy-done.23, bf16[128,2304]{1,0:T(8,128)(2,1)S(1)} %get-tuple-element.147.refs_0_, ...), custom_call_target="tpu_custom_call" | custom-call | flops 3019898880 | bytes 12189696 | tf_op jit(solution)/shard_map/weight_back/pallas_call | solution.py:885
  199.6 6.4 %input_back.1 = (f32[640,768]{1,0:T(8,128)}, f32[1,768]{1,0:T(1,128)S(1)}, f32[1,768]{1,0:T(1,128)S(1)}) custom-call(bf16[128,2304]{1,0:T(8,128)(2,1)S(1)} %get-tuple-element.147.refs_0_, bf16[512,2304]{1,0:T(8,128)(2,1)S(1)} %get-tuple-element.156.refs_0_.refs_1_, bf16[768,2304]{1,0:T(8,128)(2,1)S(1)} %copy-done, bf16[640,768]{1,0:T(8,128)(2,1)S(1)} %copy-done.8, ...), custom_call_target="tpu_custom_call" | custom-call | flops 2264924160 | bytes 10420224 | tf_op jit(solution)/shard_map/input_back/pallas_call | solution.py:928
  214.8 5.2 %all-to-all-start.2 = ((bf16[32,1,4,768]{3,2,1,0:T(4,128)(2,1)}), bf16[32,1,4,768]{3,2,1,0:T(4,128)(2,1)}, u32[]{:S(2)}, u32[]{:S(2)}) async-start(bf16[32,1,4,768]{3,2,1,0:T(4,128)(2,1)} %broadcast_in_dim.63), calls=%async_computation.2 | async-start | bytes 393216 | tf_op jit(solution)/shard_map/all_to_all | solution.py:46
  221.8 2.4 collective-permute-start.31
  226.0 5.8 %grad_of_down.1 = f32[96,768]{1,0:T(8,128)S(1)} custom-call(bf16[1280,1024]{1,0:T(8,128)(2,1)S(1)} %bitcast.75, bf16[256,768]{1,0:T(8,128)(2,1)S(1)} %bitcast.77, f32[1,256]{1,0:T(1,128)S(1)} %get-tuple-element.167.col_sum_ref, f32[1,256]{1,0:T(1,128)S(1)} %get-tuple-element.168.col_count_ref, f32[1,128]{1,0:T(1,128)S(1)} %get-tuple-element.169.live_ref, ...), custom_call_target="tpu_custom_call" | custom-call | flops 1006632960 | bytes 2621440 | tf_op jit(solution)/shard_map/grad_of_down/pallas_call | solution.py:734
  233.5 4.4 %collective-permute-done.31 = bf16[24,3072]{1,0:T(8,128)(2,1)} collective-permute-done((bf16[24,3072]{1,0:T(8,128)(2,1)}, bf16[24,3072]{1,0:T(8,128)(2,1)}, u32[]{:S(2)}, u32[]{:S(2)}) %collective-permute-start.31) | collective-permute-done | bytes 147488 | tf_op jit(solution)/shard_map/ppermute | solution.py:26
  244.7 5.1 %collective-permute-done.33.got_a = bf16[96,1536]{1,0:T(8,128)(2,1)S(1)} collective-permute-done((bf16[96,1536]{1,0:T(8,128)(2,1)S(1)}, bf16[96,1536]{1,0:T(8,128)(2,1)S(1)}, u32[]{:S(2)}, u32[]{:S(2)}) %collective-permute-start.33) | collective-permute-done | bytes 294944 | tf_op jit(solution)/shard_map/ppermute | solution.py:26
  251.1 3.8 %collective-permute-start.35 = (bf16[24,3072]{1,0:T(8,128)(2,1)S(1)}, bf16[24,3072]{1,0:T(8,128)(2,1)S(1)}, u32[]{:S(2)}, u32[]{:S(2)}) collective-permute-start(bf16[24,3072]{1,0:T(8,128)(2,1)S(1)} %get-tuple-element.200), channel_id=1, source_target_pairs={{0,8},{1,9},{2,10},{3,11},{4,12},{5,13},{6,14},{7,15},{8,0},{9,1},... | collective-permute-start | bytes 442376 | tf_op jit(solution)/shard_map/ppermute | solution.py:26
  260.6 7.0 %collective-permute-done.36 = bf16[24,3072]{1,0:T(8,128)(2,1)S(1)} collective-permute-done((bf16[24,3072]{1,0:T(8,128)(2,1)S(1)}, bf16[24,3072]{1,0:T(8,128)(2,1)S(1)}, u32[]{:S(2)}, u32[]{:S(2)}) %collective-permute-start.36) | collective-permute-done | bytes 147488 | tf_op jit(solution)/shard_map/ppermute | solution.py:26
  (249 shorter events, 98.0 us)
Async XLA Ops:
  7.2 107.1 %all-gather.2.cloned.1.call-start = ((), (), s32[]{:S(2)}) async-start(), calls=%async_computation.3 | async-start | bytes 9732096 | tf_op jit(solution)/shard_map/all_gather | solution.py:968
  10.3 29.4 %collective-permute-start = (bf16[24,3072]{1,0:T(8,128)(2,1)S(1)}, bf16[24,3072]{1,0:T(8,128)(2,1)S(1)}, u32[]{:S(2)}, u32[]{:S(2)}) collective-permute-start(bf16[24,3072]{1,0:T(8,128)(2,1)S(1)} %constant_dynamic-update-slice_fusion), channel_id=1, source_target_pairs={{0,8},{1,9},{2,10},{3,11},{4,12},{5,13},{6,14},{7,15},{8,0},{9,1},... | collective-permute-start | bytes 442376 | tf_op jit(solution)/shard_map/ppermute | solution.py:26
  13.4 26.3 %collective-permute-start.1 = (bf16[24,3072]{1,0:T(8,128)(2,1)S(1)}, bf16[24,3072]{1,0:T(8,128)(2,1)S(1)}, u32[]{:S(2)}, u32[]{:S(2)}) collective-permute-start(bf16[24,3072]{1,0:T(8,128)(2,1)S(1)} %constant_dynamic-update-slice_fusion), channel_id=1, source_target_pairs={{0,16},{1,17},{2,18},{3,19},{4,20},{5,21},{6,22},{7,23},{8,24},{9,... | collective-permute-start | bytes 442376 | tf_op jit(solution)/shard_map/ppermute | solution.py:26
  16.0 23.7 %collective-permute-start.2 = (bf16[24,3072]{1,0:T(8,128)(2,1)S(1)}, bf16[24,3072]{1,0:T(8,128)(2,1)S(1)}, u32[]{:S(2)}, u32[]{:S(2)}) collective-permute-start(bf16[24,3072]{1,0:T(8,128)(2,1)S(1)} %constant_dynamic-update-slice_fusion), channel_id=1, source_target_pairs={{0,24},{1,25},{2,26},{3,27},{4,28},{5,29},{6,30},{7,31},{8,16},{9,... | collective-permute-start | bytes 442376 | tf_op jit(solution)/shard_map/ppermute | solution.py:26
  39.8 23.0 %collective-permute-start.3 = (bf16[96,3072]{1,0:T(8,128)(2,1)S(1)}, bf16[96,3072]{1,0:T(8,128)(2,1)S(1)}, u32[]{:S(2)}, u32[]{:S(2)}) collective-permute-start(bf16[96,3072]{1,0:T(8,128)(2,1)S(1)} %pad_maximum_fusion.4.refs_0_), channel_id=1, source_target_pairs={{0,2},{1,3},{2,0},{3,1},{4,6},{5,7},{6,4},{7,5},{8,10},{9,11},{10,... | collective-permute-start | bytes 1769480 | tf_op jit(solution)/shard_map/ppermute | solution.py:26
  41.6 21.2 %collective-permute-start.4 = (bf16[96,3072]{1,0:T(8,128)(2,1)S(1)}, bf16[96,3072]{1,0:T(8,128)(2,1)}, u32[]{:S(2)}, u32[]{:S(2)}) collective-permute-start(bf16[96,3072]{1,0:T(8,128)(2,1)S(1)} %pad_maximum_fusion.4.refs_0_), channel_id=1, source_target_pairs={{0,4},{1,5},{2,6},{3,7},{4,0},{5,1},{6,2},{7,3},{8,12},{9,13},{10,... | collective-permute-start | bytes 1769480 | tf_op jit(solution)/shard_map/ppermute | solution.py:26
  58.3 24.5 %all-to-all-start = ((bf16[40,32,96]{2,0,1:T(8,128)(2,1)}), bf16[40,32,96]{2,0,1:T(8,128)(2,1)S(1)}, u32[]{:S(2)}, u32[]{:S(2)}) async-start(bf16[40,32,96]{2,0,1:T(8,128)(2,1)} %copy.75), calls=%async_computation | async-start | bytes 655360 | tf_op jit(solution)/shard_map/all_to_all | solution.py:1006
  62.8 20.0 %collective-permute-start.8 = (bf16[48,3072]{1,0:T(8,128)(2,1)S(1)}, bf16[48,3072]{1,0:T(8,128)(2,1)}, u32[]{:S(2)}, u32[]{:S(2)}) collective-permute-start(bf16[48,3072]{1,0:T(8,128)(2,1)S(1)} %slice.41), channel_id=1, source_target_pairs={{0,4},{1,5},{2,6},{3,7},{4,0},{5,1},{6,2},{7,3},{8,12},{9,13},{10,... | collective-permute-start | bytes 884744 | tf_op jit(solution)/shard_map/ppermute | solution.py:26
  65.4 17.4 %collective-permute-start.9 = (bf16[48,3072]{1,0:T(8,128)(2,1)S(1)}, bf16[48,3072]{1,0:T(8,128)(2,1)}, u32[]{:S(2)}, u32[]{:S(2)}) collective-permute-start(bf16[48,3072]{1,0:T(8,128)(2,1)S(1)} %slice.42), channel_id=1, source_target_pairs={{0,2},{1,3},{2,0},{3,1},{4,6},{5,7},{6,4},{7,5},{8,10},{9,11},{10,... | collective-permute-start | bytes 884744 | tf_op jit(solution)/shard_map/ppermute | solution.py:26
  84.4 21.1 %collective-permute-start.15 = (bf16[4,40,1024]{2,1,0:T(8,128)(2,1)S(1)}, bf16[4,40,1024]{2,1,0:T(8,128)(2,1)}, u32[]{:S(2)}, u32[]{:S(2)}) collective-permute-start(bf16[4,40,1024]{2,1,0:T(8,128)(2,1)S(1)} %bitcast.86), channel_id=1, source_target_pairs={{0,2},{1,3},{2,0},{3,1},{4,6},{5,7},{6,4},{7,5},{8,10},{9,11},{10,... | collective-permute-start | bytes 983048 | tf_op jit(solution)/shard_map/ppermute | solution.py:26
  86.0 19.5 %collective-permute-start.16 = (bf16[4,40,1024]{2,1,0:T(8,128)(2,1)S(1)}, bf16[4,40,1024]{2,1,0:T(8,128)(2,1)S(1)}, u32[]{:S(2)}, u32[]{:S(2)}) collective-permute-start(bf16[4,40,1024]{2,1,0:T(8,128)(2,1)S(1)} %bitcast.87), channel_id=1, source_target_pairs={{0,4},{1,5},{2,6},{3,7},{4,0},{5,1},{6,2},{7,3},{8,12},{9,13},{10,... | collective-permute-start | bytes 983048 | tf_op jit(solution)/shard_map/ppermute | solution.py:26
  114.3 35.3 %collective-permute-start.19 = (bf16[16,40,1024]{2,1,0:T(8,128)(2,1)}, bf16[16,40,1024]{2,1,0:T(8,128)(2,1)}, u32[]{:S(2)}, u32[]{:S(2)}) collective-permute-start(bf16[16,40,1024]{2,1,0:T(8,128)(2,1)} %bitcast.84), channel_id=1, source_target_pairs={{0,1},{1,0},{2,3},{3,2},{4,5},{5,4},{6,7},{7,6},{8,9},{9,8},{10,11... | collective-permute-start | bytes 3932168 | tf_op jit(solution)/shard_map/ppermute | solution.py:26
  125.2 24.5 %all-to-all-start.1 = ((bf16[32,8,768]{2,1,0:T(8,128)(2,1)}), bf16[32,8,768]{2,1,0:T(8,128)(2,1)S(1)}, u32[]{:S(2)}, u32[]{:S(2)}) async-start(bf16[32,8,768]{2,1,0:T(8,128)(2,1)} %broadcast_in_dim.62), calls=%async_computation.1 | async-start | bytes 786432 | tf_op jit(solution)/shard_map/all_to_all | solution.py:46
  175.1 15.4 %collective-permute-start.22 = (bf16[192,1536]{1,0:T(8,128)(2,1)S(1)}, bf16[192,1536]{1,0:T(8,128)(2,1)S(1)}, u32[]{:S(2)}, u32[]{:S(2)}) collective-permute-start(bf16[192,1536]{1,0:T(8,128)(2,1)S(1)} %get-tuple-element.153.refs_1_), channel_id=1, source_target_pairs={{0,2},{1,3},{2,0},{3,1},{4,6},{5,7},{6,4},{7,5},{8,10},{9,11},{10,... | collective-permute-start | bytes 1769480 | tf_op jit(solution)/shard_map/ppermute | solution.py:26
  176.2 15.1 %collective-permute-start.23 = (bf16[192,1536]{1,0:T(8,128)(2,1)S(1)}, bf16[192,1536]{1,0:T(8,128)(2,1)S(1)}, u32[]{:S(2)}, u32[]{:S(2)}) collective-permute-start(bf16[192,1536]{1,0:T(8,128)(2,1)S(1)} %get-tuple-element.155.refs_3_), channel_id=1, source_target_pairs={{0,4},{1,5},{2,6},{3,7},{4,0},{5,1},{6,2},{7,3},{8,12},{9,13},{10,... | collective-permute-start | bytes 1769480 | tf_op jit(solution)/shard_map/ppermute | solution.py:26
  197.0 12.2 %collective-permute-start.26 = (bf16[384,1536]{1,0:T(8,128)(2,1)S(1)}, bf16[384,1536]{1,0:T(8,128)(2,1)S(1)}, u32[]{:S(2)}, u32[]{:S(2)}) collective-permute-start(bf16[384,1536]{1,0:T(8,128)(2,1)S(1)} %get-tuple-element.171), channel_id=1, source_target_pairs={{0,1},{1,0},{2,3},{3,2},{4,5},{5,4},{6,7},{7,6},{8,9},{9,8},{10,11... | collective-permute-start | bytes 3538952 | tf_op jit(solution)/shard_map/ppermute | solution.py:26
  212.5 25.5 %collective-permute-start.28 = (bf16[192,1536]{1,0:T(8,128)(2,1)}, bf16[192,1536]{1,0:T(8,128)(2,1)}, u32[]{:S(2)}, u32[]{:S(2)}) collective-permute-start(bf16[192,1536]{1,0:T(8,128)(2,1)} %get-tuple-element.180), channel_id=1, source_target_pairs={{0,2},{1,3},{2,0},{3,1},{4,6},{5,7},{6,4},{7,5},{8,10},{9,11},{10,... | collective-permute-start | bytes 1769480 | tf_op jit(solution)/shard_map/ppermute | solution.py:26
  213.0 24.9 %collective-permute-start.29 = (bf16[192,1536]{1,0:T(8,128)(2,1)}, bf16[192,1536]{1,0:T(8,128)(2,1)}, u32[]{:S(2)}, u32[]{:S(2)}) collective-permute-start(bf16[192,1536]{1,0:T(8,128)(2,1)} %get-tuple-element.182), channel_id=1, source_target_pairs={{0,4},{1,5},{2,6},{3,7},{4,0},{5,1},{6,2},{7,3},{8,12},{9,13},{10,... | collective-permute-start | bytes 1769480 | tf_op jit(solution)/shard_map/ppermute | solution.py:26
  214.8 17.8 %all-to-all-start.2 = ((bf16[32,1,4,768]{3,2,1,0:T(4,128)(2,1)}), bf16[32,1,4,768]{3,2,1,0:T(4,128)(2,1)}, u32[]{:S(2)}, u32[]{:S(2)}) async-start(bf16[32,1,4,768]{3,2,1,0:T(4,128)(2,1)} %broadcast_in_dim.63), calls=%async_computation.2 | async-start | bytes 393216 | tf_op jit(solution)/shard_map/all_to_all | solution.py:46
  220.0 13.5 %collective-permute-start.30 = (bf16[24,3072]{1,0:T(8,128)(2,1)}, bf16[24,3072]{1,0:T(8,128)(2,1)}, u32[]{:S(2)}, u32[]{:S(2)}) collective-permute-start(bf16[24,3072]{1,0:T(8,128)(2,1)} %copy-done.21), channel_id=1, source_target_pairs={{0,8},{1,9},{2,10},{3,11},{4,12},{5,13},{6,14},{7,15},{8,0},{9,1},... | collective-permute-start | bytes 442376 | tf_op jit(solution)/shard_map/ppermute | solution.py:26
  221.8 16.2 %collective-permute-start.31 = (bf16[24,3072]{1,0:T(8,128)(2,1)}, bf16[24,3072]{1,0:T(8,128)(2,1)}, u32[]{:S(2)}, u32[]{:S(2)}) collective-permute-start(bf16[24,3072]{1,0:T(8,128)(2,1)} %copy-done.20), channel_id=1, source_target_pairs={{0,16},{1,17},{2,18},{3,19},{4,20},{5,21},{6,22},{7,23},{8,24},{9,... | collective-permute-start | bytes 442376 | tf_op jit(solution)/shard_map/ppermute | solution.py:26
  224.2 13.7 %collective-permute-start.32 = (bf16[24,3072]{1,0:T(8,128)(2,1)S(1)}, bf16[24,3072]{1,0:T(8,128)(2,1)}, u32[]{:S(2)}, u32[]{:S(2)}) collective-permute-start(bf16[24,3072]{1,0:T(8,128)(2,1)S(1)} %get-tuple-element.189), channel_id=1, source_target_pairs={{0,24},{1,25},{2,26},{3,27},{4,28},{5,29},{6,30},{7,31},{8,16},{9,... | collective-permute-start | bytes 442376 | tf_op jit(solution)/shard_map/ppermute | solution.py:26
  254.9 12.7 %collective-permute-start.36 = (bf16[24,3072]{1,0:T(8,128)(2,1)S(1)}, bf16[24,3072]{1,0:T(8,128)(2,1)S(1)}, u32[]{:S(2)}, u32[]{:S(2)}) collective-permute-start(bf16[24,3072]{1,0:T(8,128)(2,1)S(1)} %get-tuple-element.201), channel_id=1, source_target_pairs={{0,16},{1,17},{2,18},{3,19},{4,20},{5,21},{6,22},{7,23},{8,24},{9,... | collective-permute-start | bytes 442376 | tf_op jit(solution)/shard_map/ppermute | solution.py:26
  255.2 12.4 %collective-permute-start.37 = (bf16[24,3072]{1,0:T(8,128)(2,1)S(1)}, bf16[24,3072]{1,0:T(8,128)(2,1)S(1)}, u32[]{:S(2)}, u32[]{:S(2)}) collective-permute-start(bf16[24,3072]{1,0:T(8,128)(2,1)S(1)} %get-tuple-element.202), channel_id=1, source_target_pairs={{0,24},{1,25},{2,26},{3,27},{4,28},{5,29},{6,30},{7,31},{8,16},{9,... | collective-permute-start | bytes 442376 | tf_op jit(solution)/shard_map/ppermute | solution.py:26
  (69 other events, 390.4 us)
Sparse Core Ops, SparseCore 0:
  11.6 99.8 all-gather.1

commit v4 on v3

--- a/solution.py
+++ b/solution.py
@@ -60,13 +60,17 @@
     peers = lax.axis_size(AXIS)
     own = lax.axis_index(AXIS)
     per = D // peers
-    places = lax.iota(jnp.int32, D)
+    places = lax.broadcasted_iota(jnp.int32, (D, 1), 0)
     block = places // per
     target = jnp.zeros_like(block) + own
     for k, mask in enumerate(bits):
         target = target ^ (((block >> (len(bits) - 1 - k)) & 1) * mask)
-    source = target * per + places % per
-    return (source[:, None] == lax.iota(jnp.int32, D)[None, :]).astype(bf16)
+    return target * per + places % per
+
+
+def chosen(source):
+    column = lax.broadcasted_iota(jnp.int32, (source.shape[0], D), 1)
+    return jnp.where(column == source, 1.0, 0.0).astype(bf16)
 
 
 def gathered_line(shard):
@@ -80,10 +84,6 @@
 
 def in_turn(first, then):
     return lax.optimization_barrier((first, then))
-
-
-def placed(order, values):
-    return mul_bt(order, values).astype(bf16)
 
 
 def hand_on(parts, stage):
@@ -182,9 +182,9 @@
     return parts, sums
 
 
-def fold_kernel(keep_a, got_a, keep_b, got_b, *refs):
-    outs = refs[-4:]
-    half, tile = outs[0].shape[0], 256
+def fold_kernel(extra, keep_a, got_a, keep_b, got_b, *refs):
+    outs = refs[-5:] if extra else refs[-4:]
+    rows, half, tile = keep_a.shape[0], keep_a.shape[0] // 2, 256
 
     @pl.loop(0, keep_a.shape[1] // tile)
     def _(step):
@@ -193,10 +193,16 @@
             for j in range(2):
                 at = slice(j * half, (j + 1) * half)
                 total = kept[at, cols].astype(f32) + got[at, cols].astype(f32)
-                outs[2 * k + j][:, cols] = total.astype(bf16)
-
-
-def fold(parts, after=()):
+                outs[2 * k + j][:half, cols] = total.astype(bf16)
+
+    if extra:
+        came = refs[1][...] if extra > 1 else got_a[rows : rows + 16, :].astype(f32)[:8]
+        sums = refs[0][...] + came
+        outs[4][...] = sums
+        outs[1][half : half + 16, :] = jnp.concatenate([sums, sums], axis=0).astype(bf16)
+
+
+def fold(parts, after=(), sums=()):
     rows, cols = parts[0].shape
     if rows % 32:
         whole = [
@@ -204,46 +210,56 @@
             for kept, got in (parts[:2], parts[2:])
         ]
         return [part for one in whole for part in (one[: rows // 2], one[rows // 2 :])]
-    return pl.pallas_call(
-        fold_kernel,
-        out_shape=[stays((rows // 2, cols), bf16)] * 4,
-        in_specs=in_vmem(4) + anywhere(after),
-        out_specs=in_vmem(4),
+    half = (rows // 2, cols)
+    shapes = [stays(half, bf16)] * 4
+    if sums:
+        shapes[1] = stays((rows // 2 + 16, cols), bf16)
+        shapes.append(stays((8, cols), f32))
+    return pl.pallas_call(
+        functools.partial(fold_kernel, len(sums)),
+        out_shape=shapes,
+        in_specs=in_vmem(4 + len(sums)) + anywhere(after),
+        out_specs=in_vmem(len(shapes)),
         compiler_params=params(8 << 20),
         cost_estimate=cost(2 * rows * cols, 12 * rows * cols),
         name="fold",
-    )(*parts, *after)
-
-
-def fold_last_kernel(keep_a, got_a, keep_b, got_b, *refs):
-    own_ref, *outs = refs[-4:]
-    rows = own_ref.shape[0]
+    )(*parts, *sums, *after)
+
+
+def fold_last_kernel(extra, keep_a, got_a, keep_b, got_b, *refs):
+    outs = refs[-4:]
     cols = keep_a.shape[1]
+    rows = keep_a.shape[0] // 4
+    if extra:
+        sums = refs[0][...] + got_a[4 * rows : 4 * rows + 16, :].astype(f32)[:8]
     for k, (kept, got) in enumerate(((keep_a, got_a), (keep_b, got_b))):
-        total = kept[...].astype(f32) + got[...].astype(f32)
+        total = kept[...].astype(f32) + got[: 4 * rows, :].astype(f32)
         at = slice(k * cols, (k + 1) * cols)
-        own_ref[:, at] = total[:rows]
         for j, out in enumerate(outs):
-            out[:, at] = total[(j + 1) * rows : (j + 2) * rows].astype(bf16)
-
-
-def fold_last(parts, after=()):
+            part = total[j * rows : (j + 1) * rows]
+            if extra:
+                row = jnp.broadcast_to(sums[k : k + 1], (8, cols))
+                part = jnp.concatenate([part, row], axis=0)
+            out[:, at] = part.astype(out.dtype)
+
+
+def fold_last(parts, after=(), sums=()):
     rows, cols = parts[0].shape
-    shape = (rows // 4, 2 * cols)
+    shape = (rows // 4 + (8 if sums else 0), 2 * cols)
     if rows % 32:
         pairs = (parts[:2], parts[2:])
         both = [kept.astype(f32) + got.astype(f32) for kept, got in pairs]
         own, *others = jnp.split(jnp.concatenate(both, axis=1), 4)
         return [own] + [other.astype(bf16) for other in others]
     return pl.pallas_call(
-        fold_last_kernel,
+        functools.partial(fold_last_kernel, len(sums)),
         out_shape=[stays(shape, f32)] + [stays(shape, bf16)] * 3,
-        in_specs=in_vmem(4) + anywhere(after),
+        in_specs=in_vmem(4 + len(sums)) + anywhere(after),
         out_specs=in_vmem(4),
         compiler_params=params(8 << 20),
         cost_estimate=cost(2 * rows * cols, 12 * rows * cols),
         name="fold_last",
-    )(*parts, *after)
+    )(*parts, *sums, *after)
 
 
 def anywhere(after):
@@ -253,6 +269,10 @@
 def pair_cols(part, pair):
     start = part * D + pair * 2 * HEAD
     return slice(start, start + 2 * HEAD)
+
+
+def line(ref):
+    return ref[...].astype(f32).reshape(1, -1)
 
 
 def norm_rows(src, dst, gain, bias, step_rows):
@@ -293,7 +313,7 @@
     h2_ref, sum_ref, lse_ref
 ):
     rows, chunk = x_ref.shape[0], 128
-    norm_rows(x_ref, h1_ref, g1_ref[...], b1_ref[...], chunk)
+    norm_rows(x_ref, h1_ref, line(g1_ref), line(b1_ref), chunk)
 
     @pl.loop(0, 3 * D // 256)
     def _(step):
@@ -316,7 +336,7 @@
         at = pl.ds(pl.multiple_of(step * 256, 256), 256)
         mid_ref[:, at] = x_ref[:, at].astype(f32) + mul(att_ref[...], wo_ref[:, at])
 
-    norm_rows(mid_ref, h2_ref, g2_ref[...], b2_ref[...], chunk)
+    norm_rows(mid_ref, h2_ref, line(g2_ref), line(b2_ref), chunk)
     per = chunk // TXT_LEN
 
     @pl.loop(0, rows // chunk)
@@ -344,11 +364,11 @@
         compiler_params=params(),
         cost_estimate=cost(rows * D * D * 8, 14 * D * rows + 8 * D * D, rows * 128 * HEADS),
         name="text_front",
-    )(rows_in, gain1[None], bias1[None], wqkv, wo, gain2[None], bias2[None])
+    )(rows_in, gain1, bias1, wqkv, wo, gain2, bias2)
 
 
 def image_front_kernel(
-    windows, x_ref, perm_ref, g1_ref, b1_ref, g2_ref, b2_ref, *refs
+    windows, x_ref, order_ref, g1_ref, b1_ref, g2_ref, b2_ref, *refs
 ):
     h2_ref, sum_ref, w_ref, h1_ref, placed_ref, qkv_ref, att_ref, mid_ref, sems = refs[-9:]
     rows, chunk = x_ref.shape[0], 80
@@ -364,9 +384,9 @@
         @pl.loop(0, D // 256)
         def _(step):
             at = pl.ds(pl.multiple_of(step * 256, 256), 256)
-            dst[:, at] = mul_bt(src[...], perm_ref[at, :]).astype(bf16)
-
-    norm_rows(x_ref, h1_ref, g1_ref[...].astype(f32), b1_ref[...].astype(f32), chunk)
+            dst[:, at] = mul_bt(src[...], chosen(order_ref[at, :])).astype(bf16)
+
+    norm_rows(x_ref, h1_ref, line(g1_ref), line(b1_ref), chunk)
     place_columns(h1_ref, placed_ref)
     for copy in copies:
         copy.wait()
@@ -388,7 +408,7 @@
         there = pl.ds(pl.multiple_of(step * 256 + 3 * D, 256), 256)
         mid_ref[:, at] = x_ref[:, at].astype(f32) + mul(placed_ref[...], w_ref[:, there])
 
-    norm_rows(mid_ref, h2_ref, g2_ref[...].astype(f32), b2_ref[...].astype(f32), chunk)
+    norm_rows(mid_ref, h2_ref, line(g2_ref), line(b2_ref), chunk)
     for k in range(rows // IMG_LEN):
         first, last = k * IMG_LEN, (k + 1) * IMG_LEN
         start, end = first // 8 * 8, -(-last // 8) * 8
@@ -398,7 +418,7 @@
         sum_ref[k : k + 1, :] = jnp.sum(jnp.where(inside, values, 0.0), axis=0, keepdims=True)
 
 
-def image_front(rows_in, pieces, perm, gain1, bias1, gain2, bias2):
+def image_front(rows_in, pieces, source, gain1, bias1, gain2, bias2):
     rows = rows_in.shape[0]
     windows = ((0, 208, 0, 256), (208, 192, 192, 208))
     vmem = pl.BlockSpec(memory_space=pltpu.VMEM)
@@ -422,7 +442,7 @@
         compiler_params=params(),
         cost_estimate=cost(rows * D * D * 12, 8 * D * D, rows * 256 * HEADS),
         name="image_front",
-    )(rows_in, perm, gain1[None], bias1[None], gain2[None], bias2[None], *pieces)
+    )(rows_in, source, gain1, bias1, gain2, bias2, *pieces)
 
 
 def gelu_parts(inner):
@@ -584,46 +604,30 @@
     )(normed2, whole, whole, middle_sum, *after)
 
 
-def left_kernel(order_ref, h2_ref, h1_ref, att_ref, up_ref, rest_ref):
-    step = pl.program_id(0)
-
-    @pl.when(step < 2)
-    def _():
-        up_ref[0] = placed(order_ref[0], h2_ref[...])
-
-    @pl.when((step == 2) | (step == 3))
-    def _():
-        rest_ref[0] = placed(order_ref[0], h1_ref[...])
-
-    @pl.when(step == 4)
-    def _():
-        rest_ref[0] = placed(order_ref[0], att_ref[...])
-
-
-def left_factors(orders, normed2, normed1, attended):
-    rows = normed1.shape[0]
-    fixed = pl.BlockSpec((rows, D), lambda i: (0, 0))
-    return pl.pallas_call(
-        left_kernel,
-        grid=(5,),
-        out_shape=[
-            jax.ShapeDtypeStruct((2, D, rows), bf16),
-            jax.ShapeDtypeStruct((3, D, rows), bf16),
-        ],
-        in_specs=[
-            pl.BlockSpec((1, D, D), lambda i: (jnp.minimum(i % 2 + i // 4, 1), 0, 0)),
-            fixed,
-            fixed,
-            fixed,
-        ],
-        out_specs=[
-            pl.BlockSpec((1, D, rows), lambda i: (jnp.minimum(i, 1), 0, 0)),
-            pl.BlockSpec((1, D, rows), lambda i: (jnp.maximum(i - 2, 0), 0, 0)),
-        ],
+def left_kernel(count, *refs):
+    out_ref = refs[-1]
+    for k in range(count):
+        source_ref, values_ref = refs[2 * k : 2 * k + 2]
+
+        @pl.loop(0, D // 256)
+        def _(step, k=k, source_ref=source_ref, values_ref=values_ref):
+            at = pl.ds(pl.multiple_of(step * 256, 256), 256)
+            picked = mul_bt(chosen(source_ref[at, :]), values_ref[...])
+            out_ref[k, at, :] = picked.astype(bf16)
+
+
+def left_factors(*pairs):
+    rows = pairs[0][1].shape[0]
+    given = [item for pair in pairs for item in pair]
+    return pl.pallas_call(
+        functools.partial(left_kernel, len(pairs)),
+        out_shape=jax.ShapeDtypeStruct((len(pairs), D, rows), bf16),
+        in_specs=in_vmem(len(given)),
+        out_specs=pl.BlockSpec(memory_space=pltpu.VMEM),
         compiler_params=params(24 << 20),
-        cost_estimate=cost(10 * rows * D * D, 16 * rows * D + 10 * D * D),
+        cost_estimate=cost(2 * len(pairs) * rows * D * D, 4 * len(pairs) * rows * D),
         name="left_factors",
-    )(orders, normed2, normed1, attended)
+    )(*given)
 
 
 def loss_parts(text_rows, pos, image_all):
@@ -750,7 +754,7 @@
 
 def mlp_back_kernel(
     low_ref, wd_ref, slope_ref, wu_ref, lhs_ref, mid_ref, gain_ref, row_ref, keep_a, send_a, keep_b,
-    send_b, out_ref, gain_out, bias_out
+    send_b, out_ref, sums_out
 ):
     count, rows = low_ref.shape[0], slope_ref.shape[0]
     half, steps = D // 2, FF // 2 // TILE
@@ -781,17 +785,16 @@
 
     chunk = 128
     per = chunk // TXT_LEN
-    gain = gain_ref[...]
-    gain_out[...] = jnp.zeros_like(gain_out)
-    bias_out[...] = jnp.zeros_like(bias_out)
+    gain = line(gain_ref)
+    sums_out[...] = jnp.zeros_like(sums_out)
 
     @pl.loop(0, rows // chunk)
     def _(k):
         at = pl.ds(pl.multiple_of(k * chunk, chunk), chunk)
         unit, scale = norm_parts(mid_ref[at, :])
         grad = out_ref[at, :]
-        gain_out[...] += jnp.sum(grad * unit, axis=0, keepdims=True)
-        bias_out[...] += jnp.sum(grad, axis=0, keepdims=True)
+        sums_out[:, :D] += jnp.sum(grad * unit, axis=0, keepdims=True)
+        sums_out[:, D:] += jnp.sum(grad, axis=0, keepdims=True)
         row = row_ref[pl.ds(pl.multiple_of(k * per, per), per), :]
         row = jnp.broadcast_to(row[:, None, :], (per, TXT_LEN, D)).reshape(chunk, D)
         out_ref[at, :] = row + norm_back(unit, scale, gain, grad)
@@ -799,16 +802,16 @@
 
 def mlp_back(grad_row, grad_low, weight_down, slope, weight_up, lhs, middle, gain):
     rows = slope.shape[0]
-    line = jax.ShapeDtypeStruct((1, D), f32)
     return pl.pallas_call(
         mlp_back_kernel,
-        out_shape=[stays((D // 2, FF // 2), bf16)] * 4 + [stays((rows, D), f32), line, line],
+        out_shape=[stays((D // 2, FF // 2), bf16)] * 4
+        + [stays((rows, D), f32), stays((1, 2 * D), f32)],
         in_specs=in_vmem(8),
-        out_specs=in_vmem(7),
+        out_specs=in_vmem(6),
         compiler_params=params(16 << 20),
         cost_estimate=cost(4 * rows * D * FF, 4 * D * FF + 2 * rows * FF + 2 * D * FF, rows * FF),
         name="mlp_back",
-    )(grad_low, weight_down, slope, weight_up, lhs, middle, gain[None], grad_row)
+    )(grad_low, weight_down, slope, weight_up, lhs, middle, gain, grad_row)
 
 
 def attention_back_kernel(first, grad_ref, wo_ref, qkv_ref, lse_ref, *refs):
@@ -895,8 +898,8 @@
 
 def input_back_kernel(count, *refs):
     projs = refs[:count]
-    w_ref, x_ref, gain_ref, mid_ref = refs[count : count + 4]
-    out_ref, gain_out, bias_out = refs[-3:]
+    w_ref, x_ref, gain_ref, mid_ref, sums_ref = refs[count : count + 5]
+    out_ref, sums_out = refs[-2:]
     rows, chunk = x_ref.shape[0], 128
 
     @pl.loop(0, D // 256)
@@ -908,32 +911,31 @@
             out_ref[there, at] = mul_bt(part[...], w_ref[at, :])
             row += part.shape[0]
 
-    gain = gain_ref[...]
-    gain_out[...] = jnp.zeros_like(gain_out)
-    bias_out[...] = jnp.zeros_like(bias_out)
+    gain = line(gain_ref)
+    sums_out[...] = jnp.zeros_like(sums_out)
+    sums_out[1:2, :] = sums_ref[...]
 
     @pl.loop(0, rows // chunk)
     def _(k):
         at = pl.ds(pl.multiple_of(k * chunk, chunk), chunk)
         unit, scale = norm_parts(x_ref[at, :].astype(f32))
         grad = out_ref[at, :]
-        gain_out[...] += jnp.sum(grad * unit, axis=0, keepdims=True)
-        bias_out[...] += jnp.sum(grad, axis=0, keepdims=True)
+        sums_out[0:1, :D] += jnp.sum(grad * unit, axis=0, keepdims=True)
+        sums_out[0:1, D:] += jnp.sum(grad, axis=0, keepdims=True)
         out_ref[at, :] = mid_ref[at, :] + norm_back(unit, scale, gain, grad)
 
 
-def input_back(grad_projs, weight, rows_in, gain, grad_middle, after=()):
+def input_back(grad_projs, weight, rows_in, gain, grad_middle, sums, after=()):
     rows = rows_in.shape[0]
-    line = jax.ShapeDtypeStruct((1, D), f32)
     return pl.pallas_call(
         functools.partial(input_back_kernel, len(grad_projs)),
-        out_shape=[jax.ShapeDtypeStruct((rows, D), f32), line, line],
-        in_specs=in_vmem(len(grad_projs) + 4) + anywhere(after),
-        out_specs=in_vmem(3),
+        out_shape=[jax.ShapeDtypeStruct((rows, D), f32), stays((8, 2 * D), f32)],
+        in_specs=in_vmem(len(grad_projs) + 5) + anywhere(after),
+        out_specs=in_vmem(2),
         compiler_params=params(16 << 20),
         cost_estimate=cost(6 * rows * D * D, 14 * rows * D + 6 * D * D),
         name="input_back",
-    )(*grad_projs, weight, rows_in, gain[None], grad_middle, *after)
+    )(*grad_projs, weight, rows_in, gain, grad_middle, sums, *after)
 
 
 def local(
@@ -974,9 +976,9 @@
     small = peers == 32
     shard = jnp.concatenate([img_qkv.reshape(per, 3 * D), img_out.reshape(per, D)], axis=1)
     if small:
-        line, perm = gathered_line(shard), row_order((1, 4, 2, 16, 8))
+        line, source = gathered_line(shard), row_order((1, 4, 2, 16, 8))
     else:
-        line, perm = lax.all_gather(shard, AXIS, axis=0, tiled=True), jnp.eye(D, dtype=bf16)
+        line, source = lax.all_gather(shard, AXIS, axis=0, tiled=True), row_order(())
 
     normed1, project, attended, middle, normed2, middle_sum, log_sums = text_front(
         captions, txt_gain1, txt_bias1, txt_qkv, txt_out, txt_gain2, txt_bias2
@@ -996,7 +998,11 @@
     columns = lax.iota(jnp.int32, total_images)
     positive = ((matches > 0) | (owner[:, None] == columns[None, :])) & live[:, None]
 
+    order_a, order_b, tail = stage_orders()
+    source_a, source_b = row_order(order_a + tail[::-1]), row_order(order_b + tail[::-1])
     own_pack = packed(text_unit, positive.astype(bf16), ())
+    own_pack, hidden_sum, normed2 = lax.optimization_barrier((own_pack, hidden_sum, normed2))
+    lhs_up = left_factors((source_a, normed2), (source_b, normed2))
     pieces = [line]
     if small:
         held = own_pack[None]
@@ -1004,8 +1010,8 @@
         others = [swapped(held, mask) for mask in (8, 16, 24)]
         scaled_sum = (hidden_sum * inverse[:, :1]).astype(bf16)
         hidden_cols = lax.all_to_all(scaled_sum, AXIS, split_axis=1, concat_axis=0, tiled=True)
-        others, first, second, hidden_cols = lax.optimization_barrier(
-            (others, first, second, hidden_cols)
+        others, first, second, hidden_cols, lhs_up = lax.optimization_barrier(
+            (others, first, second, hidden_cols, lhs_up)
         )
         held = joined(joined(held, others[0], 8), joined(others[1], others[2], 8), 16, 1)
         text_beside, text_above = swapped(held, 2), swapped(held, 4)
@@ -1013,7 +1019,7 @@
         pieces = pieces + [swapped(piece, 1) for piece in pieces]
 
     normed_img, middle_img = image_front(
-        images, pieces, perm, img_gain1, img_bias1, img_gain2, img_bias2
+        images, pieces, source, img_gain1, img_bias1, img_gain2, img_bias2
     )
     if small:
         normed_img, text_beside, text_above = lax.optimization_barrier(
@@ -1022,18 +1028,15 @@
         across = jnp.concatenate(diagonal(text_beside, text_above), axis=0)
         held = joined(joined(held, text_beside, 2), joined(text_above, across, 2), 4, 4)
 
-    order_a, order_b, tail = stage_orders()
-    orders = jnp.stack([row_order(order_a + tail[::-1]), row_order(order_b + tail[::-1])])
     if small:
-        whole, held, orders = lax.optimization_barrier((whole, held, orders))
+        whole, held = in_turn(whole, held)
         other = swapped(held, 1)
     image_low = image_up(normed_img, whole, 0, FF, middle_img)
     if small:
         text_pack = joined(held, other, 1).reshape(-1, D + total_images)
-    image_low, normed2 = in_turn(image_low, normed2)
     image_all = spread(image_low).reshape(total_images, D)
-    lhs_up, lhs_rest = left_factors(orders, normed2, normed1, attended)
-    image_all, lhs_up = in_turn(image_all, lhs_up)
+    if small:
+        image_all, text_pack = in_turn(image_all, text_pack)
 
     if small:
         loss_value, grad_row, row_low, col_sum, col_count, live_total = loss_and_rows(
@@ -1048,7 +1051,7 @@
         grad_row = inverse[:, :1] * turned(grad, text_unit) * (1.0 / TXT_LEN)
         row_low = grad_row.astype(bf16)
 
-    *up, grad_middle, gain_two, bias_two = mlp_back(
+    *up, grad_middle, sums = mlp_back(
         grad_row, row_low, txt_down, slope, txt_up, lhs_up, middle, txt_gain2
     )
     stages = len(order_a)
@@ -1056,20 +1059,24 @@
     for stage in range(stages - 2):
         up = fold(hand_on(up, stage), (proj_one,))
     low_two, proj_two = attention_back(grad_middle, txt_out, project, log_sums, 1, 4, up)
-    up = fold(hand_on(up, stages - 2), (proj_two,))
+    proj_two, normed1 = in_turn(proj_two, normed1)
+    lhs_rest = left_factors((source_a, normed1), (source_b, normed1), (source_b, attended))
+    up = fold(hand_on(up, stages - 2), (proj_two, lhs_rest))
     projs, lows = (proj_one, proj_two), (low_one, low_two)
     rest = weight_back(lhs_rest, [projs, lows], [(0, 0, 0), (0, 0, 1), (1, 0, 2), (2, 1, 0)], up)
     up = hand_on(up, stages - 1)
-    caption_grad, gain_one, bias_one = input_back(
-        projs, txt_qkv, captions, txt_gain1, grad_middle, rest[:1]
+    caption_grad, sums = input_back(
+        projs, txt_qkv, captions, txt_gain1, grad_middle, sums, rest[:1]
     )
     caption_grad, up = in_turn(caption_grad, up)
     up = fold_last(up)
-    for stage in range(stages - 2):
-        rest = fold(hand_on(rest, stage), up[:1])
+    if small:
+        *rest, sums = fold(hand_on(rest, 0), up[:1], (sums, swapped(sums, 1)))
+    else:
+        norms = lax.psum(sums, AXIS)[:2].reshape(-1)
+        for stage in range(stages - 2):
+            rest = fold(hand_on(rest, stage), up[:1])
     up = hand_on_last(up)
-    norms = jnp.concatenate([gain_one, bias_one, gain_two, bias_two], axis=0)
-    norms = jnp.sum(spread(norms[None].astype(bf16)).astype(f32), axis=0).reshape(4, D)
     rest = hand_on(rest, stages - 2)
     if small:
         grad_down = grad_of_down(
@@ -1079,20 +1086,26 @@
         grad_down = lax.psum_scatter(
             mul_at(hidden_sum.astype(bf16), row_low), AXIS, scatter_dimension=0, tiled=True
         )
-    grad_down, rest, norms, up = lax.optimization_barrier((grad_down, rest, norms, up))
-    rest = fold(rest)
-    rest = hand_on_last(fold_last(hand_on(rest, stages - 1)))
+    grad_down, rest, up = lax.optimization_barrier((grad_down, rest, up))
+    if small:
+        *rest, sums = fold(rest, (), (sums,))
+        rest = fold_last(hand_on(rest, stages - 1), (), (sums,))
+    else:
+        rest = fold_last(hand_on(fold(rest), stages - 1))
     up_share = sum_last(*up)
-    rest_share = sum_last(*rest)
+    rest_share = sum_last(*hand_on_last(rest))
+    if small:
+        norms = rest_share[per]
+        rest_share = rest_share[:per]
     return (
         loss_value,
         caption_grad,
-        norms[0],
-        norms[1],
+        norms[:D],
+        norms[D : 2 * D],
         rest_share[:, : 3 * D].reshape(-1),
         rest_share[:, 3 * D :].reshape(-1),
-        norms[2],
-        norms[3],
+        norms[2 * D : 3 * D],
+        norms[3 * D :],
         up_share.reshape(-1),
         grad_down.reshape(-1),
     )

time: 277 us -> 269 us (0.971)
  waiting for transfers between devices: 37.5 us -> 61.3 us
  local copies, waits for them, and re-layouts: 37.7 us -> 22.5 us
  starting transfers between devices: 63.9 us -> 54.3 us
  other arithmetic: 15.4 us -> 7.21 us
    all_to_all x2 -> x1, waiting for transfers between devices: 0.57 us -> 12.5 us  [spread(): return lax.all_to_all(copies, AXIS, split_axis=0, concat_axis=0, tiled=True)]
    ppermute x38 -> x39, waiting for transfers between devices: 36.9 us -> 48.7 us  [swapped(): return lax.ppermute(value, AXIS, [(i, i ^ mask) for i in range(peers)])]
    all_to_all x2 -> x1, starting transfers between devices: 16.7 us -> 7.37 us  [spread(): return lax.all_to_all(copies, AXIS, split_axis=0, concat_axis=0, tiled=True)]
    unnamed x105 -> x65, local copies, waits for them, and re-layouts: 20 us -> 11.3 us
    broadcast_in_dim x8 -> x0, local copies, waits for them, and re-layouts: 4.67 us -> none  [the longest x1 0.6 us: image_front(): gain2[None]]
    another operation x7, other arithmetic: 4.47 us -> 1.61 us  [joined(): return jnp.stack(parts, axis=1).reshape((-1,) + held.shape[1:])]
    ppermute x38 -> x39, starting transfers between devices: 42.8 us -> 41 us  [swapped(): return lax.ppermute(value, AXIS, [(i, i ^ mask) for i in range(peers)])]
    pallas_call x7 -> x8, Pallas kernels: 10.2 us -> 10.2 us  [the longest x2 7.98 us: left_factors(): pl.pallas_call(functools.partial(left_kernel, len(pairs)), out_shape=jax....]
  transfers between devices with their start and end apart: 42 -> 42, of which waited for: 14 -> 14; matrix products, arithmetic and copies ran while one was open for 10% -> 5% of each run, Pallas kernels for 31% -> 33%
where the time goes in v4:
time: 269 us; the launch traced here: 267 us
  Pallas kernels  107 us (40%)
  waiting for transfers between devices  61.3 us (23%)
  starting transfers between devices  54.3 us (20%)
  local copies, waits for them, and re-layouts  22.5 us (8%)
  between operations  14.7 us (5%)
  other arithmetic  7.21 us (3%)
    ppermute x39, waiting for transfers between devices, swapped(): return lax.ppermute(value, AXIS, [(i, i ^ mask) for i in range(peers)])  48.7 us
    ppermute x39, starting transfers between devices, swapped(): return lax.ppermute(value, AXIS, [(i, i ^ mask) for i in range(peers)])  41 us
    pallas_call x1, Pallas kernels, text_front(): pl.pallas_call(text_front_kernel, out_shape=[jax.ShapeDtypeStruct(*item)...  18 us
    pallas_call x1, Pallas kernels, image_front(): pl.pallas_call(functools.partial(image_front_kernel, windows), out_shape=...  14 us
    all_to_all x1, waiting for transfers between devices, spread(): return lax.all_to_all(copies, AXIS, split_axis=0, concat_axis=0, tiled=True)  12.5 us
    pallas_call x1, Pallas kernels, mlp_back(): pl.pallas_call(mlp_back_kernel, out_shape=[stays((D // 2, FF // 2), bf16)...  12.4 us
    pallas_call x1, Pallas kernels, text_up(): pl.pallas_call(text_up_kernel, grid=(FF // TILE,), out_shape=[jax.ShapeDt...  12.3 us
    pallas_call x2, Pallas kernels, attention_back(): pl.pallas_call(functools.partial(attention_back_kernel, first), out_shape...  11.5 us
  transfers between devices with their start and end apart: 42, of which 14 were waited for; matrix products, arithmetic and copies ran while one was open for 5% of the time, Pallas kernels for 33%

profile of v4, /device:TPU:0, one launch (start us, length us, event | category | flops | bytes accessed | tf_op | source)
XLA Modules:
  0.0 267.4 jit_solution(14479813957651455639)
XLA Ops:
  10.3 5.1 %collective-permute-start.2 = (bf16[24,3072]{1,0:T(8,128)(2,1)S(1)}, bf16[24,3072]{1,0:T(8,128)(2,1)S(1)}, u32[]{:S(2)}, u32[]{:S(2)}) collective-permute-start(bf16[24,3072]{1,0:T(8,128)(2,1)S(1)} %constant_dynamic-update-slice_fusion), channel_id=1, source_target_pairs={{0,24},{1,25},{2,26},{3,27},{4,28},{5,29},{6,30},{7,31},{8,16},{9,... | collective-permute-start | bytes 442376 | tf_op jit(solution)/shard_map/ppermute | solution.py:26
  16.3 18.0 %text_front.1 = (bf16[640,768]{1,0:T(8,128)(2,1)}, bf16[640,2304]{1,0:T(8,128)(2,1)}, bf16[640,768]{1,0:T(8,128)(2,1)}, f32[640,768]{1,0:T(8,128)}, bf16[640,768...) custom-call(bf16[640,768]{1,0:T(8,128)(2,1)} %refs_3_.1, f32[768]{0:T(1024)} %refs_4_.1, f32[768]{0:T(1024)} %b1_ref.2, ...), custom_call_target="tpu_custom_call" | custom-call | flops 3019898880 | bytes 11599872 | tf_op jit(solution)/shard_map/text_front/pallas_call | solution.py:361
  40.3 12.3 %text_up.1 = (bf16[640,3072]{1,0:T(8,128)(2,1)}, f32[40,3072]{1,0:T(8,128)}, f32[40,768]{1,0:T(8,128)}, f32[40,128]{1,0:T(8,128)}) custom-call(bf16[640,768]{1,0:T(8,128)(2,1)} %get-tuple-element.121.h2_ref.refs_1_.refs_3_, bf16[768,3072]{1,0:T(8,128)(2,1)} %wu_ref.3, bf16[3072,768]{1,0:T(8,128)(2,1)} %wd_ref.3, f32[40,768]{1,0:T(8,128)} %get-tuple-element.112.sum_ref, ...), custom_call_target="tpu_custom_call" | custom-call | flops 3019898880 | bytes 13369344 | tf_op jit(solution)/shard_map/text_up/pallas_call | solution.py:520
  53.4 6.3 %collective-permute-done.3.refs_1_ = bf16[96,3072]{1,0:T(8,128)(2,1)} collective-permute-done((bf16[96,3072]{1,0:T(8,128)(2,1)}, bf16[96,3072]{1,0:T(8,128)(2,1)}, u32[]{:S(2)}, u32[]{:S(2)}) %collective-permute-start.3) | collective-permute-done | bytes 589856 | tf_op jit(solution)/shard_map/ppermute | solution.py:26
  63.6 5.9 %all-to-all-start = ((bf16[40,32,96]{2,0,1:T(8,128)(2,1)}), bf16[40,32,96]{2,0,1:T(8,128)(2,1)S(1)}, u32[]{:S(2)}, u32[]{:S(2)}) async-start(bf16[40,32,96]{2,0,1:T(8,128)(2,1)} %copy.64), calls=%async_computation | async-start | bytes 655360 | tf_op jit(solution)/shard_map/all_to_all | solution.py:1012
  77.1 2.5 collective-permute-start.6
  81.3 3.2 %left_factors.2.lhs_ref = bf16[2,768,640]{2,1,0:T(8,128)(2,1)S(1)} custom-call(s32[768,1]{1,0:T(8,128)S(1)} %fusion.8.refs_0_, bf16[640,768]{1,0:T(8,128)(2,1)S(1)} %copy-done.21, s32[768,1]{1,0:T(8,128)S(1)} %fusion.9.refs_2_.order_ref.refs_4_, bf16[640,768]{1,0:T(8,128)(2,1)S(1)} %copy-done.21), custom_call_target="tpu_custom_call" | custom-call | flops 1509949440 | bytes 3932160 | tf_op jit(solution)/shard_map/left_factors/pallas_call | solution.py:622
  85.9 10.6 %collective-permute-done.6 = bf16[1,40,1024]{2,1,0:T(8,128)(2,1)S(1)} collective-permute-done((bf16[1,40,1024]{2,1,0:T(8,128)(2,1)S(1)}, bf16[1,40,1024]{2,1,0:T(8,128)(2,1)S(1)}, u32[]{:S(2)}, u32[]{:S(2)}) %collective-permute-start.6) | collective-permute-done | bytes 81952 | tf_op jit(solution)/shard_map/ppermute | solution.py:26
  102.0 14.0 %image_front.1 = (bf16[400,768]{1,0:T(8,128)(2,1)}, f32[8,768]{1,0:T(8,128)}) custom-call(bf16[400,768]{1,0:T(8,128)(2,1)} %x_ref.3, s32[768,1]{1,0:T(8,128)} %copy-done.9, bf16[768]{0:T(1024)(128)(2,1)} %g1_ref.3, bf16[768]{0:T(1024)(128)(2,1)} %b1_ref.3, bf16[768]{0:T(1024)(128)(2,1)} %g2_ref.3, bf16[768]{0:T(1024)(128)(2,1)} %b2_ref.3, ...), custom_call_target="tpu_custom_call" | custom-call | flops 2831155200 | bytes 4718592 | tf_op jit(solution)/shard_map/image_front/pallas_call | solution.py:425
  118.0 4.1 %collective-permute-done.17 = bf16[2,40,1024]{2,1,0:T(8,128)(2,1)S(1)} collective-permute-done((bf16[2,40,1024]{2,1,0:T(8,128)(2,1)S(1)}, bf16[2,40,1024]{2,1,0:T(8,128)(2,1)S(1)}, u32[]{:S(2)}, u32[]{:S(2)}) %collective-permute-start.17) | collective-permute-done | bytes 163872 | tf_op jit(solution)/shard_map/ppermute | solution.py:26
  123.1 9.4 %image_up.1 = bf16[8,768]{1,0:T(8,128)(2,1)} custom-call(bf16[400,768]{1,0:T(8,128)(2,1)} %get-tuple-element.128.h2_ref, bf16[768,6144]{1,0:T(8,128)(2,1)} %all-gather.2.cloned.1.call-done.wu_ref.wd_ref, bf16[768,6144]{1,0:T(8,128)(2,1)} %all-gather.2.cloned.1.call-done.wu_ref.wd_ref, f32[8,768]{1,0:T(8,128)} %get-tuple-element.132.sum_ref), custom_call_target="tpu_custom_call" | custom-call | flops 1887436800 | bytes 9437184 | tf_op jit(solution)/shard_map/image_up/pallas_call | solution.py:588
  133.9 7.4 %all-to-all-start.1 = ((bf16[32,8,768]{2,1,0:T(8,128)(2,1)}), bf16[32,8,768]{2,1,0:T(8,128)(2,1)S(1)}, u32[]{:S(2)}, u32[]{:S(2)}) async-start(bf16[32,8,768]{2,1,0:T(8,128)(2,1)} %broadcast_in_dim.5), calls=%async_computation.1 | async-start | bytes 786432 | tf_op jit(solution)/shard_map/all_to_all | solution.py:46
  141.8 12.5 %all-to-all-done.1 = bf16[32,8,768]{2,1,0:T(8,128)(2,1)S(1)} async-done(((bf16[32,8,768]{2,1,0:T(8,128)(2,1)}), bf16[32,8,768]{2,1,0:T(8,128)(2,1)S(1)}, u32[]{:S(2)}, u32[]{:S(2)}) %all-to-all-start.1) | async-done | bytes 393248 | tf_op jit(solution)/shard_map/all_to_all | solution.py:46
  165.2 12.4 %mlp_back.1 = (bf16[384,1536]{1,0:T(8,128)(2,1)S(1)}, bf16[384,1536]{1,0:T(8,128)(2,1)S(1)}, bf16[384,1536]{1,0:T(8,128)(2,1)S(1)}, bf16[384,1536]{1,0:T(8,128)(...) custom-call(bf16[40,768]{1,0:T(8,128)(2,1)S(1)} %get-tuple-element.137.low_ref, ...), custom_call_target="tpu_custom_call" | custom-call | flops 6039797760 | bytes 18087936 | tf_op jit(solution)/shard_map/mlp_back/pallas_call | solution.py:805
  184.8 9.2 %attention_back.3 = (bf16[512,768]{1,0:T(8,128)(2,1)S(1)}, bf16[512,2304]{1,0:T(8,128)(2,1)S(1)}) custom-call(f32[640,768]{1,0:T(8,128)S(1)} %get-tuple-element.142.grad_ref.refs_5_, bf16[768,768]{1,0:T(8,128)(2,1)S(1)} %copy-done.3, bf16[640,2304]{1,0:T(8,128)(2,1)S(1)} %copy-done.1, f32[80,128]{1,0:T(8,128)S(1)} %copy-done.14, ...), custom_call_target="tpu_custom_call" | custom-call | flops 3019898880 | bytes 7471104 | tf_op jit(solution)/shard_map/attention_back/pallas_call | solution.py:855
  194.0 4.8 %left_factors.3.refs_1_.lhs_ref = bf16[3,768,640]{2,1,0:T(8,128)(2,1)S(1)} custom-call(s32[768,1]{1,0:T(8,128)S(1)} %copy-done.12, bf16[640,768]{1,0:T(8,128)(2,1)S(1)} %copy-done.22, s32[768,1]{1,0:T(8,128)S(1)} %copy-done.10, bf16[640,768]{1,0:T(8,128)(2,1)S(1)} %copy-done.22, s32[768,1]{1,0:T(8,128)S(1)} %copy-done.10, bf16[640,768]{1,0:T(8,128)(2,1)S(1)} %copy-done.23), custom_call_target="tpu_custom_call" | custom-call | flops 2264924160 | bytes 5898240 | tf_op jit(solution)/shard_map/left_factors/pallas_call | solution.py:622
  199.5 3.9 %weight_back.1 = (bf16[384,1536]{1,0:T(8,128)(2,1)S(1)}, bf16[384,1536]{1,0:T(8,128)(2,1)S(1)}, bf16[384,1536]{1,0:T(8,128)(2,1)S(1)}, bf16[384,1536]{1,0:T(8,128)(2,1)S(1)}) custom-call(bf16[3,768,640]{2,1,0:T(8,128)(2,1)S(1)} %left_factors.3.refs_1_.lhs_ref, bf16[128,2304]{1,0:T(8,128)(2,1)S(1)} %get-tuple-element.145.refs_0_, ...), custom_call_target="tpu_custom_call" | custom-call | flops 3019898880 | bytes 12189696 | tf_op jit(solution)/shard_map/weight_back/pallas_call | solution.py:888
  206.0 6.5 %input_back.1 = (f32[640,768]{1,0:T(8,128)}, f32[8,1536]{1,0:T(8,128)S(1)}) custom-call(bf16[128,2304]{1,0:T(8,128)(2,1)S(1)} %get-tuple-element.145.refs_0_, bf16[512,2304]{1,0:T(8,128)(2,1)S(1)} %get-tuple-element.156.refs_0_.refs_1_, bf16[768,2304]{1,0:T(8,128)(2,1)S(1)} %copy-done, bf16[640,768]{1,0:T(8,128)(2,1)S(1)} %copy-done.6, f32[768]{0:T(1024)S(1)} %copy-done.15, ...), custom_call_target="tpu_custom_call" | custom-call | flops 2264924160 | bytes 10420224 | tf_op jit(solution)/shard_map/input_back/pallas_call | solution.py:930
  218.3 2.6 collective-permute-start.33
  220.9 5.9 %grad_of_down.1 = f32[96,768]{1,0:T(8,128)S(1)} custom-call(bf16[1280,1024]{1,0:T(8,128)(2,1)S(1)} %bitcast.75, bf16[256,768]{1,0:T(8,128)(2,1)S(1)} %bitcast.77, f32[1,256]{1,0:T(1,128)S(1)} %get-tuple-element.169.col_sum_ref, f32[1,256]{1,0:T(1,128)S(1)} %get-tuple-element.170.col_count_ref, f32[1,128]{1,0:T(1,128)S(1)} %get-tuple-element.171.live_ref, ...), custom_call_target="tpu_custom_call" | custom-call | flops 1006632960 | bytes 2621440 | tf_op jit(solution)/shard_map/grad_of_down/pallas_call | solution.py:738
  226.8 4.0 %collective-permute-done.32 = bf16[24,3072]{1,0:T(8,128)(2,1)S(1)} collective-permute-done((bf16[24,3072]{1,0:T(8,128)(2,1)S(1)}, bf16[24,3072]{1,0:T(8,128)(2,1)S(1)}, u32[]{:S(2)}, u32[]{:S(2)}) %collective-permute-start.32) | collective-permute-done | bytes 147488 | tf_op jit(solution)/shard_map/ppermute | solution.py:26
  233.2 6.9 %collective-permute-done.35.got_b = bf16[96,1536]{1,0:T(8,128)(2,1)S(1)} collective-permute-done((bf16[96,1536]{1,0:T(8,128)(2,1)S(1)}, bf16[96,1536]{1,0:T(8,128)(2,1)S(1)}, u32[]{:S(2)}, u32[]{:S(2)}) %collective-permute-start.35) | collective-permute-done | bytes 294944 | tf_op jit(solution)/shard_map/ppermute | solution.py:26
  246.5 3.7 %collective-permute-done.38 = bf16[32,3072]{1,0:T(8,128)(2,1)S(1)} collective-permute-done((bf16[32,3072]{1,0:T(8,128)(2,1)S(1)}, bf16[32,3072]{1,0:T(8,128)(2,1)S(1)}, u32[]{:S(2)}, u32[]{:S(2)}) %collective-permute-start.38) | collective-permute-done | bytes 196640 | tf_op jit(solution)/shard_map/ppermute | solution.py:26
  250.2 8.3 %collective-permute-done.37 = bf16[32,3072]{1,0:T(8,128)(2,1)S(1)} collective-permute-done((bf16[32,3072]{1,0:T(8,128)(2,1)S(1)}, bf16[32,3072]{1,0:T(8,128)(2,1)S(1)}, u32[]{:S(2)}, u32[]{:S(2)}) %collective-permute-start.37) | collective-permute-done | bytes 196640 | tf_op jit(solution)/shard_map/ppermute | solution.py:26
  (191 shorter events, 73.5 us)
Async XLA Ops:
  7.2 115.8 %all-gather.2.cloned.1.call-start = ((), (), s32[]{:S(2)}) async-start(), calls=%async_computation.2 | async-start | bytes 9732096 | tf_op jit(solution)/shard_map/all_gather | solution.py:970
  10.3 25.3 %collective-permute-start.2 = (bf16[24,3072]{1,0:T(8,128)(2,1)S(1)}, bf16[24,3072]{1,0:T(8,128)(2,1)S(1)}, u32[]{:S(2)}, u32[]{:S(2)}) collective-permute-start(bf16[24,3072]{1,0:T(8,128)(2,1)S(1)} %constant_dynamic-update-slice_fusion), channel_id=1, source_target_pairs={{0,24},{1,25},{2,26},{3,27},{4,28},{5,29},{6,30},{7,31},{8,16},{9,... | collective-permute-start | bytes 442376 | tf_op jit(solution)/shard_map/ppermute | solution.py:26
  15.4 20.2 %collective-permute-start.1 = (bf16[24,3072]{1,0:T(8,128)(2,1)S(1)}, bf16[24,3072]{1,0:T(8,128)(2,1)S(1)}, u32[]{:S(2)}, u32[]{:S(2)}) collective-permute-start(bf16[24,3072]{1,0:T(8,128)(2,1)S(1)} %constant_dynamic-update-slice_fusion), channel_id=1, source_target_pairs={{0,16},{1,17},{2,18},{3,19},{4,20},{5,21},{6,22},{7,23},{8,24},{9,... | collective-permute-start | bytes 442376 | tf_op jit(solution)/shard_map/ppermute | solution.py:26
  15.4 20.2 %collective-permute-start = (bf16[24,3072]{1,0:T(8,128)(2,1)S(1)}, bf16[24,3072]{1,0:T(8,128)(2,1)S(1)}, u32[]{:S(2)}, u32[]{:S(2)}) collective-permute-start(bf16[24,3072]{1,0:T(8,128)(2,1)S(1)} %constant_dynamic-update-slice_fusion), channel_id=1, source_target_pairs={{0,8},{1,9},{2,10},{3,11},{4,12},{5,13},{6,14},{7,15},{8,0},{9,1},... | collective-permute-start | bytes 442376 | tf_op jit(solution)/shard_map/ppermute | solution.py:26
  36.5 23.2 %collective-permute-start.3 = (bf16[96,3072]{1,0:T(8,128)(2,1)}, bf16[96,3072]{1,0:T(8,128)(2,1)}, u32[]{:S(2)}, u32[]{:S(2)}) collective-permute-start(bf16[96,3072]{1,0:T(8,128)(2,1)} %pad_maximum_fusion.4.refs_0_), channel_id=1, source_target_pairs={{0,2},{1,3},{2,0},{3,1},{4,6},{5,7},{6,4},{7,5},{8,10},{9,11},{10,... | collective-permute-start | bytes 1769480 | tf_op jit(solution)/shard_map/ppermute | solution.py:26
  38.1 21.6 %collective-permute-start.4 = (bf16[96,3072]{1,0:T(8,128)(2,1)}, bf16[96,3072]{1,0:T(8,128)(2,1)}, u32[]{:S(2)}, u32[]{:S(2)}) collective-permute-start(bf16[96,3072]{1,0:T(8,128)(2,1)} %pad_maximum_fusion.4.refs_0_), channel_id=1, source_target_pairs={{0,4},{1,5},{2,6},{3,7},{4,0},{5,1},{6,2},{7,3},{8,12},{9,13},{10,... | collective-permute-start | bytes 1769480 | tf_op jit(solution)/shard_map/ppermute | solution.py:26
  63.6 33.6 %all-to-all-start = ((bf16[40,32,96]{2,0,1:T(8,128)(2,1)}), bf16[40,32,96]{2,0,1:T(8,128)(2,1)S(1)}, u32[]{:S(2)}, u32[]{:S(2)}) async-start(bf16[40,32,96]{2,0,1:T(8,128)(2,1)} %copy.64), calls=%async_computation | async-start | bytes 655360 | tf_op jit(solution)/shard_map/all_to_all | solution.py:1012
  70.5 26.5 %collective-permute-start.8 = (bf16[48,3072]{1,0:T(8,128)(2,1)S(1)}, bf16[48,3072]{1,0:T(8,128)(2,1)}, u32[]{:S(2)}, u32[]{:S(2)}) collective-permute-start(bf16[48,3072]{1,0:T(8,128)(2,1)S(1)} %slice.61), channel_id=1, source_target_pairs={{0,4},{1,5},{2,6},{3,7},{4,0},{5,1},{6,2},{7,3},{8,12},{9,13},{10,... | collective-permute-start | bytes 884744 | tf_op jit(solution)/shard_map/ppermute | solution.py:26
  73.2 23.9 %collective-permute-start.9 = (bf16[48,3072]{1,0:T(8,128)(2,1)S(1)}, bf16[48,3072]{1,0:T(8,128)(2,1)}, u32[]{:S(2)}, u32[]{:S(2)}) collective-permute-start(bf16[48,3072]{1,0:T(8,128)(2,1)S(1)} %slice.62), channel_id=1, source_target_pairs={{0,2},{1,3},{2,0},{3,1},{4,6},{5,7},{6,4},{7,5},{8,10},{9,11},{10,... | collective-permute-start | bytes 884744 | tf_op jit(solution)/shard_map/ppermute | solution.py:26
  77.1 19.4 %collective-permute-start.6 = (bf16[1,40,1024]{2,1,0:T(8,128)(2,1)S(1)}, bf16[1,40,1024]{2,1,0:T(8,128)(2,1)S(1)}, u32[]{:S(2)}, u32[]{:S(2)}) collective-permute-start(bf16[1,40,1024]{2,1,0:T(8,128)(2,1)S(1)} %bitcast.80), channel_id=1, source_target_pairs={{0,16},{1,17},{2,18},{3,19},{4,20},{5,21},{6,22},{7,23},{8,24},{9,... | collective-permute-start | bytes 245768 | tf_op jit(solution)/shard_map/ppermute | solution.py:26
  79.6 16.9 %collective-permute-start.7 = (bf16[1,40,1024]{2,1,0:T(8,128)(2,1)S(1)}, bf16[1,40,1024]{2,1,0:T(8,128)(2,1)S(1)}, u32[]{:S(2)}, u32[]{:S(2)}) collective-permute-start(bf16[1,40,1024]{2,1,0:T(8,128)(2,1)S(1)} %bitcast.81), channel_id=1, source_target_pairs={{0,24},{1,25},{2,26},{3,27},{4,28},{5,29},{6,30},{7,31},{8,16},{9,... | collective-permute-start | bytes 245768 | tf_op jit(solution)/shard_map/ppermute | solution.py:26
  85.9 12.9 %collective-permute-start.10 = (bf16[96,3072]{1,0:T(8,128)(2,1)}, bf16[96,3072]{1,0:T(8,128)(2,1)}, u32[]{:S(2)}, u32[]{:S(2)}) collective-permute-start(bf16[96,3072]{1,0:T(8,128)(2,1)} %pad_maximum_fusion.4.refs_0_), channel_id=1, source_target_pairs={{0,1},{1,0},{2,3},{3,2},{4,5},{5,4},{6,7},{7,6},{8,9},{9,8},{10,11... | collective-permute-start | bytes 1769480 | tf_op jit(solution)/shard_map/ppermute | solution.py:26
  98.8 17.2 %collective-permute-start.15 = (bf16[4,40,1024]{2,1,0:T(8,128)(2,1)S(1)}, bf16[4,40,1024]{2,1,0:T(8,128)(2,1)S(1)}, u32[]{:S(2)}, u32[]{:S(2)}) collective-permute-start(bf16[4,40,1024]{2,1,0:T(8,128)(2,1)S(1)} %bitcast.84), channel_id=1, source_target_pairs={{0,2},{1,3},{2,0},{3,1},{4,6},{5,7},{6,4},{7,5},{8,10},{9,11},{10,... | collective-permute-start | bytes 983048 | tf_op jit(solution)/shard_map/ppermute | solution.py:26
  100.4 15.6 %collective-permute-start.16 = (bf16[4,40,1024]{2,1,0:T(8,128)(2,1)S(1)}, bf16[4,40,1024]{2,1,0:T(8,128)(2,1)S(1)}, u32[]{:S(2)}, u32[]{:S(2)}) collective-permute-start(bf16[4,40,1024]{2,1,0:T(8,128)(2,1)S(1)} %bitcast.85), channel_id=1, source_target_pairs={{0,4},{1,5},{2,6},{3,7},{4,0},{5,1},{6,2},{7,3},{8,12},{9,13},{10,... | collective-permute-start | bytes 983048 | tf_op jit(solution)/shard_map/ppermute | solution.py:26
  123.0 18.3 %collective-permute-start.19 = (bf16[16,40,1024]{2,1,0:T(8,128)(2,1)S(1)}, bf16[16,40,1024]{2,1,0:T(8,128)(2,1)S(1)}, u32[]{:S(2)}, u32[]{:S(2)}) collective-permute-start(bf16[16,40,1024]{2,1,0:T(8,128)(2,1)S(1)} %bitcast.82), channel_id=1, source_target_pairs={{0,1},{1,0},{2,3},{3,2},{4,5},{5,4},{6,7},{7,6},{8,9},{9,8},{10,11... | collective-permute-start | bytes 3932168 | tf_op jit(solution)/shard_map/ppermute | solution.py:26
  133.9 20.3 %all-to-all-start.1 = ((bf16[32,8,768]{2,1,0:T(8,128)(2,1)}), bf16[32,8,768]{2,1,0:T(8,128)(2,1)S(1)}, u32[]{:S(2)}, u32[]{:S(2)}) async-start(bf16[32,8,768]{2,1,0:T(8,128)(2,1)} %broadcast_in_dim.5), calls=%async_computation.1 | async-start | bytes 786432 | tf_op jit(solution)/shard_map/all_to_all | solution.py:46
  182.8 16.1 %collective-permute-start.22 = (bf16[192,1536]{1,0:T(8,128)(2,1)S(1)}, bf16[192,1536]{1,0:T(8,128)(2,1)S(1)}, u32[]{:S(2)}, u32[]{:S(2)}) collective-permute-start(bf16[192,1536]{1,0:T(8,128)(2,1)S(1)} %get-tuple-element.151.refs_1_), channel_id=1, source_target_pairs={{0,2},{1,3},{2,0},{3,1},{4,6},{5,7},{6,4},{7,5},{8,10},{9,11},{10,... | collective-permute-start | bytes 1769480 | tf_op jit(solution)/shard_map/ppermute | solution.py:26
  183.5 15.4 %collective-permute-start.23 = (bf16[192,1536]{1,0:T(8,128)(2,1)S(1)}, bf16[192,1536]{1,0:T(8,128)(2,1)S(1)}, u32[]{:S(2)}, u32[]{:S(2)}) collective-permute-start(bf16[192,1536]{1,0:T(8,128)(2,1)S(1)} %get-tuple-element.153.refs_3_), channel_id=1, source_target_pairs={{0,4},{1,5},{2,6},{3,7},{4,0},{5,1},{6,2},{7,3},{8,12},{9,13},{10,... | collective-permute-start | bytes 1769480 | tf_op jit(solution)/shard_map/ppermute | solution.py:26
  214.4 16.4 %collective-permute-start.29 = (bf16[208,1536]{1,0:T(8,128)(2,1)S(1)}, bf16[208,1536]{1,0:T(8,128)(2,1)S(1)}, u32[]{:S(2)}, u32[]{:S(2)}) collective-permute-start(bf16[208,1536]{1,0:T(8,128)(2,1)S(1)} %get-tuple-element.183), channel_id=1, source_target_pairs={{0,2},{1,3},{2,0},{3,1},{4,6},{5,7},{6,4},{7,5},{8,10},{9,11},{10,... | collective-permute-start | bytes 1916936 | tf_op jit(solution)/shard_map/ppermute | solution.py:26
  215.5 15.3 %collective-permute-start.30 = (bf16[192,1536]{1,0:T(8,128)(2,1)S(1)}, bf16[192,1536]{1,0:T(8,128)(2,1)S(1)}, u32[]{:S(2)}, u32[]{:S(2)}) collective-permute-start(bf16[192,1536]{1,0:T(8,128)(2,1)S(1)} %get-tuple-element.185), channel_id=1, source_target_pairs={{0,4},{1,5},{2,6},{3,7},{4,0},{5,1},{6,2},{7,3},{8,12},{9,13},{10,... | collective-permute-start | bytes 1769480 | tf_op jit(solution)/shard_map/ppermute | solution.py:26
  217.6 13.2 %collective-permute-start.32 = (bf16[24,3072]{1,0:T(8,128)(2,1)S(1)}, bf16[24,3072]{1,0:T(8,128)(2,1)S(1)}, u32[]{:S(2)}, u32[]{:S(2)}) collective-permute-start(bf16[24,3072]{1,0:T(8,128)(2,1)S(1)} %get-tuple-element.187), channel_id=1, source_target_pairs={{0,16},{1,17},{2,18},{3,19},{4,20},{5,21},{6,22},{7,23},{8,24},{9,... | collective-permute-start | bytes 442376 | tf_op jit(solution)/shard_map/ppermute | solution.py:26
  218.3 12.5 %collective-permute-start.33 = (bf16[24,3072]{1,0:T(8,128)(2,1)S(1)}, bf16[24,3072]{1,0:T(8,128)(2,1)S(1)}, u32[]{:S(2)}, u32[]{:S(2)}) collective-permute-start(bf16[24,3072]{1,0:T(8,128)(2,1)S(1)} %get-tuple-element.188), channel_id=1, source_target_pairs={{0,24},{1,25},{2,26},{3,27},{4,28},{5,29},{6,30},{7,31},{8,16},{9,... | collective-permute-start | bytes 442376 | tf_op jit(solution)/shard_map/ppermute | solution.py:26
  241.5 17.0 %collective-permute-start.37 = (bf16[32,3072]{1,0:T(8,128)(2,1)S(1)}, bf16[32,3072]{1,0:T(8,128)(2,1)S(1)}, u32[]{:S(2)}, u32[]{:S(2)}) collective-permute-start(bf16[32,3072]{1,0:T(8,128)(2,1)S(1)} %get-tuple-element.201), channel_id=1, source_target_pairs={{0,16},{1,17},{2,18},{3,19},{4,20},{5,21},{6,22},{7,23},{8,24},{9,... | collective-permute-start | bytes 589832 | tf_op jit(solution)/shard_map/ppermute | solution.py:26
  243.4 15.1 %collective-permute-start.36 = (bf16[32,3072]{1,0:T(8,128)(2,1)S(1)}, bf16[32,3072]{1,0:T(8,128)(2,1)S(1)}, u32[]{:S(2)}, u32[]{:S(2)}) collective-permute-start(bf16[32,3072]{1,0:T(8,128)(2,1)S(1)} %get-tuple-element.200), channel_id=1, source_target_pairs={{0,8},{1,9},{2,10},{3,11},{4,12},{5,13},{6,14},{7,15},{8,0},{9,1},... | collective-permute-start | bytes 589832 | tf_op jit(solution)/shard_map/ppermute | solution.py:26
  (49 other events, 373.7 us)
Sparse Core Ops, SparseCore 0:
  11.5 103.0 all-gather.1

commit v5 on v4

--- a/solution.py
+++ b/solution.py
@@ -142,6 +142,10 @@
 
 def in_vmem(count):
     return [pl.BlockSpec(memory_space=pltpu.VMEM)] * count
+
+
+def in_hbm(*arrays):
+    return [pltpu.with_memory_space_constraint(array, pltpu.HBM) for array in arrays]
 
 
 def stays(shape, dtype):
@@ -753,24 +757,54 @@
 
 
 def mlp_back_kernel(
-    low_ref, wd_ref, slope_ref, wu_ref, lhs_ref, mid_ref, gain_ref, row_ref, keep_a, send_a, keep_b,
-    send_b, out_ref, sums_out
+    low_ref, gain_ref, row_ref, wd_hbm, slope_hbm, wu_hbm, lhs_hbm, mid_hbm, keep_a, send_a, keep_b,
+    send_b, out_ref, sums_out, wd_ref, slope_ref, wu_ref, lhs_ref, mid_ref, sems, whole_sems
 ):
-    count, rows = low_ref.shape[0], slope_ref.shape[0]
+    count, rows = low_ref.shape[0], out_ref.shape[0]
     half, steps = D // 2, FF // 2 // TILE
+
+    def copies(tile, slot):
+        at = pl.ds(pl.multiple_of(tile * TILE, TILE), TILE)
+        return (
+            pltpu.make_async_copy(wd_hbm.at[at, :], wd_ref.at[slot], sems.at[0, slot]),
+            pltpu.make_async_copy(slope_hbm.at[:, at], slope_ref.at[slot], sems.at[1, slot]),
+            pltpu.make_async_copy(wu_hbm.at[:, at], wu_ref.at[slot], sems.at[2, slot]),
+        )
+
+    lhs_copy = pltpu.make_async_copy(lhs_hbm, lhs_ref, whole_sems.at[0])
+    mid_copy = pltpu.make_async_copy(mid_hbm, mid_ref, whole_sems.at[1])
+    for copy in copies(0, 0):
+        copy.start()
+    lhs_copy.start()
     for k, (keep, send) in enumerate(((keep_a, send_a), (keep_b, send_b))):
 
         @pl.loop(0, steps)
         def _(step, k=k, keep=keep, send=send):
-            at = pl.ds(pl.multiple_of(k * (FF // 2) + step * TILE, TILE), TILE)
+            tile = k * steps + step
+            slot = lax.rem(tile, 2)
+
+            @pl.when(tile + 1 < 2 * steps)
+            def _():
+                for copy in copies(tile + 1, 1 - slot):
+                    copy.start()
+
+            for copy in copies(tile, slot):
+                copy.wait()
+            if k == 0:
+
+                @pl.when(step == 0)
+                def _():
+                    lhs_copy.wait()
+                    mid_copy.start()
+
             there = pl.ds(pl.multiple_of(step * TILE, TILE), TILE)
-            hidden = mul_bt(low_ref[...], wd_ref[at, :])
+            hidden = mul_bt(low_ref[...], wd_ref[slot])
             wide = jnp.broadcast_to(hidden[:, None, :], (count, TXT_LEN, TILE))
-            inner = (wide.reshape(rows, TILE) * slope_ref[:, at].astype(f32)).astype(bf16)
+            inner = (wide.reshape(rows, TILE) * slope_ref[slot].astype(f32)).astype(bf16)
             weight = mul(lhs_ref[k], inner).astype(bf16)
             keep[:, there] = weight[:half]
             send[:, there] = weight[half:]
-            added = mul_bt(inner, wu_ref[:, at])
+            added = mul_bt(inner, wu_ref[slot])
             if k == 0:
 
                 @pl.when(step == 0)
@@ -787,6 +821,7 @@
     per = chunk // TXT_LEN
     gain = line(gain_ref)
     sums_out[...] = jnp.zeros_like(sums_out)
+    mid_copy.wait()
 
     @pl.loop(0, rows // chunk)
     def _(k):
@@ -806,12 +841,21 @@
         mlp_back_kernel,
         out_shape=[stays((D // 2, FF // 2), bf16)] * 4
         + [stays((rows, D), f32), stays((1, 2 * D), f32)],
-        in_specs=in_vmem(8),
+        in_specs=in_vmem(3) + [pl.BlockSpec(memory_space=pltpu.HBM)] * 5,
         out_specs=in_vmem(6),
-        compiler_params=params(16 << 20),
+        scratch_shapes=[
+            pltpu.VMEM((2, TILE, D), bf16),
+            pltpu.VMEM((2, rows, TILE), bf16),
+            pltpu.VMEM((2, D, TILE), bf16),
+            pltpu.VMEM((2, D, rows), bf16),
+            pltpu.VMEM((rows, D), f32),
+            pltpu.SemaphoreType.DMA((3, 2)),
+            pltpu.SemaphoreType.DMA((2,)),
+        ],
+        compiler_params=params(28 << 20),
         cost_estimate=cost(4 * rows * D * FF, 4 * D * FF + 2 * rows * FF + 2 * D * FF, rows * FF),
         name="mlp_back",
-    )(grad_low, weight_down, slope, weight_up, lhs, middle, gain, grad_row)
+    )(grad_low, gain, grad_row, *in_hbm(weight_down, slope, weight_up, lhs, middle))
 
 
 def attention_back_kernel(first, grad_ref, wo_ref, qkv_ref, lse_ref, *refs):
@@ -988,7 +1032,9 @@
     slope, hidden_sum, text_unit, inverse = text_up(
         normed2, txt_up, txt_down, middle_sum, (line,)
     )
-    text_unit, (beside, above) = in_turn(text_unit, (beside, above))
+    text_unit, normed2, beside, above = lax.optimization_barrier(
+        (text_unit, normed2, beside, above)
+    )
 
     ends_at = jnp.cumsum(counts)
     slot_ids = lax.iota(jnp.int32, cap_local)
@@ -1001,39 +1047,35 @@
     order_a, order_b, tail = stage_orders()
     source_a, source_b = row_order(order_a + tail[::-1]), row_order(order_b + tail[::-1])
     own_pack = packed(text_unit, positive.astype(bf16), ())
-    own_pack, hidden_sum, normed2 = lax.optimization_barrier((own_pack, hidden_sum, normed2))
     lhs_up = left_factors((source_a, normed2), (source_b, normed2))
     pieces = [line]
     if small:
+        first, second = diagonal(beside, above)
+        own_pack, first, second, lhs_up = lax.optimization_barrier(
+            (own_pack, first, second, lhs_up)
+        )
         held = own_pack[None]
-        first, second = diagonal(beside, above)
         others = [swapped(held, mask) for mask in (8, 16, 24)]
+        pieces = [line, beside, above, first, second]
+        pieces = pieces + [swapped(piece, 1) for piece in pieces]
+
+    normed_img, middle_img = image_front(
+        images, pieces, source, img_gain1, img_bias1, img_gain2, img_bias2
+    )
+    if small:
         scaled_sum = (hidden_sum * inverse[:, :1]).astype(bf16)
-        hidden_cols = lax.all_to_all(scaled_sum, AXIS, split_axis=1, concat_axis=0, tiled=True)
-        others, first, second, hidden_cols, lhs_up = lax.optimization_barrier(
-            (others, first, second, hidden_cols, lhs_up)
-        )
+        normed_img, scaled_sum, others = lax.optimization_barrier((normed_img, scaled_sum, others))
         held = joined(joined(held, others[0], 8), joined(others[1], others[2], 8), 16, 1)
         text_beside, text_above = swapped(held, 2), swapped(held, 4)
-        pieces = [line, beside, above, first, second]
-        pieces = pieces + [swapped(piece, 1) for piece in pieces]
-
-    normed_img, middle_img = image_front(
-        images, pieces, source, img_gain1, img_bias1, img_gain2, img_bias2
-    )
-    if small:
-        normed_img, text_beside, text_above = lax.optimization_barrier(
-            (normed_img, text_beside, text_above)
-        )
-        across = jnp.concatenate(diagonal(text_beside, text_above), axis=0)
-        held = joined(joined(held, text_beside, 2), joined(text_above, across, 2), 4, 4)
-
-    if small:
-        whole, held = in_turn(whole, held)
-        other = swapped(held, 1)
+        hidden_cols = lax.all_to_all(scaled_sum, AXIS, split_axis=1, concat_axis=0, tiled=True)
+        whole, text_beside, text_above = lax.optimization_barrier((whole, text_beside, text_above))
+        halves = diagonal(text_beside, text_above)
     image_low = image_up(normed_img, whole, 0, FF, middle_img)
     if small:
-        text_pack = joined(held, other, 1).reshape(-1, D + total_images)
+        image_low, halves, hidden_cols = lax.optimization_barrier((image_low, halves, hidden_cols))
+        across = jnp.concatenate(halves, axis=0)
+        held = joined(joined(held, text_beside, 2), joined(text_above, across, 2), 4, 4)
+        text_pack = joined(held, swapped(held, 1), 1).reshape(-1, D + total_images)
     image_all = spread(image_low).reshape(total_images, D)
     if small:
         image_all, text_pack = in_turn(image_all, text_pack)

time: 269 us -> 251 us (0.933)
  local copies, waits for them, and re-layouts: 22.5 us -> 15.8 us
  waiting for transfers between devices: 61.3 us -> 55.2 us
  starting transfers between devices: 54.3 us -> 49.3 us
  Pallas kernels: 107 us -> 110 us
    ppermute x39, waiting for transfers between devices: 48.7 us -> 34.3 us  [swapped(): return lax.ppermute(value, AXIS, [(i, i ^ mask) for i in range(peers)])]
    all_gather x1, waiting for transfers between devices: 0.02 us -> 8.29 us  [local(): lax.all_gather(jnp.concatenate([img_up.reshape(per, FF), img_down.reshape...]
    unnamed x65 -> x69, local copies, waits for them, and re-layouts: 11.3 us -> 4.74 us
    all_to_all x1, starting transfers between devices: 7.37 us -> 2.7 us  [spread(): return lax.all_to_all(copies, AXIS, split_axis=0, concat_axis=0, tiled=True)]
  transfers between devices with their start and end apart: 42 -> 42, of which waited for: 14 -> 13; matrix products, arithmetic and copies ran while one was open for 5% -> 5% of each run, Pallas kernels for 33% -> 35%
where the time goes in v5:
time: 251 us; the launch traced here: 250 us
  Pallas kernels  110 us (44%)
  waiting for transfers between devices  55.2 us (22%)
  starting transfers between devices  49.3 us (20%)
  local copies, waits for them, and re-layouts  15.8 us (6%)
  between operations  14.8 us (6%)
  other arithmetic  5.45 us (2%)
    ppermute x39, starting transfers between devices, swapped(): return lax.ppermute(value, AXIS, [(i, i ^ mask) for i in range(peers)])  40.8 us
    ppermute x39, waiting for transfers between devices, swapped(): return lax.ppermute(value, AXIS, [(i, i ^ mask) for i in range(peers)])  34.3 us
    pallas_call x1, Pallas kernels, text_front(): pl.pallas_call(text_front_kernel, out_shape=[jax.ShapeDtypeStruct(*item)...  18.1 us
    pallas_call x1, Pallas kernels, mlp_back(): pl.pallas_call(mlp_back_kernel, out_shape=[stays((D // 2, FF // 2), bf16)...  14.8 us
    pallas_call x1, Pallas kernels, image_front(): pl.pallas_call(functools.partial(image_front_kernel, windows), out_shape=...  14 us
    all_to_all x1, waiting for transfers between devices, spread(): return lax.all_to_all(copies, AXIS, split_axis=0, concat_axis=0, tiled=True)  12.6 us
    pallas_call x1, Pallas kernels, text_up(): pl.pallas_call(text_up_kernel, grid=(FF // TILE,), out_shape=[jax.ShapeDt...  12.1 us
    pallas_call x2, Pallas kernels, attention_back(): pl.pallas_call(functools.partial(attention_back_kernel, first), out_shape...  11.5 us
  transfers between devices with their start and end apart: 42, of which 13 were waited for; matrix products, arithmetic and copies ran while one was open for 5% of the time, Pallas kernels for 35%

profile of v5, /device:TPU:0, one launch (start us, length us, event | category | flops | bytes accessed | tf_op | source)
XLA Modules:
  0.0 250.3 jit_solution(10654617439549864231)
XLA Ops:
  10.3 5.1 %collective-permute-start.2 = (bf16[24,3072]{1,0:T(8,128)(2,1)S(1)}, bf16[24,3072]{1,0:T(8,128)(2,1)S(1)}, u32[]{:S(2)}, u32[]{:S(2)}) collective-permute-start(bf16[24,3072]{1,0:T(8,128)(2,1)S(1)} %constant_dynamic-update-slice_fusion), channel_id=1, source_target_pairs={{0,24},{1,25},{2,26},{3,27},{4,28},{5,29},{6,30},{7,31},{8,16},{9,... | collective-permute-start | bytes 442376 | tf_op jit(solution)/shard_map/ppermute | solution.py:26
  16.3 18.1 %text_front.1 = (bf16[640,768]{1,0:T(8,128)(2,1)}, bf16[640,2304]{1,0:T(8,128)(2,1)}, bf16[640,768]{1,0:T(8,128)(2,1)}, f32[640,768]{1,0:T(8,128)}, bf16[640,768...) custom-call(bf16[640,768]{1,0:T(8,128)(2,1)} %refs_3_.1, f32[768]{0:T(1024)} %refs_4_.1, f32[768]{0:T(1024)} %b1_ref.2, ...), custom_call_target="tpu_custom_call" | custom-call | flops 3019898880 | bytes 11599872 | tf_op jit(solution)/shard_map/text_front/pallas_call | solution.py:365
  40.8 12.1 %text_up.1 = (bf16[640,3072]{1,0:T(8,128)(2,1)}, f32[40,3072]{1,0:T(8,128)}, f32[40,768]{1,0:T(8,128)}, f32[40,128]{1,0:T(8,128)}) custom-call(bf16[640,768]{1,0:T(8,128)(2,1)} %get-tuple-element.119.h2_ref.refs_1_.refs_3_, bf16[768,3072]{1,0:T(8,128)(2,1)} %wu_hbm.1, bf16[3072,768]{1,0:T(8,128)(2,1)} %wd_hbm.1, f32[40,768]{1,0:T(8,128)} %get-tuple-element.114.sum_ref, ...), custom_call_target="tpu_custom_call" | custom-call | flops 3019898880 | bytes 13369344 | tf_op jit(solution)/shard_map/text_up/pallas_call | solution.py:524
  53.0 6.6 %collective-permute-done.3.refs_1_ = bf16[96,3072]{1,0:T(8,128)(2,1)} collective-permute-done((bf16[96,3072]{1,0:T(8,128)(2,1)}, bf16[96,3072]{1,0:T(8,128)(2,1)}, u32[]{:S(2)}, u32[]{:S(2)}) %collective-permute-start.3) | collective-permute-done | bytes 589856 | tf_op jit(solution)/shard_map/ppermute | solution.py:26
  70.0 3.2 %left_factors.2.lhs_hbm = bf16[2,768,640]{2,1,0:T(8,128)(2,1)S(1)} custom-call(s32[768,1]{1,0:T(8,128)S(1)} %fusion.8.refs_0_, bf16[640,768]{1,0:T(8,128)(2,1)S(1)} %copy-done.19, s32[768,1]{1,0:T(8,128)S(1)} %fusion.9.refs_2_.order_ref.refs_4_, bf16[640,768]{1,0:T(8,128)(2,1)S(1)} %copy-done.19), custom_call_target="tpu_custom_call" | custom-call | flops 1509949440 | bytes 3932160 | tf_op jit(solution)/shard_map/left_factors/pallas_call | solution.py:626
  75.4 2.6 %collective-permute-start.13 = (bf16[1,40,1024]{2,1,0:T(8,128)(2,1)S(1)}, bf16[1,40,1024]{2,1,0:T(8,128)(2,1)S(1)}, u32[]{:S(2)}, u32[]{:S(2)}) collective-permute-start(bf16[1,40,1024]{2,1,0:T(8,128)(2,1)S(1)} %bitcast.82), channel_id=1, source_target_pairs={{0,16},{1,17},{2,18},{3,19},{4,20},{5,21},{6,22},{7,23},{8,24},{9,... | collective-permute-start | bytes 245768 | tf_op jit(solution)/shard_map/ppermute | solution.py:26
  79.8 14.0 %image_front.1 = (bf16[400,768]{1,0:T(8,128)(2,1)}, f32[8,768]{1,0:T(8,128)}) custom-call(bf16[400,768]{1,0:T(8,128)(2,1)} %x_ref.3, s32[768,1]{1,0:T(8,128)} %copy-done.9, bf16[768]{0:T(1024)(128)(2,1)} %g1_ref.3, bf16[768]{0:T(1024)(128)(2,1)} %b1_ref.3, bf16[768]{0:T(1024)(128)(2,1)} %g2_ref.3, bf16[768]{0:T(1024)(128)(2,1)} %b2_ref.3, ...), custom_call_target="tpu_custom_call" | custom-call | flops 2831155200 | bytes 4718592 | tf_op jit(solution)/shard_map/image_front/pallas_call | solution.py:429
  96.3 5.7 %all-to-all-start = ((bf16[40,32,96]{2,0,1:T(8,128)(2,1)}), bf16[40,32,96]{2,0,1:T(8,128)(2,1)S(1)}, u32[]{:S(2)}, u32[]{:S(2)}) async-start(bf16[40,32,96]{2,0,1:T(8,128)(2,1)} %copy.68), calls=%async_computation | async-start | bytes 655360 | tf_op jit(solution)/shard_map/all_to_all | solution.py:1070
  103.7 8.3 %all-gather.2.cloned.1.call-done.wu_ref.wd_ref = bf16[768,6144]{1,0:T(8,128)(2,1)} async-done(((bf16[24,6144]{1,0:T(8,128)(2,1)}), bf16[768,6144]{1,0:T(8,128)(2,1)}) %all-gather.2.cloned.1.call-update) | async-done | bytes 9437200 | tf_op jit(solution)/shard_map/all_gather | solution.py:1014
  115.7 9.3 %image_up.1 = bf16[8,768]{1,0:T(8,128)(2,1)} custom-call(bf16[400,768]{1,0:T(8,128)(2,1)} %get-tuple-element.126.h2_ref, bf16[768,6144]{1,0:T(8,128)(2,1)} %all-gather.2.cloned.1.call-done.wu_ref.wd_ref, bf16[768,6144]{1,0:T(8,128)(2,1)} %all-gather.2.cloned.1.call-done.wu_ref.wd_ref, f32[8,768]{1,0:T(8,128)} %get-tuple-element.131.sum_ref), custom_call_target="tpu_custom_call" | custom-call | flops 1887436800 | bytes 9437184 | tf_op jit(solution)/shard_map/image_up/pallas_call | solution.py:592
  127.1 2.7 %all-to-all-start.1 = ((bf16[32,8,768]{2,1,0:T(8,128)(2,1)}), bf16[32,8,768]{2,1,0:T(8,128)(2,1)S(1)}, u32[]{:S(2)}, u32[]{:S(2)}) async-start(bf16[32,8,768]{2,1,0:T(8,128)(2,1)} %broadcast_in_dim.5), calls=%async_computation.1 | async-start | bytes 786432 | tf_op jit(solution)/shard_map/all_to_all | solution.py:46
  130.3 12.6 %all-to-all-done.1 = bf16[32,8,768]{2,1,0:T(8,128)(2,1)S(1)} async-done(((bf16[32,8,768]{2,1,0:T(8,128)(2,1)}), bf16[32,8,768]{2,1,0:T(8,128)(2,1)S(1)}, u32[]{:S(2)}, u32[]{:S(2)}) %all-to-all-start.1) | async-done | bytes 393248 | tf_op jit(solution)/shard_map/all_to_all | solution.py:46
  145.6 14.8 %mlp_back.1 = (bf16[384,1536]{1,0:T(8,128)(2,1)S(1)}, bf16[384,1536]{1,0:T(8,128)(2,1)S(1)}, bf16[384,1536]{1,0:T(8,128)(2,1)S(1)}, bf16[384,1536]{1,0:T(8,128)(...) custom-call(bf16[40,768]{1,0:T(8,128)(2,1)S(1)} %get-tuple-element.141.low_ref, f32[768]{0:T(1024)S(1)} %copy-done.17, ...), custom_call_target="tpu_custom_call" | custom-call | flops 6039797760 | bytes 18087936 | tf_op jit(solution)/shard_map/mlp_back/pallas_call | solution.py:840
  160.9 2.3 attention_back.2
  167.6 9.2 %attention_back.3 = (bf16[512,768]{1,0:T(8,128)(2,1)S(1)}, bf16[512,2304]{1,0:T(8,128)(2,1)S(1)}) custom-call(f32[640,768]{1,0:T(8,128)S(1)} %get-tuple-element.146.grad_ref.refs_5_, bf16[768,768]{1,0:T(8,128)(2,1)S(1)} %copy-done.3, bf16[640,2304]{1,0:T(8,128)(2,1)S(1)} %copy-done.1, f32[80,128]{1,0:T(8,128)S(1)} %copy-done.15, ...), custom_call_target="tpu_custom_call" | custom-call | flops 3019898880 | bytes 7471104 | tf_op jit(solution)/shard_map/attention_back/pallas_call | solution.py:899
  176.8 4.8 %left_factors.3.refs_1_.lhs_ref = bf16[3,768,640]{2,1,0:T(8,128)(2,1)S(1)} custom-call(s32[768,1]{1,0:T(8,128)S(1)} %copy-done.12, bf16[640,768]{1,0:T(8,128)(2,1)S(1)} %copy-done.20, s32[768,1]{1,0:T(8,128)S(1)} %copy-done.10, bf16[640,768]{1,0:T(8,128)(2,1)S(1)} %copy-done.20, s32[768,1]{1,0:T(8,128)S(1)} %copy-done.10, bf16[640,768]{1,0:T(8,128)(2,1)S(1)} %copy-done.21), custom_call_target="tpu_custom_call" | custom-call | flops 2264924160 | bytes 5898240 | tf_op jit(solution)/shard_map/left_factors/pallas_call | solution.py:626
  182.2 3.9 %weight_back.1 = (bf16[384,1536]{1,0:T(8,128)(2,1)S(1)}, bf16[384,1536]{1,0:T(8,128)(2,1)S(1)}, bf16[384,1536]{1,0:T(8,128)(2,1)S(1)}, bf16[384,1536]{1,0:T(8,128)(2,1)S(1)}) custom-call(bf16[3,768,640]{2,1,0:T(8,128)(2,1)S(1)} %left_factors.3.refs_1_.lhs_ref, bf16[128,2304]{1,0:T(8,128)(2,1)S(1)} %get-tuple-element.149.refs_0_, ...), custom_call_target="tpu_custom_call" | custom-call | flops 3019898880 | bytes 12189696 | tf_op jit(solution)/shard_map/weight_back/pallas_call | solution.py:932
  188.8 6.5 %input_back.1 = (f32[640,768]{1,0:T(8,128)}, f32[8,1536]{1,0:T(8,128)S(1)}) custom-call(bf16[128,2304]{1,0:T(8,128)(2,1)S(1)} %get-tuple-element.149.refs_0_, bf16[512,2304]{1,0:T(8,128)(2,1)S(1)} %get-tuple-element.160.refs_0_.refs_1_, bf16[768,2304]{1,0:T(8,128)(2,1)S(1)} %copy-done, bf16[640,768]{1,0:T(8,128)(2,1)S(1)} %copy-done.6, f32[768]{0:T(1024)S(1)} %copy-done.16, ...), custom_call_target="tpu_custom_call" | custom-call | flops 2264924160 | bytes 10420224 | tf_op jit(solution)/shard_map/input_back/pallas_call | solution.py:974
  201.2 2.6 %collective-permute-start.33 = (bf16[24,3072]{1,0:T(8,128)(2,1)S(1)}, bf16[24,3072]{1,0:T(8,128)(2,1)S(1)}, u32[]{:S(2)}, u32[]{:S(2)}) collective-permute-start(bf16[24,3072]{1,0:T(8,128)(2,1)S(1)} %get-tuple-element.192), channel_id=1, source_target_pairs={{0,24},{1,25},{2,26},{3,27},{4,28},{5,29},{6,30},{7,31},{8,16},{9,... | collective-permute-start | bytes 442376 | tf_op jit(solution)/shard_map/ppermute | solution.py:26
  203.7 5.9 %grad_of_down.1 = f32[96,768]{1,0:T(8,128)S(1)} custom-call(bf16[1280,1024]{1,0:T(8,128)(2,1)S(1)} %bitcast.77, bf16[256,768]{1,0:T(8,128)(2,1)S(1)} %bitcast.79, f32[1,256]{1,0:T(1,128)S(1)} %get-tuple-element.173.col_sum_ref, f32[1,256]{1,0:T(1,128)S(1)} %get-tuple-element.174.col_count_ref, f32[1,128]{1,0:T(1,128)S(1)} %get-tuple-element.175.live_ref, ...), custom_call_target="tpu_custom_call" | custom-call | flops 1006632960 | bytes 2621440 | tf_op jit(solution)/shard_map/grad_of_down/pallas_call | solution.py:742
  209.6 3.9 %collective-permute-done.32 = bf16[24,3072]{1,0:T(8,128)(2,1)S(1)} collective-permute-done((bf16[24,3072]{1,0:T(8,128)(2,1)S(1)}, bf16[24,3072]{1,0:T(8,128)(2,1)S(1)}, u32[]{:S(2)}, u32[]{:S(2)}) %collective-permute-start.32) | collective-permute-done | bytes 147488 | tf_op jit(solution)/shard_map/ppermute | solution.py:26
  216.0 6.8 %collective-permute-done.35.got_b = bf16[96,1536]{1,0:T(8,128)(2,1)S(1)} collective-permute-done((bf16[96,1536]{1,0:T(8,128)(2,1)S(1)}, bf16[96,1536]{1,0:T(8,128)(2,1)S(1)}, u32[]{:S(2)}, u32[]{:S(2)}) %collective-permute-start.35) | collective-permute-done | bytes 294944 | tf_op jit(solution)/shard_map/ppermute | solution.py:26
  229.4 3.7 %collective-permute-done.38 = bf16[32,3072]{1,0:T(8,128)(2,1)S(1)} collective-permute-done((bf16[32,3072]{1,0:T(8,128)(2,1)S(1)}, bf16[32,3072]{1,0:T(8,128)(2,1)S(1)}, u32[]{:S(2)}, u32[]{:S(2)}) %collective-permute-start.38) | collective-permute-done | bytes 196640 | tf_op jit(solution)/shard_map/ppermute | solution.py:26
  233.1 8.3 %collective-permute-done.37 = bf16[32,3072]{1,0:T(8,128)(2,1)S(1)} collective-permute-done((bf16[32,3072]{1,0:T(8,128)(2,1)S(1)}, bf16[32,3072]{1,0:T(8,128)(2,1)S(1)}, u32[]{:S(2)}, u32[]{:S(2)}) %collective-permute-start.37) | collective-permute-done | bytes 196640 | tf_op jit(solution)/shard_map/ppermute | solution.py:26
  (195 shorter events, 62.4 us)
Async XLA Ops:
  7.2 104.8 %all-gather.2.cloned.1.call-start = ((), (), s32[]{:S(2)}) async-start(), calls=%async_computation.2 | async-start | bytes 9732096 | tf_op jit(solution)/shard_map/all_gather | solution.py:1014
  10.3 25.1 %collective-permute-start.2 = (bf16[24,3072]{1,0:T(8,128)(2,1)S(1)}, bf16[24,3072]{1,0:T(8,128)(2,1)S(1)}, u32[]{:S(2)}, u32[]{:S(2)}) collective-permute-start(bf16[24,3072]{1,0:T(8,128)(2,1)S(1)} %constant_dynamic-update-slice_fusion), channel_id=1, source_target_pairs={{0,24},{1,25},{2,26},{3,27},{4,28},{5,29},{6,30},{7,31},{8,16},{9,... | collective-permute-start | bytes 442376 | tf_op jit(solution)/shard_map/ppermute | solution.py:26
  15.4 20.0 %collective-permute-start.1 = (bf16[24,3072]{1,0:T(8,128)(2,1)S(1)}, bf16[24,3072]{1,0:T(8,128)(2,1)S(1)}, u32[]{:S(2)}, u32[]{:S(2)}) collective-permute-start(bf16[24,3072]{1,0:T(8,128)(2,1)S(1)} %constant_dynamic-update-slice_fusion), channel_id=1, source_target_pairs={{0,16},{1,17},{2,18},{3,19},{4,20},{5,21},{6,22},{7,23},{8,24},{9,... | collective-permute-start | bytes 442376 | tf_op jit(solution)/shard_map/ppermute | solution.py:26
  15.4 20.0 %collective-permute-start = (bf16[24,3072]{1,0:T(8,128)(2,1)S(1)}, bf16[24,3072]{1,0:T(8,128)(2,1)S(1)}, u32[]{:S(2)}, u32[]{:S(2)}) collective-permute-start(bf16[24,3072]{1,0:T(8,128)(2,1)S(1)} %constant_dynamic-update-slice_fusion), channel_id=1, source_target_pairs={{0,8},{1,9},{2,10},{3,11},{4,12},{5,13},{6,14},{7,15},{8,0},{9,1},... | collective-permute-start | bytes 442376 | tf_op jit(solution)/shard_map/ppermute | solution.py:26
  36.3 23.2 %collective-permute-start.3 = (bf16[96,3072]{1,0:T(8,128)(2,1)}, bf16[96,3072]{1,0:T(8,128)(2,1)}, u32[]{:S(2)}, u32[]{:S(2)}) collective-permute-start(bf16[96,3072]{1,0:T(8,128)(2,1)} %pad_maximum_fusion.4.refs_0_), channel_id=1, source_target_pairs={{0,2},{1,3},{2,0},{3,1},{4,6},{5,7},{6,4},{7,5},{8,10},{9,11},{10,... | collective-permute-start | bytes 1769480 | tf_op jit(solution)/shard_map/ppermute | solution.py:26
  37.9 21.6 %collective-permute-start.4 = (bf16[96,3072]{1,0:T(8,128)(2,1)}, bf16[96,3072]{1,0:T(8,128)(2,1)}, u32[]{:S(2)}, u32[]{:S(2)}) collective-permute-start(bf16[96,3072]{1,0:T(8,128)(2,1)} %pad_maximum_fusion.4.refs_0_), channel_id=1, source_target_pairs={{0,4},{1,5},{2,6},{3,7},{4,0},{5,1},{6,2},{7,3},{8,12},{9,13},{10,... | collective-permute-start | bytes 1769480 | tf_op jit(solution)/shard_map/ppermute | solution.py:26
  61.3 11.9 %collective-permute-start.5 = (bf16[48,3072]{1,0:T(8,128)(2,1)}, bf16[48,3072]{1,0:T(8,128)(2,1)}, u32[]{:S(2)}, u32[]{:S(2)}) collective-permute-start(bf16[48,3072]{1,0:T(8,128)(2,1)} %slice.61), channel_id=1, source_target_pairs={{0,4},{1,5},{2,6},{3,7},{4,0},{5,1},{6,2},{7,3},{8,12},{9,13},{10,... | collective-permute-start | bytes 884744 | tf_op jit(solution)/shard_map/ppermute | solution.py:26
  67.1 10.9 %collective-permute-start.9 = (bf16[96,3072]{1,0:T(8,128)(2,1)}, bf16[96,3072]{1,0:T(8,128)(2,1)S(1)}, u32[]{:S(2)}, u32[]{:S(2)}) collective-permute-start(bf16[96,3072]{1,0:T(8,128)(2,1)} %collective-permute-done.4.refs_2_), channel_id=1, source_target_pairs={{0,1},{1,0},{2,3},{3,2},{4,5},{5,4},{6,7},{7,6},{8,9},{9,8},{10,11... | collective-permute-start | bytes 1769480 | tf_op jit(solution)/shard_map/ppermute | solution.py:26
  73.9 19.9 %collective-permute-start.12 = (bf16[1,40,1024]{2,1,0:T(8,128)(2,1)S(1)}, bf16[1,40,1024]{2,1,0:T(8,128)(2,1)S(1)}, u32[]{:S(2)}, u32[]{:S(2)}) collective-permute-start(bf16[1,40,1024]{2,1,0:T(8,128)(2,1)S(1)} %bitcast.81), channel_id=1, source_target_pairs={{0,8},{1,9},{2,10},{3,11},{4,12},{5,13},{6,14},{7,15},{8,0},{9,1},... | collective-permute-start | bytes 245768 | tf_op jit(solution)/shard_map/ppermute | solution.py:26
  75.4 18.5 %collective-permute-start.13 = (bf16[1,40,1024]{2,1,0:T(8,128)(2,1)S(1)}, bf16[1,40,1024]{2,1,0:T(8,128)(2,1)S(1)}, u32[]{:S(2)}, u32[]{:S(2)}) collective-permute-start(bf16[1,40,1024]{2,1,0:T(8,128)(2,1)S(1)} %bitcast.82), channel_id=1, source_target_pairs={{0,16},{1,17},{2,18},{3,19},{4,20},{5,21},{6,22},{7,23},{8,24},{9,... | collective-permute-start | bytes 245768 | tf_op jit(solution)/shard_map/ppermute | solution.py:26
  78.0 15.8 %collective-permute-start.14 = (bf16[1,40,1024]{2,1,0:T(8,128)(2,1)S(1)}, bf16[1,40,1024]{2,1,0:T(8,128)(2,1)S(1)}, u32[]{:S(2)}, u32[]{:S(2)}) collective-permute-start(bf16[1,40,1024]{2,1,0:T(8,128)(2,1)S(1)} %bitcast.83), channel_id=1, source_target_pairs={{0,24},{1,25},{2,26},{3,27},{4,28},{5,29},{6,30},{7,31},{8,16},{9,... | collective-permute-start | bytes 245768 | tf_op jit(solution)/shard_map/ppermute | solution.py:26
  96.3 28.7 %all-to-all-start = ((bf16[40,32,96]{2,0,1:T(8,128)(2,1)}), bf16[40,32,96]{2,0,1:T(8,128)(2,1)S(1)}, u32[]{:S(2)}, u32[]{:S(2)}) async-start(bf16[40,32,96]{2,0,1:T(8,128)(2,1)} %copy.68), calls=%async_computation | async-start | bytes 655360 | tf_op jit(solution)/shard_map/all_to_all | solution.py:1070
  112.0 13.1 %collective-permute-start.17 = (bf16[2,40,1024]{2,1,0:T(8,128)(2,1)S(1)}, bf16[2,40,1024]{2,1,0:T(8,128)(2,1)S(1)}, u32[]{:S(2)}, u32[]{:S(2)}) collective-permute-start(bf16[2,40,1024]{2,1,0:T(8,128)(2,1)S(1)} %slice.64), channel_id=1, source_target_pairs={{0,4},{1,5},{2,6},{3,7},{4,0},{5,1},{6,2},{7,3},{8,12},{9,13},{10,... | collective-permute-start | bytes 491528 | tf_op jit(solution)/shard_map/ppermute | solution.py:26
  114.0 11.0 %collective-permute-start.18 = (bf16[2,40,1024]{2,1,0:T(8,128)(2,1)S(1)}, bf16[2,40,1024]{2,1,0:T(8,128)(2,1)S(1)}, u32[]{:S(2)}, u32[]{:S(2)}) collective-permute-start(bf16[2,40,1024]{2,1,0:T(8,128)(2,1)S(1)} %slice.65), channel_id=1, source_target_pairs={{0,2},{1,3},{2,0},{3,1},{4,6},{5,7},{6,4},{7,5},{8,10},{9,11},{10,... | collective-permute-start | bytes 491528 | tf_op jit(solution)/shard_map/ppermute | solution.py:26
  127.1 15.9 %all-to-all-start.1 = ((bf16[32,8,768]{2,1,0:T(8,128)(2,1)}), bf16[32,8,768]{2,1,0:T(8,128)(2,1)S(1)}, u32[]{:S(2)}, u32[]{:S(2)}) async-start(bf16[32,8,768]{2,1,0:T(8,128)(2,1)} %broadcast_in_dim.5), calls=%async_computation.1 | async-start | bytes 786432 | tf_op jit(solution)/shard_map/all_to_all | solution.py:46
  165.5 16.1 %collective-permute-start.22 = (bf16[192,1536]{1,0:T(8,128)(2,1)S(1)}, bf16[192,1536]{1,0:T(8,128)(2,1)S(1)}, u32[]{:S(2)}, u32[]{:S(2)}) collective-permute-start(bf16[192,1536]{1,0:T(8,128)(2,1)S(1)} %get-tuple-element.155.refs_1_), channel_id=1, source_target_pairs={{0,2},{1,3},{2,0},{3,1},{4,6},{5,7},{6,4},{7,5},{8,10},{9,11},{10,... | collective-permute-start | bytes 1769480 | tf_op jit(solution)/shard_map/ppermute | solution.py:26
  166.2 15.4 %collective-permute-start.23 = (bf16[192,1536]{1,0:T(8,128)(2,1)S(1)}, bf16[192,1536]{1,0:T(8,128)(2,1)S(1)}, u32[]{:S(2)}, u32[]{:S(2)}) collective-permute-start(bf16[192,1536]{1,0:T(8,128)(2,1)S(1)} %get-tuple-element.157.refs_3_), channel_id=1, source_target_pairs={{0,4},{1,5},{2,6},{3,7},{4,0},{5,1},{6,2},{7,3},{8,12},{9,13},{10,... | collective-permute-start | bytes 1769480 | tf_op jit(solution)/shard_map/ppermute | solution.py:26
  186.1 10.4 %collective-permute-start.26 = (bf16[384,1536]{1,0:T(8,128)(2,1)S(1)}, bf16[384,1536]{1,0:T(8,128)(2,1)S(1)}, u32[]{:S(2)}, u32[]{:S(2)}) collective-permute-start(bf16[384,1536]{1,0:T(8,128)(2,1)S(1)} %get-tuple-element.177), channel_id=1, source_target_pairs={{0,1},{1,0},{2,3},{3,2},{4,5},{5,4},{6,7},{7,6},{8,9},{9,8},{10,11... | collective-permute-start | bytes 3538952 | tf_op jit(solution)/shard_map/ppermute | solution.py:26
  197.2 16.4 %collective-permute-start.29 = (bf16[208,1536]{1,0:T(8,128)(2,1)S(1)}, bf16[208,1536]{1,0:T(8,128)(2,1)S(1)}, u32[]{:S(2)}, u32[]{:S(2)}) collective-permute-start(bf16[208,1536]{1,0:T(8,128)(2,1)S(1)} %get-tuple-element.187), channel_id=1, source_target_pairs={{0,2},{1,3},{2,0},{3,1},{4,6},{5,7},{6,4},{7,5},{8,10},{9,11},{10,... | collective-permute-start | bytes 1916936 | tf_op jit(solution)/shard_map/ppermute | solution.py:26
  198.3 15.2 %collective-permute-start.30 = (bf16[192,1536]{1,0:T(8,128)(2,1)S(1)}, bf16[192,1536]{1,0:T(8,128)(2,1)S(1)}, u32[]{:S(2)}, u32[]{:S(2)}) collective-permute-start(bf16[192,1536]{1,0:T(8,128)(2,1)S(1)} %get-tuple-element.189), channel_id=1, source_target_pairs={{0,4},{1,5},{2,6},{3,7},{4,0},{5,1},{6,2},{7,3},{8,12},{9,13},{10,... | collective-permute-start | bytes 1769480 | tf_op jit(solution)/shard_map/ppermute | solution.py:26
  200.3 13.2 %collective-permute-start.32 = (bf16[24,3072]{1,0:T(8,128)(2,1)S(1)}, bf16[24,3072]{1,0:T(8,128)(2,1)S(1)}, u32[]{:S(2)}, u32[]{:S(2)}) collective-permute-start(bf16[24,3072]{1,0:T(8,128)(2,1)S(1)} %get-tuple-element.191), channel_id=1, source_target_pairs={{0,16},{1,17},{2,18},{3,19},{4,20},{5,21},{6,22},{7,23},{8,24},{9,... | collective-permute-start | bytes 442376 | tf_op jit(solution)/shard_map/ppermute | solution.py:26
  201.2 12.4 %collective-permute-start.33 = (bf16[24,3072]{1,0:T(8,128)(2,1)S(1)}, bf16[24,3072]{1,0:T(8,128)(2,1)S(1)}, u32[]{:S(2)}, u32[]{:S(2)}) collective-permute-start(bf16[24,3072]{1,0:T(8,128)(2,1)S(1)} %get-tuple-element.192), channel_id=1, source_target_pairs={{0,24},{1,25},{2,26},{3,27},{4,28},{5,29},{6,30},{7,31},{8,16},{9,... | collective-permute-start | bytes 442376 | tf_op jit(solution)/shard_map/ppermute | solution.py:26
  224.2 17.1 %collective-permute-start.37 = (bf16[32,3072]{1,0:T(8,128)(2,1)S(1)}, bf16[32,3072]{1,0:T(8,128)(2,1)S(1)}, u32[]{:S(2)}, u32[]{:S(2)}) collective-permute-start(bf16[32,3072]{1,0:T(8,128)(2,1)S(1)} %get-tuple-element.205), channel_id=1, source_target_pairs={{0,16},{1,17},{2,18},{3,19},{4,20},{5,21},{6,22},{7,23},{8,24},{9,... | collective-permute-start | bytes 589832 | tf_op jit(solution)/shard_map/ppermute | solution.py:26
  226.2 15.1 %collective-permute-start.36 = (bf16[32,3072]{1,0:T(8,128)(2,1)S(1)}, bf16[32,3072]{1,0:T(8,128)(2,1)S(1)}, u32[]{:S(2)}, u32[]{:S(2)}) collective-permute-start(bf16[32,3072]{1,0:T(8,128)(2,1)S(1)} %get-tuple-element.204), channel_id=1, source_target_pairs={{0,8},{1,9},{2,10},{3,11},{4,12},{5,13},{6,14},{7,15},{8,0},{9,1},... | collective-permute-start | bytes 589832 | tf_op jit(solution)/shard_map/ppermute | solution.py:26
  (51 other events, 390.1 us)
Sparse Core Ops, SparseCore 0:
  10.9 101.0 all-gather.1

commit v6 on v5

--- a/solution.py
+++ b/solution.py
@@ -107,6 +107,7 @@
 
 VMEM_BYTES = 56 << 20
 TILE = 512
+EARLY = 2 * TILE
 
 
 def norm_parts(values):
@@ -374,10 +375,11 @@
 def image_front_kernel(
     windows, x_ref, order_ref, g1_ref, b1_ref, g2_ref, b2_ref, *refs
 ):
-    h2_ref, sum_ref, w_ref, h1_ref, placed_ref, qkv_ref, att_ref, mid_ref, sems = refs[-9:]
+    h2_ref, sum_ref, early_ref = refs[-10:-7]
+    w_ref, h1_ref, placed_ref, qkv_ref, att_ref, mid_ref, sems = refs[-7:]
     rows, chunk = x_ref.shape[0], 80
     copies, row = [], 0
-    for k, piece in enumerate(refs[:-9]):
+    for k, piece in enumerate(refs[:-10]):
         place = w_ref.at[pl.ds(row, piece.shape[0]), :]
         copies.append(pltpu.make_async_copy(piece, place, sems.at[k]))
         row += piece.shape[0]
@@ -413,6 +415,16 @@
         mid_ref[:, at] = x_ref[:, at].astype(f32) + mul(placed_ref[...], w_ref[:, there])
 
     norm_rows(mid_ref, h2_ref, line(g2_ref), line(b2_ref), chunk)
+    place_columns(h2_ref, placed_ref)
+    pool = pool_matrix(rows // IMG_LEN, rows, 0, IMG_LEN)
+
+    @pl.loop(0, EARLY // TILE)
+    def _(step):
+        at = pl.ds(pl.multiple_of(step * TILE, TILE), TILE)
+        there = pl.ds(pl.multiple_of(step * TILE + 4 * D, TILE), TILE)
+        value, _ = gelu_parts(mul(placed_ref[...], w_ref[:, there]))
+        early_ref[:, at] = mul(pool, value.astype(bf16))
+
     for k in range(rows // IMG_LEN):
         first, last = k * IMG_LEN, (k + 1) * IMG_LEN
         start, end = first // 8 * 8, -(-last // 8) * 8
@@ -431,11 +443,12 @@
         out_shape=[
             jax.ShapeDtypeStruct((rows, D), bf16),
             jax.ShapeDtypeStruct((rows // IMG_LEN, D), f32),
+            jax.ShapeDtypeStruct((rows // IMG_LEN, EARLY), f32),
         ],
         in_specs=[vmem] * 6 + anywhere(pieces),
-        out_specs=[vmem] * 2,
+        out_specs=[vmem] * 3,
         scratch_shapes=[
-            pltpu.VMEM((D, 4 * D), bf16),
+            pltpu.VMEM((D, 4 * D + EARLY), bf16),
             pltpu.VMEM((rows, D), bf16),
             pltpu.VMEM((rows, D), bf16),
             pltpu.VMEM((rows, 3 * D), bf16),
@@ -550,62 +563,62 @@
     )(normed2, weight_up, weight_down, middle_sum, *after)
 
 
-def image_up_kernel(fold, h2_ref, wu_ref, wd_ref, sum_ref, *refs):
-    out_ref, acc, chosen_ref = refs[-3:]
+def image_up_kernel(fold, h2_ref, wu_ref, wd_ref, first_ref, sum_ref, early_ref, out_ref, acc, picked):
     step = pl.program_id(0)
     rows, count = h2_ref.shape[0], sum_ref.shape[0]
     part = TILE // fold
+
+    def through_down(summed, groups):
+        moved = mul(two_terms(summed * (1.0 / IMG_LEN)), picked[...]).astype(bf16)
+        weight = jnp.concatenate([groups[:, k * D : (k + 1) * D] for k in range(fold)], axis=0)
+        terms = mul(moved, weight)
+        return terms[:count] + terms[count:]
 
     @pl.when(step == 0)
     def _():
         place = lax.broadcasted_iota(jnp.int32, (TILE, TILE), 0)
         col = lax.broadcasted_iota(jnp.int32, (TILE, TILE), 1)
         source = (col % part) * fold + col // part
-        chosen_ref[...] = jnp.where(place == source, 1.0, 0.0).astype(bf16)
-
-    inner = mul(h2_ref[...], wu_ref[...])
-    value, _ = gelu_parts(inner)
+        picked[...] = jnp.where(place == source, 1.0, 0.0).astype(bf16)
+        total = sum_ref[...] * (1.0 / IMG_LEN)
+        for k in range(EARLY // TILE):
+            total = total + through_down(
+                early_ref[:, k * TILE : (k + 1) * TILE], first_ref[k * part : (k + 1) * part, :]
+            )
+        acc[...] = total
+
+    value, _ = gelu_parts(mul(h2_ref[...], wu_ref[...]))
     summed = mul(pool_matrix(count, rows, 0, IMG_LEN), value.astype(bf16))
-    mean = two_terms(summed * (1.0 / IMG_LEN))
-    moved = mul(mean, chosen_ref[...]).astype(bf16)
-    weight = jnp.concatenate([wd_ref[:, k * D : (k + 1) * D] for k in range(fold)], axis=0)
-    terms = mul(moved, weight)
-    added = terms[:count] + terms[count:]
-
-    @pl.when(step == 0)
-    def _():
-        acc[...] = sum_ref[...] * (1.0 / IMG_LEN) + added
-
-    @pl.when(step > 0)
-    def _():
-        acc[...] += added
+    acc[...] += through_down(summed, wd_ref[...])
 
     @pl.when(step == pl.num_programs(0) - 1)
     def _():
         out_ref[...] = unit_rows(acc[...])[0].astype(bf16)
 
 
-def image_up(normed2, whole, up_col, down_col, middle_sum, after=()):
+def image_up(normed2, whole, middle_sum, early):
     rows, count = normed2.shape[0], middle_sum.shape[0]
     fold = FF // D
+    before, part = EARLY // TILE, TILE // fold
     fixed = lambda shape: pl.BlockSpec(shape, lambda i: (0, 0))
     return pl.pallas_call(
         functools.partial(image_up_kernel, fold),
-        grid=(FF // TILE,),
+        grid=(FF // TILE - before,),
         out_shape=jax.ShapeDtypeStruct((count, D), bf16),
         in_specs=[
             fixed((rows, D)),
-            pl.BlockSpec((D, TILE), lambda i: (0, up_col // TILE + i)),
-            pl.BlockSpec((TILE // fold, fold * D), lambda i: (i, down_col // (fold * D))),
+            pl.BlockSpec((D, TILE), lambda i: (0, FF // TILE + i)),
+            pl.BlockSpec((part, FF), lambda i: (i + before, 0)),
+            fixed((before * part, FF)),
             fixed((count, D)),
-        ]
-        + anywhere(after),
+            fixed((count, EARLY)),
+        ],
         out_specs=fixed((count, D)),
         scratch_shapes=[pltpu.VMEM((count, D), f32), pltpu.VMEM((TILE, TILE), bf16)],
         compiler_params=params(),
         cost_estimate=cost(2 * rows * D * FF, 4 * D * FF, 15 * rows * FF),
         name="image_up",
-    )(normed2, whole, whole, middle_sum, *after)
+    )(normed2, whole, whole, whole, middle_sum, early)
 
 
 def left_kernel(count, *refs):
@@ -1011,14 +1024,17 @@
     cap_local = matches.shape[0]
     total_images = matches.shape[1]
 
+    up_rows = img_up.reshape(per, FF)
     whole = lax.all_gather(
-        jnp.concatenate([img_up.reshape(per, FF), img_down.reshape(per, FF)], axis=1),
+        jnp.concatenate([img_down.reshape(per, FF), up_rows[:, EARLY:]], axis=1),
         AXIS,
         axis=0,
         tiled=True,
     )
     small = peers == 32
-    shard = jnp.concatenate([img_qkv.reshape(per, 3 * D), img_out.reshape(per, D)], axis=1)
+    shard = jnp.concatenate(
+        [img_qkv.reshape(per, 3 * D), img_out.reshape(per, D), up_rows[:, :EARLY]], axis=1
+    )
     if small:
         line, source = gathered_line(shard), row_order((1, 4, 2, 16, 8))
     else:
@@ -1059,7 +1075,7 @@
         pieces = [line, beside, above, first, second]
         pieces = pieces + [swapped(piece, 1) for piece in pieces]
 
-    normed_img, middle_img = image_front(
+    normed_img, middle_img, early = image_front(
         images, pieces, source, img_gain1, img_bias1, img_gain2, img_bias2
     )
     if small:
@@ -1070,7 +1086,7 @@
         hidden_cols = lax.all_to_all(scaled_sum, AXIS, split_axis=1, concat_axis=0, tiled=True)
         whole, text_beside, text_above = lax.optimization_barrier((whole, text_beside, text_above))
         halves = diagonal(text_beside, text_above)
-    image_low = image_up(normed_img, whole, 0, FF, middle_img)
+    image_low = image_up(normed_img, whole, middle_img, early)
     if small:
         image_low, halves, hidden_cols = lax.optimization_barrier((image_low, halves, hidden_cols))
         across = jnp.concatenate(halves, axis=0)

time: 251 us -> 258 us (1.028)
  waiting for transfers between devices: 55.2 us -> 63.8 us
  starting transfers between devices: 49.3 us -> 46.1 us
    ppermute x39, waiting for transfers between devices: 34.3 us -> 51.2 us  [swapped(): return lax.ppermute(value, AXIS, [(i, i ^ mask) for i in range(peers)])]
    all_gather x1, waiting for transfers between devices: 8.29 us -> 0.01 us  [local(): lax.all_gather(jnp.concatenate([img_down.reshape(per, FF), up_rows[:, EAR...]
    pallas_call x1, Pallas kernels: 14 us -> 16.9 us  [image_front(): pl.pallas_call(functools.partial(image_front_kernel, windows), out_shape=...]
  transfers between devices with their start and end apart: 42 -> 42, of which waited for: 13 -> 16; matrix products, arithmetic and copies ran while one was open for 5% -> 5% of each run, Pallas kernels for 35% -> 34%
where the time goes in v6:
time: 258 us; the launch traced here: 257 us
  Pallas kernels  111 us (43%)
  waiting for transfers between devices  63.8 us (25%)
  starting transfers between devices  46.1 us (18%)
  local copies, waits for them, and re-layouts  16 us (6%)
  between operations  14.9 us (6%)
  other arithmetic  5.44 us (2%)
    ppermute x39, waiting for transfers between devices, swapped(): return lax.ppermute(value, AXIS, [(i, i ^ mask) for i in range(peers)])  51.2 us
    ppermute x39, starting transfers between devices, swapped(): return lax.ppermute(value, AXIS, [(i, i ^ mask) for i in range(peers)])  38.7 us
    pallas_call x1, Pallas kernels, text_front(): pl.pallas_call(text_front_kernel, out_shape=[jax.ShapeDtypeStruct(*item)...  18 us
    pallas_call x1, Pallas kernels, image_front(): pl.pallas_call(functools.partial(image_front_kernel, windows), out_shape=...  16.9 us
    pallas_call x1, Pallas kernels, mlp_back(): pl.pallas_call(mlp_back_kernel, out_shape=[stays((D // 2, FF // 2), bf16)...  14.8 us
    all_to_all x1, waiting for transfers between devices, spread(): return lax.all_to_all(copies, AXIS, split_axis=0, concat_axis=0, tiled=True)  12.6 us
    pallas_call x1, Pallas kernels, text_up(): pl.pallas_call(text_up_kernel, grid=(FF // TILE,), out_shape=[jax.ShapeDt...  12 us
    pallas_call x2, Pallas kernels, attention_back(): pl.pallas_call(functools.partial(attention_back_kernel, first), out_shape...  11.5 us
  transfers between devices with their start and end apart: 42, of which 16 were waited for; matrix products, arithmetic and copies ran while one was open for 5% of the time, Pallas kernels for 34%

profile of v6, /device:TPU:0, one launch (start us, length us, event | category | flops | bytes accessed | tf_op | source)
XLA Modules:
  0.0 257.4 jit_solution(18417569531196046119)
XLA Ops:
  10.3 5.1 %collective-permute-start.2 = (bf16[24,4096]{1,0:T(8,128)(2,1)S(1)}, bf16[24,4096]{1,0:T(8,128)(2,1)S(1)}, u32[]{:S(2)}, u32[]{:S(2)}) collective-permute-start(bf16[24,4096]{1,0:T(8,128)(2,1)S(1)} %pad_maximum_fusion.7), channel_id=1, source_target_pairs={{0,24},{1,25},{2,26},{3,27},{4,28},{5,29},{6,30},{7,31},{8,16},{9,... | collective-permute-start | bytes 589832 | tf_op jit(solution)/shard_map/ppermute | solution.py:26
  16.0 18.0 %text_front.1 = (bf16[640,768]{1,0:T(8,128)(2,1)}, bf16[640,2304]{1,0:T(8,128)(2,1)}, bf16[640,768]{1,0:T(8,128)(2,1)}, f32[640,768]{1,0:T(8,128)}, bf16[640,768...) custom-call(bf16[640,768]{1,0:T(8,128)(2,1)} %refs_3_.1, f32[768]{0:T(1024)} %refs_4_.1, f32[768]{0:T(1024)} %b1_ref.2, ...), custom_call_target="tpu_custom_call" | custom-call | flops 3019898880 | bytes 11599872 | tf_op jit(solution)/shard_map/text_front/pallas_call | solution.py:366
  42.7 12.0 %text_up.1 = (bf16[640,3072]{1,0:T(8,128)(2,1)}, f32[40,3072]{1,0:T(8,128)}, f32[40,768]{1,0:T(8,128)}, f32[40,128]{1,0:T(8,128)}) custom-call(bf16[640,768]{1,0:T(8,128)(2,1)} %get-tuple-element.120.h2_ref.refs_1_.refs_3_, bf16[768,3072]{1,0:T(8,128)(2,1)} %wu_hbm.1, bf16[3072,768]{1,0:T(8,128)(2,1)} %wd_hbm.1, f32[40,768]{1,0:T(8,128)} %get-tuple-element.115.sum_ref, ...), custom_call_target="tpu_custom_call" | custom-call | flops 3019898880 | bytes 13369344 | tf_op jit(solution)/shard_map/text_up/pallas_call | solution.py:537
  54.7 9.1 %collective-permute-done.3.refs_1_ = bf16[96,4096]{1,0:T(8,128)(2,1)} collective-permute-done((bf16[96,4096]{1,0:T(8,128)(2,1)}, bf16[96,4096]{1,0:T(8,128)(2,1)}, u32[]{:S(2)}, u32[]{:S(2)}) %collective-permute-start.3) | collective-permute-done | bytes 786464 | tf_op jit(solution)/shard_map/ppermute | solution.py:26
  74.9 3.2 %left_factors.2.lhs_hbm = bf16[2,768,640]{2,1,0:T(8,128)(2,1)S(1)} custom-call(s32[768,1]{1,0:T(8,128)S(1)} %fusion.8.refs_0_, bf16[640,768]{1,0:T(8,128)(2,1)S(1)} %copy-done.19, s32[768,1]{1,0:T(8,128)S(1)} %fusion.9.refs_2_.order_ref.refs_4_, bf16[640,768]{1,0:T(8,128)(2,1)S(1)} %copy-done.19), custom_call_target="tpu_custom_call" | custom-call | flops 1509949440 | bytes 3932160 | tf_op jit(solution)/shard_map/left_factors/pallas_call | solution.py:639
  78.2 3.5 %collective-permute-done.5.refs_3_ = bf16[48,4096]{1,0:T(8,128)(2,1)} collective-permute-done((bf16[48,4096]{1,0:T(8,128)(2,1)}, bf16[48,4096]{1,0:T(8,128)(2,1)}, u32[]{:S(2)}, u32[]{:S(2)}) %collective-permute-start.5) | collective-permute-done | bytes 393248 | tf_op jit(solution)/shard_map/ppermute | solution.py:26
  81.7 5.3 %collective-permute-done.6.refs_4_ = bf16[48,4096]{1,0:T(8,128)(2,1)} collective-permute-done((bf16[48,4096]{1,0:T(8,128)(2,1)}, bf16[48,4096]{1,0:T(8,128)(2,1)}, u32[]{:S(2)}, u32[]{:S(2)}) %collective-permute-start.6) | collective-permute-done | bytes 393248 | tf_op jit(solution)/shard_map/ppermute | solution.py:26
  87.7 2.6 %collective-permute-start.13 = (bf16[1,40,1024]{2,1,0:T(8,128)(2,1)S(1)}, bf16[1,40,1024]{2,1,0:T(8,128)(2,1)S(1)}, u32[]{:S(2)}, u32[]{:S(2)}) collective-permute-start(bf16[1,40,1024]{2,1,0:T(8,128)(2,1)S(1)} %bitcast.82), channel_id=1, source_target_pairs={{0,16},{1,17},{2,18},{3,19},{4,20},{5,21},{6,22},{7,23},{8,24},{9,... | collective-permute-start | bytes 245768 | tf_op jit(solution)/shard_map/ppermute | solution.py:26
  93.6 16.9 %image_front.1 = (bf16[400,768]{1,0:T(8,128)(2,1)}, f32[8,768]{1,0:T(8,128)}, f32[8,1024]{1,0:T(8,128)}) custom-call(bf16[400,768]{1,0:T(8,128)(2,1)} %x_ref.3, s32[768,1]{1,0:T(8,128)} %copy-done.9, bf16[768]{0:T(1024)(128)(2,1)} %g1_ref.3, bf16[768]{0:T(1024)(128)(2,1)} %b1_ref.3, bf16[768]{0:T(1024)(128)(2,1)} %g2_ref.3, bf16[768]{0:T(1024)(128)(2,1)} %b2_ref.3, ...), custom_call_target="tpu_custom_call" | custom-call | flops 2831155200 | bytes 4718592 | tf_op jit(solution)/shard_map/image_front/pallas_call | solution.py:441
  114.4 3.6 %all-to-all-start = ((bf16[40,32,96]{2,0,1:T(8,128)(2,1)}), bf16[40,32,96]{2,0,1:T(8,128)(2,1)S(1)}, u32[]{:S(2)}, u32[]{:S(2)}) async-start(bf16[40,32,96]{2,0,1:T(8,128)(2,1)} %copy.68), calls=%async_computation | async-start | bytes 655360 | tf_op jit(solution)/shard_map/all_to_all | solution.py:1086
  123.1 8.0 %image_up.1 = bf16[8,768]{1,0:T(8,128)(2,1)} custom-call(bf16[400,768]{1,0:T(8,128)(2,1)} %get-tuple-element.127.h2_ref, bf16[768,5120]{1,0:T(8,128)(2,1)} %all-gather.2.cloned.1.call-done.wu_ref.wd_ref.first_ref, bf16[768,5120]{1,0:T(8,128)(2,1)} %all-gather.2.cloned.1.call-done.wu_ref.wd_ref.first_ref, ...), custom_call_target="tpu_custom_call" | custom-call | flops 1887436800 | bytes 9437184 | tf_op jit(solution)/shard_map/image_up/pallas_call | solution.py:604
  133.1 3.8 %all-to-all-start.1 = ((bf16[32,8,768]{2,1,0:T(8,128)(2,1)}), bf16[32,8,768]{2,1,0:T(8,128)(2,1)S(1)}, u32[]{:S(2)}, u32[]{:S(2)}) async-start(bf16[32,8,768]{2,1,0:T(8,128)(2,1)} %broadcast_in_dim.5), calls=%async_computation.1 | async-start | bytes 786432 | tf_op jit(solution)/shard_map/all_to_all | solution.py:46
  137.5 12.6 %all-to-all-done.1 = bf16[32,8,768]{2,1,0:T(8,128)(2,1)S(1)} async-done(((bf16[32,8,768]{2,1,0:T(8,128)(2,1)}), bf16[32,8,768]{2,1,0:T(8,128)(2,1)S(1)}, u32[]{:S(2)}, u32[]{:S(2)}) %all-to-all-start.1) | async-done | bytes 393248 | tf_op jit(solution)/shard_map/all_to_all | solution.py:46
  152.7 14.8 %mlp_back.1 = (bf16[384,1536]{1,0:T(8,128)(2,1)S(1)}, bf16[384,1536]{1,0:T(8,128)(2,1)S(1)}, bf16[384,1536]{1,0:T(8,128)(2,1)S(1)}, bf16[384,1536]{1,0:T(8,128)(...) custom-call(bf16[40,768]{1,0:T(8,128)(2,1)S(1)} %get-tuple-element.143.low_ref, f32[768]{0:T(1024)S(1)} %copy-done.17, ...), custom_call_target="tpu_custom_call" | custom-call | flops 6039797760 | bytes 18087936 | tf_op jit(solution)/shard_map/mlp_back/pallas_call | solution.py:853
  174.7 9.2 %attention_back.3 = (bf16[512,768]{1,0:T(8,128)(2,1)S(1)}, bf16[512,2304]{1,0:T(8,128)(2,1)S(1)}) custom-call(f32[640,768]{1,0:T(8,128)S(1)} %get-tuple-element.148.grad_ref.refs_5_, bf16[768,768]{1,0:T(8,128)(2,1)S(1)} %copy-done.3, bf16[640,2304]{1,0:T(8,128)(2,1)S(1)} %copy-done.1, f32[80,128]{1,0:T(8,128)S(1)} %copy-done.15, ...), custom_call_target="tpu_custom_call" | custom-call | flops 3019898880 | bytes 7471104 | tf_op jit(solution)/shard_map/attention_back/pallas_call | solution.py:912
  183.9 4.8 %left_factors.3.refs_1_.lhs_ref = bf16[3,768,640]{2,1,0:T(8,128)(2,1)S(1)} custom-call(s32[768,1]{1,0:T(8,128)S(1)} %copy-done.12, bf16[640,768]{1,0:T(8,128)(2,1)S(1)} %copy-done.20, s32[768,1]{1,0:T(8,128)S(1)} %copy-done.10, bf16[640,768]{1,0:T(8,128)(2,1)S(1)} %copy-done.20, s32[768,1]{1,0:T(8,128)S(1)} %copy-done.10, bf16[640,768]{1,0:T(8,128)(2,1)S(1)} %copy-done.21), custom_call_target="tpu_custom_call" | custom-call | flops 2264924160 | bytes 5898240 | tf_op jit(solution)/shard_map/left_factors/pallas_call | solution.py:639
  189.4 3.9 %weight_back.1 = (bf16[384,1536]{1,0:T(8,128)(2,1)S(1)}, bf16[384,1536]{1,0:T(8,128)(2,1)S(1)}, bf16[384,1536]{1,0:T(8,128)(2,1)S(1)}, bf16[384,1536]{1,0:T(8,128)(2,1)S(1)}) custom-call(bf16[3,768,640]{2,1,0:T(8,128)(2,1)S(1)} %left_factors.3.refs_1_.lhs_ref, bf16[128,2304]{1,0:T(8,128)(2,1)S(1)} %get-tuple-element.151.refs_0_, ...), custom_call_target="tpu_custom_call" | custom-call | flops 3019898880 | bytes 12189696 | tf_op jit(solution)/shard_map/weight_back/pallas_call | solution.py:945
  196.0 6.5 %input_back.1 = (f32[640,768]{1,0:T(8,128)}, f32[8,1536]{1,0:T(8,128)S(1)}) custom-call(bf16[128,2304]{1,0:T(8,128)(2,1)S(1)} %get-tuple-element.151.refs_0_, bf16[512,2304]{1,0:T(8,128)(2,1)S(1)} %get-tuple-element.162.refs_0_.refs_1_, bf16[768,2304]{1,0:T(8,128)(2,1)S(1)} %copy-done, bf16[640,768]{1,0:T(8,128)(2,1)S(1)} %copy-done.6, f32[768]{0:T(1024)S(1)} %copy-done.16, ...), custom_call_target="tpu_custom_call" | custom-call | flops 2264924160 | bytes 10420224 | tf_op jit(solution)/shard_map/input_back/pallas_call | solution.py:987
  208.3 2.6 collective-permute-start.33
  210.9 5.9 %grad_of_down.1 = f32[96,768]{1,0:T(8,128)S(1)} custom-call(bf16[1280,1024]{1,0:T(8,128)(2,1)S(1)} %bitcast.77, bf16[256,768]{1,0:T(8,128)(2,1)S(1)} %bitcast.79, f32[1,256]{1,0:T(1,128)S(1)} %get-tuple-element.175.col_sum_ref, f32[1,256]{1,0:T(1,128)S(1)} %get-tuple-element.176.col_count_ref, f32[1,128]{1,0:T(1,128)S(1)} %get-tuple-element.177.live_ref, ...), custom_call_target="tpu_custom_call" | custom-call | flops 1006632960 | bytes 2621440 | tf_op jit(solution)/shard_map/grad_of_down/pallas_call | solution.py:755
  216.7 3.9 %collective-permute-done.32 = bf16[24,3072]{1,0:T(8,128)(2,1)S(1)} collective-permute-done((bf16[24,3072]{1,0:T(8,128)(2,1)S(1)}, bf16[24,3072]{1,0:T(8,128)(2,1)S(1)}, u32[]{:S(2)}, u32[]{:S(2)}) %collective-permute-start.32) | collective-permute-done | bytes 147488 | tf_op jit(solution)/shard_map/ppermute | solution.py:26
  223.1 6.7 %collective-permute-done.35.got_b = bf16[96,1536]{1,0:T(8,128)(2,1)S(1)} collective-permute-done((bf16[96,1536]{1,0:T(8,128)(2,1)S(1)}, bf16[96,1536]{1,0:T(8,128)(2,1)S(1)}, u32[]{:S(2)}, u32[]{:S(2)}) %collective-permute-start.35) | collective-permute-done | bytes 294944 | tf_op jit(solution)/shard_map/ppermute | solution.py:26
  236.5 3.7 %collective-permute-done.38 = bf16[32,3072]{1,0:T(8,128)(2,1)S(1)} collective-permute-done((bf16[32,3072]{1,0:T(8,128)(2,1)S(1)}, bf16[32,3072]{1,0:T(8,128)(2,1)S(1)}, u32[]{:S(2)}, u32[]{:S(2)}) %collective-permute-start.38) | collective-permute-done | bytes 196640 | tf_op jit(solution)/shard_map/ppermute | solution.py:26
  240.2 8.3 %collective-permute-done.37 = bf16[32,3072]{1,0:T(8,128)(2,1)S(1)} collective-permute-done((bf16[32,3072]{1,0:T(8,128)(2,1)S(1)}, bf16[32,3072]{1,0:T(8,128)(2,1)S(1)}, u32[]{:S(2)}, u32[]{:S(2)}) %collective-permute-start.37) | collective-permute-done | bytes 196640 | tf_op jit(solution)/shard_map/ppermute | solution.py:26
  (196 shorter events, 68.5 us)
Async XLA Ops:
  7.2 115.6 %all-gather.2.cloned.1.call-start = ((), (), s32[]{:S(2)}) async-start(), calls=%async_computation.2 | async-start | bytes 8110080 | tf_op jit(solution)/shard_map/all_gather | solution.py:1028
  10.3 24.6 %collective-permute-start.2 = (bf16[24,4096]{1,0:T(8,128)(2,1)S(1)}, bf16[24,4096]{1,0:T(8,128)(2,1)S(1)}, u32[]{:S(2)}, u32[]{:S(2)}) collective-permute-start(bf16[24,4096]{1,0:T(8,128)(2,1)S(1)} %pad_maximum_fusion.7), channel_id=1, source_target_pairs={{0,24},{1,25},{2,26},{3,27},{4,28},{5,29},{6,30},{7,31},{8,16},{9,... | collective-permute-start | bytes 589832 | tf_op jit(solution)/shard_map/ppermute | solution.py:26
  15.4 22.0 %collective-permute-start.1 = (bf16[24,4096]{1,0:T(8,128)(2,1)S(1)}, bf16[24,4096]{1,0:T(8,128)(2,1)S(1)}, u32[]{:S(2)}, u32[]{:S(2)}) collective-permute-start(bf16[24,4096]{1,0:T(8,128)(2,1)S(1)} %pad_maximum_fusion.7), channel_id=1, source_target_pairs={{0,16},{1,17},{2,18},{3,19},{4,20},{5,21},{6,22},{7,23},{8,24},{9,... | collective-permute-start | bytes 589832 | tf_op jit(solution)/shard_map/ppermute | solution.py:26
  15.4 22.0 %collective-permute-start = (bf16[24,4096]{1,0:T(8,128)(2,1)S(1)}, bf16[24,4096]{1,0:T(8,128)(2,1)S(1)}, u32[]{:S(2)}, u32[]{:S(2)}) collective-permute-start(bf16[24,4096]{1,0:T(8,128)(2,1)S(1)} %pad_maximum_fusion.7), channel_id=1, source_target_pairs={{0,8},{1,9},{2,10},{3,11},{4,12},{5,13},{6,14},{7,15},{8,0},{9,1},... | collective-permute-start | bytes 589832 | tf_op jit(solution)/shard_map/ppermute | solution.py:26
  38.3 25.5 %collective-permute-start.3 = (bf16[96,4096]{1,0:T(8,128)(2,1)}, bf16[96,4096]{1,0:T(8,128)(2,1)}, u32[]{:S(2)}, u32[]{:S(2)}) collective-permute-start(bf16[96,4096]{1,0:T(8,128)(2,1)} %pad_maximum_fusion.2.refs_0_), channel_id=1, source_target_pairs={{0,2},{1,3},{2,0},{3,1},{4,6},{5,7},{6,4},{7,5},{8,10},{9,11},{10,... | collective-permute-start | bytes 2359304 | tf_op jit(solution)/shard_map/ppermute | solution.py:26
  39.8 24.0 %collective-permute-start.4 = (bf16[96,4096]{1,0:T(8,128)(2,1)}, bf16[96,4096]{1,0:T(8,128)(2,1)}, u32[]{:S(2)}, u32[]{:S(2)}) collective-permute-start(bf16[96,4096]{1,0:T(8,128)(2,1)} %pad_maximum_fusion.2.refs_0_), channel_id=1, source_target_pairs={{0,4},{1,5},{2,6},{3,7},{4,0},{5,1},{6,2},{7,3},{8,12},{9,13},{10,... | collective-permute-start | bytes 2359304 | tf_op jit(solution)/shard_map/ppermute | solution.py:26
  65.5 16.2 %collective-permute-start.5 = (bf16[48,4096]{1,0:T(8,128)(2,1)}, bf16[48,4096]{1,0:T(8,128)(2,1)}, u32[]{:S(2)}, u32[]{:S(2)}) collective-permute-start(bf16[48,4096]{1,0:T(8,128)(2,1)} %slice.68), channel_id=1, source_target_pairs={{0,4},{1,5},{2,6},{3,7},{4,0},{5,1},{6,2},{7,3},{8,12},{9,13},{10,... | collective-permute-start | bytes 1179656 | tf_op jit(solution)/shard_map/ppermute | solution.py:26
  69.1 17.9 %collective-permute-start.6 = (bf16[48,4096]{1,0:T(8,128)(2,1)}, bf16[48,4096]{1,0:T(8,128)(2,1)}, u32[]{:S(2)}, u32[]{:S(2)}) collective-permute-start(bf16[48,4096]{1,0:T(8,128)(2,1)} %slice.69), channel_id=1, source_target_pairs={{0,2},{1,3},{2,0},{3,1},{4,6},{5,7},{6,4},{7,5},{8,10},{9,11},{10,... | collective-permute-start | bytes 1179656 | tf_op jit(solution)/shard_map/ppermute | solution.py:26
  71.3 16.3 %collective-permute-start.7 = (bf16[96,4096]{1,0:T(8,128)(2,1)}, bf16[96,4096]{1,0:T(8,128)(2,1)S(1)}, u32[]{:S(2)}, u32[]{:S(2)}) collective-permute-start(bf16[96,4096]{1,0:T(8,128)(2,1)} %pad_maximum_fusion.2.refs_0_), channel_id=1, source_target_pairs={{0,1},{1,0},{2,3},{3,2},{4,5},{5,4},{6,7},{7,6},{8,9},{9,8},{10,11... | collective-permute-start | bytes 2359304 | tf_op jit(solution)/shard_map/ppermute | solution.py:26
  71.5 16.2 %collective-permute-start.8 = (bf16[96,4096]{1,0:T(8,128)(2,1)}, bf16[96,4096]{1,0:T(8,128)(2,1)S(1)}, u32[]{:S(2)}, u32[]{:S(2)}) collective-permute-start(bf16[96,4096]{1,0:T(8,128)(2,1)} %collective-permute-done.3.refs_1_), channel_id=1, source_target_pairs={{0,1},{1,0},{2,3},{3,2},{4,5},{5,4},{6,7},{7,6},{8,9},{9,8},{10,11... | collective-permute-start | bytes 2359304 | tf_op jit(solution)/shard_map/ppermute | solution.py:26
  72.1 18.3 %collective-permute-start.9 = (bf16[96,4096]{1,0:T(8,128)(2,1)}, bf16[96,4096]{1,0:T(8,128)(2,1)S(1)}, u32[]{:S(2)}, u32[]{:S(2)}) collective-permute-start(bf16[96,4096]{1,0:T(8,128)(2,1)} %collective-permute-done.4.refs_2_), channel_id=1, source_target_pairs={{0,1},{1,0},{2,3},{3,2},{4,5},{5,4},{6,7},{7,6},{8,9},{9,8},{10,11... | collective-permute-start | bytes 2359304 | tf_op jit(solution)/shard_map/ppermute | solution.py:26
  87.6 22.9 %collective-permute-start.12 = (bf16[1,40,1024]{2,1,0:T(8,128)(2,1)S(1)}, bf16[1,40,1024]{2,1,0:T(8,128)(2,1)S(1)}, u32[]{:S(2)}, u32[]{:S(2)}) collective-permute-start(bf16[1,40,1024]{2,1,0:T(8,128)(2,1)S(1)} %bitcast.81), channel_id=1, source_target_pairs={{0,8},{1,9},{2,10},{3,11},{4,12},{5,13},{6,14},{7,15},{8,0},{9,1},... | collective-permute-start | bytes 245768 | tf_op jit(solution)/shard_map/ppermute | solution.py:26
  87.7 22.8 %collective-permute-start.13 = (bf16[1,40,1024]{2,1,0:T(8,128)(2,1)S(1)}, bf16[1,40,1024]{2,1,0:T(8,128)(2,1)S(1)}, u32[]{:S(2)}, u32[]{:S(2)}) collective-permute-start(bf16[1,40,1024]{2,1,0:T(8,128)(2,1)S(1)} %bitcast.82), channel_id=1, source_target_pairs={{0,16},{1,17},{2,18},{3,19},{4,20},{5,21},{6,22},{7,23},{8,24},{9,... | collective-permute-start | bytes 245768 | tf_op jit(solution)/shard_map/ppermute | solution.py:26
  90.4 20.2 %collective-permute-start.14 = (bf16[1,40,1024]{2,1,0:T(8,128)(2,1)S(1)}, bf16[1,40,1024]{2,1,0:T(8,128)(2,1)S(1)}, u32[]{:S(2)}, u32[]{:S(2)}) collective-permute-start(bf16[1,40,1024]{2,1,0:T(8,128)(2,1)S(1)} %bitcast.83), channel_id=1, source_target_pairs={{0,24},{1,25},{2,26},{3,27},{4,28},{5,29},{6,30},{7,31},{8,16},{9,... | collective-permute-start | bytes 245768 | tf_op jit(solution)/shard_map/ppermute | solution.py:26
  114.4 16.7 %all-to-all-start = ((bf16[40,32,96]{2,0,1:T(8,128)(2,1)}), bf16[40,32,96]{2,0,1:T(8,128)(2,1)S(1)}, u32[]{:S(2)}, u32[]{:S(2)}) async-start(bf16[40,32,96]{2,0,1:T(8,128)(2,1)} %copy.68), calls=%async_computation | async-start | bytes 655360 | tf_op jit(solution)/shard_map/all_to_all | solution.py:1086
  133.1 17.0 %all-to-all-start.1 = ((bf16[32,8,768]{2,1,0:T(8,128)(2,1)}), bf16[32,8,768]{2,1,0:T(8,128)(2,1)S(1)}, u32[]{:S(2)}, u32[]{:S(2)}) async-start(bf16[32,8,768]{2,1,0:T(8,128)(2,1)} %broadcast_in_dim.5), calls=%async_computation.1 | async-start | bytes 786432 | tf_op jit(solution)/shard_map/all_to_all | solution.py:46
  172.7 16.1 %collective-permute-start.22 = (bf16[192,1536]{1,0:T(8,128)(2,1)S(1)}, bf16[192,1536]{1,0:T(8,128)(2,1)S(1)}, u32[]{:S(2)}, u32[]{:S(2)}) collective-permute-start(bf16[192,1536]{1,0:T(8,128)(2,1)S(1)} %get-tuple-element.157.refs_1_), channel_id=1, source_target_pairs={{0,2},{1,3},{2,0},{3,1},{4,6},{5,7},{6,4},{7,5},{8,10},{9,11},{10,... | collective-permute-start | bytes 1769480 | tf_op jit(solution)/shard_map/ppermute | solution.py:26
  173.4 15.5 %collective-permute-start.23 = (bf16[192,1536]{1,0:T(8,128)(2,1)S(1)}, bf16[192,1536]{1,0:T(8,128)(2,1)S(1)}, u32[]{:S(2)}, u32[]{:S(2)}) collective-permute-start(bf16[192,1536]{1,0:T(8,128)(2,1)S(1)} %get-tuple-element.159.refs_3_), channel_id=1, source_target_pairs={{0,4},{1,5},{2,6},{3,7},{4,0},{5,1},{6,2},{7,3},{8,12},{9,13},{10,... | collective-permute-start | bytes 1769480 | tf_op jit(solution)/shard_map/ppermute | solution.py:26
  204.3 16.4 %collective-permute-start.29 = (bf16[208,1536]{1,0:T(8,128)(2,1)S(1)}, bf16[208,1536]{1,0:T(8,128)(2,1)S(1)}, u32[]{:S(2)}, u32[]{:S(2)}) collective-permute-start(bf16[208,1536]{1,0:T(8,128)(2,1)S(1)} %get-tuple-element.189), channel_id=1, source_target_pairs={{0,2},{1,3},{2,0},{3,1},{4,6},{5,7},{6,4},{7,5},{8,10},{9,11},{10,... | collective-permute-start | bytes 1916936 | tf_op jit(solution)/shard_map/ppermute | solution.py:26
  205.5 15.2 %collective-permute-start.30 = (bf16[192,1536]{1,0:T(8,128)(2,1)S(1)}, bf16[192,1536]{1,0:T(8,128)(2,1)S(1)}, u32[]{:S(2)}, u32[]{:S(2)}) collective-permute-start(bf16[192,1536]{1,0:T(8,128)(2,1)S(1)} %get-tuple-element.191), channel_id=1, source_target_pairs={{0,4},{1,5},{2,6},{3,7},{4,0},{5,1},{6,2},{7,3},{8,12},{9,13},{10,... | collective-permute-start | bytes 1769480 | tf_op jit(solution)/shard_map/ppermute | solution.py:26
  207.5 13.2 %collective-permute-start.32 = (bf16[24,3072]{1,0:T(8,128)(2,1)S(1)}, bf16[24,3072]{1,0:T(8,128)(2,1)S(1)}, u32[]{:S(2)}, u32[]{:S(2)}) collective-permute-start(bf16[24,3072]{1,0:T(8,128)(2,1)S(1)} %get-tuple-element.193), channel_id=1, source_target_pairs={{0,16},{1,17},{2,18},{3,19},{4,20},{5,21},{6,22},{7,23},{8,24},{9,... | collective-permute-start | bytes 442376 | tf_op jit(solution)/shard_map/ppermute | solution.py:26
  208.3 12.4 %collective-permute-start.33 = (bf16[24,3072]{1,0:T(8,128)(2,1)S(1)}, bf16[24,3072]{1,0:T(8,128)(2,1)S(1)}, u32[]{:S(2)}, u32[]{:S(2)}) collective-permute-start(bf16[24,3072]{1,0:T(8,128)(2,1)S(1)} %get-tuple-element.194), channel_id=1, source_target_pairs={{0,24},{1,25},{2,26},{3,27},{4,28},{5,29},{6,30},{7,31},{8,16},{9,... | collective-permute-start | bytes 442376 | tf_op jit(solution)/shard_map/ppermute | solution.py:26
  231.4 17.1 %collective-permute-start.37 = (bf16[32,3072]{1,0:T(8,128)(2,1)S(1)}, bf16[32,3072]{1,0:T(8,128)(2,1)S(1)}, u32[]{:S(2)}, u32[]{:S(2)}) collective-permute-start(bf16[32,3072]{1,0:T(8,128)(2,1)S(1)} %get-tuple-element.207), channel_id=1, source_target_pairs={{0,16},{1,17},{2,18},{3,19},{4,20},{5,21},{6,22},{7,23},{8,24},{9,... | collective-permute-start | bytes 589832 | tf_op jit(solution)/shard_map/ppermute | solution.py:26
  233.4 15.1 %collective-permute-start.36 = (bf16[32,3072]{1,0:T(8,128)(2,1)S(1)}, bf16[32,3072]{1,0:T(8,128)(2,1)S(1)}, u32[]{:S(2)}, u32[]{:S(2)}) collective-permute-start(bf16[32,3072]{1,0:T(8,128)(2,1)S(1)} %get-tuple-element.206), channel_id=1, source_target_pairs={{0,8},{1,9},{2,10},{3,11},{4,12},{5,13},{6,14},{7,15},{8,0},{9,1},... | collective-permute-start | bytes 589832 | tf_op jit(solution)/shard_map/ppermute | solution.py:26
  (51 other events, 419.7 us)
Sparse Core Ops, SparseCore 0:
  11.5 96.9 all-gather.1

commit v7 on v6

--- a/solution.py
+++ b/solution.py
@@ -1084,12 +1084,12 @@
         held = joined(joined(held, others[0], 8), joined(others[1], others[2], 8), 16, 1)
         text_beside, text_above = swapped(held, 2), swapped(held, 4)
         hidden_cols = lax.all_to_all(scaled_sum, AXIS, split_axis=1, concat_axis=0, tiled=True)
-        whole, text_beside, text_above = lax.optimization_barrier((whole, text_beside, text_above))
-        halves = diagonal(text_beside, text_above)
     image_low = image_up(normed_img, whole, middle_img, early)
     if small:
-        image_low, halves, hidden_cols = lax.optimization_barrier((image_low, halves, hidden_cols))
-        across = jnp.concatenate(halves, axis=0)
+        image_low, text_beside, text_above, hidden_cols = lax.optimization_barrier(
+            (image_low, text_beside, text_above, hidden_cols)
+        )
+        across = jnp.concatenate(diagonal(text_beside, text_above), axis=0)
         held = joined(joined(held, text_beside, 2), joined(text_above, across, 2), 4, 4)
         text_pack = joined(held, swapped(held, 1), 1).reshape(-1, D + total_images)
     image_all = spread(image_low).reshape(total_images, D)

time: 258 us -> 264 us (1.023)
  starting transfers between devices: 46.1 us -> 49.8 us
  transfers between devices with their start and end apart: 42 -> 42, of which waited for: 16 -> 18; matrix products, arithmetic and copies ran while one was open for 5% -> 4% of each run, Pallas kernels for 34% -> 34%
where the time goes in v7:
time: 264 us; the launch traced here: 263 us
  Pallas kernels  111 us (42%)
  waiting for transfers between devices  66.3 us (25%)
  starting transfers between devices  49.8 us (19%)
  local copies, waits for them, and re-layouts  16 us (6%)
  between operations  14.8 us (6%)
  other arithmetic  5.44 us (2%)
    ppermute x39, waiting for transfers between devices, swapped(): return lax.ppermute(value, AXIS, [(i, i ^ mask) for i in range(peers)])  53.6 us
    ppermute x39, starting transfers between devices, swapped(): return lax.ppermute(value, AXIS, [(i, i ^ mask) for i in range(peers)])  41.1 us
    pallas_call x1, Pallas kernels, text_front(): pl.pallas_call(text_front_kernel, out_shape=[jax.ShapeDtypeStruct(*item)...  18 us
    pallas_call x1, Pallas kernels, image_front(): pl.pallas_call(functools.partial(image_front_kernel, windows), out_shape=...  16.9 us
    pallas_call x1, Pallas kernels, mlp_back(): pl.pallas_call(mlp_back_kernel, out_shape=[stays((D // 2, FF // 2), bf16)...  14.8 us
    all_to_all x1, waiting for transfers between devices, spread(): return lax.all_to_all(copies, AXIS, split_axis=0, concat_axis=0, tiled=True)  12.6 us
    pallas_call x1, Pallas kernels, text_up(): pl.pallas_call(text_up_kernel, grid=(FF // TILE,), out_shape=[jax.ShapeDt...  12 us
    pallas_call x2, Pallas kernels, attention_back(): pl.pallas_call(functools.partial(attention_back_kernel, first), out_shape...  11.5 us
  transfers between devices with their start and end apart: 42, of which 18 were waited for; matrix products, arithmetic and copies ran while one was open for 4% of the time, Pallas kernels for 34%

profile of v7, /device:TPU:0, one launch (start us, length us, event | category | flops | bytes accessed | tf_op | source)
XLA Modules:
  0.0 263.4 jit_solution(9818494160323886379)
XLA Ops:
  10.3 5.1 %collective-permute-start.2 = (bf16[24,4096]{1,0:T(8,128)(2,1)S(1)}, bf16[24,4096]{1,0:T(8,128)(2,1)S(1)}, u32[]{:S(2)}, u32[]{:S(2)}) collective-permute-start(bf16[24,4096]{1,0:T(8,128)(2,1)S(1)} %pad_maximum_fusion.7), channel_id=1, source_target_pairs={{0,24},{1,25},{2,26},{3,27},{4,28},{5,29},{6,30},{7,31},{8,16},{9,... | collective-permute-start | bytes 589832 | tf_op jit(solution)/shard_map/ppermute | solution.py:26
  16.0 18.0 %text_front.1 = (bf16[640,768]{1,0:T(8,128)(2,1)}, bf16[640,2304]{1,0:T(8,128)(2,1)}, bf16[640,768]{1,0:T(8,128)(2,1)}, f32[640,768]{1,0:T(8,128)}, bf16[640,768...) custom-call(bf16[640,768]{1,0:T(8,128)(2,1)} %refs_3_.1, f32[768]{0:T(1024)} %refs_4_.1, f32[768]{0:T(1024)} %b1_ref.2, ...), custom_call_target="tpu_custom_call" | custom-call | flops 3019898880 | bytes 11599872 | tf_op jit(solution)/shard_map/text_front/pallas_call | solution.py:366
  42.7 12.0 %text_up.1 = (bf16[640,3072]{1,0:T(8,128)(2,1)}, f32[40,3072]{1,0:T(8,128)}, f32[40,768]{1,0:T(8,128)}, f32[40,128]{1,0:T(8,128)}) custom-call(bf16[640,768]{1,0:T(8,128)(2,1)} %get-tuple-element.117.h2_ref.refs_1_.refs_3_, bf16[768,3072]{1,0:T(8,128)(2,1)} %wu_hbm.1, bf16[3072,768]{1,0:T(8,128)(2,1)} %wd_hbm.1, f32[40,768]{1,0:T(8,128)} %get-tuple-element.112.sum_ref, ...), custom_call_target="tpu_custom_call" | custom-call | flops 3019898880 | bytes 13369344 | tf_op jit(solution)/shard_map/text_up/pallas_call | solution.py:537
  54.7 9.1 %collective-permute-done.3.refs_1_ = bf16[96,4096]{1,0:T(8,128)(2,1)} collective-permute-done((bf16[96,4096]{1,0:T(8,128)(2,1)}, bf16[96,4096]{1,0:T(8,128)(2,1)}, u32[]{:S(2)}, u32[]{:S(2)}) %collective-permute-start.3) | collective-permute-done | bytes 786464 | tf_op jit(solution)/shard_map/ppermute | solution.py:26
  74.9 3.2 %left_factors.2.lhs_hbm = bf16[2,768,640]{2,1,0:T(8,128)(2,1)S(1)} custom-call(s32[768,1]{1,0:T(8,128)S(1)} %fusion.8.refs_0_, bf16[640,768]{1,0:T(8,128)(2,1)S(1)} %copy-done.19, s32[768,1]{1,0:T(8,128)S(1)} %fusion.9.refs_2_.order_ref.refs_4_, bf16[640,768]{1,0:T(8,128)(2,1)S(1)} %copy-done.19), custom_call_target="tpu_custom_call" | custom-call | flops 1509949440 | bytes 3932160 | tf_op jit(solution)/shard_map/left_factors/pallas_call | solution.py:639
  78.2 3.5 %collective-permute-done.5.refs_3_ = bf16[48,4096]{1,0:T(8,128)(2,1)} collective-permute-done((bf16[48,4096]{1,0:T(8,128)(2,1)}, bf16[48,4096]{1,0:T(8,128)(2,1)}, u32[]{:S(2)}, u32[]{:S(2)}) %collective-permute-start.5) | collective-permute-done | bytes 393248 | tf_op jit(solution)/shard_map/ppermute | solution.py:26
  81.7 5.3 %collective-permute-done.6.refs_4_ = bf16[48,4096]{1,0:T(8,128)(2,1)} collective-permute-done((bf16[48,4096]{1,0:T(8,128)(2,1)}, bf16[48,4096]{1,0:T(8,128)(2,1)}, u32[]{:S(2)}, u32[]{:S(2)}) %collective-permute-start.6) | collective-permute-done | bytes 393248 | tf_op jit(solution)/shard_map/ppermute | solution.py:26
  87.7 2.6 collective-permute-start.13
  93.6 16.9 %image_front.1 = (bf16[400,768]{1,0:T(8,128)(2,1)}, f32[8,768]{1,0:T(8,128)}, f32[8,1024]{1,0:T(8,128)}) custom-call(bf16[400,768]{1,0:T(8,128)(2,1)} %x_ref.3, s32[768,1]{1,0:T(8,128)} %copy-done.9, bf16[768]{0:T(1024)(128)(2,1)} %g1_ref.3, bf16[768]{0:T(1024)(128)(2,1)} %b1_ref.3, bf16[768]{0:T(1024)(128)(2,1)} %g2_ref.3, bf16[768]{0:T(1024)(128)(2,1)} %b2_ref.3, ...), custom_call_target="tpu_custom_call" | custom-call | flops 2831155200 | bytes 4718592 | tf_op jit(solution)/shard_map/image_front/pallas_call | solution.py:441
  111.7 3.8 %all-to-all-start = ((bf16[40,32,96]{2,0,1:T(8,128)(2,1)}), bf16[40,32,96]{2,0,1:T(8,128)(2,1)S(1)}, u32[]{:S(2)}, u32[]{:S(2)}) async-start(bf16[40,32,96]{2,0,1:T(8,128)(2,1)} %copy.68), calls=%async_computation | async-start | bytes 655360 | tf_op jit(solution)/shard_map/all_to_all | solution.py:1086
  119.0 8.0 %image_up.1 = bf16[8,768]{1,0:T(8,128)(2,1)} custom-call(bf16[400,768]{1,0:T(8,128)(2,1)} %get-tuple-element.124.h2_ref, bf16[768,5120]{1,0:T(8,128)(2,1)} %all-gather.2.cloned.1.call-done.wu_ref.wd_ref.first_ref, bf16[768,5120]{1,0:T(8,128)(2,1)} %all-gather.2.cloned.1.call-done.wu_ref.wd_ref.first_ref, ...), custom_call_target="tpu_custom_call" | custom-call | flops 1887436800 | bytes 9437184 | tf_op jit(solution)/shard_map/image_up/pallas_call | solution.py:604
  131.5 3.8 %collective-permute-done.17 = bf16[2,40,1024]{2,1,0:T(8,128)(2,1)S(1)} collective-permute-done((bf16[2,40,1024]{2,1,0:T(8,128)(2,1)S(1)}, bf16[2,40,1024]{2,1,0:T(8,128)(2,1)S(1)}, u32[]{:S(2)}, u32[]{:S(2)}) %collective-permute-start.17) | collective-permute-done | bytes 163872 | tf_op jit(solution)/shard_map/ppermute | solution.py:26
  138.1 4.8 %all-to-all-start.1 = ((bf16[32,8,768]{2,1,0:T(8,128)(2,1)}), bf16[32,8,768]{2,1,0:T(8,128)(2,1)S(1)}, u32[]{:S(2)}, u32[]{:S(2)}) async-start(bf16[32,8,768]{2,1,0:T(8,128)(2,1)} %broadcast_in_dim.5), calls=%async_computation.1 | async-start | bytes 786432 | tf_op jit(solution)/shard_map/all_to_all | solution.py:46
  143.4 12.6 %all-to-all-done.1 = bf16[32,8,768]{2,1,0:T(8,128)(2,1)S(1)} async-done(((bf16[32,8,768]{2,1,0:T(8,128)(2,1)}), bf16[32,8,768]{2,1,0:T(8,128)(2,1)S(1)}, u32[]{:S(2)}, u32[]{:S(2)}) %all-to-all-start.1) | async-done | bytes 393248 | tf_op jit(solution)/shard_map/all_to_all | solution.py:46
  158.7 14.8 %mlp_back.1 = (bf16[384,1536]{1,0:T(8,128)(2,1)S(1)}, bf16[384,1536]{1,0:T(8,128)(2,1)S(1)}, bf16[384,1536]{1,0:T(8,128)(2,1)S(1)}, bf16[384,1536]{1,0:T(8,128)(...) custom-call(bf16[40,768]{1,0:T(8,128)(2,1)S(1)} %get-tuple-element.137.low_ref, f32[768]{0:T(1024)S(1)} %copy-done.17, ...), custom_call_target="tpu_custom_call" | custom-call | flops 6039797760 | bytes 18087936 | tf_op jit(solution)/shard_map/mlp_back/pallas_call | solution.py:853
  180.7 9.2 %attention_back.3 = (bf16[512,768]{1,0:T(8,128)(2,1)S(1)}, bf16[512,2304]{1,0:T(8,128)(2,1)S(1)}) custom-call(f32[640,768]{1,0:T(8,128)S(1)} %get-tuple-element.142.grad_ref.refs_5_, bf16[768,768]{1,0:T(8,128)(2,1)S(1)} %copy-done.3, bf16[640,2304]{1,0:T(8,128)(2,1)S(1)} %copy-done.1, f32[80,128]{1,0:T(8,128)S(1)} %copy-done.15, ...), custom_call_target="tpu_custom_call" | custom-call | flops 3019898880 | bytes 7471104 | tf_op jit(solution)/shard_map/attention_back/pallas_call | solution.py:912
  189.9 4.8 %left_factors.3.refs_1_.lhs_ref = bf16[3,768,640]{2,1,0:T(8,128)(2,1)S(1)} custom-call(s32[768,1]{1,0:T(8,128)S(1)} %copy-done.12, bf16[640,768]{1,0:T(8,128)(2,1)S(1)} %copy-done.20, s32[768,1]{1,0:T(8,128)S(1)} %copy-done.10, bf16[640,768]{1,0:T(8,128)(2,1)S(1)} %copy-done.20, s32[768,1]{1,0:T(8,128)S(1)} %copy-done.10, bf16[640,768]{1,0:T(8,128)(2,1)S(1)} %copy-done.21), custom_call_target="tpu_custom_call" | custom-call | flops 2264924160 | bytes 5898240 | tf_op jit(solution)/shard_map/left_factors/pallas_call | solution.py:639
  195.4 3.9 %weight_back.1 = (bf16[384,1536]{1,0:T(8,128)(2,1)S(1)}, bf16[384,1536]{1,0:T(8,128)(2,1)S(1)}, bf16[384,1536]{1,0:T(8,128)(2,1)S(1)}, bf16[384,1536]{1,0:T(8,128)(2,1)S(1)}) custom-call(bf16[3,768,640]{2,1,0:T(8,128)(2,1)S(1)} %left_factors.3.refs_1_.lhs_ref, bf16[128,2304]{1,0:T(8,128)(2,1)S(1)} %get-tuple-element.145.refs_0_, ...), custom_call_target="tpu_custom_call" | custom-call | flops 3019898880 | bytes 12189696 | tf_op jit(solution)/shard_map/weight_back/pallas_call | solution.py:945
  202.0 6.5 %input_back.1 = (f32[640,768]{1,0:T(8,128)}, f32[8,1536]{1,0:T(8,128)S(1)}) custom-call(bf16[128,2304]{1,0:T(8,128)(2,1)S(1)} %get-tuple-element.145.refs_0_, bf16[512,2304]{1,0:T(8,128)(2,1)S(1)} %get-tuple-element.156.refs_0_.refs_1_, bf16[768,2304]{1,0:T(8,128)(2,1)S(1)} %copy-done, bf16[640,768]{1,0:T(8,128)(2,1)S(1)} %copy-done.6, f32[768]{0:T(1024)S(1)} %copy-done.16, ...), custom_call_target="tpu_custom_call" | custom-call | flops 2264924160 | bytes 10420224 | tf_op jit(solution)/shard_map/input_back/pallas_call | solution.py:987
  216.9 5.9 %grad_of_down.1 = f32[96,768]{1,0:T(8,128)S(1)} custom-call(bf16[1280,1024]{1,0:T(8,128)(2,1)S(1)} %bitcast.77, bf16[256,768]{1,0:T(8,128)(2,1)S(1)} %bitcast.79, f32[1,256]{1,0:T(1,128)S(1)} %get-tuple-element.169.col_sum_ref, f32[1,256]{1,0:T(1,128)S(1)} %get-tuple-element.170.col_count_ref, f32[1,128]{1,0:T(1,128)S(1)} %get-tuple-element.171.live_ref, ...), custom_call_target="tpu_custom_call" | custom-call | flops 1006632960 | bytes 2621440 | tf_op jit(solution)/shard_map/grad_of_down/pallas_call | solution.py:755
  222.7 3.9 %collective-permute-done.32 = bf16[24,3072]{1,0:T(8,128)(2,1)S(1)} collective-permute-done((bf16[24,3072]{1,0:T(8,128)(2,1)S(1)}, bf16[24,3072]{1,0:T(8,128)(2,1)S(1)}, u32[]{:S(2)}, u32[]{:S(2)}) %collective-permute-start.32) | collective-permute-done | bytes 147488 | tf_op jit(solution)/shard_map/ppermute | solution.py:26
  229.1 6.7 %collective-permute-done.35.got_b = bf16[96,1536]{1,0:T(8,128)(2,1)S(1)} collective-permute-done((bf16[96,1536]{1,0:T(8,128)(2,1)S(1)}, bf16[96,1536]{1,0:T(8,128)(2,1)S(1)}, u32[]{:S(2)}, u32[]{:S(2)}) %collective-permute-start.35) | collective-permute-done | bytes 294944 | tf_op jit(solution)/shard_map/ppermute | solution.py:26
  242.5 3.7 %collective-permute-done.38 = bf16[32,3072]{1,0:T(8,128)(2,1)S(1)} collective-permute-done((bf16[32,3072]{1,0:T(8,128)(2,1)S(1)}, bf16[32,3072]{1,0:T(8,128)(2,1)S(1)}, u32[]{:S(2)}, u32[]{:S(2)}) %collective-permute-start.38) | collective-permute-done | bytes 196640 | tf_op jit(solution)/shard_map/ppermute | solution.py:26
  246.2 8.3 %collective-permute-done.37 = bf16[32,3072]{1,0:T(8,128)(2,1)S(1)} collective-permute-done((bf16[32,3072]{1,0:T(8,128)(2,1)S(1)}, bf16[32,3072]{1,0:T(8,128)(2,1)S(1)}, u32[]{:S(2)}, u32[]{:S(2)}) %collective-permute-start.37) | collective-permute-done | bytes 196640 | tf_op jit(solution)/shard_map/ppermute | solution.py:26
  (196 shorter events, 72.2 us)
Async XLA Ops:
  7.2 111.8 %all-gather.2.cloned.1.call-start = ((), (), s32[]{:S(2)}) async-start(), calls=%async_computation.2 | async-start | bytes 8110080 | tf_op jit(solution)/shard_map/all_gather | solution.py:1028
  10.3 24.6 %collective-permute-start.2 = (bf16[24,4096]{1,0:T(8,128)(2,1)S(1)}, bf16[24,4096]{1,0:T(8,128)(2,1)S(1)}, u32[]{:S(2)}, u32[]{:S(2)}) collective-permute-start(bf16[24,4096]{1,0:T(8,128)(2,1)S(1)} %pad_maximum_fusion.7), channel_id=1, source_target_pairs={{0,24},{1,25},{2,26},{3,27},{4,28},{5,29},{6,30},{7,31},{8,16},{9,... | collective-permute-start | bytes 589832 | tf_op jit(solution)/shard_map/ppermute | solution.py:26
  15.4 22.0 %collective-permute-start.1 = (bf16[24,4096]{1,0:T(8,128)(2,1)S(1)}, bf16[24,4096]{1,0:T(8,128)(2,1)S(1)}, u32[]{:S(2)}, u32[]{:S(2)}) collective-permute-start(bf16[24,4096]{1,0:T(8,128)(2,1)S(1)} %pad_maximum_fusion.7), channel_id=1, source_target_pairs={{0,16},{1,17},{2,18},{3,19},{4,20},{5,21},{6,22},{7,23},{8,24},{9,... | collective-permute-start | bytes 589832 | tf_op jit(solution)/shard_map/ppermute | solution.py:26
  15.4 22.0 %collective-permute-start = (bf16[24,4096]{1,0:T(8,128)(2,1)S(1)}, bf16[24,4096]{1,0:T(8,128)(2,1)S(1)}, u32[]{:S(2)}, u32[]{:S(2)}) collective-permute-start(bf16[24,4096]{1,0:T(8,128)(2,1)S(1)} %pad_maximum_fusion.7), channel_id=1, source_target_pairs={{0,8},{1,9},{2,10},{3,11},{4,12},{5,13},{6,14},{7,15},{8,0},{9,1},... | collective-permute-start | bytes 589832 | tf_op jit(solution)/shard_map/ppermute | solution.py:26
  38.3 25.5 %collective-permute-start.3 = (bf16[96,4096]{1,0:T(8,128)(2,1)}, bf16[96,4096]{1,0:T(8,128)(2,1)}, u32[]{:S(2)}, u32[]{:S(2)}) collective-permute-start(bf16[96,4096]{1,0:T(8,128)(2,1)} %pad_maximum_fusion.2.refs_0_), channel_id=1, source_target_pairs={{0,2},{1,3},{2,0},{3,1},{4,6},{5,7},{6,4},{7,5},{8,10},{9,11},{10,... | collective-permute-start | bytes 2359304 | tf_op jit(solution)/shard_map/ppermute | solution.py:26
  39.8 24.0 %collective-permute-start.4 = (bf16[96,4096]{1,0:T(8,128)(2,1)}, bf16[96,4096]{1,0:T(8,128)(2,1)}, u32[]{:S(2)}, u32[]{:S(2)}) collective-permute-start(bf16[96,4096]{1,0:T(8,128)(2,1)} %pad_maximum_fusion.2.refs_0_), channel_id=1, source_target_pairs={{0,4},{1,5},{2,6},{3,7},{4,0},{5,1},{6,2},{7,3},{8,12},{9,13},{10,... | collective-permute-start | bytes 2359304 | tf_op jit(solution)/shard_map/ppermute | solution.py:26
  65.5 16.2 %collective-permute-start.5 = (bf16[48,4096]{1,0:T(8,128)(2,1)}, bf16[48,4096]{1,0:T(8,128)(2,1)}, u32[]{:S(2)}, u32[]{:S(2)}) collective-permute-start(bf16[48,4096]{1,0:T(8,128)(2,1)} %slice.68), channel_id=1, source_target_pairs={{0,4},{1,5},{2,6},{3,7},{4,0},{5,1},{6,2},{7,3},{8,12},{9,13},{10,... | collective-permute-start | bytes 1179656 | tf_op jit(solution)/shard_map/ppermute | solution.py:26
  69.1 17.9 %collective-permute-start.6 = (bf16[48,4096]{1,0:T(8,128)(2,1)}, bf16[48,4096]{1,0:T(8,128)(2,1)}, u32[]{:S(2)}, u32[]{:S(2)}) collective-permute-start(bf16[48,4096]{1,0:T(8,128)(2,1)} %slice.69), channel_id=1, source_target_pairs={{0,2},{1,3},{2,0},{3,1},{4,6},{5,7},{6,4},{7,5},{8,10},{9,11},{10,... | collective-permute-start | bytes 1179656 | tf_op jit(solution)/shard_map/ppermute | solution.py:26
  71.3 16.3 %collective-permute-start.7 = (bf16[96,4096]{1,0:T(8,128)(2,1)}, bf16[96,4096]{1,0:T(8,128)(2,1)S(1)}, u32[]{:S(2)}, u32[]{:S(2)}) collective-permute-start(bf16[96,4096]{1,0:T(8,128)(2,1)} %pad_maximum_fusion.2.refs_0_), channel_id=1, source_target_pairs={{0,1},{1,0},{2,3},{3,2},{4,5},{5,4},{6,7},{7,6},{8,9},{9,8},{10,11... | collective-permute-start | bytes 2359304 | tf_op jit(solution)/shard_map/ppermute | solution.py:26
  71.5 16.2 %collective-permute-start.8 = (bf16[96,4096]{1,0:T(8,128)(2,1)}, bf16[96,4096]{1,0:T(8,128)(2,1)S(1)}, u32[]{:S(2)}, u32[]{:S(2)}) collective-permute-start(bf16[96,4096]{1,0:T(8,128)(2,1)} %collective-permute-done.3.refs_1_), channel_id=1, source_target_pairs={{0,1},{1,0},{2,3},{3,2},{4,5},{5,4},{6,7},{7,6},{8,9},{9,8},{10,11... | collective-permute-start | bytes 2359304 | tf_op jit(solution)/shard_map/ppermute | solution.py:26
  72.1 18.3 %collective-permute-start.9 = (bf16[96,4096]{1,0:T(8,128)(2,1)}, bf16[96,4096]{1,0:T(8,128)(2,1)S(1)}, u32[]{:S(2)}, u32[]{:S(2)}) collective-permute-start(bf16[96,4096]{1,0:T(8,128)(2,1)} %collective-permute-done.4.refs_2_), channel_id=1, source_target_pairs={{0,1},{1,0},{2,3},{3,2},{4,5},{5,4},{6,7},{7,6},{8,9},{9,8},{10,11... | collective-permute-start | bytes 2359304 | tf_op jit(solution)/shard_map/ppermute | solution.py:26
  87.6 22.9 %collective-permute-start.12 = (bf16[1,40,1024]{2,1,0:T(8,128)(2,1)S(1)}, bf16[1,40,1024]{2,1,0:T(8,128)(2,1)S(1)}, u32[]{:S(2)}, u32[]{:S(2)}) collective-permute-start(bf16[1,40,1024]{2,1,0:T(8,128)(2,1)S(1)} %bitcast.81), channel_id=1, source_target_pairs={{0,8},{1,9},{2,10},{3,11},{4,12},{5,13},{6,14},{7,15},{8,0},{9,1},... | collective-permute-start | bytes 245768 | tf_op jit(solution)/shard_map/ppermute | solution.py:26
  87.7 22.8 %collective-permute-start.13 = (bf16[1,40,1024]{2,1,0:T(8,128)(2,1)S(1)}, bf16[1,40,1024]{2,1,0:T(8,128)(2,1)S(1)}, u32[]{:S(2)}, u32[]{:S(2)}) collective-permute-start(bf16[1,40,1024]{2,1,0:T(8,128)(2,1)S(1)} %bitcast.82), channel_id=1, source_target_pairs={{0,16},{1,17},{2,18},{3,19},{4,20},{5,21},{6,22},{7,23},{8,24},{9,... | collective-permute-start | bytes 245768 | tf_op jit(solution)/shard_map/ppermute | solution.py:26
  90.4 20.2 %collective-permute-start.14 = (bf16[1,40,1024]{2,1,0:T(8,128)(2,1)S(1)}, bf16[1,40,1024]{2,1,0:T(8,128)(2,1)S(1)}, u32[]{:S(2)}, u32[]{:S(2)}) collective-permute-start(bf16[1,40,1024]{2,1,0:T(8,128)(2,1)S(1)} %bitcast.83), channel_id=1, source_target_pairs={{0,24},{1,25},{2,26},{3,27},{4,28},{5,29},{6,30},{7,31},{8,16},{9,... | collective-permute-start | bytes 245768 | tf_op jit(solution)/shard_map/ppermute | solution.py:26
  111.7 17.8 %all-to-all-start = ((bf16[40,32,96]{2,0,1:T(8,128)(2,1)}), bf16[40,32,96]{2,0,1:T(8,128)(2,1)S(1)}, u32[]{:S(2)}, u32[]{:S(2)}) async-start(bf16[40,32,96]{2,0,1:T(8,128)(2,1)} %copy.68), calls=%async_computation | async-start | bytes 655360 | tf_op jit(solution)/shard_map/all_to_all | solution.py:1086
  115.7 13.2 %collective-permute-start.15 = (bf16[4,40,1024]{2,1,0:T(8,128)(2,1)S(1)}, bf16[4,40,1024]{2,1,0:T(8,128)(2,1)S(1)}, u32[]{:S(2)}, u32[]{:S(2)}) collective-permute-start(bf16[4,40,1024]{2,1,0:T(8,128)(2,1)S(1)} %bitcast.85), channel_id=1, source_target_pairs={{0,2},{1,3},{2,0},{3,1},{4,6},{5,7},{6,4},{7,5},{8,10},{9,11},{10,... | collective-permute-start | bytes 983048 | tf_op jit(solution)/shard_map/ppermute | solution.py:26
  138.1 18.0 %all-to-all-start.1 = ((bf16[32,8,768]{2,1,0:T(8,128)(2,1)}), bf16[32,8,768]{2,1,0:T(8,128)(2,1)S(1)}, u32[]{:S(2)}, u32[]{:S(2)}) async-start(bf16[32,8,768]{2,1,0:T(8,128)(2,1)} %broadcast_in_dim.5), calls=%async_computation.1 | async-start | bytes 786432 | tf_op jit(solution)/shard_map/all_to_all | solution.py:46
  178.7 16.1 %collective-permute-start.22 = (bf16[192,1536]{1,0:T(8,128)(2,1)S(1)}, bf16[192,1536]{1,0:T(8,128)(2,1)S(1)}, u32[]{:S(2)}, u32[]{:S(2)}) collective-permute-start(bf16[192,1536]{1,0:T(8,128)(2,1)S(1)} %get-tuple-element.151.refs_1_), channel_id=1, source_target_pairs={{0,2},{1,3},{2,0},{3,1},{4,6},{5,7},{6,4},{7,5},{8,10},{9,11},{10,... | collective-permute-start | bytes 1769480 | tf_op jit(solution)/shard_map/ppermute | solution.py:26
  179.3 15.5 %collective-permute-start.23 = (bf16[192,1536]{1,0:T(8,128)(2,1)S(1)}, bf16[192,1536]{1,0:T(8,128)(2,1)S(1)}, u32[]{:S(2)}, u32[]{:S(2)}) collective-permute-start(bf16[192,1536]{1,0:T(8,128)(2,1)S(1)} %get-tuple-element.153.refs_3_), channel_id=1, source_target_pairs={{0,4},{1,5},{2,6},{3,7},{4,0},{5,1},{6,2},{7,3},{8,12},{9,13},{10,... | collective-permute-start | bytes 1769480 | tf_op jit(solution)/shard_map/ppermute | solution.py:26
  210.3 16.4 %collective-permute-start.29 = (bf16[208,1536]{1,0:T(8,128)(2,1)S(1)}, bf16[208,1536]{1,0:T(8,128)(2,1)S(1)}, u32[]{:S(2)}, u32[]{:S(2)}) collective-permute-start(bf16[208,1536]{1,0:T(8,128)(2,1)S(1)} %get-tuple-element.183), channel_id=1, source_target_pairs={{0,2},{1,3},{2,0},{3,1},{4,6},{5,7},{6,4},{7,5},{8,10},{9,11},{10,... | collective-permute-start | bytes 1916936 | tf_op jit(solution)/shard_map/ppermute | solution.py:26
  211.5 15.2 %collective-permute-start.30 = (bf16[192,1536]{1,0:T(8,128)(2,1)S(1)}, bf16[192,1536]{1,0:T(8,128)(2,1)S(1)}, u32[]{:S(2)}, u32[]{:S(2)}) collective-permute-start(bf16[192,1536]{1,0:T(8,128)(2,1)S(1)} %get-tuple-element.185), channel_id=1, source_target_pairs={{0,4},{1,5},{2,6},{3,7},{4,0},{5,1},{6,2},{7,3},{8,12},{9,13},{10,... | collective-permute-start | bytes 1769480 | tf_op jit(solution)/shard_map/ppermute | solution.py:26
  213.5 13.2 %collective-permute-start.32 = (bf16[24,3072]{1,0:T(8,128)(2,1)S(1)}, bf16[24,3072]{1,0:T(8,128)(2,1)S(1)}, u32[]{:S(2)}, u32[]{:S(2)}) collective-permute-start(bf16[24,3072]{1,0:T(8,128)(2,1)S(1)} %get-tuple-element.187), channel_id=1, source_target_pairs={{0,16},{1,17},{2,18},{3,19},{4,20},{5,21},{6,22},{7,23},{8,24},{9,... | collective-permute-start | bytes 442376 | tf_op jit(solution)/shard_map/ppermute | solution.py:26
  237.3 17.2 %collective-permute-start.37 = (bf16[32,3072]{1,0:T(8,128)(2,1)S(1)}, bf16[32,3072]{1,0:T(8,128)(2,1)S(1)}, u32[]{:S(2)}, u32[]{:S(2)}) collective-permute-start(bf16[32,3072]{1,0:T(8,128)(2,1)S(1)} %get-tuple-element.201), channel_id=1, source_target_pairs={{0,16},{1,17},{2,18},{3,19},{4,20},{5,21},{6,22},{7,23},{8,24},{9,... | collective-permute-start | bytes 589832 | tf_op jit(solution)/shard_map/ppermute | solution.py:26
  239.4 15.1 %collective-permute-start.36 = (bf16[32,3072]{1,0:T(8,128)(2,1)S(1)}, bf16[32,3072]{1,0:T(8,128)(2,1)S(1)}, u32[]{:S(2)}, u32[]{:S(2)}) collective-permute-start(bf16[32,3072]{1,0:T(8,128)(2,1)S(1)} %get-tuple-element.200), channel_id=1, source_target_pairs={{0,8},{1,9},{2,10},{3,11},{4,12},{5,13},{6,14},{7,15},{8,0},{9,1},... | collective-permute-start | bytes 589832 | tf_op jit(solution)/shard_map/ppermute | solution.py:26
  (51 other events, 420.7 us)
Sparse Core Ops, SparseCore 0:
  11.5 96.9 all-gather.1

commit v8 on v6

--- a/solution.py
+++ b/solution.py
@@ -107,7 +107,7 @@
 
 VMEM_BYTES = 56 << 20
 TILE = 512
-EARLY = 2 * TILE
+EARLY = TILE
 
 
 def norm_parts(values):

time: 258 us -> 245 us (0.950)
  waiting for transfers between devices: 63.8 us -> 52.5 us
  local copies, waits for them, and re-layouts: 16 us -> 11.3 us
  starting transfers between devices: 46.1 us -> 48.7 us
    ppermute x39, waiting for transfers between devices: 51.2 us -> 36.9 us  [swapped(): return lax.ppermute(value, AXIS, [(i, i ^ mask) for i in range(peers)])]
    slice x4, local copies, waits for them, and re-layouts: 3.55 us -> 0.07 us  [diagonal(): return (swapped(beside[:half], 4), swapped(above[half:], 2))]
    all_gather x1, waiting for transfers between devices: 0.01 us -> 2.89 us  [local(): lax.all_gather(jnp.concatenate([img_down.reshape(per, FF), up_rows[:, EAR...]
    ppermute x39, starting transfers between devices: 38.7 us -> 41.3 us  [swapped(): return lax.ppermute(value, AXIS, [(i, i ^ mask) for i in range(peers)])]
  transfers between devices with their start and end apart: 42 -> 42, of which waited for: 16 -> 15; matrix products, arithmetic and copies ran while one was open for 5% -> 3% of each run, Pallas kernels for 34% -> 36%
where the time goes in v8:
time: 245 us; the launch traced here: 244 us
  Pallas kernels  111 us (45%)
  waiting for transfers between devices  52.5 us (21%)
  starting transfers between devices  48.7 us (20%)
  between operations  14.9 us (6%)
  local copies, waits for them, and re-layouts  11.3 us (5%)
  other arithmetic  5.5 us (2%)
    ppermute x39, starting transfers between devices, swapped(): return lax.ppermute(value, AXIS, [(i, i ^ mask) for i in range(peers)])  41.3 us
    ppermute x39, waiting for transfers between devices, swapped(): return lax.ppermute(value, AXIS, [(i, i ^ mask) for i in range(peers)])  36.9 us
    pallas_call x1, Pallas kernels, text_front(): pl.pallas_call(text_front_kernel, out_shape=[jax.ShapeDtypeStruct(*item)...  18 us
    pallas_call x1, Pallas kernels, image_front(): pl.pallas_call(functools.partial(image_front_kernel, windows), out_shape=...  15.8 us
    pallas_call x1, Pallas kernels, mlp_back(): pl.pallas_call(mlp_back_kernel, out_shape=[stays((D // 2, FF // 2), bf16)...  14.8 us
    all_to_all x1, waiting for transfers between devices, spread(): return lax.all_to_all(copies, AXIS, split_axis=0, concat_axis=0, tiled=True)  12.6 us
    pallas_call x1, Pallas kernels, text_up(): pl.pallas_call(text_up_kernel, grid=(FF // TILE,), out_shape=[jax.ShapeDt...  12.2 us
    pallas_call x2, Pallas kernels, attention_back(): pl.pallas_call(functools.partial(attention_back_kernel, first), out_shape...  11.5 us
  transfers between devices with their start and end apart: 42, of which 15 were waited for; matrix products, arithmetic and copies ran while one was open for 3% of the time, Pallas kernels for 36%

profile of v8, /device:TPU:0, one launch (start us, length us, event | category | flops | bytes accessed | tf_op | source)
XLA Modules:
  0.0 243.9 jit_solution(2139608166399506492)
XLA Ops:
  10.3 5.1 %collective-permute-start.2 = (bf16[24,3584]{1,0:T(8,128)(2,1)S(1)}, bf16[24,3584]{1,0:T(8,128)(2,1)S(1)}, u32[]{:S(2)}, u32[]{:S(2)}) collective-permute-start(bf16[24,3584]{1,0:T(8,128)(2,1)S(1)} %pad_maximum_fusion.7), channel_id=1, source_target_pairs={{0,24},{1,25},{2,26},{3,27},{4,28},{5,29},{6,30},{7,31},{8,16},{9,... | collective-permute-start | bytes 516104 | tf_op jit(solution)/shard_map/ppermute | solution.py:26
  16.9 18.0 %text_front.1 = (bf16[640,768]{1,0:T(8,128)(2,1)}, bf16[640,2304]{1,0:T(8,128)(2,1)}, bf16[640,768]{1,0:T(8,128)(2,1)}, f32[640,768]{1,0:T(8,128)}, bf16[640,768...) custom-call(bf16[640,768]{1,0:T(8,128)(2,1)} %refs_3_.1, f32[768]{0:T(1024)} %refs_4_.1, f32[768]{0:T(1024)} %b1_ref.2, ...), custom_call_target="tpu_custom_call" | custom-call | flops 3019898880 | bytes 11599872 | tf_op jit(solution)/shard_map/text_front/pallas_call | solution.py:366
  40.9 12.2 %text_up.1 = (bf16[640,3072]{1,0:T(8,128)(2,1)}, f32[40,3072]{1,0:T(8,128)}, f32[40,768]{1,0:T(8,128)}, f32[40,128]{1,0:T(8,128)}) custom-call(bf16[640,768]{1,0:T(8,128)(2,1)} %get-tuple-element.120.h2_ref.refs_1_.refs_3_, bf16[768,3072]{1,0:T(8,128)(2,1)} %wu_hbm.1, bf16[3072,768]{1,0:T(8,128)(2,1)} %wd_hbm.1, f32[40,768]{1,0:T(8,128)} %get-tuple-element.115.sum_ref, ...), custom_call_target="tpu_custom_call" | custom-call | flops 3019898880 | bytes 13369344 | tf_op jit(solution)/shard_map/text_up/pallas_call | solution.py:537
  53.1 8.5 %collective-permute-done.3.refs_1_ = bf16[96,3584]{1,0:T(8,128)(2,1)S(1)} collective-permute-done((bf16[96,3584]{1,0:T(8,128)(2,1)}, bf16[96,3584]{1,0:T(8,128)(2,1)S(1)}, u32[]{:S(2)}, u32[]{:S(2)}) %collective-permute-start.3) | collective-permute-done | bytes 688160 | tf_op jit(solution)/shard_map/ppermute | solution.py:26
  67.6 3.2 %left_factors.2.lhs_hbm = bf16[2,768,640]{2,1,0:T(8,128)(2,1)S(1)} custom-call(s32[768,1]{1,0:T(8,128)S(1)} %fusion.8.refs_0_, bf16[640,768]{1,0:T(8,128)(2,1)S(1)} %copy-done.19, s32[768,1]{1,0:T(8,128)S(1)} %fusion.9.refs_2_.order_ref.refs_4_, bf16[640,768]{1,0:T(8,128)(2,1)S(1)} %copy-done.19), custom_call_target="tpu_custom_call" | custom-call | flops 1509949440 | bytes 3932160 | tf_op jit(solution)/shard_map/left_factors/pallas_call | solution.py:639
  73.6 2.3 collective-permute-start.13
  77.9 15.8 %image_front.1 = (bf16[400,768]{1,0:T(8,128)(2,1)}, f32[8,768]{1,0:T(8,128)}, f32[8,512]{1,0:T(8,128)}) custom-call(bf16[400,768]{1,0:T(8,128)(2,1)} %x_ref.3, s32[768,1]{1,0:T(8,128)} %copy-done.9, bf16[768]{0:T(1024)(128)(2,1)} %g1_ref.3, bf16[768]{0:T(1024)(128)(2,1)} %b1_ref.3, bf16[768]{0:T(1024)(128)(2,1)} %g2_ref.3, bf16[768]{0:T(1024)(128)(2,1)} %b2_ref.3, ...), custom_call_target="tpu_custom_call" | custom-call | flops 2831155200 | bytes 4718592 | tf_op jit(solution)/shard_map/image_front/pallas_call | solution.py:441
  97.2 4.8 %all-to-all-start = ((bf16[40,32,96]{2,0,1:T(8,128)(2,1)}), bf16[40,32,96]{2,0,1:T(8,128)(2,1)S(1)}, u32[]{:S(2)}, u32[]{:S(2)}) async-start(bf16[40,32,96]{2,0,1:T(8,128)(2,1)} %copy.68), calls=%async_computation | async-start | bytes 655360 | tf_op jit(solution)/shard_map/all_to_all | solution.py:1086
  103.9 2.9 %all-gather.2.cloned.1.call-done.wu_ref.wd_ref.first_ref = bf16[768,5632]{1,0:T(8,128)(2,1)} async-done(((bf16[24,5632]{1,0:T(8,128)(2,1)}), bf16[768,5632]{1,0:T(8,128)(2,1)}) %all-gather.2.cloned.1.call-update) | async-done | bytes 8650768 | tf_op jit(solution)/shard_map/all_gather | solution.py:1028
  110.0 8.8 %image_up.1 = bf16[8,768]{1,0:T(8,128)(2,1)} custom-call(bf16[400,768]{1,0:T(8,128)(2,1)} %get-tuple-element.127.h2_ref, bf16[768,5632]{1,0:T(8,128)(2,1)} %all-gather.2.cloned.1.call-done.wu_ref.wd_ref.first_ref, bf16[768,5632]{1,0:T(8,128)(2,1)} %all-gather.2.cloned.1.call-done.wu_ref.wd_ref.first_ref, ...), custom_call_target="tpu_custom_call" | custom-call | flops 1887436800 | bytes 9437184 | tf_op jit(solution)/shard_map/image_up/pallas_call | solution.py:604
  120.7 2.6 %all-to-all-start.1 = ((bf16[32,8,768]{2,1,0:T(8,128)(2,1)}), bf16[32,8,768]{2,1,0:T(8,128)(2,1)S(1)}, u32[]{:S(2)}, u32[]{:S(2)}) async-start(bf16[32,8,768]{2,1,0:T(8,128)(2,1)} %broadcast_in_dim.5), calls=%async_computation.1 | async-start | bytes 786432 | tf_op jit(solution)/shard_map/all_to_all | solution.py:46
  123.9 12.6 %all-to-all-done.1 = bf16[32,8,768]{2,1,0:T(8,128)(2,1)S(1)} async-done(((bf16[32,8,768]{2,1,0:T(8,128)(2,1)}), bf16[32,8,768]{2,1,0:T(8,128)(2,1)S(1)}, u32[]{:S(2)}, u32[]{:S(2)}) %all-to-all-start.1) | async-done | bytes 393248 | tf_op jit(solution)/shard_map/all_to_all | solution.py:46
  139.1 14.8 %mlp_back.1 = (bf16[384,1536]{1,0:T(8,128)(2,1)S(1)}, bf16[384,1536]{1,0:T(8,128)(2,1)S(1)}, bf16[384,1536]{1,0:T(8,128)(2,1)S(1)}, bf16[384,1536]{1,0:T(8,128)(...) custom-call(bf16[40,768]{1,0:T(8,128)(2,1)S(1)} %get-tuple-element.143.low_ref, f32[768]{0:T(1024)S(1)} %copy-done.17, ...), custom_call_target="tpu_custom_call" | custom-call | flops 6039797760 | bytes 18087936 | tf_op jit(solution)/shard_map/mlp_back/pallas_call | solution.py:853
  154.5 2.3 attention_back.2
  161.2 9.2 %attention_back.3 = (bf16[512,768]{1,0:T(8,128)(2,1)S(1)}, bf16[512,2304]{1,0:T(8,128)(2,1)S(1)}) custom-call(f32[640,768]{1,0:T(8,128)S(1)} %get-tuple-element.148.grad_ref.refs_5_, bf16[768,768]{1,0:T(8,128)(2,1)S(1)} %copy-done.3, bf16[640,2304]{1,0:T(8,128)(2,1)S(1)} %copy-done.1, f32[80,128]{1,0:T(8,128)S(1)} %copy-done.15, ...), custom_call_target="tpu_custom_call" | custom-call | flops 3019898880 | bytes 7471104 | tf_op jit(solution)/shard_map/attention_back/pallas_call | solution.py:912
  170.4 4.8 %left_factors.3.refs_1_.lhs_ref = bf16[3,768,640]{2,1,0:T(8,128)(2,1)S(1)} custom-call(s32[768,1]{1,0:T(8,128)S(1)} %copy-done.12, bf16[640,768]{1,0:T(8,128)(2,1)S(1)} %copy-done.20, s32[768,1]{1,0:T(8,128)S(1)} %copy-done.10, bf16[640,768]{1,0:T(8,128)(2,1)S(1)} %copy-done.20, s32[768,1]{1,0:T(8,128)S(1)} %copy-done.10, bf16[640,768]{1,0:T(8,128)(2,1)S(1)} %copy-done.21), custom_call_target="tpu_custom_call" | custom-call | flops 2264924160 | bytes 5898240 | tf_op jit(solution)/shard_map/left_factors/pallas_call | solution.py:639
  175.8 3.9 %weight_back.1 = (bf16[384,1536]{1,0:T(8,128)(2,1)S(1)}, bf16[384,1536]{1,0:T(8,128)(2,1)S(1)}, bf16[384,1536]{1,0:T(8,128)(2,1)S(1)}, bf16[384,1536]{1,0:T(8,128)(2,1)S(1)}) custom-call(bf16[3,768,640]{2,1,0:T(8,128)(2,1)S(1)} %left_factors.3.refs_1_.lhs_ref, bf16[128,2304]{1,0:T(8,128)(2,1)S(1)} %get-tuple-element.151.refs_0_, ...), custom_call_target="tpu_custom_call" | custom-call | flops 3019898880 | bytes 12189696 | tf_op jit(solution)/shard_map/weight_back/pallas_call | solution.py:945
  182.4 6.5 %input_back.1 = (f32[640,768]{1,0:T(8,128)}, f32[8,1536]{1,0:T(8,128)S(1)}) custom-call(bf16[128,2304]{1,0:T(8,128)(2,1)S(1)} %get-tuple-element.151.refs_0_, bf16[512,2304]{1,0:T(8,128)(2,1)S(1)} %get-tuple-element.162.refs_0_.refs_1_, bf16[768,2304]{1,0:T(8,128)(2,1)S(1)} %copy-done, bf16[640,768]{1,0:T(8,128)(2,1)S(1)} %copy-done.6, f32[768]{0:T(1024)S(1)} %copy-done.16, ...), custom_call_target="tpu_custom_call" | custom-call | flops 2264924160 | bytes 10420224 | tf_op jit(solution)/shard_map/input_back/pallas_call | solution.py:987
  194.6 2.7 %collective-permute-start.33 = (bf16[24,3072]{1,0:T(8,128)(2,1)S(1)}, bf16[24,3072]{1,0:T(8,128)(2,1)S(1)}, u32[]{:S(2)}, u32[]{:S(2)}) collective-permute-start(bf16[24,3072]{1,0:T(8,128)(2,1)S(1)} %get-tuple-element.194), channel_id=1, source_target_pairs={{0,24},{1,25},{2,26},{3,27},{4,28},{5,29},{6,30},{7,31},{8,16},{9,... | collective-permute-start | bytes 442376 | tf_op jit(solution)/shard_map/ppermute | solution.py:26
  197.3 5.9 %grad_of_down.1 = f32[96,768]{1,0:T(8,128)S(1)} custom-call(bf16[1280,1024]{1,0:T(8,128)(2,1)S(1)} %bitcast.77, bf16[256,768]{1,0:T(8,128)(2,1)S(1)} %bitcast.79, f32[1,256]{1,0:T(1,128)S(1)} %get-tuple-element.175.col_sum_ref, f32[1,256]{1,0:T(1,128)S(1)} %get-tuple-element.176.col_count_ref, f32[1,128]{1,0:T(1,128)S(1)} %get-tuple-element.177.live_ref, ...), custom_call_target="tpu_custom_call" | custom-call | flops 1006632960 | bytes 2621440 | tf_op jit(solution)/shard_map/grad_of_down/pallas_call | solution.py:755
  203.2 3.9 %collective-permute-done.32 = bf16[24,3072]{1,0:T(8,128)(2,1)S(1)} collective-permute-done((bf16[24,3072]{1,0:T(8,128)(2,1)S(1)}, bf16[24,3072]{1,0:T(8,128)(2,1)S(1)}, u32[]{:S(2)}, u32[]{:S(2)}) %collective-permute-start.32) | collective-permute-done | bytes 147488 | tf_op jit(solution)/shard_map/ppermute | solution.py:26
  209.6 6.8 %collective-permute-done.35.got_b = bf16[96,1536]{1,0:T(8,128)(2,1)S(1)} collective-permute-done((bf16[96,1536]{1,0:T(8,128)(2,1)S(1)}, bf16[96,1536]{1,0:T(8,128)(2,1)S(1)}, u32[]{:S(2)}, u32[]{:S(2)}) %collective-permute-start.35) | collective-permute-done | bytes 294944 | tf_op jit(solution)/shard_map/ppermute | solution.py:26
  223.0 3.7 %collective-permute-done.38 = bf16[32,3072]{1,0:T(8,128)(2,1)S(1)} collective-permute-done((bf16[32,3072]{1,0:T(8,128)(2,1)S(1)}, bf16[32,3072]{1,0:T(8,128)(2,1)S(1)}, u32[]{:S(2)}, u32[]{:S(2)}) %collective-permute-start.38) | collective-permute-done | bytes 196640 | tf_op jit(solution)/shard_map/ppermute | solution.py:26
  226.7 8.3 %collective-permute-done.37 = bf16[32,3072]{1,0:T(8,128)(2,1)S(1)} collective-permute-done((bf16[32,3072]{1,0:T(8,128)(2,1)S(1)}, bf16[32,3072]{1,0:T(8,128)(2,1)S(1)}, u32[]{:S(2)}, u32[]{:S(2)}) %collective-permute-start.37) | collective-permute-done | bytes 196640 | tf_op jit(solution)/shard_map/ppermute | solution.py:26
  (198 shorter events, 59.5 us)
Async XLA Ops:
  7.2 99.6 %all-gather.2.cloned.1.call-start = ((), (), s32[]{:S(2)}) async-start(), calls=%async_computation.2 | async-start | bytes 8921088 | tf_op jit(solution)/shard_map/all_gather | solution.py:1028
  10.3 25.7 %collective-permute-start.2 = (bf16[24,3584]{1,0:T(8,128)(2,1)S(1)}, bf16[24,3584]{1,0:T(8,128)(2,1)S(1)}, u32[]{:S(2)}, u32[]{:S(2)}) collective-permute-start(bf16[24,3584]{1,0:T(8,128)(2,1)S(1)} %pad_maximum_fusion.7), channel_id=1, source_target_pairs={{0,24},{1,25},{2,26},{3,27},{4,28},{5,29},{6,30},{7,31},{8,16},{9,... | collective-permute-start | bytes 516104 | tf_op jit(solution)/shard_map/ppermute | solution.py:26
  15.4 20.6 %collective-permute-start.1 = (bf16[24,3584]{1,0:T(8,128)(2,1)S(1)}, bf16[24,3584]{1,0:T(8,128)(2,1)S(1)}, u32[]{:S(2)}, u32[]{:S(2)}) collective-permute-start(bf16[24,3584]{1,0:T(8,128)(2,1)S(1)} %pad_maximum_fusion.7), channel_id=1, source_target_pairs={{0,16},{1,17},{2,18},{3,19},{4,20},{5,21},{6,22},{7,23},{8,24},{9,... | collective-permute-start | bytes 516104 | tf_op jit(solution)/shard_map/ppermute | solution.py:26
  15.4 20.6 %collective-permute-start = (bf16[24,3584]{1,0:T(8,128)(2,1)S(1)}, bf16[24,3584]{1,0:T(8,128)(2,1)S(1)}, u32[]{:S(2)}, u32[]{:S(2)}) collective-permute-start(bf16[24,3584]{1,0:T(8,128)(2,1)S(1)} %pad_maximum_fusion.7), channel_id=1, source_target_pairs={{0,8},{1,9},{2,10},{3,11},{4,12},{5,13},{6,14},{7,15},{8,0},{9,1},... | collective-permute-start | bytes 516104 | tf_op jit(solution)/shard_map/ppermute | solution.py:26
  37.0 24.5 %collective-permute-start.3 = (bf16[96,3584]{1,0:T(8,128)(2,1)}, bf16[96,3584]{1,0:T(8,128)(2,1)S(1)}, u32[]{:S(2)}, u32[]{:S(2)}) collective-permute-start(bf16[96,3584]{1,0:T(8,128)(2,1)} %pad_maximum_fusion.2.refs_0_), channel_id=1, source_target_pairs={{0,2},{1,3},{2,0},{3,1},{4,6},{5,7},{6,4},{7,5},{8,10},{9,11},{10,... | collective-permute-start | bytes 2064392 | tf_op jit(solution)/shard_map/ppermute | solution.py:26
  38.7 22.9 %collective-permute-start.4 = (bf16[96,3584]{1,0:T(8,128)(2,1)}, bf16[96,3584]{1,0:T(8,128)(2,1)S(1)}, u32[]{:S(2)}, u32[]{:S(2)}) collective-permute-start(bf16[96,3584]{1,0:T(8,128)(2,1)} %pad_maximum_fusion.2.refs_0_), channel_id=1, source_target_pairs={{0,4},{1,5},{2,6},{3,7},{4,0},{5,1},{6,2},{7,3},{8,12},{9,13},{10,... | collective-permute-start | bytes 2064392 | tf_op jit(solution)/shard_map/ppermute | solution.py:26
  72.0 21.7 %collective-permute-start.12 = (bf16[1,40,1024]{2,1,0:T(8,128)(2,1)S(1)}, bf16[1,40,1024]{2,1,0:T(8,128)(2,1)S(1)}, u32[]{:S(2)}, u32[]{:S(2)}) collective-permute-start(bf16[1,40,1024]{2,1,0:T(8,128)(2,1)S(1)} %bitcast.81), channel_id=1, source_target_pairs={{0,8},{1,9},{2,10},{3,11},{4,12},{5,13},{6,14},{7,15},{8,0},{9,1},... | collective-permute-start | bytes 245768 | tf_op jit(solution)/shard_map/ppermute | solution.py:26
  73.6 20.1 %collective-permute-start.13 = (bf16[1,40,1024]{2,1,0:T(8,128)(2,1)S(1)}, bf16[1,40,1024]{2,1,0:T(8,128)(2,1)S(1)}, u32[]{:S(2)}, u32[]{:S(2)}) collective-permute-start(bf16[1,40,1024]{2,1,0:T(8,128)(2,1)S(1)} %bitcast.82), channel_id=1, source_target_pairs={{0,16},{1,17},{2,18},{3,19},{4,20},{5,21},{6,22},{7,23},{8,24},{9,... | collective-permute-start | bytes 245768 | tf_op jit(solution)/shard_map/ppermute | solution.py:26
  76.0 17.8 %collective-permute-start.14 = (bf16[1,40,1024]{2,1,0:T(8,128)(2,1)S(1)}, bf16[1,40,1024]{2,1,0:T(8,128)(2,1)S(1)}, u32[]{:S(2)}, u32[]{:S(2)}) collective-permute-start(bf16[1,40,1024]{2,1,0:T(8,128)(2,1)S(1)} %bitcast.83), channel_id=1, source_target_pairs={{0,24},{1,25},{2,26},{3,27},{4,28},{5,29},{6,30},{7,31},{8,16},{9,... | collective-permute-start | bytes 245768 | tf_op jit(solution)/shard_map/ppermute | solution.py:26
  97.2 21.6 %all-to-all-start = ((bf16[40,32,96]{2,0,1:T(8,128)(2,1)}), bf16[40,32,96]{2,0,1:T(8,128)(2,1)S(1)}, u32[]{:S(2)}, u32[]{:S(2)}) async-start(bf16[40,32,96]{2,0,1:T(8,128)(2,1)} %copy.68), calls=%async_computation | async-start | bytes 655360 | tf_op jit(solution)/shard_map/all_to_all | solution.py:1086
  106.8 11.9 %collective-permute-start.17 = (bf16[2,40,1024]{2,1,0:T(8,128)(2,1)S(1)}, bf16[2,40,1024]{2,1,0:T(8,128)(2,1)S(1)}, u32[]{:S(2)}, u32[]{:S(2)}) collective-permute-start(bf16[2,40,1024]{2,1,0:T(8,128)(2,1)S(1)} %slice.72), channel_id=1, source_target_pairs={{0,4},{1,5},{2,6},{3,7},{4,0},{5,1},{6,2},{7,3},{8,12},{9,13},{10,... | collective-permute-start | bytes 491528 | tf_op jit(solution)/shard_map/ppermute | solution.py:26
  108.4 10.4 %collective-permute-start.18 = (bf16[2,40,1024]{2,1,0:T(8,128)(2,1)S(1)}, bf16[2,40,1024]{2,1,0:T(8,128)(2,1)S(1)}, u32[]{:S(2)}, u32[]{:S(2)}) collective-permute-start(bf16[2,40,1024]{2,1,0:T(8,128)(2,1)S(1)} %slice.73), channel_id=1, source_target_pairs={{0,2},{1,3},{2,0},{3,1},{4,6},{5,7},{6,4},{7,5},{8,10},{9,11},{10,... | collective-permute-start | bytes 491528 | tf_op jit(solution)/shard_map/ppermute | solution.py:26
  120.7 15.8 %all-to-all-start.1 = ((bf16[32,8,768]{2,1,0:T(8,128)(2,1)}), bf16[32,8,768]{2,1,0:T(8,128)(2,1)S(1)}, u32[]{:S(2)}, u32[]{:S(2)}) async-start(bf16[32,8,768]{2,1,0:T(8,128)(2,1)} %broadcast_in_dim.5), calls=%async_computation.1 | async-start | bytes 786432 | tf_op jit(solution)/shard_map/all_to_all | solution.py:46
  159.1 16.1 %collective-permute-start.22 = (bf16[192,1536]{1,0:T(8,128)(2,1)S(1)}, bf16[192,1536]{1,0:T(8,128)(2,1)S(1)}, u32[]{:S(2)}, u32[]{:S(2)}) collective-permute-start(bf16[192,1536]{1,0:T(8,128)(2,1)S(1)} %get-tuple-element.157.refs_1_), channel_id=1, source_target_pairs={{0,2},{1,3},{2,0},{3,1},{4,6},{5,7},{6,4},{7,5},{8,10},{9,11},{10,... | collective-permute-start | bytes 1769480 | tf_op jit(solution)/shard_map/ppermute | solution.py:26
  159.8 15.5 %collective-permute-start.23 = (bf16[192,1536]{1,0:T(8,128)(2,1)S(1)}, bf16[192,1536]{1,0:T(8,128)(2,1)S(1)}, u32[]{:S(2)}, u32[]{:S(2)}) collective-permute-start(bf16[192,1536]{1,0:T(8,128)(2,1)S(1)} %get-tuple-element.159.refs_3_), channel_id=1, source_target_pairs={{0,4},{1,5},{2,6},{3,7},{4,0},{5,1},{6,2},{7,3},{8,12},{9,13},{10,... | collective-permute-start | bytes 1769480 | tf_op jit(solution)/shard_map/ppermute | solution.py:26
  179.7 10.4 %collective-permute-start.26 = (bf16[384,1536]{1,0:T(8,128)(2,1)S(1)}, bf16[384,1536]{1,0:T(8,128)(2,1)S(1)}, u32[]{:S(2)}, u32[]{:S(2)}) collective-permute-start(bf16[384,1536]{1,0:T(8,128)(2,1)S(1)} %get-tuple-element.179), channel_id=1, source_target_pairs={{0,1},{1,0},{2,3},{3,2},{4,5},{5,4},{6,7},{7,6},{8,9},{9,8},{10,11... | collective-permute-start | bytes 3538952 | tf_op jit(solution)/shard_map/ppermute | solution.py:26
  179.8 10.3 %collective-permute-start.27 = (bf16[384,1536]{1,0:T(8,128)(2,1)S(1)}, bf16[384,1536]{1,0:T(8,128)(2,1)S(1)}, u32[]{:S(2)}, u32[]{:S(2)}) collective-permute-start(bf16[384,1536]{1,0:T(8,128)(2,1)S(1)} %get-tuple-element.181), channel_id=1, source_target_pairs={{0,1},{1,0},{2,3},{3,2},{4,5},{5,4},{6,7},{7,6},{8,9},{9,8},{10,11... | collective-permute-start | bytes 3538952 | tf_op jit(solution)/shard_map/ppermute | solution.py:26
  190.8 16.4 %collective-permute-start.29 = (bf16[208,1536]{1,0:T(8,128)(2,1)S(1)}, bf16[208,1536]{1,0:T(8,128)(2,1)S(1)}, u32[]{:S(2)}, u32[]{:S(2)}) collective-permute-start(bf16[208,1536]{1,0:T(8,128)(2,1)S(1)} %get-tuple-element.189), channel_id=1, source_target_pairs={{0,2},{1,3},{2,0},{3,1},{4,6},{5,7},{6,4},{7,5},{8,10},{9,11},{10,... | collective-permute-start | bytes 1916936 | tf_op jit(solution)/shard_map/ppermute | solution.py:26
  191.9 15.2 %collective-permute-start.30 = (bf16[192,1536]{1,0:T(8,128)(2,1)S(1)}, bf16[192,1536]{1,0:T(8,128)(2,1)S(1)}, u32[]{:S(2)}, u32[]{:S(2)}) collective-permute-start(bf16[192,1536]{1,0:T(8,128)(2,1)S(1)} %get-tuple-element.191), channel_id=1, source_target_pairs={{0,4},{1,5},{2,6},{3,7},{4,0},{5,1},{6,2},{7,3},{8,12},{9,13},{10,... | collective-permute-start | bytes 1769480 | tf_op jit(solution)/shard_map/ppermute | solution.py:26
  192.9 10.3 %collective-permute-start.31 = (bf16[24,3072]{1,0:T(8,128)(2,1)S(1)}, bf16[24,3072]{1,0:T(8,128)(2,1)S(1)}, u32[]{:S(2)}, u32[]{:S(2)}) collective-permute-start(bf16[24,3072]{1,0:T(8,128)(2,1)S(1)} %get-tuple-element.192), channel_id=1, source_target_pairs={{0,8},{1,9},{2,10},{3,11},{4,12},{5,13},{6,14},{7,15},{8,0},{9,1},... | collective-permute-start | bytes 442376 | tf_op jit(solution)/shard_map/ppermute | solution.py:26
  193.9 13.2 %collective-permute-start.32 = (bf16[24,3072]{1,0:T(8,128)(2,1)S(1)}, bf16[24,3072]{1,0:T(8,128)(2,1)S(1)}, u32[]{:S(2)}, u32[]{:S(2)}) collective-permute-start(bf16[24,3072]{1,0:T(8,128)(2,1)S(1)} %get-tuple-element.193), channel_id=1, source_target_pairs={{0,16},{1,17},{2,18},{3,19},{4,20},{5,21},{6,22},{7,23},{8,24},{9,... | collective-permute-start | bytes 442376 | tf_op jit(solution)/shard_map/ppermute | solution.py:26
  194.6 12.5 %collective-permute-start.33 = (bf16[24,3072]{1,0:T(8,128)(2,1)S(1)}, bf16[24,3072]{1,0:T(8,128)(2,1)S(1)}, u32[]{:S(2)}, u32[]{:S(2)}) collective-permute-start(bf16[24,3072]{1,0:T(8,128)(2,1)S(1)} %get-tuple-element.194), channel_id=1, source_target_pairs={{0,24},{1,25},{2,26},{3,27},{4,28},{5,29},{6,30},{7,31},{8,16},{9,... | collective-permute-start | bytes 442376 | tf_op jit(solution)/shard_map/ppermute | solution.py:26
  217.7 17.2 %collective-permute-start.37 = (bf16[32,3072]{1,0:T(8,128)(2,1)S(1)}, bf16[32,3072]{1,0:T(8,128)(2,1)S(1)}, u32[]{:S(2)}, u32[]{:S(2)}) collective-permute-start(bf16[32,3072]{1,0:T(8,128)(2,1)S(1)} %get-tuple-element.207), channel_id=1, source_target_pairs={{0,16},{1,17},{2,18},{3,19},{4,20},{5,21},{6,22},{7,23},{8,24},{9,... | collective-permute-start | bytes 589832 | tf_op jit(solution)/shard_map/ppermute | solution.py:26
  219.8 15.1 %collective-permute-start.36 = (bf16[32,3072]{1,0:T(8,128)(2,1)S(1)}, bf16[32,3072]{1,0:T(8,128)(2,1)S(1)}, u32[]{:S(2)}, u32[]{:S(2)}) collective-permute-start(bf16[32,3072]{1,0:T(8,128)(2,1)S(1)} %get-tuple-element.206), channel_id=1, source_target_pairs={{0,8},{1,9},{2,10},{3,11},{4,12},{5,13},{6,14},{7,15},{8,0},{9,1},... | collective-permute-start | bytes 589832 | tf_op jit(solution)/shard_map/ppermute | solution.py:26
  (52 other events, 414.7 us)
Sparse Core Ops, SparseCore 0:
  11.5 95.2 all-gather.1

commit v9 on v8

--- a/solution.py
+++ b/solution.py
@@ -40,9 +40,7 @@
     return jnp.stack(parts, axis=1).reshape((-1,) + held.shape[1:])
 
 
-def spread(block):
-    peers = lax.axis_size(AXIS)
-    copies = jnp.broadcast_to(block[None], (peers,) + block.shape)
+def exchanged(copies):
     return lax.all_to_all(copies, AXIS, split_axis=0, concat_axis=0, tiled=True)
 
 
@@ -593,10 +591,11 @@
 
     @pl.when(step == pl.num_programs(0) - 1)
     def _():
-        out_ref[...] = unit_rows(acc[...])[0].astype(bf16)
-
-
-def image_up(normed2, whole, middle_sum, early):
+        unit = unit_rows(acc[...])[0].astype(bf16)
+        out_ref[...] = jnp.broadcast_to(unit[None], out_ref.shape)
+
+
+def image_up(normed2, whole, middle_sum, early, peers):
     rows, count = normed2.shape[0], middle_sum.shape[0]
     fold = FF // D
     before, part = EARLY // TILE, TILE // fold
@@ -604,7 +603,7 @@
     return pl.pallas_call(
         functools.partial(image_up_kernel, fold),
         grid=(FF // TILE - before,),
-        out_shape=jax.ShapeDtypeStruct((count, D), bf16),
+        out_shape=jax.ShapeDtypeStruct((peers, count, D), bf16),
         in_specs=[
             fixed((rows, D)),
             pl.BlockSpec((D, TILE), lambda i: (0, FF // TILE + i)),
@@ -613,7 +612,7 @@
             fixed((count, D)),
             fixed((count, EARLY)),
         ],
-        out_specs=fixed((count, D)),
+        out_specs=pl.BlockSpec((peers, count, D), lambda i: (0, 0, 0)),
         scratch_shapes=[pltpu.VMEM((count, D), f32), pltpu.VMEM((TILE, TILE), bf16)],
         compiler_params=params(),
         cost_estimate=cost(2 * rows * D * FF, 4 * D * FF, 15 * rows * FF),
@@ -690,7 +689,7 @@
     return grad - unit * jnp.sum(grad * unit, axis=-1, keepdims=True)
 
 
-def loss_kernel(
+def loss_into(
     pack_ref, image_ref, own_ref, unit_ref, inv_ref, loss_ref, row_ref, low_ref, col_sum_ref,
     col_count_ref, live_ref
 ):
@@ -714,21 +713,6 @@
     low_ref[...] = row.astype(bf16)
 
 
-def loss_and_rows(pack, image_all, own_pack, unit, inverse):
-    images, count = image_all.shape[0], own_pack.shape[0]
-    shapes = [(1, 128), (count, D), (count, D), (1, images), (1, images), (1, 128)]
-    kinds = [f32, f32, bf16, f32, f32, f32]
-    return pl.pallas_call(
-        loss_kernel,
-        out_shape=[jax.ShapeDtypeStruct(*item) for item in zip(shapes, kinds)],
-        in_specs=in_vmem(5),
-        out_specs=in_vmem(len(shapes)),
-        compiler_params=params(16 << 20),
-        cost_estimate=cost(2 * pack.shape[0] * images * D, 2 * pack.size, pack.shape[0] * images),
-        name="loss_and_rows",
-    )(pack, image_all, own_pack, unit, inverse)
-
-
 def down_kernel(pack_ref, image_ref, col_sum_ref, col_count_ref, live_ref, hid_ref, *refs):
     step, out_ref = pl.program_id(0), refs[-1]
     text_rows = pack_ref[:, :D]
@@ -769,10 +753,12 @@
     )(pack, image_all, col_sum, col_count, live_total, hidden_cols, *after)
 
 
-def mlp_back_kernel(
-    low_ref, gain_ref, row_ref, wd_hbm, slope_hbm, wu_hbm, lhs_hbm, mid_hbm, keep_a, send_a, keep_b,
-    send_b, out_ref, sums_out, wd_ref, slope_ref, wu_ref, lhs_ref, mid_ref, sems, whole_sems
-):
+def mlp_back_kernel(with_loss, gain_ref, *refs):
+    given, refs = (refs[:5], refs[5:]) if with_loss else (refs[:2], refs[2:])
+    wd_hbm, slope_hbm, wu_hbm, lhs_hbm, mid_hbm = refs[:5]
+    keep_a, send_a, keep_b, send_b, out_ref, sums_out = refs[5:11]
+    wd_ref, slope_ref, wu_ref, lhs_ref, mid_ref, sems, whole_sems = refs[-7:]
+    low_ref, row_ref = refs[-9:-7] if with_loss else given
     count, rows = low_ref.shape[0], out_ref.shape[0]
     half, steps = D // 2, FF // 2 // TILE
 
@@ -789,6 +775,9 @@
     for copy in copies(0, 0):
         copy.start()
     lhs_copy.start()
+    if with_loss:
+        loss_ref, *stats = refs[11:15]
+        loss_into(*given, loss_ref, row_ref, low_ref, *stats)
     for k, (keep, send) in enumerate(((keep_a, send_a), (keep_b, send_b))):
 
         @pl.loop(0, steps)
@@ -848,27 +837,34 @@
         out_ref[at, :] = row + norm_back(unit, scale, gain, grad)
 
 
-def mlp_back(grad_row, grad_low, weight_down, slope, weight_up, lhs, middle, gain):
-    rows = slope.shape[0]
-    return pl.pallas_call(
-        mlp_back_kernel,
-        out_shape=[stays((D // 2, FF // 2), bf16)] * 4
-        + [stays((rows, D), f32), stays((1, 2 * D), f32)],
-        in_specs=in_vmem(3) + [pl.BlockSpec(memory_space=pltpu.HBM)] * 5,
-        out_specs=in_vmem(6),
-        scratch_shapes=[
-            pltpu.VMEM((2, TILE, D), bf16),
-            pltpu.VMEM((2, rows, TILE), bf16),
-            pltpu.VMEM((2, D, TILE), bf16),
-            pltpu.VMEM((2, D, rows), bf16),
-            pltpu.VMEM((rows, D), f32),
-            pltpu.SemaphoreType.DMA((3, 2)),
-            pltpu.SemaphoreType.DMA((2,)),
-        ],
-        compiler_params=params(28 << 20),
+def mlp_back(given, weight_down, slope, weight_up, lhs, middle, gain):
+    rows, count = slope.shape[0], given[-2].shape[0]
+    with_loss = len(given) == 5
+    shapes = [stays((D // 2, FF // 2), bf16)] * 4 + [stays((rows, D), f32), stays((1, 2 * D), f32)]
+    scratch = [
+        pltpu.VMEM((2, TILE, D), bf16),
+        pltpu.VMEM((2, rows, TILE), bf16),
+        pltpu.VMEM((2, D, TILE), bf16),
+        pltpu.VMEM((2, D, rows), bf16),
+        pltpu.VMEM((rows, D), f32),
+        pltpu.SemaphoreType.DMA((3, 2)),
+        pltpu.SemaphoreType.DMA((2,)),
+    ]
+    if with_loss:
+        images = given[1].shape[0]
+        wide = [(1, 128), (1, images), (1, images), (1, 128)]
+        shapes += [jax.ShapeDtypeStruct(shape, f32) for shape in wide]
+        scratch = [pltpu.VMEM((count, D), bf16), pltpu.VMEM((count, D), f32)] + scratch
+    return pl.pallas_call(
+        functools.partial(mlp_back_kernel, with_loss),
+        out_shape=shapes,
+        in_specs=in_vmem(1 + len(given)) + [pl.BlockSpec(memory_space=pltpu.HBM)] * 5,
+        out_specs=in_vmem(len(shapes)),
+        scratch_shapes=scratch,
+        compiler_params=params(32 << 20),
         cost_estimate=cost(4 * rows * D * FF, 4 * D * FF + 2 * rows * FF + 2 * D * FF, rows * FF),
         name="mlp_back",
-    )(grad_low, gain, grad_row, *in_hbm(weight_down, slope, weight_up, lhs, middle))
+    )(gain, *given, *in_hbm(weight_down, slope, weight_up, lhs, middle))
 
 
 def attention_back_kernel(first, grad_ref, wo_ref, qkv_ref, lse_ref, *refs):
@@ -1086,37 +1082,37 @@
         hidden_cols = lax.all_to_all(scaled_sum, AXIS, split_axis=1, concat_axis=0, tiled=True)
         whole, text_beside, text_above = lax.optimization_barrier((whole, text_beside, text_above))
         halves = diagonal(text_beside, text_above)
-    image_low = image_up(normed_img, whole, middle_img, early)
+    image_low = image_up(normed_img, whole, middle_img, early, peers)
     if small:
         image_low, halves, hidden_cols = lax.optimization_barrier((image_low, halves, hidden_cols))
         across = jnp.concatenate(halves, axis=0)
         held = joined(joined(held, text_beside, 2), joined(text_above, across, 2), 4, 4)
         text_pack = joined(held, swapped(held, 1), 1).reshape(-1, D + total_images)
-    image_all = spread(image_low).reshape(total_images, D)
+    image_all = exchanged(image_low).reshape(total_images, D)
     if small:
         image_all, text_pack = in_turn(image_all, text_pack)
 
     if small:
-        loss_value, grad_row, row_low, col_sum, col_count, live_total = loss_and_rows(
-            text_pack, image_all, own_pack, text_unit, inverse
-        )
-        loss_value = loss_value[0, 0]
+        given = (text_pack, image_all, own_pack, text_unit, inverse)
     else:
         text_low, pos = own_pack[:, :D], own_pack[:, D:].astype(f32)
-        sums = lax.psum(sums_over_captions(text_low, pos, image_all), AXIS)
-        loss_value = loss_from(sums)[0, 0]
-        grad = grad_of_unit(text_low, pos, image_all, sums[0], sums[1], sums[4])
+        totals = lax.psum(sums_over_captions(text_low, pos, image_all), AXIS)
+        loss_value = loss_from(totals)
+        grad = grad_of_unit(text_low, pos, image_all, totals[0], totals[1], totals[4])
         grad_row = inverse[:, :1] * turned(grad, text_unit) * (1.0 / TXT_LEN)
         row_low = grad_row.astype(bf16)
-
-    *up, grad_middle, sums = mlp_back(
-        grad_row, row_low, txt_down, slope, txt_up, lhs_up, middle, txt_gain2
-    )
+        given = (row_low, grad_row)
+
+    *up, grad_middle, sums = mlp_back(given, txt_down, slope, txt_up, lhs_up, middle, txt_gain2)
+    if small:
+        *up, grad_middle, sums, loss_value, col_sum, col_count, live_total = (
+            *up, grad_middle, sums
+        )
     stages = len(order_a)
-    low_one, proj_one = attention_back(grad_middle, txt_out, project, log_sums, 0, 1)
+    low_one, proj_one = attention_back(grad_middle, txt_out, project, log_sums, 0, 2)
     for stage in range(stages - 2):
         up = fold(hand_on(up, stage), (proj_one,))
-    low_two, proj_two = attention_back(grad_middle, txt_out, project, log_sums, 1, 4, up)
+    low_two, proj_two = attention_back(grad_middle, txt_out, project, log_sums, 2, 3, up)
     proj_two, normed1 = in_turn(proj_two, normed1)
     lhs_rest = left_factors((source_a, normed1), (source_b, normed1), (source_b, attended))
     up = fold(hand_on(up, stages - 2), (proj_two, lhs_rest))
@@ -1156,7 +1152,7 @@
         norms = rest_share[per]
         rest_share = rest_share[:per]
     return (
-        loss_value,
+        loss_value[0, 0],
         caption_grad,
         norms[:D],
         norms[D : 2 * D],

time: 245 us -> 243 us (level)
    pallas_call x2 -> x1, Pallas kernels: 16.7 us -> 16 us  [mlp_back(): pl.pallas_call(functools.partial(mlp_back_kernel, with_loss), out_shape=s...]
  transfers between devices with their start and end apart: 42 -> 42, of which waited for: 15 -> 16; matrix products, arithmetic and copies ran while one was open for 3% -> 3% of each run, Pallas kernels for 36% -> 36%
where the time goes in v9:
time: 243 us; the launch traced here: 242 us
  Pallas kernels  110 us (45%)
  waiting for transfers between devices  51.6 us (21%)
  starting transfers between devices  50.4 us (21%)
  between operations  14.9 us (6%)
  local copies, waits for them, and re-layouts  9.43 us (4%)
  other arithmetic  5.5 us (2%)
    ppermute x39, starting transfers between devices, swapped(): return lax.ppermute(value, AXIS, [(i, i ^ mask) for i in range(peers)])  42 us
    ppermute x39, waiting for transfers between devices, swapped(): return lax.ppermute(value, AXIS, [(i, i ^ mask) for i in range(peers)])  36.4 us
    pallas_call x1, Pallas kernels, text_front(): pl.pallas_call(text_front_kernel, out_shape=[jax.ShapeDtypeStruct(*item)...  18 us
    pallas_call x1, Pallas kernels, mlp_back(): pl.pallas_call(functools.partial(mlp_back_kernel, with_loss), out_shape=s...  16 us
    pallas_call x1, Pallas kernels, image_front(): pl.pallas_call(functools.partial(image_front_kernel, windows), out_shape=...  15.8 us
    all_to_all x1, waiting for transfers between devices, exchanged(): return lax.all_to_all(copies, AXIS, split_axis=0, concat_axis=0, tiled=True)  12.6 us
    pallas_call x1, Pallas kernels, text_up(): pl.pallas_call(text_up_kernel, grid=(FF // TILE,), out_shape=[jax.ShapeDt...  12 us
    pallas_call x2, Pallas kernels, attention_back(): pl.pallas_call(functools.partial(attention_back_kernel, first), out_shape...  11.5 us
  transfers between devices with their start and end apart: 42, of which 16 were waited for; matrix products, arithmetic and copies ran while one was open for 3% of the time, Pallas kernels for 36%

profile of v9, /device:TPU:0, one launch (start us, length us, event | category | flops | bytes accessed | tf_op | source)
XLA Modules:
  0.0 241.6 jit_solution(13264490947362621311)
XLA Ops:
  10.3 3.1 %collective-permute-start = (bf16[24,3584]{1,0:T(8,128)(2,1)S(1)}, bf16[24,3584]{1,0:T(8,128)(2,1)S(1)}, u32[]{:S(2)}, u32[]{:S(2)}) collective-permute-start(bf16[24,3584]{1,0:T(8,128)(2,1)S(1)} %pad_maximum_fusion.7), channel_id=1, source_target_pairs={{0,8},{1,9},{2,10},{3,11},{4,12},{5,13},{6,14},{7,15},{8,0},{9,1},... | collective-permute-start | bytes 516104 | tf_op jit(solution)/shard_map/ppermute | solution.py:26
  13.4 2.6 %collective-permute-start.1 = (bf16[24,3584]{1,0:T(8,128)(2,1)S(1)}, bf16[24,3584]{1,0:T(8,128)(2,1)S(1)}, u32[]{:S(2)}, u32[]{:S(2)}) collective-permute-start(bf16[24,3584]{1,0:T(8,128)(2,1)S(1)} %pad_maximum_fusion.7), channel_id=1, source_target_pairs={{0,16},{1,17},{2,18},{3,19},{4,20},{5,21},{6,22},{7,23},{8,24},{9,... | collective-permute-start | bytes 516104 | tf_op jit(solution)/shard_map/ppermute | solution.py:26
  16.8 18.0 %text_front.1 = (bf16[640,768]{1,0:T(8,128)(2,1)}, bf16[640,2304]{1,0:T(8,128)(2,1)}, bf16[640,768]{1,0:T(8,128)(2,1)}, f32[640,768]{1,0:T(8,128)}, bf16[640,768...) custom-call(bf16[640,768]{1,0:T(8,128)(2,1)} %refs_3_.1, f32[768]{0:T(1024)} %refs_4_.1, f32[768]{0:T(1024)} %b1_ref.2, ...), custom_call_target="tpu_custom_call" | custom-call | flops 3019898880 | bytes 11599872 | tf_op jit(solution)/shard_map/text_front/pallas_call | solution.py:364
  40.9 12.0 %text_up.1 = (bf16[640,3072]{1,0:T(8,128)(2,1)}, f32[40,3072]{1,0:T(8,128)}, f32[40,768]{1,0:T(8,128)}, f32[40,128]{1,0:T(8,128)}) custom-call(bf16[640,768]{1,0:T(8,128)(2,1)} %get-tuple-element.118.h2_ref.refs_1_.refs_3_, bf16[768,3072]{1,0:T(8,128)(2,1)} %refs_7_.1, bf16[3072,768]{1,0:T(8,128)(2,1)} %refs_5_.1, f32[40,768]{1,0:T(8,128)} %get-tuple-element.113.sum_ref, ...), custom_call_target="tpu_custom_call" | custom-call | flops 3019898880 | bytes 13369344 | tf_op jit(solution)/shard_map/text_up/pallas_call | solution.py:535
  52.9 8.6 %collective-permute-done.3.refs_1_ = bf16[96,3584]{1,0:T(8,128)(2,1)S(1)} collective-permute-done((bf16[96,3584]{1,0:T(8,128)(2,1)}, bf16[96,3584]{1,0:T(8,128)(2,1)S(1)}, u32[]{:S(2)}, u32[]{:S(2)}) %collective-permute-start.3) | collective-permute-done | bytes 688160 | tf_op jit(solution)/shard_map/ppermute | solution.py:26
  67.5 3.2 %left_factors.2.refs_8_ = bf16[2,768,640]{2,1,0:T(8,128)(2,1)S(1)} custom-call(s32[768,1]{1,0:T(8,128)S(1)} %fusion.8.refs_0_, bf16[640,768]{1,0:T(8,128)(2,1)S(1)} %copy-done.19, s32[768,1]{1,0:T(8,128)S(1)} %fusion.9.refs_2_.order_ref.refs_4_, bf16[640,768]{1,0:T(8,128)(2,1)S(1)} %copy-done.19), custom_call_target="tpu_custom_call" | custom-call | flops 1509949440 | bytes 3932160 | tf_op jit(solution)/shard_map/left_factors/pallas_call | solution.py:638
  72.6 3.0 %collective-permute-start.13 = (bf16[1,40,1024]{2,1,0:T(8,128)(2,1)S(1)}, bf16[1,40,1024]{2,1,0:T(8,128)(2,1)S(1)}, u32[]{:S(2)}, u32[]{:S(2)}) collective-permute-start(bf16[1,40,1024]{2,1,0:T(8,128)(2,1)S(1)} %bitcast.82), channel_id=1, source_target_pairs={{0,16},{1,17},{2,18},{3,19},{4,20},{5,21},{6,22},{7,23},{8,24},{9,... | collective-permute-start | bytes 245768 | tf_op jit(solution)/shard_map/ppermute | solution.py:26
  78.2 15.8 %image_front.1 = (bf16[400,768]{1,0:T(8,128)(2,1)}, f32[8,768]{1,0:T(8,128)}, f32[8,512]{1,0:T(8,128)}) custom-call(bf16[400,768]{1,0:T(8,128)(2,1)} %x_ref.3, s32[768,1]{1,0:T(8,128)} %copy-done.7, bf16[768]{0:T(1024)(128)(2,1)} %g1_ref.3, bf16[768]{0:T(1024)(128)(2,1)} %b1_ref.3, bf16[768]{0:T(1024)(128)(2,1)} %g2_ref.3, bf16[768]{0:T(1024)(128)(2,1)} %b2_ref.3, ...), custom_call_target="tpu_custom_call" | custom-call | flops 2831155200 | bytes 4718592 | tf_op jit(solution)/shard_map/image_front/pallas_call | solution.py:439
  97.1 5.3 %all-to-all-start = ((bf16[40,32,96]{2,0,1:T(8,128)(2,1)}), bf16[40,32,96]{2,0,1:T(8,128)(2,1)S(1)}, u32[]{:S(2)}, u32[]{:S(2)}) async-start(bf16[40,32,96]{2,0,1:T(8,128)(2,1)} %copy.68), calls=%async_computation | async-start | bytes 655360 | tf_op jit(solution)/shard_map/all_to_all | solution.py:1082
  110.7 8.9 %image_up.1 = bf16[32,8,768]{2,1,0:T(8,128)(2,1)} custom-call(bf16[400,768]{1,0:T(8,128)(2,1)} %get-tuple-element.125.h2_ref, bf16[768,5632]{1,0:T(8,128)(2,1)} %all-gather.2.cloned.1.call-done.wu_ref.wd_ref.first_ref, bf16[768,5632]{1,0:T(8,128)(2,1)} %all-gather.2.cloned.1.call-done.wu_ref.wd_ref.first_ref, ...), custom_call_target="tpu_custom_call" | custom-call | flops 1887436800 | bytes 9437184 | tf_op jit(solution)/shard_map/image_up/pallas_call | solution.py:603
  120.3 3.1 %all-to-all-start.1 = ((bf16[32,8,768]{2,1,0:T(8,128)(2,1)}), bf16[32,8,768]{2,1,0:T(8,128)(2,1)S(1)}, u32[]{:S(2)}, u32[]{:S(2)}) async-start(bf16[32,8,768]{2,1,0:T(8,128)(2,1)} %image_up.1), calls=%async_computation.1 | async-start | bytes 786432 | tf_op jit(solution)/shard_map/all_to_all | solution.py:44
  124.0 12.6 %all-to-all-done.1 = bf16[32,8,768]{2,1,0:T(8,128)(2,1)S(1)} async-done(((bf16[32,8,768]{2,1,0:T(8,128)(2,1)}), bf16[32,8,768]{2,1,0:T(8,128)(2,1)S(1)}, u32[]{:S(2)}, u32[]{:S(2)}) %all-to-all-start.1) | async-done | bytes 393248 | tf_op jit(solution)/shard_map/all_to_all | solution.py:44
  137.3 16.0 %mlp_back.1 = (bf16[384,1536]{1,0:T(8,128)(2,1)S(1)}, bf16[384,1536]{1,0:T(8,128)(2,1)S(1)}, bf16[384,1536]{1,0:T(8,128)(2,1)S(1)}, bf16[384,1536]{1,0:T(8,128)(...) custom-call(f32[768]{0:T(1024)S(1)} %copy-done.17, ...), custom_call_target="tpu_custom_call" | custom-call | flops 6039797760 | bytes 18087936 | tf_op jit(solution)/shard_map/mlp_back/pallas_call | solution.py:858
  153.9 4.6 %attention_back.2 = (bf16[256,768]{1,0:T(8,128)(2,1)S(1)}, bf16[256,2304]{1,0:T(8,128)(2,1)S(1)}) custom-call(f32[640,768]{1,0:T(8,128)S(1)} %get-tuple-element.144.grad_ref.refs_5_, bf16[768,768]{1,0:T(8,128)(2,1)S(1)} %copy-done.1, bf16[640,2304]{1,0:T(8,128)(2,1)S(1)} %copy-done, f32[80,128]{1,0:T(8,128)S(1)} %copy-done.12), custom_call_target="tpu_custom_call" | custom-call | flops 1509949440 | bytes 4325376 | tf_op jit(solution)/shard_map/attention_back/pallas_call | solution.py:908
  161.2 6.9 %attention_back.3 = (bf16[384,768]{1,0:T(8,128)(2,1)S(1)}, bf16[384,2304]{1,0:T(8,128)(2,1)S(1)}) custom-call(f32[640,768]{1,0:T(8,128)S(1)} %get-tuple-element.144.grad_ref.refs_5_, bf16[768,768]{1,0:T(8,128)(2,1)S(1)} %copy-done.1, bf16[640,2304]{1,0:T(8,128)(2,1)S(1)} %copy-done, f32[80,128]{1,0:T(8,128)S(1)} %copy-done.12, ...), custom_call_target="tpu_custom_call" | custom-call | flops 2264924160 | bytes 5898240 | tf_op jit(solution)/shard_map/attention_back/pallas_call | solution.py:908
  168.1 4.8 %left_factors.3.refs_1_.lhs_ref = bf16[3,768,640]{2,1,0:T(8,128)(2,1)S(1)} custom-call(s32[768,1]{1,0:T(8,128)S(1)} %copy-done.10, bf16[640,768]{1,0:T(8,128)(2,1)S(1)} %copy-done.20, s32[768,1]{1,0:T(8,128)S(1)} %copy-done.8, bf16[640,768]{1,0:T(8,128)(2,1)S(1)} %copy-done.20, s32[768,1]{1,0:T(8,128)S(1)} %copy-done.8, bf16[640,768]{1,0:T(8,128)(2,1)S(1)} %copy-done.21), custom_call_target="tpu_custom_call" | custom-call | flops 2264924160 | bytes 5898240 | tf_op jit(solution)/shard_map/left_factors/pallas_call | solution.py:638
  175.7 3.9 %weight_back.1 = (bf16[384,1536]{1,0:T(8,128)(2,1)S(1)}, bf16[384,1536]{1,0:T(8,128)(2,1)S(1)}, bf16[384,1536]{1,0:T(8,128)(2,1)S(1)}, bf16[384,1536]{1,0:T(8,128)(2,1)S(1)}) custom-call(bf16[3,768,640]{2,1,0:T(8,128)(2,1)S(1)} %left_factors.3.refs_1_.lhs_ref, bf16[256,2304]{1,0:T(8,128)(2,1)S(1)} %get-tuple-element.147.refs_0_, ...), custom_call_target="tpu_custom_call" | custom-call | flops 3019898880 | bytes 12189696 | tf_op jit(solution)/shard_map/weight_back/pallas_call | solution.py:941
  182.3 5.9 %input_back.1 = (f32[640,768]{1,0:T(8,128)}, f32[8,1536]{1,0:T(8,128)S(1)}) custom-call(bf16[256,2304]{1,0:T(8,128)(2,1)S(1)} %get-tuple-element.147.refs_0_, bf16[384,2304]{1,0:T(8,128)(2,1)S(1)} %get-tuple-element.158.refs_0_.refs_1_, bf16[768,2304]{1,0:T(8,128)(2,1)S(1)} %copy-done.2, bf16[640,768]{1,0:T(8,128)(2,1)S(1)} %copy-done.6, ...), custom_call_target="tpu_custom_call" | custom-call | flops 2264924160 | bytes 10420224 | tf_op jit(solution)/shard_map/input_back/pallas_call | solution.py:983
  194.5 2.7 %collective-permute-start.33 = (bf16[24,3072]{1,0:T(8,128)(2,1)S(1)}, bf16[24,3072]{1,0:T(8,128)(2,1)S(1)}, u32[]{:S(2)}, u32[]{:S(2)}) collective-permute-start(bf16[24,3072]{1,0:T(8,128)(2,1)S(1)} %get-tuple-element.190), channel_id=1, source_target_pairs={{0,24},{1,25},{2,26},{3,27},{4,28},{5,29},{6,30},{7,31},{8,16},{9,... | collective-permute-start | bytes 442376 | tf_op jit(solution)/shard_map/ppermute | solution.py:26
  197.2 5.9 %grad_of_down.1 = f32[96,768]{1,0:T(8,128)S(1)} custom-call(bf16[1280,1024]{1,0:T(8,128)(2,1)S(1)} %bitcast.77, bf16[256,768]{1,0:T(8,128)(2,1)S(1)} %bitcast.79, f32[1,256]{1,0:T(1,128)S(1)} %get-tuple-element.171.col_sum_ref, f32[1,256]{1,0:T(1,128)S(1)} %get-tuple-element.172.col_count_ref, f32[1,128]{1,0:T(1,128)S(1)} %get-tuple-element.173.live_ref, ...), custom_call_target="tpu_custom_call" | custom-call | flops 1006632960 | bytes 2621440 | tf_op jit(solution)/shard_map/grad_of_down/pallas_call | solution.py:739
  203.1 3.5 %collective-permute-done.32 = bf16[24,3072]{1,0:T(8,128)(2,1)S(1)} collective-permute-done((bf16[24,3072]{1,0:T(8,128)(2,1)S(1)}, bf16[24,3072]{1,0:T(8,128)(2,1)S(1)}, u32[]{:S(2)}, u32[]{:S(2)}) %collective-permute-start.32) | collective-permute-done | bytes 147488 | tf_op jit(solution)/shard_map/ppermute | solution.py:26
  208.9 6.3 %collective-permute-done.35.got_b = bf16[96,1536]{1,0:T(8,128)(2,1)S(1)} collective-permute-done((bf16[96,1536]{1,0:T(8,128)(2,1)S(1)}, bf16[96,1536]{1,0:T(8,128)(2,1)S(1)}, u32[]{:S(2)}, u32[]{:S(2)}) %collective-permute-start.35) | collective-permute-done | bytes 294944 | tf_op jit(solution)/shard_map/ppermute | solution.py:26
  221.8 3.4 %collective-permute-done.36 = bf16[32,3072]{1,0:T(8,128)(2,1)S(1)} collective-permute-done((bf16[32,3072]{1,0:T(8,128)(2,1)S(1)}, bf16[32,3072]{1,0:T(8,128)(2,1)S(1)}, u32[]{:S(2)}, u32[]{:S(2)}) %collective-permute-start.36) | collective-permute-done | bytes 196640 | tf_op jit(solution)/shard_map/ppermute | solution.py:26
  225.2 7.4 %collective-permute-done.37 = bf16[32,3072]{1,0:T(8,128)(2,1)S(1)} collective-permute-done((bf16[32,3072]{1,0:T(8,128)(2,1)S(1)}, bf16[32,3072]{1,0:T(8,128)(2,1)S(1)}, u32[]{:S(2)}, u32[]{:S(2)}) %collective-permute-start.37) | collective-permute-done | bytes 196640 | tf_op jit(solution)/shard_map/ppermute | solution.py:26
  (196 shorter events, 59.0 us)
Async XLA Ops:
  7.2 100.3 %all-gather.2.cloned.1.call-start = ((), (), s32[]{:S(2)}) async-start(), calls=%async_computation.2 | async-start | bytes 8921088 | tf_op jit(solution)/shard_map/all_gather | solution.py:1024
  10.3 25.7 %collective-permute-start = (bf16[24,3584]{1,0:T(8,128)(2,1)S(1)}, bf16[24,3584]{1,0:T(8,128)(2,1)S(1)}, u32[]{:S(2)}, u32[]{:S(2)}) collective-permute-start(bf16[24,3584]{1,0:T(8,128)(2,1)S(1)} %pad_maximum_fusion.7), channel_id=1, source_target_pairs={{0,8},{1,9},{2,10},{3,11},{4,12},{5,13},{6,14},{7,15},{8,0},{9,1},... | collective-permute-start | bytes 516104 | tf_op jit(solution)/shard_map/ppermute | solution.py:26
  13.4 22.6 %collective-permute-start.1 = (bf16[24,3584]{1,0:T(8,128)(2,1)S(1)}, bf16[24,3584]{1,0:T(8,128)(2,1)S(1)}, u32[]{:S(2)}, u32[]{:S(2)}) collective-permute-start(bf16[24,3584]{1,0:T(8,128)(2,1)S(1)} %pad_maximum_fusion.7), channel_id=1, source_target_pairs={{0,16},{1,17},{2,18},{3,19},{4,20},{5,21},{6,22},{7,23},{8,24},{9,... | collective-permute-start | bytes 516104 | tf_op jit(solution)/shard_map/ppermute | solution.py:26
  15.9 20.0 %collective-permute-start.2 = (bf16[24,3584]{1,0:T(8,128)(2,1)S(1)}, bf16[24,3584]{1,0:T(8,128)(2,1)S(1)}, u32[]{:S(2)}, u32[]{:S(2)}) collective-permute-start(bf16[24,3584]{1,0:T(8,128)(2,1)S(1)} %pad_maximum_fusion.7), channel_id=1, source_target_pairs={{0,24},{1,25},{2,26},{3,27},{4,28},{5,29},{6,30},{7,31},{8,16},{9,... | collective-permute-start | bytes 516104 | tf_op jit(solution)/shard_map/ppermute | solution.py:26
  37.0 24.5 %collective-permute-start.3 = (bf16[96,3584]{1,0:T(8,128)(2,1)}, bf16[96,3584]{1,0:T(8,128)(2,1)S(1)}, u32[]{:S(2)}, u32[]{:S(2)}) collective-permute-start(bf16[96,3584]{1,0:T(8,128)(2,1)} %pad_maximum_fusion.2.refs_0_), channel_id=1, source_target_pairs={{0,2},{1,3},{2,0},{3,1},{4,6},{5,7},{6,4},{7,5},{8,10},{9,11},{10,... | collective-permute-start | bytes 2064392 | tf_op jit(solution)/shard_map/ppermute | solution.py:26
  38.7 22.8 %collective-permute-start.4 = (bf16[96,3584]{1,0:T(8,128)(2,1)}, bf16[96,3584]{1,0:T(8,128)(2,1)S(1)}, u32[]{:S(2)}, u32[]{:S(2)}) collective-permute-start(bf16[96,3584]{1,0:T(8,128)(2,1)} %pad_maximum_fusion.2.refs_0_), channel_id=1, source_target_pairs={{0,4},{1,5},{2,6},{3,7},{4,0},{5,1},{6,2},{7,3},{8,12},{9,13},{10,... | collective-permute-start | bytes 2064392 | tf_op jit(solution)/shard_map/ppermute | solution.py:26
  65.3 12.0 %collective-permute-start.8 = (bf16[96,3584]{1,0:T(8,128)(2,1)S(1)}, bf16[96,3584]{1,0:T(8,128)(2,1)S(1)}, u32[]{:S(2)}, u32[]{:S(2)}) collective-permute-start(bf16[96,3584]{1,0:T(8,128)(2,1)S(1)} %collective-permute-done.3.refs_1_), channel_id=1, source_target_pairs={{0,1},{1,0},{2,3},{3,2},{4,5},{5,4},{6,7},{7,6},{8,9},{9,8},{10,11... | collective-permute-start | bytes 2064392 | tf_op jit(solution)/shard_map/ppermute | solution.py:26
  65.9 11.5 %collective-permute-start.9 = (bf16[96,3584]{1,0:T(8,128)(2,1)S(1)}, bf16[96,3584]{1,0:T(8,128)(2,1)}, u32[]{:S(2)}, u32[]{:S(2)}) collective-permute-start(bf16[96,3584]{1,0:T(8,128)(2,1)S(1)} %collective-permute-done.4.refs_2_), channel_id=1, source_target_pairs={{0,1},{1,0},{2,3},{3,2},{4,5},{5,4},{6,7},{7,6},{8,9},{9,8},{10,11... | collective-permute-start | bytes 2064392 | tf_op jit(solution)/shard_map/ppermute | solution.py:26
  71.6 22.4 %collective-permute-start.12 = (bf16[1,40,1024]{2,1,0:T(8,128)(2,1)S(1)}, bf16[1,40,1024]{2,1,0:T(8,128)(2,1)S(1)}, u32[]{:S(2)}, u32[]{:S(2)}) collective-permute-start(bf16[1,40,1024]{2,1,0:T(8,128)(2,1)S(1)} %bitcast.81), channel_id=1, source_target_pairs={{0,8},{1,9},{2,10},{3,11},{4,12},{5,13},{6,14},{7,15},{8,0},{9,1},... | collective-permute-start | bytes 245768 | tf_op jit(solution)/shard_map/ppermute | solution.py:26
  72.6 21.4 %collective-permute-start.13 = (bf16[1,40,1024]{2,1,0:T(8,128)(2,1)S(1)}, bf16[1,40,1024]{2,1,0:T(8,128)(2,1)S(1)}, u32[]{:S(2)}, u32[]{:S(2)}) collective-permute-start(bf16[1,40,1024]{2,1,0:T(8,128)(2,1)S(1)} %bitcast.82), channel_id=1, source_target_pairs={{0,16},{1,17},{2,18},{3,19},{4,20},{5,21},{6,22},{7,23},{8,24},{9,... | collective-permute-start | bytes 245768 | tf_op jit(solution)/shard_map/ppermute | solution.py:26
  75.7 18.4 %collective-permute-start.14 = (bf16[1,40,1024]{2,1,0:T(8,128)(2,1)S(1)}, bf16[1,40,1024]{2,1,0:T(8,128)(2,1)S(1)}, u32[]{:S(2)}, u32[]{:S(2)}) collective-permute-start(bf16[1,40,1024]{2,1,0:T(8,128)(2,1)S(1)} %bitcast.83), channel_id=1, source_target_pairs={{0,24},{1,25},{2,26},{3,27},{4,28},{5,29},{6,30},{7,31},{8,16},{9,... | collective-permute-start | bytes 245768 | tf_op jit(solution)/shard_map/ppermute | solution.py:26
  97.1 22.5 %all-to-all-start = ((bf16[40,32,96]{2,0,1:T(8,128)(2,1)}), bf16[40,32,96]{2,0,1:T(8,128)(2,1)S(1)}, u32[]{:S(2)}, u32[]{:S(2)}) async-start(bf16[40,32,96]{2,0,1:T(8,128)(2,1)} %copy.68), calls=%async_computation | async-start | bytes 655360 | tf_op jit(solution)/shard_map/all_to_all | solution.py:1082
  107.5 12.1 %collective-permute-start.17 = (bf16[2,40,1024]{2,1,0:T(8,128)(2,1)S(1)}, bf16[2,40,1024]{2,1,0:T(8,128)(2,1)S(1)}, u32[]{:S(2)}, u32[]{:S(2)}) collective-permute-start(bf16[2,40,1024]{2,1,0:T(8,128)(2,1)S(1)} %slice.72), channel_id=1, source_target_pairs={{0,4},{1,5},{2,6},{3,7},{4,0},{5,1},{6,2},{7,3},{8,12},{9,13},{10,... | collective-permute-start | bytes 491528 | tf_op jit(solution)/shard_map/ppermute | solution.py:26
  109.1 10.6 %collective-permute-start.18 = (bf16[2,40,1024]{2,1,0:T(8,128)(2,1)S(1)}, bf16[2,40,1024]{2,1,0:T(8,128)(2,1)S(1)}, u32[]{:S(2)}, u32[]{:S(2)}) collective-permute-start(bf16[2,40,1024]{2,1,0:T(8,128)(2,1)S(1)} %slice.73), channel_id=1, source_target_pairs={{0,2},{1,3},{2,0},{3,1},{4,6},{5,7},{6,4},{7,5},{8,10},{9,11},{10,... | collective-permute-start | bytes 491528 | tf_op jit(solution)/shard_map/ppermute | solution.py:26
  120.3 16.3 %all-to-all-start.1 = ((bf16[32,8,768]{2,1,0:T(8,128)(2,1)}), bf16[32,8,768]{2,1,0:T(8,128)(2,1)S(1)}, u32[]{:S(2)}, u32[]{:S(2)}) async-start(bf16[32,8,768]{2,1,0:T(8,128)(2,1)} %image_up.1), calls=%async_computation.1 | async-start | bytes 786432 | tf_op jit(solution)/shard_map/all_to_all | solution.py:44
  159.1 15.4 %collective-permute-start.22 = (bf16[192,1536]{1,0:T(8,128)(2,1)S(1)}, bf16[192,1536]{1,0:T(8,128)(2,1)S(1)}, u32[]{:S(2)}, u32[]{:S(2)}) collective-permute-start(bf16[192,1536]{1,0:T(8,128)(2,1)S(1)} %get-tuple-element.153.refs_1_), channel_id=1, source_target_pairs={{0,2},{1,3},{2,0},{3,1},{4,6},{5,7},{6,4},{7,5},{8,10},{9,11},{10,... | collective-permute-start | bytes 1769480 | tf_op jit(solution)/shard_map/ppermute | solution.py:26
  159.8 15.4 %collective-permute-start.23 = (bf16[192,1536]{1,0:T(8,128)(2,1)S(1)}, bf16[192,1536]{1,0:T(8,128)(2,1)S(1)}, u32[]{:S(2)}, u32[]{:S(2)}) collective-permute-start(bf16[192,1536]{1,0:T(8,128)(2,1)S(1)} %get-tuple-element.155.refs_3_), channel_id=1, source_target_pairs={{0,4},{1,5},{2,6},{3,7},{4,0},{5,1},{6,2},{7,3},{8,12},{9,13},{10,... | collective-permute-start | bytes 1769480 | tf_op jit(solution)/shard_map/ppermute | solution.py:26
  179.6 10.5 %collective-permute-start.26 = (bf16[384,1536]{1,0:T(8,128)(2,1)S(1)}, bf16[384,1536]{1,0:T(8,128)(2,1)S(1)}, u32[]{:S(2)}, u32[]{:S(2)}) collective-permute-start(bf16[384,1536]{1,0:T(8,128)(2,1)S(1)} %get-tuple-element.175), channel_id=1, source_target_pairs={{0,1},{1,0},{2,3},{3,2},{4,5},{5,4},{6,7},{7,6},{8,9},{9,8},{10,11... | collective-permute-start | bytes 3538952 | tf_op jit(solution)/shard_map/ppermute | solution.py:26
  190.7 15.9 %collective-permute-start.29 = (bf16[208,1536]{1,0:T(8,128)(2,1)S(1)}, bf16[208,1536]{1,0:T(8,128)(2,1)S(1)}, u32[]{:S(2)}, u32[]{:S(2)}) collective-permute-start(bf16[208,1536]{1,0:T(8,128)(2,1)S(1)} %get-tuple-element.185), channel_id=1, source_target_pairs={{0,2},{1,3},{2,0},{3,1},{4,6},{5,7},{6,4},{7,5},{8,10},{9,11},{10,... | collective-permute-start | bytes 1916936 | tf_op jit(solution)/shard_map/ppermute | solution.py:26
  191.8 14.8 %collective-permute-start.30 = (bf16[192,1536]{1,0:T(8,128)(2,1)S(1)}, bf16[192,1536]{1,0:T(8,128)(2,1)S(1)}, u32[]{:S(2)}, u32[]{:S(2)}) collective-permute-start(bf16[192,1536]{1,0:T(8,128)(2,1)S(1)} %get-tuple-element.187), channel_id=1, source_target_pairs={{0,4},{1,5},{2,6},{3,7},{4,0},{5,1},{6,2},{7,3},{8,12},{9,13},{10,... | collective-permute-start | bytes 1769480 | tf_op jit(solution)/shard_map/ppermute | solution.py:26
  193.8 12.8 %collective-permute-start.32 = (bf16[24,3072]{1,0:T(8,128)(2,1)S(1)}, bf16[24,3072]{1,0:T(8,128)(2,1)S(1)}, u32[]{:S(2)}, u32[]{:S(2)}) collective-permute-start(bf16[24,3072]{1,0:T(8,128)(2,1)S(1)} %get-tuple-element.189), channel_id=1, source_target_pairs={{0,16},{1,17},{2,18},{3,19},{4,20},{5,21},{6,22},{7,23},{8,24},{9,... | collective-permute-start | bytes 442376 | tf_op jit(solution)/shard_map/ppermute | solution.py:26
  194.5 12.1 %collective-permute-start.33 = (bf16[24,3072]{1,0:T(8,128)(2,1)S(1)}, bf16[24,3072]{1,0:T(8,128)(2,1)S(1)}, u32[]{:S(2)}, u32[]{:S(2)}) collective-permute-start(bf16[24,3072]{1,0:T(8,128)(2,1)S(1)} %get-tuple-element.190), channel_id=1, source_target_pairs={{0,24},{1,25},{2,26},{3,27},{4,28},{5,29},{6,30},{7,31},{8,16},{9,... | collective-permute-start | bytes 442376 | tf_op jit(solution)/shard_map/ppermute | solution.py:26
  217.8 14.8 %collective-permute-start.37 = (bf16[32,3072]{1,0:T(8,128)(2,1)S(1)}, bf16[32,3072]{1,0:T(8,128)(2,1)S(1)}, u32[]{:S(2)}, u32[]{:S(2)}) collective-permute-start(bf16[32,3072]{1,0:T(8,128)(2,1)S(1)} %get-tuple-element.203), channel_id=1, source_target_pairs={{0,16},{1,17},{2,18},{3,19},{4,20},{5,21},{6,22},{7,23},{8,24},{9,... | collective-permute-start | bytes 589832 | tf_op jit(solution)/shard_map/ppermute | solution.py:26
  217.8 14.8 %collective-permute-start.38 = (bf16[32,3072]{1,0:T(8,128)(2,1)S(1)}, bf16[32,3072]{1,0:T(8,128)(2,1)S(1)}, u32[]{:S(2)}, u32[]{:S(2)}) collective-permute-start(bf16[32,3072]{1,0:T(8,128)(2,1)S(1)} %get-tuple-element.204), channel_id=1, source_target_pairs={{0,24},{1,25},{2,26},{3,27},{4,28},{5,29},{6,30},{7,31},{8,16},{9,... | collective-permute-start | bytes 589832 | tf_op jit(solution)/shard_map/ppermute | solution.py:26
  (52 other events, 430.3 us)
Sparse Core Ops, SparseCore 0:
  11.5 95.9 all-gather.1

commit v10 on v9

--- a/solution.py
+++ b/solution.py
@@ -1080,7 +1080,9 @@
         held = joined(joined(held, others[0], 8), joined(others[1], others[2], 8), 16, 1)
         text_beside, text_above = swapped(held, 2), swapped(held, 4)
         hidden_cols = lax.all_to_all(scaled_sum, AXIS, split_axis=1, concat_axis=0, tiled=True)
-        whole, text_beside, text_above = lax.optimization_barrier((whole, text_beside, text_above))
+        normed_img, text_beside, text_above = lax.optimization_barrier(
+            (normed_img, text_beside, text_above)
+        )
         halves = diagonal(text_beside, text_above)
     image_low = image_up(normed_img, whole, middle_img, early, peers)
     if small:

time: 243 us -> 243 us (level)
    all_to_all x1, starting transfers between devices: 3.07 us -> 6.05 us  [exchanged(): return lax.all_to_all(copies, AXIS, split_axis=0, concat_axis=0, tiled=True)]
where the time goes in v10:
time: 243 us; the launch traced here: 242 us
  Pallas kernels  110 us (45%)
  starting transfers between devices  51.7 us (21%)
  waiting for transfers between devices  50.4 us (21%)
  between operations  14.9 us (6%)
  local copies, waits for them, and re-layouts  9.43 us (4%)
  other arithmetic  5.5 us (2%)
    ppermute x39, starting transfers between devices, swapped(): return lax.ppermute(value, AXIS, [(i, i ^ mask) for i in range(peers)])  40.3 us
    ppermute x39, waiting for transfers between devices, swapped(): return lax.ppermute(value, AXIS, [(i, i ^ mask) for i in range(peers)])  36.4 us
    pallas_call x1, Pallas kernels, text_front(): pl.pallas_call(text_front_kernel, out_shape=[jax.ShapeDtypeStruct(*item)...  18 us
    pallas_call x1, Pallas kernels, mlp_back(): pl.pallas_call(functools.partial(mlp_back_kernel, with_loss), out_shape=s...  16 us
    pallas_call x1, Pallas kernels, image_front(): pl.pallas_call(functools.partial(image_front_kernel, windows), out_shape=...  15.8 us
    all_to_all x1, waiting for transfers between devices, exchanged(): return lax.all_to_all(copies, AXIS, split_axis=0, concat_axis=0, tiled=True)  12.6 us
    pallas_call x1, Pallas kernels, text_up(): pl.pallas_call(text_up_kernel, grid=(FF // TILE,), out_shape=[jax.ShapeDt...  12 us
    pallas_call x2, Pallas kernels, attention_back(): pl.pallas_call(functools.partial(attention_back_kernel, first), out_shape...  11.5 us
  transfers between devices with their start and end apart: 42, of which 16 were waited for; matrix products, arithmetic and copies ran while one was open for 3% of the time, Pallas kernels for 36%

profile of v10, /device:TPU:0, one launch (start us, length us, event | category | flops | bytes accessed | tf_op | source)
XLA Modules:
  0.0 241.6 jit_solution(15329263740120531055)
XLA Ops:
  10.3 3.1 %collective-permute-start = (bf16[24,3584]{1,0:T(8,128)(2,1)S(1)}, bf16[24,3584]{1,0:T(8,128)(2,1)S(1)}, u32[]{:S(2)}, u32[]{:S(2)}) collective-permute-start(bf16[24,3584]{1,0:T(8,128)(2,1)S(1)} %pad_maximum_fusion.7), channel_id=1, source_target_pairs={{0,8},{1,9},{2,10},{3,11},{4,12},{5,13},{6,14},{7,15},{8,0},{9,1},... | collective-permute-start | bytes 516104 | tf_op jit(solution)/shard_map/ppermute | solution.py:26
  13.4 2.6 %collective-permute-start.1 = (bf16[24,3584]{1,0:T(8,128)(2,1)S(1)}, bf16[24,3584]{1,0:T(8,128)(2,1)S(1)}, u32[]{:S(2)}, u32[]{:S(2)}) collective-permute-start(bf16[24,3584]{1,0:T(8,128)(2,1)S(1)} %pad_maximum_fusion.7), channel_id=1, source_target_pairs={{0,16},{1,17},{2,18},{3,19},{4,20},{5,21},{6,22},{7,23},{8,24},{9,... | collective-permute-start | bytes 516104 | tf_op jit(solution)/shard_map/ppermute | solution.py:26
  16.8 18.0 %text_front.1 = (bf16[640,768]{1,0:T(8,128)(2,1)}, bf16[640,2304]{1,0:T(8,128)(2,1)}, bf16[640,768]{1,0:T(8,128)(2,1)}, f32[640,768]{1,0:T(8,128)}, bf16[640,768...) custom-call(bf16[640,768]{1,0:T(8,128)(2,1)} %refs_3_.1, f32[768]{0:T(1024)} %refs_4_.1, f32[768]{0:T(1024)} %b1_ref.2, ...), custom_call_target="tpu_custom_call" | custom-call | flops 3019898880 | bytes 11599872 | tf_op jit(solution)/shard_map/text_front/pallas_call | solution.py:364
  40.9 12.0 %text_up.1 = (bf16[640,3072]{1,0:T(8,128)(2,1)}, f32[40,3072]{1,0:T(8,128)}, f32[40,768]{1,0:T(8,128)}, f32[40,128]{1,0:T(8,128)}) custom-call(bf16[640,768]{1,0:T(8,128)(2,1)} %get-tuple-element.118.h2_ref.refs_1_.refs_3_, bf16[768,3072]{1,0:T(8,128)(2,1)} %refs_7_.1, bf16[3072,768]{1,0:T(8,128)(2,1)} %refs_5_.1, f32[40,768]{1,0:T(8,128)} %get-tuple-element.113.sum_ref, ...), custom_call_target="tpu_custom_call" | custom-call | flops 3019898880 | bytes 13369344 | tf_op jit(solution)/shard_map/text_up/pallas_call | solution.py:535
  52.9 8.6 %collective-permute-done.3.refs_1_ = bf16[96,3584]{1,0:T(8,128)(2,1)S(1)} collective-permute-done((bf16[96,3584]{1,0:T(8,128)(2,1)}, bf16[96,3584]{1,0:T(8,128)(2,1)S(1)}, u32[]{:S(2)}, u32[]{:S(2)}) %collective-permute-start.3) | collective-permute-done | bytes 688160 | tf_op jit(solution)/shard_map/ppermute | solution.py:26
  67.5 3.2 %left_factors.2.refs_8_ = bf16[2,768,640]{2,1,0:T(8,128)(2,1)S(1)} custom-call(s32[768,1]{1,0:T(8,128)S(1)} %fusion.8.refs_0_, bf16[640,768]{1,0:T(8,128)(2,1)S(1)} %copy-done.19, s32[768,1]{1,0:T(8,128)S(1)} %fusion.9.refs_2_.order_ref.refs_4_, bf16[640,768]{1,0:T(8,128)(2,1)S(1)} %copy-done.19), custom_call_target="tpu_custom_call" | custom-call | flops 1509949440 | bytes 3932160 | tf_op jit(solution)/shard_map/left_factors/pallas_call | solution.py:638
  72.6 3.0 %collective-permute-start.13 = (bf16[1,40,1024]{2,1,0:T(8,128)(2,1)S(1)}, bf16[1,40,1024]{2,1,0:T(8,128)(2,1)S(1)}, u32[]{:S(2)}, u32[]{:S(2)}) collective-permute-start(bf16[1,40,1024]{2,1,0:T(8,128)(2,1)S(1)} %bitcast.82), channel_id=1, source_target_pairs={{0,16},{1,17},{2,18},{3,19},{4,20},{5,21},{6,22},{7,23},{8,24},{9,... | collective-permute-start | bytes 245768 | tf_op jit(solution)/shard_map/ppermute | solution.py:26
  78.2 15.8 %image_front.1 = (bf16[400,768]{1,0:T(8,128)(2,1)}, f32[8,768]{1,0:T(8,128)}, f32[8,512]{1,0:T(8,128)}) custom-call(bf16[400,768]{1,0:T(8,128)(2,1)} %x_ref.3, s32[768,1]{1,0:T(8,128)} %copy-done.7, bf16[768]{0:T(1024)(128)(2,1)} %g1_ref.3, bf16[768]{0:T(1024)(128)(2,1)} %b1_ref.3, bf16[768]{0:T(1024)(128)(2,1)} %g2_ref.3, bf16[768]{0:T(1024)(128)(2,1)} %b2_ref.3, ...), custom_call_target="tpu_custom_call" | custom-call | flops 2831155200 | bytes 4718592 | tf_op jit(solution)/shard_map/image_front/pallas_call | solution.py:439
  97.1 5.3 %all-to-all-start = ((bf16[40,32,96]{2,0,1:T(8,128)(2,1)}), bf16[40,32,96]{2,0,1:T(8,128)(2,1)S(1)}, u32[]{:S(2)}, u32[]{:S(2)}) async-start(bf16[40,32,96]{2,0,1:T(8,128)(2,1)} %copy.68), calls=%async_computation | async-start | bytes 655360 | tf_op jit(solution)/shard_map/all_to_all | solution.py:1082
  107.5 8.9 %image_up.1 = bf16[32,8,768]{2,1,0:T(8,128)(2,1)} custom-call(bf16[400,768]{1,0:T(8,128)(2,1)} %get-tuple-element.129.h2_ref, bf16[768,5632]{1,0:T(8,128)(2,1)} %all-gather.2.cloned.1.call-done.wu_ref.wd_ref.first_ref, bf16[768,5632]{1,0:T(8,128)(2,1)} %all-gather.2.cloned.1.call-done.wu_ref.wd_ref.first_ref, ...), custom_call_target="tpu_custom_call" | custom-call | flops 1887436800 | bytes 9437184 | tf_op jit(solution)/shard_map/image_up/pallas_call | solution.py:603
  117.4 6.0 %all-to-all-start.1 = ((bf16[32,8,768]{2,1,0:T(8,128)(2,1)}), bf16[32,8,768]{2,1,0:T(8,128)(2,1)S(1)}, u32[]{:S(2)}, u32[]{:S(2)}) async-start(bf16[32,8,768]{2,1,0:T(8,128)(2,1)} %image_up.1), calls=%async_computation.1 | async-start | bytes 786432 | tf_op jit(solution)/shard_map/all_to_all | solution.py:44
  124.0 12.6 %all-to-all-done.1 = bf16[32,8,768]{2,1,0:T(8,128)(2,1)S(1)} async-done(((bf16[32,8,768]{2,1,0:T(8,128)(2,1)}), bf16[32,8,768]{2,1,0:T(8,128)(2,1)S(1)}, u32[]{:S(2)}, u32[]{:S(2)}) %all-to-all-start.1) | async-done | bytes 393248 | tf_op jit(solution)/shard_map/all_to_all | solution.py:44
  137.4 16.0 %mlp_back.1 = (bf16[384,1536]{1,0:T(8,128)(2,1)S(1)}, bf16[384,1536]{1,0:T(8,128)(2,1)S(1)}, bf16[384,1536]{1,0:T(8,128)(2,1)S(1)}, bf16[384,1536]{1,0:T(8,128)(...) custom-call(f32[768]{0:T(1024)S(1)} %copy-done.17, ...), custom_call_target="tpu_custom_call" | custom-call | flops 6039797760 | bytes 18087936 | tf_op jit(solution)/shard_map/mlp_back/pallas_call | solution.py:858
  154.0 4.6 %attention_back.2 = (bf16[256,768]{1,0:T(8,128)(2,1)S(1)}, bf16[256,2304]{1,0:T(8,128)(2,1)S(1)}) custom-call(f32[640,768]{1,0:T(8,128)S(1)} %get-tuple-element.144.grad_ref.refs_5_, bf16[768,768]{1,0:T(8,128)(2,1)S(1)} %copy-done.1, bf16[640,2304]{1,0:T(8,128)(2,1)S(1)} %copy-done, f32[80,128]{1,0:T(8,128)S(1)} %copy-done.12), custom_call_target="tpu_custom_call" | custom-call | flops 1509949440 | bytes 4325376 | tf_op jit(solution)/shard_map/attention_back/pallas_call | solution.py:908
  161.2 6.9 %attention_back.3 = (bf16[384,768]{1,0:T(8,128)(2,1)S(1)}, bf16[384,2304]{1,0:T(8,128)(2,1)S(1)}) custom-call(f32[640,768]{1,0:T(8,128)S(1)} %get-tuple-element.144.grad_ref.refs_5_, bf16[768,768]{1,0:T(8,128)(2,1)S(1)} %copy-done.1, bf16[640,2304]{1,0:T(8,128)(2,1)S(1)} %copy-done, f32[80,128]{1,0:T(8,128)S(1)} %copy-done.12, ...), custom_call_target="tpu_custom_call" | custom-call | flops 2264924160 | bytes 5898240 | tf_op jit(solution)/shard_map/attention_back/pallas_call | solution.py:908
  168.1 4.8 %left_factors.3.refs_1_.lhs_ref = bf16[3,768,640]{2,1,0:T(8,128)(2,1)S(1)} custom-call(s32[768,1]{1,0:T(8,128)S(1)} %copy-done.10, bf16[640,768]{1,0:T(8,128)(2,1)S(1)} %copy-done.20, s32[768,1]{1,0:T(8,128)S(1)} %copy-done.8, bf16[640,768]{1,0:T(8,128)(2,1)S(1)} %copy-done.20, s32[768,1]{1,0:T(8,128)S(1)} %copy-done.8, bf16[640,768]{1,0:T(8,128)(2,1)S(1)} %copy-done.21), custom_call_target="tpu_custom_call" | custom-call | flops 2264924160 | bytes 5898240 | tf_op jit(solution)/shard_map/left_factors/pallas_call | solution.py:638
  175.7 3.9 %weight_back.1 = (bf16[384,1536]{1,0:T(8,128)(2,1)S(1)}, bf16[384,1536]{1,0:T(8,128)(2,1)S(1)}, bf16[384,1536]{1,0:T(8,128)(2,1)S(1)}, bf16[384,1536]{1,0:T(8,128)(2,1)S(1)}) custom-call(bf16[3,768,640]{2,1,0:T(8,128)(2,1)S(1)} %left_factors.3.refs_1_.lhs_ref, bf16[256,2304]{1,0:T(8,128)(2,1)S(1)} %get-tuple-element.147.refs_0_, ...), custom_call_target="tpu_custom_call" | custom-call | flops 3019898880 | bytes 12189696 | tf_op jit(solution)/shard_map/weight_back/pallas_call | solution.py:941
  182.3 5.9 %input_back.1 = (f32[640,768]{1,0:T(8,128)}, f32[8,1536]{1,0:T(8,128)S(1)}) custom-call(bf16[256,2304]{1,0:T(8,128)(2,1)S(1)} %get-tuple-element.147.refs_0_, bf16[384,2304]{1,0:T(8,128)(2,1)S(1)} %get-tuple-element.158.refs_0_.refs_1_, bf16[768,2304]{1,0:T(8,128)(2,1)S(1)} %copy-done.2, bf16[640,768]{1,0:T(8,128)(2,1)S(1)} %copy-done.6, ...), custom_call_target="tpu_custom_call" | custom-call | flops 2264924160 | bytes 10420224 | tf_op jit(solution)/shard_map/input_back/pallas_call | solution.py:983
  194.5 2.7 %collective-permute-start.33 = (bf16[24,3072]{1,0:T(8,128)(2,1)S(1)}, bf16[24,3072]{1,0:T(8,128)(2,1)S(1)}, u32[]{:S(2)}, u32[]{:S(2)}) collective-permute-start(bf16[24,3072]{1,0:T(8,128)(2,1)S(1)} %get-tuple-element.190), channel_id=1, source_target_pairs={{0,24},{1,25},{2,26},{3,27},{4,28},{5,29},{6,30},{7,31},{8,16},{9,... | collective-permute-start | bytes 442376 | tf_op jit(solution)/shard_map/ppermute | solution.py:26
  197.3 5.9 %grad_of_down.1 = f32[96,768]{1,0:T(8,128)S(1)} custom-call(bf16[1280,1024]{1,0:T(8,128)(2,1)S(1)} %bitcast.77, bf16[256,768]{1,0:T(8,128)(2,1)S(1)} %bitcast.79, f32[1,256]{1,0:T(1,128)S(1)} %get-tuple-element.171.col_sum_ref, f32[1,256]{1,0:T(1,128)S(1)} %get-tuple-element.172.col_count_ref, f32[1,128]{1,0:T(1,128)S(1)} %get-tuple-element.173.live_ref, ...), custom_call_target="tpu_custom_call" | custom-call | flops 1006632960 | bytes 2621440 | tf_op jit(solution)/shard_map/grad_of_down/pallas_call | solution.py:739
  203.1 3.5 %collective-permute-done.32 = bf16[24,3072]{1,0:T(8,128)(2,1)S(1)} collective-permute-done((bf16[24,3072]{1,0:T(8,128)(2,1)S(1)}, bf16[24,3072]{1,0:T(8,128)(2,1)S(1)}, u32[]{:S(2)}, u32[]{:S(2)}) %collective-permute-start.32) | collective-permute-done | bytes 147488 | tf_op jit(solution)/shard_map/ppermute | solution.py:26
  208.9 6.3 %collective-permute-done.35.got_b = bf16[96,1536]{1,0:T(8,128)(2,1)S(1)} collective-permute-done((bf16[96,1536]{1,0:T(8,128)(2,1)S(1)}, bf16[96,1536]{1,0:T(8,128)(2,1)S(1)}, u32[]{:S(2)}, u32[]{:S(2)}) %collective-permute-start.35) | collective-permute-done | bytes 294944 | tf_op jit(solution)/shard_map/ppermute | solution.py:26
  221.9 3.4 %collective-permute-done.36 = bf16[32,3072]{1,0:T(8,128)(2,1)S(1)} collective-permute-done((bf16[32,3072]{1,0:T(8,128)(2,1)S(1)}, bf16[32,3072]{1,0:T(8,128)(2,1)S(1)}, u32[]{:S(2)}, u32[]{:S(2)}) %collective-permute-start.36) | collective-permute-done | bytes 196640 | tf_op jit(solution)/shard_map/ppermute | solution.py:26
  225.3 7.4 %collective-permute-done.37 = bf16[32,3072]{1,0:T(8,128)(2,1)S(1)} collective-permute-done((bf16[32,3072]{1,0:T(8,128)(2,1)S(1)}, bf16[32,3072]{1,0:T(8,128)(2,1)S(1)}, u32[]{:S(2)}, u32[]{:S(2)}) %collective-permute-start.37) | collective-permute-done | bytes 196640 | tf_op jit(solution)/shard_map/ppermute | solution.py:26
  (196 shorter events, 56.1 us)
Async XLA Ops:
  7.2 100.3 %all-gather.2.cloned.1.call-start = ((), (), s32[]{:S(2)}) async-start(), calls=%async_computation.2 | async-start | bytes 8921088 | tf_op jit(solution)/shard_map/all_gather | solution.py:1024
  10.3 25.7 %collective-permute-start = (bf16[24,3584]{1,0:T(8,128)(2,1)S(1)}, bf16[24,3584]{1,0:T(8,128)(2,1)S(1)}, u32[]{:S(2)}, u32[]{:S(2)}) collective-permute-start(bf16[24,3584]{1,0:T(8,128)(2,1)S(1)} %pad_maximum_fusion.7), channel_id=1, source_target_pairs={{0,8},{1,9},{2,10},{3,11},{4,12},{5,13},{6,14},{7,15},{8,0},{9,1},... | collective-permute-start | bytes 516104 | tf_op jit(solution)/shard_map/ppermute | solution.py:26
  13.4 22.6 %collective-permute-start.1 = (bf16[24,3584]{1,0:T(8,128)(2,1)S(1)}, bf16[24,3584]{1,0:T(8,128)(2,1)S(1)}, u32[]{:S(2)}, u32[]{:S(2)}) collective-permute-start(bf16[24,3584]{1,0:T(8,128)(2,1)S(1)} %pad_maximum_fusion.7), channel_id=1, source_target_pairs={{0,16},{1,17},{2,18},{3,19},{4,20},{5,21},{6,22},{7,23},{8,24},{9,... | collective-permute-start | bytes 516104 | tf_op jit(solution)/shard_map/ppermute | solution.py:26
  15.9 20.0 %collective-permute-start.2 = (bf16[24,3584]{1,0:T(8,128)(2,1)S(1)}, bf16[24,3584]{1,0:T(8,128)(2,1)S(1)}, u32[]{:S(2)}, u32[]{:S(2)}) collective-permute-start(bf16[24,3584]{1,0:T(8,128)(2,1)S(1)} %pad_maximum_fusion.7), channel_id=1, source_target_pairs={{0,24},{1,25},{2,26},{3,27},{4,28},{5,29},{6,30},{7,31},{8,16},{9,... | collective-permute-start | bytes 516104 | tf_op jit(solution)/shard_map/ppermute | solution.py:26
  37.0 24.5 %collective-permute-start.3 = (bf16[96,3584]{1,0:T(8,128)(2,1)}, bf16[96,3584]{1,0:T(8,128)(2,1)S(1)}, u32[]{:S(2)}, u32[]{:S(2)}) collective-permute-start(bf16[96,3584]{1,0:T(8,128)(2,1)} %pad_maximum_fusion.2.refs_0_), channel_id=1, source_target_pairs={{0,2},{1,3},{2,0},{3,1},{4,6},{5,7},{6,4},{7,5},{8,10},{9,11},{10,... | collective-permute-start | bytes 2064392 | tf_op jit(solution)/shard_map/ppermute | solution.py:26
  38.7 22.8 %collective-permute-start.4 = (bf16[96,3584]{1,0:T(8,128)(2,1)}, bf16[96,3584]{1,0:T(8,128)(2,1)S(1)}, u32[]{:S(2)}, u32[]{:S(2)}) collective-permute-start(bf16[96,3584]{1,0:T(8,128)(2,1)} %pad_maximum_fusion.2.refs_0_), channel_id=1, source_target_pairs={{0,4},{1,5},{2,6},{3,7},{4,0},{5,1},{6,2},{7,3},{8,12},{9,13},{10,... | collective-permute-start | bytes 2064392 | tf_op jit(solution)/shard_map/ppermute | solution.py:26
  65.3 12.0 %collective-permute-start.8 = (bf16[96,3584]{1,0:T(8,128)(2,1)S(1)}, bf16[96,3584]{1,0:T(8,128)(2,1)S(1)}, u32[]{:S(2)}, u32[]{:S(2)}) collective-permute-start(bf16[96,3584]{1,0:T(8,128)(2,1)S(1)} %collective-permute-done.3.refs_1_), channel_id=1, source_target_pairs={{0,1},{1,0},{2,3},{3,2},{4,5},{5,4},{6,7},{7,6},{8,9},{9,8},{10,11... | collective-permute-start | bytes 2064392 | tf_op jit(solution)/shard_map/ppermute | solution.py:26
  65.9 11.5 %collective-permute-start.9 = (bf16[96,3584]{1,0:T(8,128)(2,1)S(1)}, bf16[96,3584]{1,0:T(8,128)(2,1)}, u32[]{:S(2)}, u32[]{:S(2)}) collective-permute-start(bf16[96,3584]{1,0:T(8,128)(2,1)S(1)} %collective-permute-done.4.refs_2_), channel_id=1, source_target_pairs={{0,1},{1,0},{2,3},{3,2},{4,5},{5,4},{6,7},{7,6},{8,9},{9,8},{10,11... | collective-permute-start | bytes 2064392 | tf_op jit(solution)/shard_map/ppermute | solution.py:26
  71.6 22.4 %collective-permute-start.12 = (bf16[1,40,1024]{2,1,0:T(8,128)(2,1)S(1)}, bf16[1,40,1024]{2,1,0:T(8,128)(2,1)S(1)}, u32[]{:S(2)}, u32[]{:S(2)}) collective-permute-start(bf16[1,40,1024]{2,1,0:T(8,128)(2,1)S(1)} %bitcast.81), channel_id=1, source_target_pairs={{0,8},{1,9},{2,10},{3,11},{4,12},{5,13},{6,14},{7,15},{8,0},{9,1},... | collective-permute-start | bytes 245768 | tf_op jit(solution)/shard_map/ppermute | solution.py:26
  72.6 21.4 %collective-permute-start.13 = (bf16[1,40,1024]{2,1,0:T(8,128)(2,1)S(1)}, bf16[1,40,1024]{2,1,0:T(8,128)(2,1)S(1)}, u32[]{:S(2)}, u32[]{:S(2)}) collective-permute-start(bf16[1,40,1024]{2,1,0:T(8,128)(2,1)S(1)} %bitcast.82), channel_id=1, source_target_pairs={{0,16},{1,17},{2,18},{3,19},{4,20},{5,21},{6,22},{7,23},{8,24},{9,... | collective-permute-start | bytes 245768 | tf_op jit(solution)/shard_map/ppermute | solution.py:26
  75.7 18.4 %collective-permute-start.14 = (bf16[1,40,1024]{2,1,0:T(8,128)(2,1)S(1)}, bf16[1,40,1024]{2,1,0:T(8,128)(2,1)S(1)}, u32[]{:S(2)}, u32[]{:S(2)}) collective-permute-start(bf16[1,40,1024]{2,1,0:T(8,128)(2,1)S(1)} %bitcast.83), channel_id=1, source_target_pairs={{0,24},{1,25},{2,26},{3,27},{4,28},{5,29},{6,30},{7,31},{8,16},{9,... | collective-permute-start | bytes 245768 | tf_op jit(solution)/shard_map/ppermute | solution.py:26
  97.1 19.3 %all-to-all-start = ((bf16[40,32,96]{2,0,1:T(8,128)(2,1)}), bf16[40,32,96]{2,0,1:T(8,128)(2,1)S(1)}, u32[]{:S(2)}, u32[]{:S(2)}) async-start(bf16[40,32,96]{2,0,1:T(8,128)(2,1)} %copy.68), calls=%async_computation | async-start | bytes 655360 | tf_op jit(solution)/shard_map/all_to_all | solution.py:1082
  104.9 11.5 %collective-permute-start.17 = (bf16[2,40,1024]{2,1,0:T(8,128)(2,1)S(1)}, bf16[2,40,1024]{2,1,0:T(8,128)(2,1)S(1)}, u32[]{:S(2)}, u32[]{:S(2)}) collective-permute-start(bf16[2,40,1024]{2,1,0:T(8,128)(2,1)S(1)} %slice.72), channel_id=1, source_target_pairs={{0,4},{1,5},{2,6},{3,7},{4,0},{5,1},{6,2},{7,3},{8,12},{9,13},{10,... | collective-permute-start | bytes 491528 | tf_op jit(solution)/shard_map/ppermute | solution.py:26
  105.3 11.1 %collective-permute-start.18 = (bf16[2,40,1024]{2,1,0:T(8,128)(2,1)S(1)}, bf16[2,40,1024]{2,1,0:T(8,128)(2,1)S(1)}, u32[]{:S(2)}, u32[]{:S(2)}) collective-permute-start(bf16[2,40,1024]{2,1,0:T(8,128)(2,1)S(1)} %slice.73), channel_id=1, source_target_pairs={{0,2},{1,3},{2,0},{3,1},{4,6},{5,7},{6,4},{7,5},{8,10},{9,11},{10,... | collective-permute-start | bytes 491528 | tf_op jit(solution)/shard_map/ppermute | solution.py:26
  117.4 19.2 %all-to-all-start.1 = ((bf16[32,8,768]{2,1,0:T(8,128)(2,1)}), bf16[32,8,768]{2,1,0:T(8,128)(2,1)S(1)}, u32[]{:S(2)}, u32[]{:S(2)}) async-start(bf16[32,8,768]{2,1,0:T(8,128)(2,1)} %image_up.1), calls=%async_computation.1 | async-start | bytes 786432 | tf_op jit(solution)/shard_map/all_to_all | solution.py:44
  159.2 15.4 %collective-permute-start.22 = (bf16[192,1536]{1,0:T(8,128)(2,1)S(1)}, bf16[192,1536]{1,0:T(8,128)(2,1)S(1)}, u32[]{:S(2)}, u32[]{:S(2)}) collective-permute-start(bf16[192,1536]{1,0:T(8,128)(2,1)S(1)} %get-tuple-element.153.refs_1_), channel_id=1, source_target_pairs={{0,2},{1,3},{2,0},{3,1},{4,6},{5,7},{6,4},{7,5},{8,10},{9,11},{10,... | collective-permute-start | bytes 1769480 | tf_op jit(solution)/shard_map/ppermute | solution.py:26
  159.8 15.4 %collective-permute-start.23 = (bf16[192,1536]{1,0:T(8,128)(2,1)S(1)}, bf16[192,1536]{1,0:T(8,128)(2,1)S(1)}, u32[]{:S(2)}, u32[]{:S(2)}) collective-permute-start(bf16[192,1536]{1,0:T(8,128)(2,1)S(1)} %get-tuple-element.155.refs_3_), channel_id=1, source_target_pairs={{0,4},{1,5},{2,6},{3,7},{4,0},{5,1},{6,2},{7,3},{8,12},{9,13},{10,... | collective-permute-start | bytes 1769480 | tf_op jit(solution)/shard_map/ppermute | solution.py:26
  179.6 10.5 %collective-permute-start.26 = (bf16[384,1536]{1,0:T(8,128)(2,1)S(1)}, bf16[384,1536]{1,0:T(8,128)(2,1)S(1)}, u32[]{:S(2)}, u32[]{:S(2)}) collective-permute-start(bf16[384,1536]{1,0:T(8,128)(2,1)S(1)} %get-tuple-element.175), channel_id=1, source_target_pairs={{0,1},{1,0},{2,3},{3,2},{4,5},{5,4},{6,7},{7,6},{8,9},{9,8},{10,11... | collective-permute-start | bytes 3538952 | tf_op jit(solution)/shard_map/ppermute | solution.py:26
  190.7 15.9 %collective-permute-start.29 = (bf16[208,1536]{1,0:T(8,128)(2,1)S(1)}, bf16[208,1536]{1,0:T(8,128)(2,1)S(1)}, u32[]{:S(2)}, u32[]{:S(2)}) collective-permute-start(bf16[208,1536]{1,0:T(8,128)(2,1)S(1)} %get-tuple-element.185), channel_id=1, source_target_pairs={{0,2},{1,3},{2,0},{3,1},{4,6},{5,7},{6,4},{7,5},{8,10},{9,11},{10,... | collective-permute-start | bytes 1916936 | tf_op jit(solution)/shard_map/ppermute | solution.py:26
  191.8 14.8 %collective-permute-start.30 = (bf16[192,1536]{1,0:T(8,128)(2,1)S(1)}, bf16[192,1536]{1,0:T(8,128)(2,1)S(1)}, u32[]{:S(2)}, u32[]{:S(2)}) collective-permute-start(bf16[192,1536]{1,0:T(8,128)(2,1)S(1)} %get-tuple-element.187), channel_id=1, source_target_pairs={{0,4},{1,5},{2,6},{3,7},{4,0},{5,1},{6,2},{7,3},{8,12},{9,13},{10,... | collective-permute-start | bytes 1769480 | tf_op jit(solution)/shard_map/ppermute | solution.py:26
  193.9 12.8 %collective-permute-start.32 = (bf16[24,3072]{1,0:T(8,128)(2,1)S(1)}, bf16[24,3072]{1,0:T(8,128)(2,1)S(1)}, u32[]{:S(2)}, u32[]{:S(2)}) collective-permute-start(bf16[24,3072]{1,0:T(8,128)(2,1)S(1)} %get-tuple-element.189), channel_id=1, source_target_pairs={{0,16},{1,17},{2,18},{3,19},{4,20},{5,21},{6,22},{7,23},{8,24},{9,... | collective-permute-start | bytes 442376 | tf_op jit(solution)/shard_map/ppermute | solution.py:26
  194.5 12.1 %collective-permute-start.33 = (bf16[24,3072]{1,0:T(8,128)(2,1)S(1)}, bf16[24,3072]{1,0:T(8,128)(2,1)S(1)}, u32[]{:S(2)}, u32[]{:S(2)}) collective-permute-start(bf16[24,3072]{1,0:T(8,128)(2,1)S(1)} %get-tuple-element.190), channel_id=1, source_target_pairs={{0,24},{1,25},{2,26},{3,27},{4,28},{5,29},{6,30},{7,31},{8,16},{9,... | collective-permute-start | bytes 442376 | tf_op jit(solution)/shard_map/ppermute | solution.py:26
  217.9 14.8 %collective-permute-start.37 = (bf16[32,3072]{1,0:T(8,128)(2,1)S(1)}, bf16[32,3072]{1,0:T(8,128)(2,1)S(1)}, u32[]{:S(2)}, u32[]{:S(2)}) collective-permute-start(bf16[32,3072]{1,0:T(8,128)(2,1)S(1)} %get-tuple-element.203), channel_id=1, source_target_pairs={{0,16},{1,17},{2,18},{3,19},{4,20},{5,21},{6,22},{7,23},{8,24},{9,... | collective-permute-start | bytes 589832 | tf_op jit(solution)/shard_map/ppermute | solution.py:26
  217.9 14.8 %collective-permute-start.38 = (bf16[32,3072]{1,0:T(8,128)(2,1)S(1)}, bf16[32,3072]{1,0:T(8,128)(2,1)S(1)}, u32[]{:S(2)}, u32[]{:S(2)}) collective-permute-start(bf16[32,3072]{1,0:T(8,128)(2,1)S(1)} %get-tuple-element.204), channel_id=1, source_target_pairs={{0,24},{1,25},{2,26},{3,27},{4,28},{5,29},{6,30},{7,31},{8,16},{9,... | collective-permute-start | bytes 589832 | tf_op jit(solution)/shard_map/ppermute | solution.py:26
  (52 other events, 433.5 us)
Sparse Core Ops, SparseCore 0:
  11.5 95.9 all-gather.1

commit v11 on v10

--- a/solution.py
+++ b/solution.py
@@ -753,28 +753,38 @@
     )(pack, image_all, col_sum, col_count, live_total, hidden_cols, *after)
 
 
+def load_kernel(*refs):
+    count = (len(refs) - 1) // 2
+    sems = refs[-1]
+    copies = [
+        pltpu.make_async_copy(refs[k], refs[count + k], sems.at[k]) for k in range(count)
+    ]
+    for copy in copies:
+        copy.start()
+    for copy in copies:
+        copy.wait()
+
+
+def loaded(*arrays):
+    return pl.pallas_call(
+        load_kernel,
+        out_shape=[stays(array.shape, array.dtype) for array in arrays],
+        in_specs=[pl.BlockSpec(memory_space=pltpu.HBM)] * len(arrays),
+        out_specs=in_vmem(len(arrays)),
+        scratch_shapes=[pltpu.SemaphoreType.DMA((len(arrays),))],
+        compiler_params=params(4 << 20),
+        cost_estimate=cost(0, sum(2 * array.size * array.dtype.itemsize for array in arrays)),
+        name="loaded",
+    )(*in_hbm(*arrays))
+
+
 def mlp_back_kernel(with_loss, gain_ref, *refs):
     given, refs = (refs[:5], refs[5:]) if with_loss else (refs[:2], refs[2:])
-    wd_hbm, slope_hbm, wu_hbm, lhs_hbm, mid_hbm = refs[:5]
+    wd_ref, slope_ref, wu_ref, lhs_ref, mid_ref = refs[:5]
     keep_a, send_a, keep_b, send_b, out_ref, sums_out = refs[5:11]
-    wd_ref, slope_ref, wu_ref, lhs_ref, mid_ref, sems, whole_sems = refs[-7:]
-    low_ref, row_ref = refs[-9:-7] if with_loss else given
+    low_ref, row_ref = refs[-2:] if with_loss else given
     count, rows = low_ref.shape[0], out_ref.shape[0]
     half, steps = D // 2, FF // 2 // TILE
-
-    def copies(tile, slot):
-        at = pl.ds(pl.multiple_of(tile * TILE, TILE), TILE)
-        return (
-            pltpu.make_async_copy(wd_hbm.at[at, :], wd_ref.at[slot], sems.at[0, slot]),
-            pltpu.make_async_copy(slope_hbm.at[:, at], slope_ref.at[slot], sems.at[1, slot]),
-            pltpu.make_async_copy(wu_hbm.at[:, at], wu_ref.at[slot], sems.at[2, slot]),
-        )
-
-    lhs_copy = pltpu.make_async_copy(lhs_hbm, lhs_ref, whole_sems.at[0])
-    mid_copy = pltpu.make_async_copy(mid_hbm, mid_ref, whole_sems.at[1])
-    for copy in copies(0, 0):
-        copy.start()
-    lhs_copy.start()
     if with_loss:
         loss_ref, *stats = refs[11:15]
         loss_into(*given, loss_ref, row_ref, low_ref, *stats)
@@ -782,31 +792,15 @@
 
         @pl.loop(0, steps)
         def _(step, k=k, keep=keep, send=send):
-            tile = k * steps + step
-            slot = lax.rem(tile, 2)
-
-            @pl.when(tile + 1 < 2 * steps)
-            def _():
-                for copy in copies(tile + 1, 1 - slot):
-                    copy.start()
-
-            for copy in copies(tile, slot):
-                copy.wait()
-            if k == 0:
-
-                @pl.when(step == 0)
-                def _():
-                    lhs_copy.wait()
-                    mid_copy.start()
-
+            at = pl.ds(pl.multiple_of(k * (FF // 2) + step * TILE, TILE), TILE)
             there = pl.ds(pl.multiple_of(step * TILE, TILE), TILE)
-            hidden = mul_bt(low_ref[...], wd_ref[slot])
+            hidden = mul_bt(low_ref[...], wd_ref[at, :])
             wide = jnp.broadcast_to(hidden[:, None, :], (count, TXT_LEN, TILE))
-            inner = (wide.reshape(rows, TILE) * slope_ref[slot].astype(f32)).astype(bf16)
+            inner = (wide.reshape(rows, TILE) * slope_ref[:, at].astype(f32)).astype(bf16)
             weight = mul(lhs_ref[k], inner).astype(bf16)
             keep[:, there] = weight[:half]
             send[:, there] = weight[half:]
-            added = mul_bt(inner, wu_ref[slot])
+            added = mul_bt(inner, wu_ref[:, at])
             if k == 0:
 
                 @pl.when(step == 0)
@@ -823,7 +817,6 @@
     per = chunk // TXT_LEN
     gain = line(gain_ref)
     sums_out[...] = jnp.zeros_like(sums_out)
-    mid_copy.wait()
 
     @pl.loop(0, rows // chunk)
     def _(k):
@@ -841,30 +834,22 @@
     rows, count = slope.shape[0], given[-2].shape[0]
     with_loss = len(given) == 5
     shapes = [stays((D // 2, FF // 2), bf16)] * 4 + [stays((rows, D), f32), stays((1, 2 * D), f32)]
-    scratch = [
-        pltpu.VMEM((2, TILE, D), bf16),
-        pltpu.VMEM((2, rows, TILE), bf16),
-        pltpu.VMEM((2, D, TILE), bf16),
-        pltpu.VMEM((2, D, rows), bf16),
-        pltpu.VMEM((rows, D), f32),
-        pltpu.SemaphoreType.DMA((3, 2)),
-        pltpu.SemaphoreType.DMA((2,)),
-    ]
+    scratch = []
     if with_loss:
         images = given[1].shape[0]
         wide = [(1, 128), (1, images), (1, images), (1, 128)]
         shapes += [jax.ShapeDtypeStruct(shape, f32) for shape in wide]
-        scratch = [pltpu.VMEM((count, D), bf16), pltpu.VMEM((count, D), f32)] + scratch
+        scratch = [pltpu.VMEM((count, D), bf16), pltpu.VMEM((count, D), f32)]
     return pl.pallas_call(
         functools.partial(mlp_back_kernel, with_loss),
         out_shape=shapes,
-        in_specs=in_vmem(1 + len(given)) + [pl.BlockSpec(memory_space=pltpu.HBM)] * 5,
+        in_specs=in_vmem(6 + len(given)),
         out_specs=in_vmem(len(shapes)),
         scratch_shapes=scratch,
-        compiler_params=params(32 << 20),
+        compiler_params=params(16 << 20),
         cost_estimate=cost(4 * rows * D * FF, 4 * D * FF + 2 * rows * FF + 2 * D * FF, rows * FF),
         name="mlp_back",
-    )(gain, *given, *in_hbm(weight_down, slope, weight_up, lhs, middle))
+    )(gain, *given, weight_down, slope, weight_up, lhs, middle)
 
 
 def attention_back_kernel(first, grad_ref, wo_ref, qkv_ref, lse_ref, *refs):
@@ -1089,10 +1074,14 @@
         image_low, halves, hidden_cols = lax.optimization_barrier((image_low, halves, hidden_cols))
         across = jnp.concatenate(halves, axis=0)
         held = joined(joined(held, text_beside, 2), joined(text_above, across, 2), 4, 4)
-        text_pack = joined(held, swapped(held, 1), 1).reshape(-1, D + total_images)
+        other, slope = in_turn(swapped(held, 1), slope)
+        text_pack = joined(held, other, 1).reshape(-1, D + total_images)
     image_all = exchanged(image_low).reshape(total_images, D)
     if small:
         image_all, text_pack = in_turn(image_all, text_pack)
+
+    heavy = loaded(txt_down, slope, txt_up, lhs_up, middle)
+    image_all, heavy = in_turn(image_all, heavy)
 
     if small:
         given = (text_pack, image_all, own_pack, text_unit, inverse)
@@ -1105,7 +1094,7 @@
         row_low = grad_row.astype(bf16)
         given = (row_low, grad_row)
 
-    *up, grad_middle, sums = mlp_back(given, txt_down, slope, txt_up, lhs_up, middle, txt_gain2)
+    *up, grad_middle, sums = mlp_back(given, *heavy, txt_gain2)
     if small:
         *up, grad_middle, sums, loss_value, col_sum, col_count, live_total = (
             *up, grad_middle, sums

time: 243 us -> 245 us (level)
  Pallas kernels: 110 us -> 114 us
  starting transfers between devices: 51.7 us -> 49.1 us
    pallas_call x0 -> x1, Pallas kernels: none -> 6.07 us  [loaded(): pl.pallas_call(load_kernel, out_shape=[stays(array.shape, array.dtype) fo...]
  transfers between devices with their start and end apart: 42 -> 42, of which waited for: 16 -> 15; matrix products, arithmetic and copies ran while one was open for 3% -> 3% of each run, Pallas kernels for 36% -> 36%
where the time goes in v11:
time: 245 us; the launch traced here: 243 us
  Pallas kernels  114 us (47%)
  waiting for transfers between devices  49.6 us (20%)
  starting transfers between devices  49.1 us (20%)
  between operations  14.9 us (6%)
  local copies, waits for them, and re-layouts  10.6 us (4%)
  other arithmetic  5.46 us (2%)
    ppermute x39, starting transfers between devices, swapped(): return lax.ppermute(value, AXIS, [(i, i ^ mask) for i in range(peers)])  38.6 us
    ppermute x39, waiting for transfers between devices, swapped(): return lax.ppermute(value, AXIS, [(i, i ^ mask) for i in range(peers)])  36.9 us
    pallas_call x1, Pallas kernels, text_front(): pl.pallas_call(text_front_kernel, out_shape=[jax.ShapeDtypeStruct(*item)...  18 us
    pallas_call x1, Pallas kernels, image_front(): pl.pallas_call(functools.partial(image_front_kernel, windows), out_shape=...  15.8 us
    pallas_call x1, Pallas kernels, mlp_back(): pl.pallas_call(functools.partial(mlp_back_kernel, with_loss), out_shape=s...  13.9 us
    all_to_all x1, waiting for transfers between devices, exchanged(): return lax.all_to_all(copies, AXIS, split_axis=0, concat_axis=0, tiled=True)  12.6 us
    pallas_call x1, Pallas kernels, text_up(): pl.pallas_call(text_up_kernel, grid=(FF // TILE,), out_shape=[jax.ShapeDt...  12.2 us
    pallas_call x2, Pallas kernels, attention_back(): pl.pallas_call(functools.partial(attention_back_kernel, first), out_shape...  11.5 us
  transfers between devices with their start and end apart: 42, of which 15 were waited for; matrix products, arithmetic and copies ran while one was open for 3% of the time, Pallas kernels for 36%

profile of v11, /device:TPU:0, one launch (start us, length us, event | category | flops | bytes accessed | tf_op | source)
XLA Modules:
  0.0 243.4 jit_solution(14685003702603566072)
XLA Ops:
  10.3 5.1 %collective-permute-start.2 = (bf16[24,3584]{1,0:T(8,128)(2,1)S(1)}, bf16[24,3584]{1,0:T(8,128)(2,1)S(1)}, u32[]{:S(2)}, u32[]{:S(2)}) collective-permute-start(bf16[24,3584]{1,0:T(8,128)(2,1)S(1)} %pad_maximum_fusion.7), channel_id=1, source_target_pairs={{0,24},{1,25},{2,26},{3,27},{4,28},{5,29},{6,30},{7,31},{8,16},{9,... | collective-permute-start | bytes 516104 | tf_op jit(solution)/shard_map/ppermute | solution.py:26
  16.9 18.0 %text_front.1 = (bf16[640,768]{1,0:T(8,128)(2,1)}, bf16[640,2304]{1,0:T(8,128)(2,1)}, bf16[640,768]{1,0:T(8,128)(2,1)}, f32[640,768]{1,0:T(8,128)}, bf16[640,768...) custom-call(bf16[640,768]{1,0:T(8,128)(2,1)} %refs_3_.1, f32[768]{0:T(1024)} %refs_4_.1, f32[768]{0:T(1024)} %b1_ref.2, ...), custom_call_target="tpu_custom_call" | custom-call | flops 3019898880 | bytes 11599872 | tf_op jit(solution)/shard_map/text_front/pallas_call | solution.py:364
  40.8 12.2 %text_up.1 = (bf16[640,3072]{1,0:T(8,128)(2,1)}, f32[40,3072]{1,0:T(8,128)}, f32[40,768]{1,0:T(8,128)}, f32[40,128]{1,0:T(8,128)}) custom-call(bf16[640,768]{1,0:T(8,128)(2,1)} %get-tuple-element.131.h2_ref.refs_1_.refs_3_, bf16[768,3072]{1,0:T(8,128)(2,1)} %refs_2_.2, bf16[3072,768]{1,0:T(8,128)(2,1)} %refs_0_.1, f32[40,768]{1,0:T(8,128)} %get-tuple-element.126.sum_ref, ...), custom_call_target="tpu_custom_call" | custom-call | flops 3019898880 | bytes 13369344 | tf_op jit(solution)/shard_map/text_up/pallas_call | solution.py:535
  53.1 4.6 %collective-permute-done.4.refs_2_ = bf16[96,3584]{1,0:T(8,128)(2,1)S(1)} collective-permute-done((bf16[96,3584]{1,0:T(8,128)(2,1)}, bf16[96,3584]{1,0:T(8,128)(2,1)S(1)}, u32[]{:S(2)}, u32[]{:S(2)}) %collective-permute-start.4) | collective-permute-done | bytes 688160 | tf_op jit(solution)/shard_map/ppermute | solution.py:26
  57.7 5.1 %collective-permute-done.3.refs_1_ = bf16[96,3584]{1,0:T(8,128)(2,1)S(1)} collective-permute-done((bf16[96,3584]{1,0:T(8,128)(2,1)}, bf16[96,3584]{1,0:T(8,128)(2,1)S(1)}, u32[]{:S(2)}, u32[]{:S(2)}) %collective-permute-start.3) | collective-permute-done | bytes 688160 | tf_op jit(solution)/shard_map/ppermute | solution.py:26
  67.7 3.2 %left_factors.2.refs_3_ = bf16[2,768,640]{2,1,0:T(8,128)(2,1)S(1)} custom-call(s32[768,1]{1,0:T(8,128)S(1)} %fusion.8.refs_0_, bf16[640,768]{1,0:T(8,128)(2,1)S(1)} %copy-done.18, s32[768,1]{1,0:T(8,128)S(1)} %fusion.9.refs_2_.order_ref.refs_4_, bf16[640,768]{1,0:T(8,128)(2,1)S(1)} %copy-done.18), custom_call_target="tpu_custom_call" | custom-call | flops 1509949440 | bytes 3932160 | tf_op jit(solution)/shard_map/left_factors/pallas_call | solution.py:638
  73.0 3.5 %collective-permute-start.14 = (bf16[1,40,1024]{2,1,0:T(8,128)(2,1)S(1)}, bf16[1,40,1024]{2,1,0:T(8,128)(2,1)S(1)}, u32[]{:S(2)}, u32[]{:S(2)}) collective-permute-start(bf16[1,40,1024]{2,1,0:T(8,128)(2,1)S(1)} %bitcast.81), channel_id=1, source_target_pairs={{0,24},{1,25},{2,26},{3,27},{4,28},{5,29},{6,30},{7,31},{8,16},{9,... | collective-permute-start | bytes 245768 | tf_op jit(solution)/shard_map/ppermute | solution.py:26
  78.9 15.8 %image_front.1 = (bf16[400,768]{1,0:T(8,128)(2,1)}, f32[8,768]{1,0:T(8,128)}, f32[8,512]{1,0:T(8,128)}) custom-call(bf16[400,768]{1,0:T(8,128)(2,1)} %x_ref.3, s32[768,1]{1,0:T(8,128)} %copy-done.8, bf16[768]{0:T(1024)(128)(2,1)} %g1_ref.3, bf16[768]{0:T(1024)(128)(2,1)} %b1_ref.3, bf16[768]{0:T(1024)(128)(2,1)} %g2_ref.3, bf16[768]{0:T(1024)(128)(2,1)} %b2_ref.3, ...), custom_call_target="tpu_custom_call" | custom-call | flops 2831155200 | bytes 4718592 | tf_op jit(solution)/shard_map/image_front/pallas_call | solution.py:439
  98.2 5.0 %all-to-all-start = ((bf16[40,32,96]{2,0,1:T(8,128)(2,1)}), bf16[40,32,96]{2,0,1:T(8,128)(2,1)S(1)}, u32[]{:S(2)}, u32[]{:S(2)}) async-start(bf16[40,32,96]{2,0,1:T(8,128)(2,1)} %copy.68), calls=%async_computation | async-start | bytes 655360 | tf_op jit(solution)/shard_map/all_to_all | solution.py:1067
  106.8 8.9 %image_up.1 = bf16[32,8,768]{2,1,0:T(8,128)(2,1)} custom-call(bf16[400,768]{1,0:T(8,128)(2,1)} %get-tuple-element.142.h2_ref, bf16[768,5632]{1,0:T(8,128)(2,1)} %all-gather.2.cloned.1.call-done.wu_ref.wd_ref.first_ref, bf16[768,5632]{1,0:T(8,128)(2,1)} %all-gather.2.cloned.1.call-done.wu_ref.wd_ref.first_ref, ...), custom_call_target="tpu_custom_call" | custom-call | flops 1887436800 | bytes 9437184 | tf_op jit(solution)/shard_map/image_up/pallas_call | solution.py:603
  116.6 5.5 %all-to-all-start.1 = ((bf16[32,8,768]{2,1,0:T(8,128)(2,1)}), bf16[32,8,768]{2,1,0:T(8,128)(2,1)S(1)}, u32[]{:S(2)}, u32[]{:S(2)}) async-start(bf16[32,8,768]{2,1,0:T(8,128)(2,1)} %image_up.1), calls=%async_computation.1 | async-start | bytes 786432 | tf_op jit(solution)/shard_map/all_to_all | solution.py:44
  122.6 12.6 %all-to-all-done.1 = bf16[32,8,768]{2,1,0:T(8,128)(2,1)S(1)} async-done(((bf16[32,8,768]{2,1,0:T(8,128)(2,1)}), bf16[32,8,768]{2,1,0:T(8,128)(2,1)S(1)}, u32[]{:S(2)}, u32[]{:S(2)}) %all-to-all-start.1) | async-done | bytes 393248 | tf_op jit(solution)/shard_map/all_to_all | solution.py:44
  135.3 6.1 %loaded.1 = (bf16[3072,768]{1,0:T(8,128)(2,1)S(1)}, bf16[640,3072]{1,0:T(8,128)(2,1)S(1)}, bf16[768,3072]{1,0:T(8,128)(2,1)S(1)}, bf16[2,768,640]{2,1,0:T(8,128)(2,1)S(1)}, f32[640,768]{1,0:T(8,128)S(1)}) custom-call(bf16[3072,768]{1,0:T(8,128)(2,1)} %refs_0_.1, bf16[640,3072]{1,0:T(8,128)(2,1)} %get-tuple-element.155.refs_1_, bf16[768,3072]{1,0:T(8,128)(2,1)} %refs_2_.2, ...), custom_call_target="tpu_custom_call" | custom-call | bytes 34603008 | tf_op jit(solution)/shard_map/loaded/pallas_call | solution.py:769
  141.4 13.9 %mlp_back.1 = (bf16[384,1536]{1,0:T(8,128)(2,1)S(1)}, bf16[384,1536]{1,0:T(8,128)(2,1)S(1)}, bf16[384,1536]{1,0:T(8,128)(2,1)S(1)}, bf16[384,1536]{1,0:T(8,128)(...) custom-call(f32[768]{0:T(1024)S(1)} %copy-done.17, ...), custom_call_target="tpu_custom_call" | custom-call | flops 6039797760 | bytes 18087936 | tf_op jit(solution)/shard_map/mlp_back/pallas_call | solution.py:843
  155.9 4.6 %attention_back.2 = (bf16[256,768]{1,0:T(8,128)(2,1)S(1)}, bf16[256,2304]{1,0:T(8,128)(2,1)S(1)}) custom-call(f32[640,768]{1,0:T(8,128)S(1)} %get-tuple-element.170.grad_ref.refs_5_, bf16[768,768]{1,0:T(8,128)(2,1)S(1)} %copy-done.1, bf16[640,2304]{1,0:T(8,128)(2,1)S(1)} %copy-done, f32[80,128]{1,0:T(8,128)S(1)} %copy-done.13), custom_call_target="tpu_custom_call" | custom-call | flops 1509949440 | bytes 4325376 | tf_op jit(solution)/shard_map/attention_back/pallas_call | solution.py:893
  163.1 6.9 %attention_back.3 = (bf16[384,768]{1,0:T(8,128)(2,1)S(1)}, bf16[384,2304]{1,0:T(8,128)(2,1)S(1)}) custom-call(f32[640,768]{1,0:T(8,128)S(1)} %get-tuple-element.170.grad_ref.refs_5_, bf16[768,768]{1,0:T(8,128)(2,1)S(1)} %copy-done.1, bf16[640,2304]{1,0:T(8,128)(2,1)S(1)} %copy-done, f32[80,128]{1,0:T(8,128)S(1)} %copy-done.13, ...), custom_call_target="tpu_custom_call" | custom-call | flops 2264924160 | bytes 5898240 | tf_op jit(solution)/shard_map/attention_back/pallas_call | solution.py:893
  170.0 4.8 %left_factors.3.refs_1_.lhs_ref = bf16[3,768,640]{2,1,0:T(8,128)(2,1)S(1)} custom-call(s32[768,1]{1,0:T(8,128)S(1)} %copy-done.11, bf16[640,768]{1,0:T(8,128)(2,1)S(1)} %copy-done.19, s32[768,1]{1,0:T(8,128)S(1)} %copy-done.9, bf16[640,768]{1,0:T(8,128)(2,1)S(1)} %copy-done.19, s32[768,1]{1,0:T(8,128)S(1)} %copy-done.9, bf16[640,768]{1,0:T(8,128)(2,1)S(1)} %copy-done.20), custom_call_target="tpu_custom_call" | custom-call | flops 2264924160 | bytes 5898240 | tf_op jit(solution)/shard_map/left_factors/pallas_call | solution.py:638
  177.6 3.9 %weight_back.1 = (bf16[384,1536]{1,0:T(8,128)(2,1)S(1)}, bf16[384,1536]{1,0:T(8,128)(2,1)S(1)}, bf16[384,1536]{1,0:T(8,128)(2,1)S(1)}, bf16[384,1536]{1,0:T(8,128)(2,1)S(1)}) custom-call(bf16[3,768,640]{2,1,0:T(8,128)(2,1)S(1)} %left_factors.3.refs_1_.lhs_ref, bf16[256,2304]{1,0:T(8,128)(2,1)S(1)} %get-tuple-element.173.refs_0_, ...), custom_call_target="tpu_custom_call" | custom-call | flops 3019898880 | bytes 12189696 | tf_op jit(solution)/shard_map/weight_back/pallas_call | solution.py:926
  184.1 5.9 %input_back.1 = (f32[640,768]{1,0:T(8,128)}, f32[8,1536]{1,0:T(8,128)S(1)}) custom-call(bf16[256,2304]{1,0:T(8,128)(2,1)S(1)} %get-tuple-element.173.refs_0_, bf16[384,2304]{1,0:T(8,128)(2,1)S(1)} %get-tuple-element.184.refs_0_.refs_1_, bf16[768,2304]{1,0:T(8,128)(2,1)S(1)} %copy-done.2, bf16[640,768]{1,0:T(8,128)(2,1)S(1)} %copy-done.7, ...), custom_call_target="tpu_custom_call" | custom-call | flops 2264924160 | bytes 10420224 | tf_op jit(solution)/shard_map/input_back/pallas_call | solution.py:968
  199.1 5.9 %grad_of_down.1 = f32[96,768]{1,0:T(8,128)S(1)} custom-call(bf16[1280,1024]{1,0:T(8,128)(2,1)S(1)} %bitcast.77, bf16[256,768]{1,0:T(8,128)(2,1)S(1)} %bitcast.79, f32[1,256]{1,0:T(1,128)S(1)} %get-tuple-element.197.col_sum_ref, f32[1,256]{1,0:T(1,128)S(1)} %get-tuple-element.198.col_count_ref, f32[1,128]{1,0:T(1,128)S(1)} %get-tuple-element.199.live_ref, ...), custom_call_target="tpu_custom_call" | custom-call | flops 1006632960 | bytes 2621440 | tf_op jit(solution)/shard_map/grad_of_down/pallas_call | solution.py:739
  205.0 3.4 %collective-permute-done.32 = bf16[24,3072]{1,0:T(8,128)(2,1)S(1)} collective-permute-done((bf16[24,3072]{1,0:T(8,128)(2,1)S(1)}, bf16[24,3072]{1,0:T(8,128)(2,1)S(1)}, u32[]{:S(2)}, u32[]{:S(2)}) %collective-permute-start.32) | collective-permute-done | bytes 147488 | tf_op jit(solution)/shard_map/ppermute | solution.py:26
  210.7 6.2 %collective-permute-done.35.got_b = bf16[96,1536]{1,0:T(8,128)(2,1)S(1)} collective-permute-done((bf16[96,1536]{1,0:T(8,128)(2,1)S(1)}, bf16[96,1536]{1,0:T(8,128)(2,1)S(1)}, u32[]{:S(2)}, u32[]{:S(2)}) %collective-permute-start.35) | collective-permute-done | bytes 294944 | tf_op jit(solution)/shard_map/ppermute | solution.py:26
  223.7 3.4 %collective-permute-done.36 = bf16[32,3072]{1,0:T(8,128)(2,1)S(1)} collective-permute-done((bf16[32,3072]{1,0:T(8,128)(2,1)S(1)}, bf16[32,3072]{1,0:T(8,128)(2,1)S(1)}, u32[]{:S(2)}, u32[]{:S(2)}) %collective-permute-start.36) | collective-permute-done | bytes 196640 | tf_op jit(solution)/shard_map/ppermute | solution.py:26
  227.1 7.4 %collective-permute-done.37 = bf16[32,3072]{1,0:T(8,128)(2,1)S(1)} collective-permute-done((bf16[32,3072]{1,0:T(8,128)(2,1)S(1)}, bf16[32,3072]{1,0:T(8,128)(2,1)S(1)}, u32[]{:S(2)}, u32[]{:S(2)}) %collective-permute-start.37) | collective-permute-done | bytes 196640 | tf_op jit(solution)/shard_map/ppermute | solution.py:26
  (199 shorter events, 56.6 us)
Async XLA Ops:
  7.2 99.6 %all-gather.2.cloned.1.call-start = ((), (), s32[]{:S(2)}) async-start(), calls=%async_computation.2 | async-start | bytes 8921088 | tf_op jit(solution)/shard_map/all_gather | solution.py:1009
  10.3 25.7 %collective-permute-start.2 = (bf16[24,3584]{1,0:T(8,128)(2,1)S(1)}, bf16[24,3584]{1,0:T(8,128)(2,1)S(1)}, u32[]{:S(2)}, u32[]{:S(2)}) collective-permute-start(bf16[24,3584]{1,0:T(8,128)(2,1)S(1)} %pad_maximum_fusion.7), channel_id=1, source_target_pairs={{0,24},{1,25},{2,26},{3,27},{4,28},{5,29},{6,30},{7,31},{8,16},{9,... | collective-permute-start | bytes 516104 | tf_op jit(solution)/shard_map/ppermute | solution.py:26
  15.4 20.6 %collective-permute-start.1 = (bf16[24,3584]{1,0:T(8,128)(2,1)S(1)}, bf16[24,3584]{1,0:T(8,128)(2,1)S(1)}, u32[]{:S(2)}, u32[]{:S(2)}) collective-permute-start(bf16[24,3584]{1,0:T(8,128)(2,1)S(1)} %pad_maximum_fusion.7), channel_id=1, source_target_pairs={{0,16},{1,17},{2,18},{3,19},{4,20},{5,21},{6,22},{7,23},{8,24},{9,... | collective-permute-start | bytes 516104 | tf_op jit(solution)/shard_map/ppermute | solution.py:26
  15.4 20.6 %collective-permute-start = (bf16[24,3584]{1,0:T(8,128)(2,1)S(1)}, bf16[24,3584]{1,0:T(8,128)(2,1)S(1)}, u32[]{:S(2)}, u32[]{:S(2)}) collective-permute-start(bf16[24,3584]{1,0:T(8,128)(2,1)S(1)} %pad_maximum_fusion.7), channel_id=1, source_target_pairs={{0,8},{1,9},{2,10},{3,11},{4,12},{5,13},{6,14},{7,15},{8,0},{9,1},... | collective-permute-start | bytes 516104 | tf_op jit(solution)/shard_map/ppermute | solution.py:26
  37.0 20.7 %collective-permute-start.4 = (bf16[96,3584]{1,0:T(8,128)(2,1)}, bf16[96,3584]{1,0:T(8,128)(2,1)S(1)}, u32[]{:S(2)}, u32[]{:S(2)}) collective-permute-start(bf16[96,3584]{1,0:T(8,128)(2,1)} %pad_maximum_fusion.2.refs_0_), channel_id=1, source_target_pairs={{0,4},{1,5},{2,6},{3,7},{4,0},{5,1},{6,2},{7,3},{8,12},{9,13},{10,... | collective-permute-start | bytes 2064392 | tf_op jit(solution)/shard_map/ppermute | solution.py:26
  38.7 24.1 %collective-permute-start.3 = (bf16[96,3584]{1,0:T(8,128)(2,1)}, bf16[96,3584]{1,0:T(8,128)(2,1)S(1)}, u32[]{:S(2)}, u32[]{:S(2)}) collective-permute-start(bf16[96,3584]{1,0:T(8,128)(2,1)} %pad_maximum_fusion.2.refs_0_), channel_id=1, source_target_pairs={{0,2},{1,3},{2,0},{3,1},{4,6},{5,7},{6,4},{7,5},{8,10},{9,11},{10,... | collective-permute-start | bytes 2064392 | tf_op jit(solution)/shard_map/ppermute | solution.py:26
  65.5 11.0 %collective-permute-start.8 = (bf16[96,3584]{1,0:T(8,128)(2,1)S(1)}, bf16[96,3584]{1,0:T(8,128)(2,1)S(1)}, u32[]{:S(2)}, u32[]{:S(2)}) collective-permute-start(bf16[96,3584]{1,0:T(8,128)(2,1)S(1)} %collective-permute-done.3.refs_1_), channel_id=1, source_target_pairs={{0,1},{1,0},{2,3},{3,2},{4,5},{5,4},{6,7},{7,6},{8,9},{9,8},{10,11... | collective-permute-start | bytes 2064392 | tf_op jit(solution)/shard_map/ppermute | solution.py:26
  66.1 10.5 %collective-permute-start.9 = (bf16[96,3584]{1,0:T(8,128)(2,1)S(1)}, bf16[96,3584]{1,0:T(8,128)(2,1)S(1)}, u32[]{:S(2)}, u32[]{:S(2)}) collective-permute-start(bf16[96,3584]{1,0:T(8,128)(2,1)S(1)} %collective-permute-done.4.refs_2_), channel_id=1, source_target_pairs={{0,1},{1,0},{2,3},{3,2},{4,5},{5,4},{6,7},{7,6},{8,9},{9,8},{10,11... | collective-permute-start | bytes 2064392 | tf_op jit(solution)/shard_map/ppermute | solution.py:26
  73.0 21.7 %collective-permute-start.14 = (bf16[1,40,1024]{2,1,0:T(8,128)(2,1)S(1)}, bf16[1,40,1024]{2,1,0:T(8,128)(2,1)S(1)}, u32[]{:S(2)}, u32[]{:S(2)}) collective-permute-start(bf16[1,40,1024]{2,1,0:T(8,128)(2,1)S(1)} %bitcast.81), channel_id=1, source_target_pairs={{0,24},{1,25},{2,26},{3,27},{4,28},{5,29},{6,30},{7,31},{8,16},{9,... | collective-permute-start | bytes 245768 | tf_op jit(solution)/shard_map/ppermute | solution.py:26
  76.5 18.2 %collective-permute-start.13 = (bf16[1,40,1024]{2,1,0:T(8,128)(2,1)S(1)}, bf16[1,40,1024]{2,1,0:T(8,128)(2,1)S(1)}, u32[]{:S(2)}, u32[]{:S(2)}) collective-permute-start(bf16[1,40,1024]{2,1,0:T(8,128)(2,1)S(1)} %bitcast.82), channel_id=1, source_target_pairs={{0,16},{1,17},{2,18},{3,19},{4,20},{5,21},{6,22},{7,23},{8,24},{9,... | collective-permute-start | bytes 245768 | tf_op jit(solution)/shard_map/ppermute | solution.py:26
  76.6 18.2 %collective-permute-start.12 = (bf16[1,40,1024]{2,1,0:T(8,128)(2,1)S(1)}, bf16[1,40,1024]{2,1,0:T(8,128)(2,1)S(1)}, u32[]{:S(2)}, u32[]{:S(2)}) collective-permute-start(bf16[1,40,1024]{2,1,0:T(8,128)(2,1)S(1)} %bitcast.83), channel_id=1, source_target_pairs={{0,8},{1,9},{2,10},{3,11},{4,12},{5,13},{6,14},{7,15},{8,0},{9,1},... | collective-permute-start | bytes 245768 | tf_op jit(solution)/shard_map/ppermute | solution.py:26
  98.2 17.6 %all-to-all-start = ((bf16[40,32,96]{2,0,1:T(8,128)(2,1)}), bf16[40,32,96]{2,0,1:T(8,128)(2,1)S(1)}, u32[]{:S(2)}, u32[]{:S(2)}) async-start(bf16[40,32,96]{2,0,1:T(8,128)(2,1)} %copy.68), calls=%async_computation | async-start | bytes 655360 | tf_op jit(solution)/shard_map/all_to_all | solution.py:1067
  116.6 18.6 %all-to-all-start.1 = ((bf16[32,8,768]{2,1,0:T(8,128)(2,1)}), bf16[32,8,768]{2,1,0:T(8,128)(2,1)S(1)}, u32[]{:S(2)}, u32[]{:S(2)}) async-start(bf16[32,8,768]{2,1,0:T(8,128)(2,1)} %image_up.1), calls=%async_computation.1 | async-start | bytes 786432 | tf_op jit(solution)/shard_map/all_to_all | solution.py:44
  161.1 15.3 %collective-permute-start.22 = (bf16[192,1536]{1,0:T(8,128)(2,1)S(1)}, bf16[192,1536]{1,0:T(8,128)(2,1)S(1)}, u32[]{:S(2)}, u32[]{:S(2)}) collective-permute-start(bf16[192,1536]{1,0:T(8,128)(2,1)S(1)} %get-tuple-element.179.refs_1_), channel_id=1, source_target_pairs={{0,2},{1,3},{2,0},{3,1},{4,6},{5,7},{6,4},{7,5},{8,10},{9,11},{10,... | collective-permute-start | bytes 1769480 | tf_op jit(solution)/shard_map/ppermute | solution.py:26
  161.6 15.4 %collective-permute-start.23 = (bf16[192,1536]{1,0:T(8,128)(2,1)S(1)}, bf16[192,1536]{1,0:T(8,128)(2,1)S(1)}, u32[]{:S(2)}, u32[]{:S(2)}) collective-permute-start(bf16[192,1536]{1,0:T(8,128)(2,1)S(1)} %get-tuple-element.181.refs_3_), channel_id=1, source_target_pairs={{0,4},{1,5},{2,6},{3,7},{4,0},{5,1},{6,2},{7,3},{8,12},{9,13},{10,... | collective-permute-start | bytes 1769480 | tf_op jit(solution)/shard_map/ppermute | solution.py:26
  181.5 10.4 %collective-permute-start.26 = (bf16[384,1536]{1,0:T(8,128)(2,1)S(1)}, bf16[384,1536]{1,0:T(8,128)(2,1)S(1)}, u32[]{:S(2)}, u32[]{:S(2)}) collective-permute-start(bf16[384,1536]{1,0:T(8,128)(2,1)S(1)} %get-tuple-element.201), channel_id=1, source_target_pairs={{0,1},{1,0},{2,3},{3,2},{4,5},{5,4},{6,7},{7,6},{8,9},{9,8},{10,11... | collective-permute-start | bytes 3538952 | tf_op jit(solution)/shard_map/ppermute | solution.py:26
  181.6 10.4 %collective-permute-start.27 = (bf16[384,1536]{1,0:T(8,128)(2,1)S(1)}, bf16[384,1536]{1,0:T(8,128)(2,1)S(1)}, u32[]{:S(2)}, u32[]{:S(2)}) collective-permute-start(bf16[384,1536]{1,0:T(8,128)(2,1)S(1)} %get-tuple-element.203), channel_id=1, source_target_pairs={{0,1},{1,0},{2,3},{3,2},{4,5},{5,4},{6,7},{7,6},{8,9},{9,8},{10,11... | collective-permute-start | bytes 3538952 | tf_op jit(solution)/shard_map/ppermute | solution.py:26
  192.5 15.9 %collective-permute-start.29 = (bf16[208,1536]{1,0:T(8,128)(2,1)S(1)}, bf16[208,1536]{1,0:T(8,128)(2,1)S(1)}, u32[]{:S(2)}, u32[]{:S(2)}) collective-permute-start(bf16[208,1536]{1,0:T(8,128)(2,1)S(1)} %get-tuple-element.211), channel_id=1, source_target_pairs={{0,2},{1,3},{2,0},{3,1},{4,6},{5,7},{6,4},{7,5},{8,10},{9,11},{10,... | collective-permute-start | bytes 1916936 | tf_op jit(solution)/shard_map/ppermute | solution.py:26
  193.6 14.8 %collective-permute-start.30 = (bf16[192,1536]{1,0:T(8,128)(2,1)S(1)}, bf16[192,1536]{1,0:T(8,128)(2,1)S(1)}, u32[]{:S(2)}, u32[]{:S(2)}) collective-permute-start(bf16[192,1536]{1,0:T(8,128)(2,1)S(1)} %get-tuple-element.213), channel_id=1, source_target_pairs={{0,4},{1,5},{2,6},{3,7},{4,0},{5,1},{6,2},{7,3},{8,12},{9,13},{10,... | collective-permute-start | bytes 1769480 | tf_op jit(solution)/shard_map/ppermute | solution.py:26
  194.7 10.3 %collective-permute-start.31 = (bf16[24,3072]{1,0:T(8,128)(2,1)S(1)}, bf16[24,3072]{1,0:T(8,128)(2,1)S(1)}, u32[]{:S(2)}, u32[]{:S(2)}) collective-permute-start(bf16[24,3072]{1,0:T(8,128)(2,1)S(1)} %get-tuple-element.214), channel_id=1, source_target_pairs={{0,8},{1,9},{2,10},{3,11},{4,12},{5,13},{6,14},{7,15},{8,0},{9,1},... | collective-permute-start | bytes 442376 | tf_op jit(solution)/shard_map/ppermute | solution.py:26
  195.7 12.7 %collective-permute-start.32 = (bf16[24,3072]{1,0:T(8,128)(2,1)S(1)}, bf16[24,3072]{1,0:T(8,128)(2,1)S(1)}, u32[]{:S(2)}, u32[]{:S(2)}) collective-permute-start(bf16[24,3072]{1,0:T(8,128)(2,1)S(1)} %get-tuple-element.215), channel_id=1, source_target_pairs={{0,16},{1,17},{2,18},{3,19},{4,20},{5,21},{6,22},{7,23},{8,24},{9,... | collective-permute-start | bytes 442376 | tf_op jit(solution)/shard_map/ppermute | solution.py:26
  196.3 12.1 %collective-permute-start.33 = (bf16[24,3072]{1,0:T(8,128)(2,1)S(1)}, bf16[24,3072]{1,0:T(8,128)(2,1)S(1)}, u32[]{:S(2)}, u32[]{:S(2)}) collective-permute-start(bf16[24,3072]{1,0:T(8,128)(2,1)S(1)} %get-tuple-element.216), channel_id=1, source_target_pairs={{0,24},{1,25},{2,26},{3,27},{4,28},{5,29},{6,30},{7,31},{8,16},{9,... | collective-permute-start | bytes 442376 | tf_op jit(solution)/shard_map/ppermute | solution.py:26
  219.7 14.8 %collective-permute-start.37 = (bf16[32,3072]{1,0:T(8,128)(2,1)S(1)}, bf16[32,3072]{1,0:T(8,128)(2,1)S(1)}, u32[]{:S(2)}, u32[]{:S(2)}) collective-permute-start(bf16[32,3072]{1,0:T(8,128)(2,1)S(1)} %get-tuple-element.229), channel_id=1, source_target_pairs={{0,16},{1,17},{2,18},{3,19},{4,20},{5,21},{6,22},{7,23},{8,24},{9,... | collective-permute-start | bytes 589832 | tf_op jit(solution)/shard_map/ppermute | solution.py:26
  219.7 14.8 %collective-permute-start.38 = (bf16[32,3072]{1,0:T(8,128)(2,1)S(1)}, bf16[32,3072]{1,0:T(8,128)(2,1)S(1)}, u32[]{:S(2)}, u32[]{:S(2)}) collective-permute-start(bf16[32,3072]{1,0:T(8,128)(2,1)S(1)} %get-tuple-element.230), channel_id=1, source_target_pairs={{0,24},{1,25},{2,26},{3,27},{4,28},{5,29},{6,30},{7,31},{8,16},{9,... | collective-permute-start | bytes 589832 | tf_op jit(solution)/shard_map/ppermute | solution.py:26
  (53 other events, 397.7 us)
Sparse Core Ops, SparseCore 0:
  11.5 95.2 all-gather.1

commit v12 on v11

--- a/solution.py
+++ b/solution.py
@@ -1075,13 +1075,12 @@
         across = jnp.concatenate(halves, axis=0)
         held = joined(joined(held, text_beside, 2), joined(text_above, across, 2), 4, 4)
         other, slope = in_turn(swapped(held, 1), slope)
+        heavy = loaded(txt_down, slope, txt_up, lhs_up, middle)
+        other, heavy = in_turn(other, heavy)
         text_pack = joined(held, other, 1).reshape(-1, D + total_images)
     image_all = exchanged(image_low).reshape(total_images, D)
     if small:
         image_all, text_pack = in_turn(image_all, text_pack)
-
-    heavy = loaded(txt_down, slope, txt_up, lhs_up, middle)
-    image_all, heavy = in_turn(image_all, heavy)
 
     if small:
         given = (text_pack, image_all, own_pack, text_unit, inverse)
@@ -1093,6 +1092,7 @@
         grad_row = inverse[:, :1] * turned(grad, text_unit) * (1.0 / TXT_LEN)
         row_low = grad_row.astype(bf16)
         given = (row_low, grad_row)
+        heavy = (txt_down, slope, txt_up, lhs_up, middle)
 
     *up, grad_middle, sums = mlp_back(given, *heavy, txt_gain2)
     if small:

time: 245 us -> 254 us (1.037)
  local copies, waits for them, and re-layouts: 10.6 us -> 30.6 us
  waiting for transfers between devices: 49.6 us -> 39 us
    unnamed x72 -> x94, local copies, waits for them, and re-layouts: 3.65 us -> 23.7 us
    all_to_all x1, waiting for transfers between devices: 12.6 us -> 0.01 us  [exchanged(): return lax.all_to_all(copies, AXIS, split_axis=0, concat_axis=0, tiled=True)]
  transfers between devices with their start and end apart: 42 -> 42, of which waited for: 15 -> 13; matrix products, arithmetic and copies ran while one was open for 3% -> 3% of each run, Pallas kernels for 36% -> 37%
where the time goes in v12:
time: 254 us; the launch traced here: 253 us
  Pallas kernels  114 us (45%)
  starting transfers between devices  49.6 us (20%)
  waiting for transfers between devices  39 us (15%)
  local copies, waits for them, and re-layouts  30.6 us (12%)
  between operations  14.9 us (6%)
  other arithmetic  5.47 us (2%)
    ppermute x39, starting transfers between devices, swapped(): return lax.ppermute(value, AXIS, [(i, i ^ mask) for i in range(peers)])  39.1 us
    ppermute x39, waiting for transfers between devices, swapped(): return lax.ppermute(value, AXIS, [(i, i ^ mask) for i in range(peers)])  38.9 us
    unnamed x94, local copies, waits for them, and re-layouts  23.7 us
    pallas_call x1, Pallas kernels, text_front(): pl.pallas_call(text_front_kernel, out_shape=[jax.ShapeDtypeStruct(*item)...  18 us
    pallas_call x1, Pallas kernels, image_front(): pl.pallas_call(functools.partial(image_front_kernel, windows), out_shape=...  15.8 us
    pallas_call x1, Pallas kernels, mlp_back(): pl.pallas_call(functools.partial(mlp_back_kernel, with_loss), out_shape=s...  13.8 us
    pallas_call x1, Pallas kernels, text_up(): pl.pallas_call(text_up_kernel, grid=(FF // TILE,), out_shape=[jax.ShapeDt...  12.2 us
    pallas_call x2, Pallas kernels, attention_back(): pl.pallas_call(functools.partial(attention_back_kernel, first), out_shape...  11.5 us
  transfers between devices with their start and end apart: 42, of which 13 were waited for; matrix products, arithmetic and copies ran while one was open for 3% of the time, Pallas kernels for 37%

profile of v12, /device:TPU:0, one launch (start us, length us, event | category | flops | bytes accessed | tf_op | source)
XLA Modules:
  0.0 253.2 jit_solution(16065441202649058252)
XLA Ops:
  10.3 5.1 %collective-permute-start.2 = (bf16[24,3584]{1,0:T(8,128)(2,1)S(1)}, bf16[24,3584]{1,0:T(8,128)(2,1)S(1)}, u32[]{:S(2)}, u32[]{:S(2)}) collective-permute-start(bf16[24,3584]{1,0:T(8,128)(2,1)S(1)} %pad_maximum_fusion.7), channel_id=1, source_target_pairs={{0,24},{1,25},{2,26},{3,27},{4,28},{5,29},{6,30},{7,31},{8,16},{9,... | collective-permute-start | bytes 516104 | tf_op jit(solution)/shard_map/ppermute | solution.py:26
  16.9 18.0 %text_front.1 = (bf16[640,768]{1,0:T(8,128)(2,1)}, bf16[640,2304]{1,0:T(8,128)(2,1)}, bf16[640,768]{1,0:T(8,128)(2,1)}, f32[640,768]{1,0:T(8,128)}, bf16[640,768...) custom-call(bf16[640,768]{1,0:T(8,128)(2,1)} %refs_3_.1, f32[768]{0:T(1024)} %refs_4_.1, f32[768]{0:T(1024)} %b1_ref.2, ...), custom_call_target="tpu_custom_call" | custom-call | flops 3019898880 | bytes 11599872 | tf_op jit(solution)/shard_map/text_front/pallas_call | solution.py:364
  40.8 12.2 %text_up.1 = (bf16[640,3072]{1,0:T(8,128)(2,1)}, f32[40,3072]{1,0:T(8,128)}, f32[40,768]{1,0:T(8,128)}, f32[40,128]{1,0:T(8,128)}) custom-call(bf16[640,768]{1,0:T(8,128)(2,1)} %get-tuple-element.131.h2_ref.refs_1_.refs_3_, bf16[768,3072]{1,0:T(8,128)(2,1)} %refs_2_.2, bf16[3072,768]{1,0:T(8,128)(2,1)} %refs_0_.1, f32[40,768]{1,0:T(8,128)} %get-tuple-element.126.sum_ref, ...), custom_call_target="tpu_custom_call" | custom-call | flops 3019898880 | bytes 13369344 | tf_op jit(solution)/shard_map/text_up/pallas_call | solution.py:535
  53.1 4.6 %collective-permute-done.4.refs_2_ = bf16[96,3584]{1,0:T(8,128)(2,1)S(1)} collective-permute-done((bf16[96,3584]{1,0:T(8,128)(2,1)}, bf16[96,3584]{1,0:T(8,128)(2,1)S(1)}, u32[]{:S(2)}, u32[]{:S(2)}) %collective-permute-start.4) | collective-permute-done | bytes 688160 | tf_op jit(solution)/shard_map/ppermute | solution.py:26
  57.7 5.1 %collective-permute-done.3.refs_1_ = bf16[96,3584]{1,0:T(8,128)(2,1)S(1)} collective-permute-done((bf16[96,3584]{1,0:T(8,128)(2,1)}, bf16[96,3584]{1,0:T(8,128)(2,1)S(1)}, u32[]{:S(2)}, u32[]{:S(2)}) %collective-permute-start.3) | collective-permute-done | bytes 688160 | tf_op jit(solution)/shard_map/ppermute | solution.py:26
  67.7 3.2 %left_factors.2.refs_3_ = bf16[2,768,640]{2,1,0:T(8,128)(2,1)S(1)} custom-call(s32[768,1]{1,0:T(8,128)S(1)} %fusion.8.refs_0_, bf16[640,768]{1,0:T(8,128)(2,1)S(1)} %copy-done.29, s32[768,1]{1,0:T(8,128)S(1)} %fusion.9.refs_2_.order_ref.refs_4_, bf16[640,768]{1,0:T(8,128)(2,1)S(1)} %copy-done.29), custom_call_target="tpu_custom_call" | custom-call | flops 1509949440 | bytes 3932160 | tf_op jit(solution)/shard_map/left_factors/pallas_call | solution.py:638
  73.0 3.5 %collective-permute-start.14 = (bf16[1,40,1024]{2,1,0:T(8,128)(2,1)S(1)}, bf16[1,40,1024]{2,1,0:T(8,128)(2,1)S(1)}, u32[]{:S(2)}, u32[]{:S(2)}) collective-permute-start(bf16[1,40,1024]{2,1,0:T(8,128)(2,1)S(1)} %bitcast.81), channel_id=1, source_target_pairs={{0,24},{1,25},{2,26},{3,27},{4,28},{5,29},{6,30},{7,31},{8,16},{9,... | collective-permute-start | bytes 245768 | tf_op jit(solution)/shard_map/ppermute | solution.py:26
  78.9 15.8 %image_front.1 = (bf16[400,768]{1,0:T(8,128)(2,1)}, f32[8,768]{1,0:T(8,128)}, f32[8,512]{1,0:T(8,128)}) custom-call(bf16[400,768]{1,0:T(8,128)(2,1)} %x_ref.3, s32[768,1]{1,0:T(8,128)} %copy-done.8, bf16[768]{0:T(1024)(128)(2,1)} %g1_ref.3, bf16[768]{0:T(1024)(128)(2,1)} %b1_ref.3, bf16[768]{0:T(1024)(128)(2,1)} %g2_ref.3, bf16[768]{0:T(1024)(128)(2,1)} %b2_ref.3, ...), custom_call_target="tpu_custom_call" | custom-call | flops 2831155200 | bytes 4718592 | tf_op jit(solution)/shard_map/image_front/pallas_call | solution.py:439
  98.2 5.0 %all-to-all-start = ((bf16[40,32,96]{2,0,1:T(8,128)(2,1)}), bf16[40,32,96]{2,0,1:T(8,128)(2,1)S(1)}, u32[]{:S(2)}, u32[]{:S(2)}) async-start(bf16[40,32,96]{2,0,1:T(8,128)(2,1)} %copy.68), calls=%async_computation | async-start | bytes 655360 | tf_op jit(solution)/shard_map/all_to_all | solution.py:1067
  106.8 8.9 %image_up.1 = bf16[32,8,768]{2,1,0:T(8,128)(2,1)} custom-call(bf16[400,768]{1,0:T(8,128)(2,1)} %get-tuple-element.142.h2_ref, bf16[768,5632]{1,0:T(8,128)(2,1)} %all-gather.2.cloned.1.call-done.wu_ref.wd_ref.first_ref, bf16[768,5632]{1,0:T(8,128)(2,1)} %all-gather.2.cloned.1.call-done.wu_ref.wd_ref.first_ref, ...), custom_call_target="tpu_custom_call" | custom-call | flops 1887436800 | bytes 9437184 | tf_op jit(solution)/shard_map/image_up/pallas_call | solution.py:603
  116.7 5.4 %all-to-all-start.1 = ((bf16[32,8,768]{2,1,0:T(8,128)(2,1)}), bf16[32,8,768]{2,1,0:T(8,128)(2,1)S(1)}, u32[]{:S(2)}, u32[]{:S(2)}) async-start(bf16[32,8,768]{2,1,0:T(8,128)(2,1)} %image_up.1), calls=%async_computation.1 | async-start | bytes 786432 | tf_op jit(solution)/shard_map/all_to_all | solution.py:44
  122.1 6.1 %loaded.1 = (bf16[3072,768]{1,0:T(8,128)(2,1)S(1)}, bf16[640,3072]{1,0:T(8,128)(2,1)S(1)}, bf16[768,3072]{1,0:T(8,128)(2,1)S(1)}, bf16[2,768,640]{2,1,0:T(8,128)(2,1)S(1)}, f32[640,768]{1,0:T(8,128)S(1)}) custom-call(bf16[3072,768]{1,0:T(8,128)(2,1)} %refs_0_.1, bf16[640,3072]{1,0:T(8,128)(2,1)} %get-tuple-element.153.refs_1_, bf16[768,3072]{1,0:T(8,128)(2,1)} %refs_2_.2, ...), custom_call_target="tpu_custom_call" | custom-call | bytes 34603008 | tf_op jit(solution)/shard_map/loaded/pallas_call | solution.py:769
  148.8 13.8 %mlp_back.1 = (bf16[384,1536]{1,0:T(8,128)(2,1)S(1)}, bf16[384,1536]{1,0:T(8,128)(2,1)S(1)}, bf16[384,1536]{1,0:T(8,128)(2,1)S(1)}, bf16[384,1536]{1,0:T(8,128)(...) custom-call(f32[768]{0:T(1024)S(1)} %copy-done.28, ...), custom_call_target="tpu_custom_call" | custom-call | flops 6039797760 | bytes 18087936 | tf_op jit(solution)/shard_map/mlp_back/pallas_call | solution.py:843
  163.1 4.6 %attention_back.2 = (bf16[256,768]{1,0:T(8,128)(2,1)S(1)}, bf16[256,2304]{1,0:T(8,128)(2,1)S(1)}) custom-call(f32[640,768]{1,0:T(8,128)S(1)} %get-tuple-element.170.grad_ref.refs_5_, bf16[768,768]{1,0:T(8,128)(2,1)S(1)} %copy-done.1, bf16[640,2304]{1,0:T(8,128)(2,1)S(1)} %copy-done, f32[80,128]{1,0:T(8,128)S(1)} %copy-done.13), custom_call_target="tpu_custom_call" | custom-call | flops 1509949440 | bytes 4325376 | tf_op jit(solution)/shard_map/attention_back/pallas_call | solution.py:893
  171.6 6.9 %attention_back.3 = (bf16[384,768]{1,0:T(8,128)(2,1)S(1)}, bf16[384,2304]{1,0:T(8,128)(2,1)S(1)}) custom-call(f32[640,768]{1,0:T(8,128)S(1)} %get-tuple-element.170.grad_ref.refs_5_, bf16[768,768]{1,0:T(8,128)(2,1)S(1)} %copy-done.1, bf16[640,2304]{1,0:T(8,128)(2,1)S(1)} %copy-done, f32[80,128]{1,0:T(8,128)S(1)} %copy-done.13, ...), custom_call_target="tpu_custom_call" | custom-call | flops 2264924160 | bytes 5898240 | tf_op jit(solution)/shard_map/attention_back/pallas_call | solution.py:893
  178.5 4.8 %left_factors.3.refs_1_.lhs_ref = bf16[3,768,640]{2,1,0:T(8,128)(2,1)S(1)} custom-call(s32[768,1]{1,0:T(8,128)S(1)} %copy-done.11, bf16[640,768]{1,0:T(8,128)(2,1)S(1)} %copy-done.30, s32[768,1]{1,0:T(8,128)S(1)} %copy-done.9, bf16[640,768]{1,0:T(8,128)(2,1)S(1)} %copy-done.30, s32[768,1]{1,0:T(8,128)S(1)} %copy-done.9, bf16[640,768]{1,0:T(8,128)(2,1)S(1)} %copy-done.31), custom_call_target="tpu_custom_call" | custom-call | flops 2264924160 | bytes 5898240 | tf_op jit(solution)/shard_map/left_factors/pallas_call | solution.py:638
  185.8 3.8 %weight_back.1 = (bf16[384,1536]{1,0:T(8,128)(2,1)S(1)}, bf16[384,1536]{1,0:T(8,128)(2,1)S(1)}, bf16[384,1536]{1,0:T(8,128)(2,1)S(1)}, bf16[384,1536]{1,0:T(8,128)(2,1)S(1)}) custom-call(bf16[3,768,640]{2,1,0:T(8,128)(2,1)S(1)} %left_factors.3.refs_1_.lhs_ref, bf16[256,2304]{1,0:T(8,128)(2,1)S(1)} %get-tuple-element.173.refs_0_, ...), custom_call_target="tpu_custom_call" | custom-call | flops 3019898880 | bytes 12189696 | tf_op jit(solution)/shard_map/weight_back/pallas_call | solution.py:926
  192.3 5.9 %input_back.1 = (f32[640,768]{1,0:T(8,128)}, f32[8,1536]{1,0:T(8,128)S(1)}) custom-call(bf16[256,2304]{1,0:T(8,128)(2,1)S(1)} %get-tuple-element.173.refs_0_, bf16[384,2304]{1,0:T(8,128)(2,1)S(1)} %get-tuple-element.184.refs_0_.refs_1_, bf16[768,2304]{1,0:T(8,128)(2,1)S(1)} %copy-done.2, bf16[640,768]{1,0:T(8,128)(2,1)S(1)} %copy-done.7, ...), custom_call_target="tpu_custom_call" | custom-call | flops 2264924160 | bytes 10420224 | tf_op jit(solution)/shard_map/input_back/pallas_call | solution.py:968
  203.8 2.4 collective-permute-start.32
  206.5 5.9 %grad_of_down.1 = f32[96,768]{1,0:T(8,128)S(1)} custom-call(bf16[1280,1024]{1,0:T(8,128)(2,1)S(1)} %bitcast.77, bf16[256,768]{1,0:T(8,128)(2,1)S(1)} %bitcast.79, f32[1,256]{1,0:T(1,128)S(1)} %get-tuple-element.197.col_sum_ref, f32[1,256]{1,0:T(1,128)S(1)} %get-tuple-element.198.col_count_ref, f32[1,128]{1,0:T(1,128)S(1)} %get-tuple-element.199.live_ref, ...), custom_call_target="tpu_custom_call" | custom-call | flops 1006632960 | bytes 2621440 | tf_op jit(solution)/shard_map/grad_of_down/pallas_call | solution.py:739
  212.4 5.0 %collective-permute-done.32 = bf16[24,3072]{1,0:T(8,128)(2,1)S(1)} collective-permute-done((bf16[24,3072]{1,0:T(8,128)(2,1)S(1)}, bf16[24,3072]{1,0:T(8,128)(2,1)S(1)}, u32[]{:S(2)}, u32[]{:S(2)}) %collective-permute-start.32) | collective-permute-done | bytes 147488 | tf_op jit(solution)/shard_map/ppermute | solution.py:26
  219.8 6.2 %collective-permute-done.35.got_b = bf16[96,1536]{1,0:T(8,128)(2,1)S(1)} collective-permute-done((bf16[96,1536]{1,0:T(8,128)(2,1)S(1)}, bf16[96,1536]{1,0:T(8,128)(2,1)S(1)}, u32[]{:S(2)}, u32[]{:S(2)}) %collective-permute-start.35) | collective-permute-done | bytes 294944 | tf_op jit(solution)/shard_map/ppermute | solution.py:26
  226.2 2.5 collective-permute-start.36
  234.0 10.2 %collective-permute-done.37 = bf16[32,3072]{1,0:T(8,128)(2,1)S(1)} collective-permute-done((bf16[32,3072]{1,0:T(8,128)(2,1)S(1)}, bf16[32,3072]{1,0:T(8,128)(2,1)S(1)}, u32[]{:S(2)}, u32[]{:S(2)}) %collective-permute-start.37) | collective-permute-done | bytes 196640 | tf_op jit(solution)/shard_map/ppermute | solution.py:26
  (221 shorter events, 73.4 us)
Async XLA Ops:
  7.2 99.6 %all-gather.2.cloned.1.call-start = ((), (), s32[]{:S(2)}) async-start(), calls=%async_computation.2 | async-start | bytes 8921088 | tf_op jit(solution)/shard_map/all_gather | solution.py:1009
  10.3 25.7 %collective-permute-start.2 = (bf16[24,3584]{1,0:T(8,128)(2,1)S(1)}, bf16[24,3584]{1,0:T(8,128)(2,1)S(1)}, u32[]{:S(2)}, u32[]{:S(2)}) collective-permute-start(bf16[24,3584]{1,0:T(8,128)(2,1)S(1)} %pad_maximum_fusion.7), channel_id=1, source_target_pairs={{0,24},{1,25},{2,26},{3,27},{4,28},{5,29},{6,30},{7,31},{8,16},{9,... | collective-permute-start | bytes 516104 | tf_op jit(solution)/shard_map/ppermute | solution.py:26
  15.4 20.6 %collective-permute-start.1 = (bf16[24,3584]{1,0:T(8,128)(2,1)S(1)}, bf16[24,3584]{1,0:T(8,128)(2,1)S(1)}, u32[]{:S(2)}, u32[]{:S(2)}) collective-permute-start(bf16[24,3584]{1,0:T(8,128)(2,1)S(1)} %pad_maximum_fusion.7), channel_id=1, source_target_pairs={{0,16},{1,17},{2,18},{3,19},{4,20},{5,21},{6,22},{7,23},{8,24},{9,... | collective-permute-start | bytes 516104 | tf_op jit(solution)/shard_map/ppermute | solution.py:26
  15.4 20.6 %collective-permute-start = (bf16[24,3584]{1,0:T(8,128)(2,1)S(1)}, bf16[24,3584]{1,0:T(8,128)(2,1)S(1)}, u32[]{:S(2)}, u32[]{:S(2)}) collective-permute-start(bf16[24,3584]{1,0:T(8,128)(2,1)S(1)} %pad_maximum_fusion.7), channel_id=1, source_target_pairs={{0,8},{1,9},{2,10},{3,11},{4,12},{5,13},{6,14},{7,15},{8,0},{9,1},... | collective-permute-start | bytes 516104 | tf_op jit(solution)/shard_map/ppermute | solution.py:26
  37.0 20.7 %collective-permute-start.4 = (bf16[96,3584]{1,0:T(8,128)(2,1)}, bf16[96,3584]{1,0:T(8,128)(2,1)S(1)}, u32[]{:S(2)}, u32[]{:S(2)}) collective-permute-start(bf16[96,3584]{1,0:T(8,128)(2,1)} %pad_maximum_fusion.2.refs_0_), channel_id=1, source_target_pairs={{0,4},{1,5},{2,6},{3,7},{4,0},{5,1},{6,2},{7,3},{8,12},{9,13},{10,... | collective-permute-start | bytes 2064392 | tf_op jit(solution)/shard_map/ppermute | solution.py:26
  38.6 24.1 %collective-permute-start.3 = (bf16[96,3584]{1,0:T(8,128)(2,1)}, bf16[96,3584]{1,0:T(8,128)(2,1)S(1)}, u32[]{:S(2)}, u32[]{:S(2)}) collective-permute-start(bf16[96,3584]{1,0:T(8,128)(2,1)} %pad_maximum_fusion.2.refs_0_), channel_id=1, source_target_pairs={{0,2},{1,3},{2,0},{3,1},{4,6},{5,7},{6,4},{7,5},{8,10},{9,11},{10,... | collective-permute-start | bytes 2064392 | tf_op jit(solution)/shard_map/ppermute | solution.py:26
  65.5 11.0 %collective-permute-start.8 = (bf16[96,3584]{1,0:T(8,128)(2,1)S(1)}, bf16[96,3584]{1,0:T(8,128)(2,1)S(1)}, u32[]{:S(2)}, u32[]{:S(2)}) collective-permute-start(bf16[96,3584]{1,0:T(8,128)(2,1)S(1)} %collective-permute-done.3.refs_1_), channel_id=1, source_target_pairs={{0,1},{1,0},{2,3},{3,2},{4,5},{5,4},{6,7},{7,6},{8,9},{9,8},{10,11... | collective-permute-start | bytes 2064392 | tf_op jit(solution)/shard_map/ppermute | solution.py:26
  66.0 10.5 %collective-permute-start.9 = (bf16[96,3584]{1,0:T(8,128)(2,1)S(1)}, bf16[96,3584]{1,0:T(8,128)(2,1)S(1)}, u32[]{:S(2)}, u32[]{:S(2)}) collective-permute-start(bf16[96,3584]{1,0:T(8,128)(2,1)S(1)} %collective-permute-done.4.refs_2_), channel_id=1, source_target_pairs={{0,1},{1,0},{2,3},{3,2},{4,5},{5,4},{6,7},{7,6},{8,9},{9,8},{10,11... | collective-permute-start | bytes 2064392 | tf_op jit(solution)/shard_map/ppermute | solution.py:26
  73.0 21.8 %collective-permute-start.14 = (bf16[1,40,1024]{2,1,0:T(8,128)(2,1)S(1)}, bf16[1,40,1024]{2,1,0:T(8,128)(2,1)S(1)}, u32[]{:S(2)}, u32[]{:S(2)}) collective-permute-start(bf16[1,40,1024]{2,1,0:T(8,128)(2,1)S(1)} %bitcast.81), channel_id=1, source_target_pairs={{0,24},{1,25},{2,26},{3,27},{4,28},{5,29},{6,30},{7,31},{8,16},{9,... | collective-permute-start | bytes 245768 | tf_op jit(solution)/shard_map/ppermute | solution.py:26
  76.5 18.2 %collective-permute-start.13 = (bf16[1,40,1024]{2,1,0:T(8,128)(2,1)S(1)}, bf16[1,40,1024]{2,1,0:T(8,128)(2,1)S(1)}, u32[]{:S(2)}, u32[]{:S(2)}) collective-permute-start(bf16[1,40,1024]{2,1,0:T(8,128)(2,1)S(1)} %bitcast.82), channel_id=1, source_target_pairs={{0,16},{1,17},{2,18},{3,19},{4,20},{5,21},{6,22},{7,23},{8,24},{9,... | collective-permute-start | bytes 245768 | tf_op jit(solution)/shard_map/ppermute | solution.py:26
  76.5 18.2 %collective-permute-start.12 = (bf16[1,40,1024]{2,1,0:T(8,128)(2,1)S(1)}, bf16[1,40,1024]{2,1,0:T(8,128)(2,1)S(1)}, u32[]{:S(2)}, u32[]{:S(2)}) collective-permute-start(bf16[1,40,1024]{2,1,0:T(8,128)(2,1)S(1)} %bitcast.83), channel_id=1, source_target_pairs={{0,8},{1,9},{2,10},{3,11},{4,12},{5,13},{6,14},{7,15},{8,0},{9,1},... | collective-permute-start | bytes 245768 | tf_op jit(solution)/shard_map/ppermute | solution.py:26
  98.2 17.6 %all-to-all-start = ((bf16[40,32,96]{2,0,1:T(8,128)(2,1)}), bf16[40,32,96]{2,0,1:T(8,128)(2,1)S(1)}, u32[]{:S(2)}, u32[]{:S(2)}) async-start(bf16[40,32,96]{2,0,1:T(8,128)(2,1)} %copy.68), calls=%async_computation | async-start | bytes 655360 | tf_op jit(solution)/shard_map/all_to_all | solution.py:1067
  116.7 20.8 %all-to-all-start.1 = ((bf16[32,8,768]{2,1,0:T(8,128)(2,1)}), bf16[32,8,768]{2,1,0:T(8,128)(2,1)S(1)}, u32[]{:S(2)}, u32[]{:S(2)}) async-start(bf16[32,8,768]{2,1,0:T(8,128)(2,1)} %image_up.1), calls=%async_computation.1 | async-start | bytes 786432 | tf_op jit(solution)/shard_map/all_to_all | solution.py:44
  168.3 15.6 %collective-permute-start.22 = (bf16[192,1536]{1,0:T(8,128)(2,1)S(1)}, bf16[192,1536]{1,0:T(8,128)(2,1)S(1)}, u32[]{:S(2)}, u32[]{:S(2)}) collective-permute-start(bf16[192,1536]{1,0:T(8,128)(2,1)S(1)} %get-tuple-element.179.refs_1_), channel_id=1, source_target_pairs={{0,2},{1,3},{2,0},{3,1},{4,6},{5,7},{6,4},{7,5},{8,10},{9,11},{10,... | collective-permute-start | bytes 1769480 | tf_op jit(solution)/shard_map/ppermute | solution.py:26
  170.1 15.1 %collective-permute-start.23 = (bf16[192,1536]{1,0:T(8,128)(2,1)S(1)}, bf16[192,1536]{1,0:T(8,128)(2,1)S(1)}, u32[]{:S(2)}, u32[]{:S(2)}) collective-permute-start(bf16[192,1536]{1,0:T(8,128)(2,1)S(1)} %get-tuple-element.181.refs_3_), channel_id=1, source_target_pairs={{0,4},{1,5},{2,6},{3,7},{4,0},{5,1},{6,2},{7,3},{8,12},{9,13},{10,... | collective-permute-start | bytes 1769480 | tf_op jit(solution)/shard_map/ppermute | solution.py:26
  189.6 10.9 %collective-permute-start.26 = (bf16[384,1536]{1,0:T(8,128)(2,1)S(1)}, bf16[384,1536]{1,0:T(8,128)(2,1)S(1)}, u32[]{:S(2)}, u32[]{:S(2)}) collective-permute-start(bf16[384,1536]{1,0:T(8,128)(2,1)S(1)} %get-tuple-element.201), channel_id=1, source_target_pairs={{0,1},{1,0},{2,3},{3,2},{4,5},{5,4},{6,7},{7,6},{8,9},{9,8},{10,11... | collective-permute-start | bytes 3538952 | tf_op jit(solution)/shard_map/ppermute | solution.py:26
  189.7 10.8 %collective-permute-start.27 = (bf16[384,1536]{1,0:T(8,128)(2,1)S(1)}, bf16[384,1536]{1,0:T(8,128)(2,1)S(1)}, u32[]{:S(2)}, u32[]{:S(2)}) collective-permute-start(bf16[384,1536]{1,0:T(8,128)(2,1)S(1)} %get-tuple-element.203), channel_id=1, source_target_pairs={{0,1},{1,0},{2,3},{3,2},{4,5},{5,4},{6,7},{7,6},{8,9},{9,8},{10,11... | collective-permute-start | bytes 3538952 | tf_op jit(solution)/shard_map/ppermute | solution.py:26
  201.1 16.3 %collective-permute-start.29 = (bf16[208,1536]{1,0:T(8,128)(2,1)S(1)}, bf16[208,1536]{1,0:T(8,128)(2,1)S(1)}, u32[]{:S(2)}, u32[]{:S(2)}) collective-permute-start(bf16[208,1536]{1,0:T(8,128)(2,1)S(1)} %get-tuple-element.211), channel_id=1, source_target_pairs={{0,2},{1,3},{2,0},{3,1},{4,6},{5,7},{6,4},{7,5},{8,10},{9,11},{10,... | collective-permute-start | bytes 1916936 | tf_op jit(solution)/shard_map/ppermute | solution.py:26
  201.8 15.6 %collective-permute-start.30 = (bf16[192,1536]{1,0:T(8,128)(2,1)S(1)}, bf16[192,1536]{1,0:T(8,128)(2,1)S(1)}, u32[]{:S(2)}, u32[]{:S(2)}) collective-permute-start(bf16[192,1536]{1,0:T(8,128)(2,1)S(1)} %get-tuple-element.213), channel_id=1, source_target_pairs={{0,4},{1,5},{2,6},{3,7},{4,0},{5,1},{6,2},{7,3},{8,12},{9,13},{10,... | collective-permute-start | bytes 1769480 | tf_op jit(solution)/shard_map/ppermute | solution.py:26
  202.1 10.3 %collective-permute-start.31 = (bf16[24,3072]{1,0:T(8,128)(2,1)S(1)}, bf16[24,3072]{1,0:T(8,128)(2,1)S(1)}, u32[]{:S(2)}, u32[]{:S(2)}) collective-permute-start(bf16[24,3072]{1,0:T(8,128)(2,1)S(1)} %get-tuple-element.214), channel_id=1, source_target_pairs={{0,8},{1,9},{2,10},{3,11},{4,12},{5,13},{6,14},{7,15},{8,0},{9,1},... | collective-permute-start | bytes 442376 | tf_op jit(solution)/shard_map/ppermute | solution.py:26
  203.8 13.6 %collective-permute-start.32 = (bf16[24,3072]{1,0:T(8,128)(2,1)S(1)}, bf16[24,3072]{1,0:T(8,128)(2,1)S(1)}, u32[]{:S(2)}, u32[]{:S(2)}) collective-permute-start(bf16[24,3072]{1,0:T(8,128)(2,1)S(1)} %get-tuple-element.215), channel_id=1, source_target_pairs={{0,16},{1,17},{2,18},{3,19},{4,20},{5,21},{6,22},{7,23},{8,24},{9,... | collective-permute-start | bytes 442376 | tf_op jit(solution)/shard_map/ppermute | solution.py:26
  206.2 11.2 %collective-permute-start.33 = (bf16[24,3072]{1,0:T(8,128)(2,1)S(1)}, bf16[24,3072]{1,0:T(8,128)(2,1)S(1)}, u32[]{:S(2)}, u32[]{:S(2)}) collective-permute-start(bf16[24,3072]{1,0:T(8,128)(2,1)S(1)} %get-tuple-element.216), channel_id=1, source_target_pairs={{0,24},{1,25},{2,26},{3,27},{4,28},{5,29},{6,30},{7,31},{8,16},{9,... | collective-permute-start | bytes 442376 | tf_op jit(solution)/shard_map/ppermute | solution.py:26
  228.7 15.6 %collective-permute-start.37 = (bf16[32,3072]{1,0:T(8,128)(2,1)S(1)}, bf16[32,3072]{1,0:T(8,128)(2,1)S(1)}, u32[]{:S(2)}, u32[]{:S(2)}) collective-permute-start(bf16[32,3072]{1,0:T(8,128)(2,1)S(1)} %get-tuple-element.229), channel_id=1, source_target_pairs={{0,16},{1,17},{2,18},{3,19},{4,20},{5,21},{6,22},{7,23},{8,24},{9,... | collective-permute-start | bytes 589832 | tf_op jit(solution)/shard_map/ppermute | solution.py:26
  229.9 14.4 %collective-permute-start.38 = (bf16[32,3072]{1,0:T(8,128)(2,1)S(1)}, bf16[32,3072]{1,0:T(8,128)(2,1)S(1)}, u32[]{:S(2)}, u32[]{:S(2)}) collective-permute-start(bf16[32,3072]{1,0:T(8,128)(2,1)S(1)} %get-tuple-element.230), channel_id=1, source_target_pairs={{0,24},{1,25},{2,26},{3,27},{4,28},{5,29},{6,30},{7,31},{8,16},{9,... | collective-permute-start | bytes 589832 | tf_op jit(solution)/shard_map/ppermute | solution.py:26
  (64 other events, 404.4 us)
Sparse Core Ops, SparseCore 0:
  11.5 95.2 all-gather.1
